TPU v7x, 32 devices: a whole 2x2x4 slice. The times are simulated.
32 devices in a mesh: own: 4 (over y, x), rep: 8 (over z, core).
Axes of the slice: x: 2, y: 2, z: 4, core: 2. Of those that a mesh axis runs over, the one named last changes fastest.
Arguments:
- tokens: bfloat16 [4096, 2048], P(('own', 'rep')), may hold values from -6 to 6
- cotangent: bfloat16 [4096, 2048], P(('own', 'rep')), may hold values from -3 to 3
- route: int32 [4096, 1], P(('own', 'rep')), may hold values from 0 to 7; in each aligned block of 128 rows (0 to 127, 128 to 255, ...) at most 24 rows name the same one
- host: int32 [8], replicated, may hold values from 0 to 7, each once
- w_gate: bfloat16 [8, 2048, 256], P('rep', 'own'), may hold values from -0.125 to 0.125
- w_up: bfloat16 [8, 2048, 256], P('rep', 'own'), may hold values from -0.125 to 0.125
- w_down_t: bfloat16 [8, 2048, 256], P('rep', 'own'), may hold values from -0.375 to 0.375
Outputs:
- x_grad: bfloat16 [4096, 2048], P(('own', 'rep'))
- grad_gate: float32 [8, 2048, 256], P('rep', 'own')
- grad_up: float32 [8, 2048, 256], P('rep', 'own')
- grad_down_t: float32 [8, 2048, 256], P('rep', 'own')
Inputs may be any that keep to these rules, and one draw needn't show every extreme that they name: `route`: among the 128 tokens of one device no hot expert is named more than 24 times, and in every draw some expert is named exactly 24 times on some device. `host`: each replica group serves exactly one hot expert.
All inputs are finite; a program needn't handle non-finite values.
Results may differ from a plain program's by a relative error of at most 0.017.
Values may be sent and summed in bfloat16 or wider, within the bound.
No kernel may reach another device: no remote copies, remote signals or barrier semaphores. Data moves between devices by JAX's collectives and lax.ppermute only.
A program may use at most 64 MiB of HBM per device.

v0:
```python
import jax
import jax.numpy as jnp
from jax import lax
from jax.sharding import PartitionSpec as P


def times_rows(left, right):
    return lax.dot_general(
        left, right, (((1,), (1,)), ((), ())), preferred_element_type=jnp.float32
    )


def first_contract(left, right):
    return lax.dot_general(
        left, right, (((0,), (0,)), ((), ())), preferred_element_type=jnp.float32
    )


def shards(tokens, cotangent, route, host, w_gate, w_up, w_down_t):
    tok_rows, model_width = tokens.shape
    hot_count = host.shape[0]
    hidden_width = w_gate.shape[2]
    capacity = max(2, (3 * tok_rows + 2 * hot_count - 1) // (2 * hot_count))
    slot_rows = hot_count * capacity
    labels = lax.broadcasted_iota(jnp.int32, (tok_rows, hot_count), 1)
    target = jnp.sum(jnp.where(route == labels, host[None, :], 0), axis=1)
    marked = (target[:, None] == labels).astype(jnp.int32)
    arrival = jnp.sum(jnp.cumsum(marked, axis=0) * marked, axis=1) - 1
    position = target * capacity + arrival
    slot_ids = lax.broadcasted_iota(jnp.int32, (slot_rows, tok_rows), 0)
    token_ids = lax.broadcasted_iota(jnp.int32, (slot_rows, tok_rows), 1)
    matched = slot_ids == position[None, :]
    filled = jnp.any(matched, axis=1)
    source_row = jnp.sum(jnp.where(matched, token_ids, 0), axis=1)
    zero_row = jnp.zeros((), jnp.bfloat16)
    send_x = jnp.where(filled[:, None], tokens[source_row], zero_row)
    send_dy = jnp.where(filled[:, None], cotangent[source_row], zero_row)
    recv_x, recv_dy = (
        lax.all_to_all(
            send_x.reshape(hot_count, capacity, model_width),
            "rep",
            split_axis=0,
            concat_axis=0,
            tiled=True,
        ),
        lax.all_to_all(
            send_dy.reshape(hot_count, capacity, model_width),
            "rep",
            split_axis=0,
            concat_axis=0,
            tiled=True,
        ),
    )
    slot_x = recv_x.reshape(slot_rows, model_width)
    slot_dy = recv_dy.reshape(slot_rows, model_width)
    gate_piece = w_gate[0]
    up_piece = w_up[0]
    down_piece = w_down_t[0]
    full_gate, full_up, full_down = (
        lax.all_gather(gate_piece, "own", axis=0, tiled=True),
        lax.all_gather(up_piece, "own", axis=0, tiled=True),
        lax.all_gather(down_piece, "own", axis=0, tiled=True),
    )
    gate_act = jnp.dot(slot_x, full_gate, preferred_element_type=jnp.float32)
    up_act = jnp.dot(slot_x, full_up, preferred_element_type=jnp.float32)
    back_grad = jnp.dot(slot_dy, full_down, preferred_element_type=jnp.float32)
    sigmoid_g = jax.nn.sigmoid(gate_act)
    silu_gate = gate_act * sigmoid_g
    hidden = (silu_gate * up_act).astype(jnp.bfloat16)
    grad_gate_h = (back_grad * up_act * sigmoid_g * (1.0 + gate_act * (1.0 - sigmoid_g))).astype(
        jnp.bfloat16
    )
    grad_up_h = (back_grad * silu_gate).astype(jnp.bfloat16)
    slot_grad = (times_rows(grad_gate_h, full_gate) + times_rows(grad_up_h, full_up)).astype(
        jnp.bfloat16
    )
    returned = lax.all_to_all(
        slot_grad.reshape(hot_count, capacity, model_width),
        "rep",
        split_axis=0,
        concat_axis=0,
        tiled=True,
    )
    x_grad = returned.reshape(slot_rows, model_width)[position]
    summed = lax.psum_scatter(
        jnp.concatenate(
            [
                first_contract(slot_x, grad_gate_h),
                first_contract(slot_x, grad_up_h),
                first_contract(slot_dy, hidden),
            ],
            axis=1,
        ).astype(jnp.bfloat16),
        "own",
        scatter_dimension=0,
        tiled=True,
    ).astype(jnp.float32)
    grad_gate = summed[:, :hidden_width][None]
    grad_up = summed[:, hidden_width : 2 * hidden_width][None]
    grad_down_t = summed[:, 2 * hidden_width :][None]
    return (x_grad, grad_gate, grad_up, grad_down_t)


def solution(mesh):
    return jax.shard_map(
        shards,
        mesh=mesh,
        in_specs=(
            P(("own", "rep"), None),
            P(("own", "rep"), None),
            P(("own", "rep"), None),
            P(),
            P("rep", "own", None),
            P("rep", "own", None),
            P("rep", "own", None),
        ),
        out_specs=(
            P(("own", "rep"), None),
            P("rep", "own", None),
            P("rep", "own", None),
            P("rep", "own", None),
        ),
        check_vma=False,
    )
```

profile of v0, /device:TPU:0, one launch (start us, length us, event | category | flops | bytes accessed | tf_op | source)
XLA Modules:
  0.0 156.0 jit_solution(9186180722055977611)
XLA Ops:
  7.2 0.0 copy-start
  7.2 0.0 all-gather.11.cloned.1.call-start
  7.2 0.7 all-gather.11.cloned.1.call-update
  7.9 0.0 all-gather.9.cloned.1.call-start
  8.0 0.7 all-gather.9.cloned.1.call-update
  8.7 0.8 select_reduce_fusion.2
  9.5 0.1 fusion.12
  9.6 0.2 reduce_window_sum.11
  9.8 0.2 select_reduce_fusion.1
  10.0 0.1 fusion.11
  10.1 0.1 select_reduce_fusion
  10.2 0.1 broadcast_in_dim.53
  10.3 0.0 copy-done
  10.3 0.0 copy-start.1
  10.3 1.1 gather_fusion.1
  11.5 0.0 copy-done.1
  11.5 1.1 gather_fusion
  12.7 1.1 broadcast_select_fusion.1
  13.8 27.1 %all_to_all.15 = bf16[8,24,2048]{2,1,0:T(8,128)(2,1)S(1)} all-to-all(bf16[8,24,2048]{2,1,0:T(8,128)(2,1)S(1)} %get-tuple-element.24), channel_id=1, replica_groups=mesh['own'=4,'rep'=8] {'rep'}, dimensions={0} | all-to-all | bytes 1572864 | tf_op jit(solution)/shard_map/all_to_all | solution.py:39
  40.9 3.5 %all-to-all-start = ((bf16[8,24,2048]{2,1,0:T(8,128)(2,1)}), bf16[8,24,2048]{2,1,0:T(8,128)(2,1)S(1)}, u32[]{:S(2)}, u32[]{:S(2)}) async-start(bf16[8,24,2048]{2,1,0:T(8,128)(2,1)} %get-tuple-element.23), calls=%async_computation | async-start | bytes 1572864 | tf_op jit(solution)/shard_map/all_to_all | solution.py:46
  44.4 0.0 all-gather.7.cloned.1.call-start
  44.5 0.7 all-gather.7.cloned.1.call-update
  45.2 0.0 reduce-scatter.2.cloned.1.call-start
  45.2 0.0 all-gather.11.cloned.1.call-done
  45.2 1.6 %fusion.3 = f32[192,256]{1,0:T(8,128)S(1)} fusion(bf16[192,2048]{1,0:T(8,128)(2,1)S(1)} %bitcast.45, bf16[1,2048,256]{2,1,0:T(8,128)(2,1)} %all-gather.11.cloned.1.call-done), kind=kOutput, calls=%fused_computation.11 | convolution fusion | flops 201326592 | bytes 2031616 | tf_op jit(solution)/shard_map/dot_general | solution.py:64
  46.8 20.9 %all-gather.9.cloned.1.call-done = bf16[1,2048,256]{2,1,0:T(8,128)(2,1)} async-done(((bf16[1,512,256]{2,1,0:T(8,128)(2,1)}), bf16[1,2048,256]{2,1,0:T(8,128)(2,1)}) %all-gather.9.cloned.1.call-update) | async-done | bytes 1048592 | tf_op jit(solution)/shard_map/all_gather | solution.py:61
  67.7 1.6 %fusion.6 = f32[192,256]{1,0:T(8,128)S(1)} fusion(bf16[192,2048]{1,0:T(8,128)(2,1)S(1)} %bitcast.46, bf16[1,2048,256]{2,1,0:T(8,128)(2,1)} %all-gather.9.cloned.1.call-done), kind=kOutput, calls=%fused_computation.14 | convolution fusion | flops 201326592 | bytes 2031616 | tf_op jit(solution)/shard_map/dot_general | solution.py:65
  69.3 0.0 all-to-all-done
  69.4 0.5 convolution_convert_fusion
  69.9 26.4 %all-gather.7.cloned.1.call-done = bf16[1,2048,256]{2,1,0:T(8,128)(2,1)} async-done(((bf16[1,512,256]{2,1,0:T(8,128)(2,1)}), bf16[1,2048,256]{2,1,0:T(8,128)(2,1)}) %all-gather.7.cloned.1.call-update) | async-done | bytes 1048592 | tf_op jit(solution)/shard_map/all_gather | solution.py:62
  96.2 1.6 %multiply_convert_fusion.1 = (bf16[192,256]{1,0:T(8,128)(2,1)S(1)}, bf16[192,256]{1,0:T(8,128)(2,1)S(1)}) fusion(f32[192,256]{1,0:T(8,128)S(1)} %fusion.3, f32[192,256]{1,0:T(8,128)S(1)} %fusion.6, bf16[192,2048]{1,0:T(8,128)(2,1)S(1)} %bitcast.50, bf16[1,2048,256]{2,1,0:T(8,128)(2,1)} %all-gather.7.cloned.1.call-done), kind=kOutput, calls=%fused_computation.24 | convolution fusion | flops 201965568 | bytes 2424832 | tf_op jit(solution)/shard_map/dot_general | solution.py:66
  97.8 0.0 copy-start.4
  97.9 0.0 copy-start.6
  97.9 0.5 convolution_convert_fusion.1
  98.4 0.1 copy-done.4
  98.5 0.0 copy-done.6
  98.5 0.5 convolution_convert_fusion.2
  99.0 1.9 %pad_maximum_fusion = bf16[2048,768]{0,1:T(8,128)(2,1)} fusion(bf16[2048,256]{0,1:T(8,128)(2,1)S(1)} %convolution_convert_fusion, bf16[2048,256]{0,1:T(8,128)(2,1)S(1)} %convolution_convert_fusion.1, bf16[2048,256]{0,1:T(8,128)(2,1)S(1)} %convolution_convert_fusion.2), kind=kLoop, calls=%fused_computation.3 | loop fusion | flops 9437184 | bytes 6291456 | tf_op jit(solution)/shard_map/concatenate | solution.py:86
  100.9 0.0 copy-start.3
  100.9 0.0 copy-start.7
  100.9 0.0 copy-start.2
  100.9 0.0 copy-start.5
  100.9 0.0 reduce-scatter.2.cloned.1.call-update
  100.9 1.2 copy-done.3
  102.1 0.0 copy-done.7
  102.1 0.5 fusion.1
  102.6 0.0 copy-done.2
  102.6 0.0 copy-done.5
  102.6 1.4 fusion
  104.0 4.6 %all-to-all-start.2 = ((bf16[8,24,2048]{2,1,0:T(8,128)(2,1)}), bf16[8,24,2048]{2,1,0:T(8,128)(2,1)S(1)}, u32[]{:S(2)}, u32[]{:S(2)}) async-start(bf16[8,24,2048]{2,1,0:T(8,128)(2,1)} %bitcast.10), calls=%async_computation.2 | async-start | bytes 1572864 | tf_op jit(solution)/shard_map/all_to_all | solution.py:77
  108.6 21.0 %all-to-all-done.2 = bf16[8,24,2048]{2,1,0:T(8,128)(2,1)S(1)} async-done(((bf16[8,24,2048]{2,1,0:T(8,128)(2,1)}), bf16[8,24,2048]{2,1,0:T(8,128)(2,1)S(1)}, u32[]{:S(2)}, u32[]{:S(2)}) %all-to-all-start.2) | async-done | bytes 786464 | tf_op jit(solution)/shard_map/all_to_all | solution.py:77
  129.6 1.7 %gather_fusion.2 = bf16[128,2048]{1,0:T(8,128)(2,1)} fusion(bf16[192,2048]{1,0:T(8,128)(2,1)S(1)} %bitcast.44, s32[1024]{0:T(1024)S(1)} %pad_clamp_fusion), kind=kCustom, calls=%fused_computation.2 | custom fusion | bytes 1049088 | tf_op jit(solution)/shard_map/gather | solution.py:84
  131.3 13.7 %reduce-scatter.2.cloned.1.call-done = bf16[512,768]{0,1:T(8,128)(2,1)} async-done(((bf16[2048,768]{0,1:T(8,128)(2,1)}), bf16[512,768]{0,1:T(8,128)(2,1)}) %reduce-scatter.2.cloned.1.call-update) | async-done | bytes 786448 | tf_op jit(solution)/shard_map/reduce_scatter | solution.py:85
  145.0 1.3 convert_element_type.24
  146.4 0.1 slice_bitcast_fusion
  146.5 1.0 copy.19
  147.5 1.0 copy.18
  148.5 1.0 copy.17
  (4 shorter events, 0.0 us)
Async XLA Ops:
  7.2 3.2 %copy-start = (bf16[128,2048]{1,0:T(8,128)(2,1)S(1)}, bf16[128,2048]{1,0:T(8,128)(2,1)}, u32[]{:S(2)}) copy-start(bf16[128,2048]{1,0:T(8,128)(2,1)} %param.7) | copy-start | bytes 1572868
  7.2 38.0 %all-gather.11.cloned.1.call-start = ((), (), s32[]{:S(2)}) async-start(), calls=%async_computation.7 | async-start | bytes 1310720 | tf_op jit(solution)/shard_map/all_gather | solution.py:60
  7.9 59.8 %all-gather.9.cloned.1.call-start = ((), (), s32[]{:S(2)}) async-start(), calls=%async_computation.6 | async-start | bytes 1310720 | tf_op jit(solution)/shard_map/all_gather | solution.py:61
  10.3 1.2 copy-start.1
  40.9 28.5 %all-to-all-start = ((bf16[8,24,2048]{2,1,0:T(8,128)(2,1)}), bf16[8,24,2048]{2,1,0:T(8,128)(2,1)S(1)}, u32[]{:S(2)}, u32[]{:S(2)}) async-start(bf16[8,24,2048]{2,1,0:T(8,128)(2,1)} %get-tuple-element.23), calls=%async_computation | async-start | bytes 1572864 | tf_op jit(solution)/shard_map/all_to_all | solution.py:46
  44.4 51.8 %all-gather.7.cloned.1.call-start = ((), (), s32[]{:S(2)}) async-start(), calls=%async_computation.5 | async-start | bytes 1310720 | tf_op jit(solution)/shard_map/all_gather | solution.py:62
  45.2 99.9 %reduce-scatter.2.cloned.1.call-start = ((), (), s32[]{:S(2)}) async-start(), calls=%async_computation.4 | async-start | bytes 3932160 | tf_op jit(solution)/shard_map/reduce_scatter | solution.py:85
  97.8 0.6 copy-start.4
  97.9 0.7 copy-start.6
  100.9 1.2 copy-start.3
  100.9 1.2 copy-start.7
  100.9 1.7 %copy-start.2 = (bf16[1,2048,256]{2,1,0:T(8,128)(2,1)S(1)}, bf16[1,2048,256]{2,1,0:T(8,128)(2,1)}, u32[]{:S(2)}) copy-start(bf16[1,2048,256]{2,1,0:T(8,128)(2,1)} %all-gather.9.cloned.1.call-done) | copy-start | bytes 3145732
  100.9 1.7 %copy-start.5 = (bf16[192,256]{1,0:T(8,128)(2,1)S(1)}, bf16[192,256]{1,0:T(8,128)(2,1)}, u32[]{:S(2)}) copy-start(bf16[192,256]{1,0:T(8,128)(2,1)} %copy-done.4) | copy-start | bytes 294916
  104.0 25.6 %all-to-all-start.2 = ((bf16[8,24,2048]{2,1,0:T(8,128)(2,1)}), bf16[8,24,2048]{2,1,0:T(8,128)(2,1)S(1)}, u32[]{:S(2)}, u32[]{:S(2)}) async-start(bf16[8,24,2048]{2,1,0:T(8,128)(2,1)} %bitcast.10), calls=%async_computation.2 | async-start | bytes 1572864 | tf_op jit(solution)/shard_map/all_to_all | solution.py:77
Sparse Core Ops, SparseCore 0:
  9.9 29.3 all-gather.10
  41.1 26.6 all-gather.8
  69.6 26.6 all-gather.6
  101.0 43.9 reduce-scatter.1
where the time goes:
time: 156 us
  waiting for transfers between devices  84 us (54%)
  blocking collectives  27.1 us (17%)
  between operations  14 us (9%)
  local copies, waits for them, and re-layouts  8.6 us (6%)
  starting transfers between devices  8.32 us (5%)
  matrix products  8.19 us (5%)
  other arithmetic  5.85 us (4%)
    all_to_all x1, blocking collectives, shards(): lax.all_to_all(send_x.reshape(hot_count, capacity, model_width), 'rep', s...  27.1 us
    all_gather x1, waiting for transfers between devices, shards(): lax.all_gather(down_piece, 'own', axis=0, tiled=True)  26.4 us
    all_to_all x1, waiting for transfers between devices, shards(): lax.all_to_all(slot_grad.reshape(hot_count, capacity, model_width), 'rep'...  21 us
    all_gather x1, waiting for transfers between devices, shards(): lax.all_gather(up_piece, 'own', axis=0, tiled=True)  20.9 us
    reduce_scatter x1, waiting for transfers between devices, shards(): lax.psum_scatter(jnp.concatenate([first_contract(slot_x, grad_gate_h), fi...  13.7 us
    all_to_all x1, starting transfers between devices, shards(): lax.all_to_all(slot_grad.reshape(hot_count, capacity, model_width), 'rep'...  4.62 us
    unnamed x19, local copies, waits for them, and re-layouts  4.37 us
    all_to_all x1, starting transfers between devices, shards(): lax.all_to_all(send_dy.reshape(hot_count, capacity, model_width), 'rep',...  3.55 us
  transfers between devices with their start and end apart: 6, of which 4 were waited for; matrix products, arithmetic and copies ran while one was open for 8% of the time, Pallas kernels for 0%

commit v1 on v0

v1 whole, which is shorter than its diff:
```python
import functools

import jax
import jax.numpy as jnp
from jax import lax
from jax.experimental import pallas as pl
from jax.experimental.pallas import tpu as pltpu
from jax.sharding import PartitionSpec as P

VMEM = pl.BlockSpec(memory_space=pltpu.VMEM)
SMEM = pl.BlockSpec(memory_space=pltpu.SMEM)
PARAMS = pltpu.CompilerParams(vmem_limit_bytes=48 * 1024 * 1024)


def dot(left, right, left_dim, right_dim):
    return lax.dot_general(
        left, right, (((left_dim,), (right_dim,)), ((), ())), preferred_element_type=jnp.float32
    )


def pack_kernel(hot, capacity, parts, rank_ref, host_ref, route_ref, x_ref, dy_ref, pick_ref, *send_refs):
    rows = route_ref.shape[0]
    lanes = pick_ref.shape[1]
    width = max(128, hot)
    lane = lax.broadcasted_iota(jnp.int32, (rows, width), 1)
    base = jnp.zeros((1, width), jnp.int32)
    lane_row = lax.broadcasted_iota(jnp.int32, (1, width), 1)
    for e in range(hot):
        base = jnp.where(lane_row == e, (host_ref[e] ^ rank_ref[0]) * capacity, base)
    marked = route_ref[...] == lane
    marked_f = jnp.where(marked, 1.0, 0.0)
    earlier = jnp.where(
        lax.broadcasted_iota(jnp.int32, (rows, rows), 1) < lax.broadcasted_iota(jnp.int32, (rows, rows), 0), 1.0, 0.0
    )
    before = dot(earlier.astype(jnp.bfloat16), marked_f.astype(jnp.bfloat16), 1, 0).astype(jnp.int32)
    position = jnp.sum(jnp.where(marked, before + base, 0), axis=1, keepdims=True)
    pick = jnp.where(lax.broadcasted_iota(jnp.int32, (rows, lanes), 1) == position, 1.0, 0.0)
    pick_ref[...] = pick.astype(jnp.bfloat16)
    turned = pick.T.astype(jnp.bfloat16)
    if parts == 1:
        send_refs[0][...] = jnp.concatenate(
            [dot(turned, x_ref[...], 1, 0), dot(turned, dy_ref[...], 1, 0)], axis=1
        ).astype(jnp.bfloat16)
        return
    for which, ref in enumerate((x_ref, dy_ref)):
        filled = dot(turned, ref[...], 1, 0)
        for k in range(parts):
            send_refs[2 * k + which][...] = filled[k * capacity : (k + 1) * capacity].astype(jnp.bfloat16)


def main_kernel(n_own, parts, capacity, own_ref, x_ref, dy_ref, *refs):
    gates, ups, downs = refs[:n_own], refs[n_own : 2 * n_own], refs[2 * n_own : 3 * n_own]
    back_refs = refs[3 * n_own : 3 * n_own + parts]
    own_term_ref, *term_refs = refs[3 * n_own + parts :]
    slots = x_ref.shape[0]
    depth, hidden_width = gates[0].shape
    own = own_ref[0]
    columns = [pl.ds(pl.multiple_of((own ^ k) * depth, depth), depth) for k in range(n_own)]
    gate_act = jnp.zeros((slots, hidden_width), jnp.float32)
    up_act = jnp.zeros((slots, hidden_width), jnp.float32)
    back_grad = jnp.zeros((slots, hidden_width), jnp.float32)
    for k in range(n_own):
        x_part = x_ref[:, columns[k]]
        gate_act += dot(x_part, gates[k][...], 1, 0)
        up_act += dot(x_part, ups[k][...], 1, 0)
        back_grad += dot(dy_ref[:, columns[k]], downs[k][...], 1, 0)
    sigmoid_g = jax.nn.sigmoid(gate_act)
    silu_gate = gate_act * sigmoid_g
    hidden = (silu_gate * up_act).astype(jnp.bfloat16)
    grad_gate_h = (back_grad * up_act * sigmoid_g * (1.0 + gate_act * (1.0 - sigmoid_g))).astype(jnp.bfloat16)
    grad_up_h = (back_grad * silu_gate).astype(jnp.bfloat16)
    for k in range(n_own):
        slot_grad = dot(grad_gate_h, gates[k][...], 1, 1) + dot(grad_up_h, ups[k][...], 1, 1)
        rows = slots // parts
        for j in range(parts):
            back_refs[j][:, columns[k]] = slot_grad[j * rows : (j + 1) * rows].astype(jnp.bfloat16)
    for k in range(n_own):
        x_part = x_ref[:, columns[k]]
        terms = (
            dot(x_part, grad_gate_h, 0, 0),
            dot(x_part, grad_up_h, 0, 0),
            dot(dy_ref[:, columns[k]], hidden, 0, 0),
        )
        into = own_term_ref if k == 0 else term_refs[k - 1]
        for i, term in enumerate(terms):
            into[:, i * hidden_width : (i + 1) * hidden_width] = term.astype(into.dtype)


def sum_kernel(n_terms, own_ref, *refs):
    hidden_width = refs[-1].shape[1]
    for i, out_ref in enumerate(refs[n_terms:]):
        at = slice(i * hidden_width, (i + 1) * hidden_width)
        total = own_ref[:, at]
        for ref in refs[:n_terms]:
            total = total + ref[:, at].astype(jnp.float32)
        out_ref[...] = total


def shards(n_own, n_rep, tokens, cotangent, route, host, w_gate, w_up, w_down_t):
    tok_rows, model_width = tokens.shape
    hot = host.shape[0]
    hidden_width = w_gate.shape[2]
    depth = w_gate.shape[1]
    capacity = max(2, (3 * tok_rows + 2 * hot - 1) // (2 * hot))
    slots = hot * capacity
    own = lax.axis_index("own").astype(jnp.int32).reshape(1)
    rank = lax.axis_index("rep").astype(jnp.int32).reshape(1)
    parts = n_rep if capacity % 8 == 0 else 1

    def swap(value, axis, size, k):
        return lax.ppermute(value, axis, [(i, i ^ k) for i in range(size)])

    def gather(piece):
        return [piece] + [swap(piece, "own", n_own, k) for k in range(1, n_own)]

    gates, ups, downs = gather(w_gate[0]), gather(w_up[0]), gather(w_down_t[0])

    if parts > 1:
        sends = [jax.ShapeDtypeStruct((capacity, model_width), jnp.bfloat16)] * (2 * parts)
    else:
        sends = [jax.ShapeDtypeStruct((slots, 2 * model_width), jnp.bfloat16)]
        rank = jnp.zeros_like(rank)
    pick, *sent = pl.pallas_call(
        functools.partial(pack_kernel, hot, capacity, parts),
        out_shape=[jax.ShapeDtypeStruct((tok_rows, slots), jnp.bfloat16)] + sends,
        in_specs=[SMEM, SMEM, VMEM, VMEM, VMEM],
        out_specs=[VMEM] * (1 + len(sends)),
        compiler_params=PARAMS,
    )(rank, host, route, tokens, cotangent)

    def whole_exchange(value):
        return lax.all_to_all(
            value.reshape(hot, capacity, -1), "rep", split_axis=0, concat_axis=0, tiled=True
        ).reshape(slots, -1)

    if parts > 1:
        got = sent[:2] + [swap(sent[i], "rep", n_rep, i // 2) for i in range(2, 2 * parts)]
        slot_x, slot_dy = jnp.concatenate(got[0::2]), jnp.concatenate(got[1::2])
    else:
        got = whole_exchange(sent[0])
        slot_x, slot_dy = got[:, :model_width], got[:, model_width:]

    backs = [jax.ShapeDtypeStruct((slots // parts, model_width), jnp.bfloat16)] * parts
    term = (depth, 3 * hidden_width)
    terms = [jax.ShapeDtypeStruct(term, jnp.float32)] + [jax.ShapeDtypeStruct(term, jnp.bfloat16)] * (n_own - 1)
    outs = pl.pallas_call(
        functools.partial(main_kernel, n_own, parts, capacity),
        out_shape=backs + terms,
        in_specs=[SMEM] + [VMEM] * (2 + 3 * n_own),
        out_specs=[VMEM] * (parts + n_own),
        compiler_params=PARAMS,
    )(own, slot_x, slot_dy, *gates, *ups, *downs)
    back, own_term, sent_terms = outs[:parts], outs[parts], outs[parts + 1 :]

    if parts > 1:
        returned = jnp.concatenate([back[0]] + [swap(back[k], "rep", n_rep, k) for k in range(1, parts)])
    else:
        returned = whole_exchange(back[0])
    got_terms = [swap(sent_terms[k - 1], "own", n_own, k) for k in range(1, n_own)]
    x_grad = dot(pick, returned, 1, 0).astype(jnp.bfloat16)
    grads = pl.pallas_call(
        functools.partial(sum_kernel, n_own - 1),
        out_shape=[jax.ShapeDtypeStruct((depth, hidden_width), jnp.float32)] * 3,
        in_specs=[VMEM] * n_own,
        out_specs=[VMEM] * 3,
        compiler_params=PARAMS,
    )(own_term, *got_terms)
    return (x_grad, *(grad[None] for grad in grads))


def solution(mesh):
    return jax.shard_map(
        functools.partial(shards, mesh.shape["own"], mesh.shape["rep"]),
        mesh=mesh,
        in_specs=(
            P(("own", "rep"), None),
            P(("own", "rep"), None),
            P(("own", "rep"), None),
            P(),
            P("rep", "own", None),
            P("rep", "own", None),
            P("rep", "own", None),
        ),
        out_specs=(
            P(("own", "rep"), None),
            P("rep", "own", None),
            P("rep", "own", None),
            P("rep", "own", None),
        ),
        check_vma=False,
    )
```

time: 156 us -> 142 us (0.910); the launches traced: 156 us -> 140 us
  starting transfers between devices: 8.32 us -> 44.4 us
  blocking collectives: 27.1 us -> 0 us
  between operations: 14 us -> 0.75 us
  waiting for transfers between devices: 84 us -> 72 us
  Pallas kernels: 0 us -> 8.16 us
  matrix products: 8.19 us -> 1.09 us
  other arithmetic: 5.85 us -> 0 us
  local copies, waits for them, and re-layouts: 8.6 us -> 13.2 us
    ppermute x0 -> x33, waiting for transfers between devices: none -> 72 us  [swap(): return lax.ppermute(value, axis, [(i, i ^ k) for i in range(size)])]
    all_gather x3 -> x0, waiting for transfers between devices: 47.3 us -> none  [the longest x1 26.4 us: shards(): lax.all_gather(down_piece, 'own', axis=0, tiled=True)]
    ppermute x0 -> x33, starting transfers between devices: none -> 44.4 us  [swap(): return lax.ppermute(value, axis, [(i, i ^ k) for i in range(size)])]
    all_to_all x1 -> x0, blocking collectives: 27.1 us -> none  [shards(): lax.all_to_all(send_x.reshape(hot_count, capacity, model_width), 'rep', s...]
    all_to_all x2 -> x0, waiting for transfers between devices: 21 us -> none  [the longest x1 21 us: shards(): lax.all_to_all(slot_grad.reshape(hot_count, capacity, model_width), 'rep'...]
    reduce_scatter x1 -> x0, waiting for transfers between devices: 13.7 us -> none  [shards(): lax.psum_scatter(jnp.concatenate([first_contract(slot_x, grad_gate_h), fi...]
    all_to_all x2 -> x0, starting transfers between devices: 8.16 us -> none  [the longest x1 4.62 us: shards(): lax.all_to_all(slot_grad.reshape(hot_count, capacity, model_width), 'rep'...]
    pallas_call x0 -> x3, Pallas kernels: none -> 8.16 us  [the longest x1 5.34 us: shards(): pl.pallas_call(functools.partial(main_kernel, n_own, parts, capacity), ou...]
  transfers between devices with their start and end apart: 6 -> 33, of which waited for: 4 -> 17; matrix products, arithmetic and copies ran while one was open for 8% -> 8% of each run, Pallas kernels for 0% -> 1%
where the time goes in v1:
time: 142 us; the launch traced here: 140 us
  waiting for transfers between devices  72 us (51%)
  starting transfers between devices  44.4 us (31%)
  local copies, waits for them, and re-layouts  13.2 us (9%)
  Pallas kernels  8.16 us (6%)
    ppermute x33, waiting for transfers between devices, swap(): return lax.ppermute(value, axis, [(i, i ^ k) for i in range(size)])  72 us
    ppermute x33, starting transfers between devices, swap(): return lax.ppermute(value, axis, [(i, i ^ k) for i in range(size)])  44.4 us
    unnamed x35, local copies, waits for them, and re-layouts  11.9 us
    pallas_call x1, Pallas kernels, shards(): pl.pallas_call(functools.partial(main_kernel, n_own, parts, capacity), ou...  5.34 us
  transfers between devices with their start and end apart: 33, of which 17 were waited for; matrix products, arithmetic and copies ran while one was open for 8% of the time, Pallas kernels for 1%

profile of v1, /device:TPU:0, one launch (start us, length us, event | category | flops | bytes accessed | tf_op | source)
XLA Modules:
  0.0 139.5 jit_solution(8543032319950137086)
XLA Ops:
  0.6 4.0 %collective-permute-start.16 = (bf16[512,256]{1,0:T(8,128)(2,1)}, bf16[512,256]{1,0:T(8,128)(2,1)S(1)}, u32[]{:S(2)}, u32[]{:S(2)}) collective-permute-start(bf16[512,256]{1,0:T(8,128)(2,1)} %bitcast.10), channel_id=1, source_target_pairs={{0,24},{8,16},{16,8},{24,0},{1,25},{9,17},{17,9},{25,1},{2,26},{10... | collective-permute-start | bytes 786440 | tf_op jit(solution)/shard_map/ppermute | solution.py:111
  4.6 0.5 collective-permute-start.15
  5.2 0.8 copy.11.route_ref
  6.0 1.0 copy-done.1
  7.0 1.0 copy-done.2
  8.1 0.7 copy-done.6
  8.7 1.5 %shard_map.102 = (bf16[128,192]{1,0:T(8,128)(2,1)S(1)}, bf16[24,2048]{1,0:T(8,128)(2,1)S(1)}, bf16[24,2048]{1,0:T(8,128)(2,1)S(1)}, bf16[24,2048]{1,0:T(8,128)(2...) custom-call(s32[1]{0:T(128)} %bitcast.rank_ref, ...), custom_call_target="tpu_custom_call" | custom-call | tf_op jit(solution)/shard_map/pallas_call | solution.py:123
  10.3 2.0 %collective-permute-start.1 = (bf16[24,2048]{1,0:T(8,128)(2,1)S(1)}, bf16[24,2048]{1,0:T(8,128)(2,1)S(1)}, u32[]{:S(2)}, u32[]{:S(2)}) collective-permute-start(bf16[24,2048]{1,0:T(8,128)(2,1)S(1)} %get-tuple-element.39), channel_id=1, source_target_pairs={{0,2},{1,3},{2,0},{3,1},{4,6},{5,7},{6,4},{7,5},{8,10},{9,11},{10,... | collective-permute-start | bytes 294920 | tf_op jit(solution)/shard_map/ppermute | solution.py:111
  12.3 0.7 constant_dynamic-update-slice_fusion.7
  13.3 0.6 constant_dynamic-update-slice_fusion.6
  13.9 1.8 %collective-permute-done.1 = bf16[24,2048]{1,0:T(8,128)(2,1)S(1)} collective-permute-done((bf16[24,2048]{1,0:T(8,128)(2,1)S(1)}, bf16[24,2048]{1,0:T(8,128)(2,1)S(1)}, u32[]{:S(2)}, u32[]{:S(2)}) %collective-permute-start.1) | collective-permute-done | bytes 98336 | tf_op jit(solution)/shard_map/ppermute | solution.py:111
  15.7 2.8 %collective-permute-start.3 = (bf16[24,2048]{1,0:T(8,128)(2,1)S(1)}, bf16[24,2048]{1,0:T(8,128)(2,1)S(1)}, u32[]{:S(2)}, u32[]{:S(2)}) collective-permute-start(bf16[24,2048]{1,0:T(8,128)(2,1)S(1)} %get-tuple-element.41), channel_id=1, source_target_pairs={{0,4},{1,5},{2,6},{3,7},{4,0},{5,1},{6,2},{7,3},{8,12},{9,13},{10,... | collective-permute-start | bytes 294920 | tf_op jit(solution)/shard_map/ppermute | solution.py:111
  18.5 0.6 constant_dynamic-update-slice_fusion.5
  19.1 1.0 collective-permute-start.4
  20.1 0.7 constant_dynamic-update-slice_fusion.4
  20.8 2.7 %collective-permute-done.3 = bf16[24,2048]{1,0:T(8,128)(2,1)S(1)} collective-permute-done((bf16[24,2048]{1,0:T(8,128)(2,1)S(1)}, bf16[24,2048]{1,0:T(8,128)(2,1)S(1)}, u32[]{:S(2)}, u32[]{:S(2)}) %collective-permute-start.3) | collective-permute-done | bytes 98336 | tf_op jit(solution)/shard_map/ppermute | solution.py:111
  23.5 5.6 %collective-permute-start.5 = (bf16[24,2048]{1,0:T(8,128)(2,1)S(1)}, bf16[24,2048]{1,0:T(8,128)(2,1)S(1)}, u32[]{:S(2)}, u32[]{:S(2)}) collective-permute-start(bf16[24,2048]{1,0:T(8,128)(2,1)S(1)} %get-tuple-element.43), channel_id=1, source_target_pairs={{0,6},{1,7},{2,4},{3,5},{4,2},{5,3},{6,0},{7,1},{8,14},{9,15},{10,... | collective-permute-start | bytes 294920 | tf_op jit(solution)/shard_map/ppermute | solution.py:111
  29.1 0.6 constant_dynamic-update-slice_fusion.3
  29.8 0.9 collective-permute-start.6
  30.6 0.6 constant_dynamic-update-slice_fusion.2
  31.3 0.5 collective-permute-done.5
  31.8 0.6 constant_dynamic-update-slice_fusion.1
  32.4 3.8 %collective-permute-done.6 = bf16[24,2048]{1,0:T(8,128)(2,1)S(1)} collective-permute-done((bf16[24,2048]{1,0:T(8,128)(2,1)S(1)}, bf16[24,2048]{1,0:T(8,128)(2,1)S(1)}, u32[]{:S(2)}, u32[]{:S(2)}) %collective-permute-start.6) | collective-permute-done | bytes 98336 | tf_op jit(solution)/shard_map/ppermute | solution.py:111
  36.6 0.6 constant_dynamic-update-slice_fusion.x_ref
  37.2 0.7 collective-permute-start.9
  37.9 0.6 constant_dynamic-update-slice_fusion.14
  38.5 3.1 %collective-permute-done.8 = bf16[24,2048]{1,0:T(8,128)(2,1)S(1)} collective-permute-done((bf16[24,2048]{1,0:T(8,128)(2,1)S(1)}, bf16[24,2048]{1,0:T(8,128)(2,1)S(1)}, u32[]{:S(2)}, u32[]{:S(2)}) %collective-permute-start.8) | collective-permute-done | bytes 98336 | tf_op jit(solution)/shard_map/ppermute | solution.py:111
  41.6 2.3 %collective-permute-start.10 = (bf16[24,2048]{1,0:T(8,128)(2,1)S(1)}, bf16[24,2048]{1,0:T(8,128)(2,1)S(1)}, u32[]{:S(2)}, u32[]{:S(2)}) collective-permute-start(bf16[24,2048]{1,0:T(8,128)(2,1)S(1)} %get-tuple-element.49), channel_id=1, source_target_pairs={{0,4},{1,5},{2,6},{3,7},{4,0},{5,1},{6,2},{7,3},{8,12},{9,13},{10,... | collective-permute-start | bytes 294920 | tf_op jit(solution)/shard_map/ppermute | solution.py:111
  43.9 0.6 constant_dynamic-update-slice_fusion.13
  44.7 0.6 constant_dynamic-update-slice_fusion.12
  45.4 4.8 %collective-permute-done.10 = bf16[24,2048]{1,0:T(8,128)(2,1)S(1)} collective-permute-done((bf16[24,2048]{1,0:T(8,128)(2,1)S(1)}, bf16[24,2048]{1,0:T(8,128)(2,1)S(1)}, u32[]{:S(2)}, u32[]{:S(2)}) %collective-permute-start.10) | collective-permute-done | bytes 98336 | tf_op jit(solution)/shard_map/ppermute | solution.py:111
  50.2 2.4 %collective-permute-start.19 = (bf16[512,256]{1,0:T(8,128)(2,1)S(1)}, bf16[512,256]{1,0:T(8,128)(2,1)S(1)}, u32[]{:S(2)}, u32[]{:S(2)}) collective-permute-start(bf16[512,256]{1,0:T(8,128)(2,1)S(1)} %bitcast.14), channel_id=1, source_target_pairs={{0,24},{8,16},{16,8},{24,0},{1,25},{9,17},{17,9},{25,1},{2,26},{10... | collective-permute-start | bytes 786440 | tf_op jit(solution)/shard_map/ppermute | solution.py:111
  52.7 1.8 %collective-permute-start.12 = (bf16[24,2048]{1,0:T(8,128)(2,1)S(1)}, bf16[24,2048]{1,0:T(8,128)(2,1)S(1)}, u32[]{:S(2)}, u32[]{:S(2)}) collective-permute-start(bf16[24,2048]{1,0:T(8,128)(2,1)S(1)} %get-tuple-element.51), channel_id=1, source_target_pairs={{0,6},{1,7},{2,4},{3,5},{4,2},{5,3},{6,0},{7,1},{8,14},{9,15},{10,... | collective-permute-start | bytes 294920 | tf_op jit(solution)/shard_map/ppermute | solution.py:111
  54.5 0.6 constant_dynamic-update-slice_fusion.11
  55.1 4.0 %collective-permute-done.12 = bf16[24,2048]{1,0:T(8,128)(2,1)S(1)} collective-permute-done((bf16[24,2048]{1,0:T(8,128)(2,1)S(1)}, bf16[24,2048]{1,0:T(8,128)(2,1)S(1)}, u32[]{:S(2)}, u32[]{:S(2)}) %collective-permute-start.12) | collective-permute-done | bytes 98336 | tf_op jit(solution)/shard_map/ppermute | solution.py:111
  59.1 0.9 collective-permute-start.13
  60.0 0.6 constant_dynamic-update-slice_fusion.10
  60.7 4.3 %collective-permute-done.13 = bf16[24,2048]{1,0:T(8,128)(2,1)S(1)} collective-permute-done((bf16[24,2048]{1,0:T(8,128)(2,1)S(1)}, bf16[24,2048]{1,0:T(8,128)(2,1)S(1)}, u32[]{:S(2)}, u32[]{:S(2)}) %collective-permute-start.13) | collective-permute-done | bytes 98336 | tf_op jit(solution)/shard_map/ppermute | solution.py:111
  65.0 1.4 %collective-permute-start.18 = (bf16[512,256]{1,0:T(8,128)(2,1)S(1)}, bf16[512,256]{1,0:T(8,128)(2,1)S(1)}, u32[]{:S(2)}, u32[]{:S(2)}) collective-permute-start(bf16[512,256]{1,0:T(8,128)(2,1)S(1)} %bitcast.15), channel_id=1, source_target_pairs={{0,16},{8,24},{16,0},{24,8},{1,17},{9,25},{17,1},{25,9},{2,18},{10... | collective-permute-start | bytes 786440 | tf_op jit(solution)/shard_map/ppermute | solution.py:111
  66.4 1.5 %collective-permute-start.17 = (bf16[512,256]{1,0:T(8,128)(2,1)S(1)}, bf16[512,256]{1,0:T(8,128)(2,1)S(1)}, u32[]{:S(2)}, u32[]{:S(2)}) collective-permute-start(bf16[512,256]{1,0:T(8,128)(2,1)S(1)} %bitcast.16), channel_id=1, source_target_pairs={{0,8},{8,0},{16,24},{24,16},{1,9},{9,1},{17,25},{25,17},{2,10},{10... | collective-permute-start | bytes 786440 | tf_op jit(solution)/shard_map/ppermute | solution.py:111
  67.9 0.6 collective-permute-start.22
  68.5 1.4 %collective-permute-start.21 = (bf16[512,256]{1,0:T(8,128)(2,1)S(1)}, bf16[512,256]{1,0:T(8,128)(2,1)S(1)}, u32[]{:S(2)}, u32[]{:S(2)}) collective-permute-start(bf16[512,256]{1,0:T(8,128)(2,1)S(1)} %bitcast.19), channel_id=1, source_target_pairs={{0,16},{8,24},{16,0},{24,8},{1,17},{9,25},{17,1},{25,9},{2,18},{10... | collective-permute-start | bytes 786440 | tf_op jit(solution)/shard_map/ppermute | solution.py:111
  69.9 1.5 %collective-permute-start.20 = (bf16[512,256]{1,0:T(8,128)(2,1)S(1)}, bf16[512,256]{1,0:T(8,128)(2,1)S(1)}, u32[]{:S(2)}, u32[]{:S(2)}) collective-permute-start(bf16[512,256]{1,0:T(8,128)(2,1)S(1)} %bitcast.20), channel_id=1, source_target_pairs={{0,8},{8,0},{16,24},{24,16},{1,9},{9,1},{17,25},{25,17},{2,10},{10... | collective-permute-start | bytes 786440 | tf_op jit(solution)/shard_map/ppermute | solution.py:111
  71.4 0.6 constant_dynamic-update-slice_fusion.9
  72.0 0.6 constant_dynamic-update-slice_fusion.8.dy_ref
  72.7 5.7 %collective-permute-done.18.refs_6_ = bf16[512,256]{1,0:T(8,128)(2,1)S(1)} collective-permute-done((bf16[512,256]{1,0:T(8,128)(2,1)S(1)}, bf16[512,256]{1,0:T(8,128)(2,1)S(1)}, u32[]{:S(2)}, u32[]{:S(2)}) %collective-permute-start.18) | collective-permute-done | bytes 262176 | tf_op jit(solution)/shard_map/ppermute | solution.py:111
  78.3 3.0 %collective-permute-done.22.refs_11_ = bf16[512,256]{1,0:T(8,128)(2,1)S(1)} collective-permute-done((bf16[512,256]{1,0:T(8,128)(2,1)S(1)}, bf16[512,256]{1,0:T(8,128)(2,1)S(1)}, u32[]{:S(2)}, u32[]{:S(2)}) %collective-permute-start.22) | collective-permute-done | bytes 262176 | tf_op jit(solution)/shard_map/ppermute | solution.py:111
  81.4 2.5 %collective-permute-done.21.refs_10_ = bf16[512,256]{1,0:T(8,128)(2,1)S(1)} collective-permute-done((bf16[512,256]{1,0:T(8,128)(2,1)S(1)}, bf16[512,256]{1,0:T(8,128)(2,1)S(1)}, u32[]{:S(2)}, u32[]{:S(2)}) %collective-permute-start.21) | collective-permute-done | bytes 262176 | tf_op jit(solution)/shard_map/ppermute | solution.py:111
  83.9 1.5 %collective-permute-done.20.refs_9_ = bf16[512,256]{1,0:T(8,128)(2,1)S(1)} collective-permute-done((bf16[512,256]{1,0:T(8,128)(2,1)S(1)}, bf16[512,256]{1,0:T(8,128)(2,1)S(1)}, u32[]{:S(2)}, u32[]{:S(2)}) %collective-permute-start.20) | collective-permute-done | bytes 262176 | tf_op jit(solution)/shard_map/ppermute | solution.py:111
  85.4 5.3 %shard_map.103 = (bf16[24,2048]{1,0:T(8,128)(2,1)S(1)}, bf16[24,2048]{1,0:T(8,128)(2,1)S(1)}, bf16[24,2048]{1,0:T(8,128)(2,1)S(1)}, bf16[24,2048]{1,0:T(8,128)(2...) custom-call(s32[1]{0:T(128)} %bitcast.1.own_ref, ...), custom_call_target="tpu_custom_call" | custom-call | tf_op jit(solution)/shard_map/pallas_call | solution.py:146
  90.8 1.9 %collective-permute-start.25 = (bf16[24,2048]{1,0:T(8,128)(2,1)S(1)}, bf16[24,2048]{1,0:T(8,128)(2,1)S(1)}, u32[]{:S(2)}, u32[]{:S(2)}) collective-permute-start(bf16[24,2048]{1,0:T(8,128)(2,1)S(1)} %get-tuple-element.56), channel_id=1, source_target_pairs={{0,3},{1,2},{2,1},{3,0},{4,7},{5,6},{6,5},{7,4},{8,11},{9,10},{10,... | collective-permute-start | bytes 294920 | tf_op jit(solution)/shard_map/ppermute | solution.py:111
  92.6 1.2 collective-permute-start.26
  93.8 1.3 collective-permute-start.27
  95.2 2.4 %collective-permute-start.28 = (bf16[24,2048]{1,0:T(8,128)(2,1)S(1)}, bf16[24,2048]{1,0:T(8,128)(2,1)S(1)}, u32[]{:S(2)}, u32[]{:S(2)}) collective-permute-start(bf16[24,2048]{1,0:T(8,128)(2,1)S(1)} %get-tuple-element.59), channel_id=1, source_target_pairs={{0,6},{1,7},{2,4},{3,5},{4,2},{5,3},{6,0},{7,1},{8,14},{9,15},{10,... | collective-permute-start | bytes 294920 | tf_op jit(solution)/shard_map/ppermute | solution.py:111
  97.6 1.4 collective-permute-start.29
  99.0 1.1 collective-permute-done.25
  100.1 1.5 %collective-permute-start.30 = (bf16[512,768]{1,0:T(8,128)(2,1)S(1)}, bf16[512,768]{1,0:T(8,128)(2,1)S(1)}, u32[]{:S(2)}, u32[]{:S(2)}) collective-permute-start(bf16[512,768]{1,0:T(8,128)(2,1)S(1)} %get-tuple-element.62), channel_id=1, source_target_pairs={{0,8},{8,0},{16,24},{24,16},{1,9},{9,1},{17,25},{25,17},{2,10},{10... | collective-permute-start | bytes 2359304 | tf_op jit(solution)/shard_map/ppermute | solution.py:111
  101.6 6.0 %collective-permute-done.26 = bf16[24,2048]{1,0:T(8,128)(2,1)S(1)} collective-permute-done((bf16[24,2048]{1,0:T(8,128)(2,1)S(1)}, bf16[24,2048]{1,0:T(8,128)(2,1)S(1)}, u32[]{:S(2)}, u32[]{:S(2)}) %collective-permute-start.26) | collective-permute-done | bytes 98336 | tf_op jit(solution)/shard_map/ppermute | solution.py:111
  107.8 0.6 collective-permute-done.27
  108.4 2.2 %collective-permute-start.32 = (bf16[512,768]{1,0:T(8,128)(2,1)}, bf16[512,768]{1,0:T(8,128)(2,1)S(1)}, u32[]{:S(2)}, u32[]{:S(2)}) collective-permute-start(bf16[512,768]{1,0:T(8,128)(2,1)} %get-tuple-element.64), channel_id=1, source_target_pairs={{0,24},{8,16},{16,8},{24,0},{1,25},{9,17},{17,9},{25,1},{2,26},{10... | collective-permute-start | bytes 2359304 | tf_op jit(solution)/shard_map/ppermute | solution.py:111
  110.7 1.1 convolution_convert_fusion
  111.8 8.6 %collective-permute-done.30.refs_0_ = bf16[512,768]{1,0:T(8,128)(2,1)S(1)} collective-permute-done((bf16[512,768]{1,0:T(8,128)(2,1)S(1)}, bf16[512,768]{1,0:T(8,128)(2,1)S(1)}, u32[]{:S(2)}, u32[]{:S(2)}) %collective-permute-start.30) | collective-permute-done | bytes 786464 | tf_op jit(solution)/shard_map/ppermute | solution.py:111
  120.4 17.7 %collective-permute-done.31.refs_1_ = bf16[512,768]{1,0:T(8,128)(2,1)S(1)} collective-permute-done((bf16[512,768]{1,0:T(8,128)(2,1)S(1)}, bf16[512,768]{1,0:T(8,128)(2,1)S(1)}, u32[]{:S(2)}, u32[]{:S(2)}) %collective-permute-start.31) | collective-permute-done | bytes 786464 | tf_op jit(solution)/shard_map/ppermute | solution.py:111
  138.2 1.4 shard_map.104
  (44 shorter events, 1.3 us)
Async XLA Ops:
  0.6 65.8 %collective-permute-start.16 = (bf16[512,256]{1,0:T(8,128)(2,1)}, bf16[512,256]{1,0:T(8,128)(2,1)S(1)}, u32[]{:S(2)}, u32[]{:S(2)}) collective-permute-start(bf16[512,256]{1,0:T(8,128)(2,1)} %bitcast.10), channel_id=1, source_target_pairs={{0,24},{8,16},{16,8},{24,0},{1,25},{9,17},{17,9},{25,1},{2,26},{10... | collective-permute-start | bytes 786440 | tf_op jit(solution)/shard_map/ppermute | solution.py:111
  4.6 63.3 %collective-permute-start.15 = (bf16[512,256]{1,0:T(8,128)(2,1)}, bf16[512,256]{1,0:T(8,128)(2,1)S(1)}, u32[]{:S(2)}, u32[]{:S(2)}) collective-permute-start(bf16[512,256]{1,0:T(8,128)(2,1)} %bitcast.11), channel_id=1, source_target_pairs={{0,16},{8,24},{16,0},{24,8},{1,17},{9,25},{17,1},{25,9},{2,18},{10... | collective-permute-start | bytes 786440 | tf_op jit(solution)/shard_map/ppermute | solution.py:111
  5.1 63.4 %collective-permute-start.14 = (bf16[512,256]{1,0:T(8,128)(2,1)}, bf16[512,256]{1,0:T(8,128)(2,1)S(1)}, u32[]{:S(2)}, u32[]{:S(2)}) collective-permute-start(bf16[512,256]{1,0:T(8,128)(2,1)} %bitcast.12), channel_id=1, source_target_pairs={{0,8},{8,0},{16,24},{24,16},{1,9},{9,1},{17,25},{25,17},{2,10},{10... | collective-permute-start | bytes 786440 | tf_op jit(solution)/shard_map/ppermute | solution.py:111
  6.0 1.0 copy-start.1
  7.0 1.0 copy-start.2
  8.1 0.7 copy-start.6
  8.7 41.5 %copy-start.4 = (bf16[1,512,256]{2,1,0:T(8,128)(2,1)S(1)}, bf16[1,512,256]{2,1,0:T(8,128)(2,1)}, u32[]{:S(2)}) copy-start(bf16[1,512,256]{2,1,0:T(8,128)(2,1)} %param.12) | copy-start | bytes 786436
  10.2 57.7 %copy-start.5 = (bf16[1,512,256]{2,1,0:T(8,128)(2,1)S(1)}, bf16[1,512,256]{2,1,0:T(8,128)(2,1)}, u32[]{:S(2)}) copy-start(bf16[1,512,256]{2,1,0:T(8,128)(2,1)} %param.13) | copy-start | bytes 786436
  10.2 2.8 %collective-permute-start = (bf16[24,2048]{1,0:T(8,128)(2,1)S(1)}, bf16[24,2048]{1,0:T(8,128)(2,1)S(1)}, u32[]{:S(2)}, u32[]{:S(2)}) collective-permute-start(bf16[24,2048]{1,0:T(8,128)(2,1)S(1)} %get-tuple-element.38), channel_id=1, source_target_pairs={{0,1},{1,0},{2,3},{3,2},{4,5},{5,4},{6,7},{7,6},{8,9},{9,8},{10,11... | collective-permute-start | bytes 294920 | tf_op jit(solution)/shard_map/ppermute | solution.py:111
  10.3 5.4 %collective-permute-start.1 = (bf16[24,2048]{1,0:T(8,128)(2,1)S(1)}, bf16[24,2048]{1,0:T(8,128)(2,1)S(1)}, u32[]{:S(2)}, u32[]{:S(2)}) collective-permute-start(bf16[24,2048]{1,0:T(8,128)(2,1)S(1)} %get-tuple-element.39), channel_id=1, source_target_pairs={{0,2},{1,3},{2,0},{3,1},{4,6},{5,7},{6,4},{7,5},{8,10},{9,11},{10,... | collective-permute-start | bytes 294920 | tf_op jit(solution)/shard_map/ppermute | solution.py:111
  12.3 73.1 %copy-start.3 = (bf16[1,512,256]{2,1,0:T(8,128)(2,1)S(1)}, bf16[1,512,256]{2,1,0:T(8,128)(2,1)}, u32[]{:S(2)}) copy-start(bf16[1,512,256]{2,1,0:T(8,128)(2,1)} %param.11) | copy-start | bytes 786436
  13.0 6.1 %collective-permute-start.2 = (bf16[24,2048]{1,0:T(8,128)(2,1)S(1)}, bf16[24,2048]{1,0:T(8,128)(2,1)S(1)}, u32[]{:S(2)}, u32[]{:S(2)}) collective-permute-start(bf16[24,2048]{1,0:T(8,128)(2,1)S(1)} %get-tuple-element.40), channel_id=1, source_target_pairs={{0,3},{1,2},{2,1},{3,0},{4,7},{5,6},{6,5},{7,4},{8,11},{9,10},{10,... | collective-permute-start | bytes 294920 | tf_op jit(solution)/shard_map/ppermute | solution.py:111
  15.7 7.8 %collective-permute-start.3 = (bf16[24,2048]{1,0:T(8,128)(2,1)S(1)}, bf16[24,2048]{1,0:T(8,128)(2,1)S(1)}, u32[]{:S(2)}, u32[]{:S(2)}) collective-permute-start(bf16[24,2048]{1,0:T(8,128)(2,1)S(1)} %get-tuple-element.41), channel_id=1, source_target_pairs={{0,4},{1,5},{2,6},{3,7},{4,0},{5,1},{6,2},{7,3},{8,12},{9,13},{10,... | collective-permute-start | bytes 294920 | tf_op jit(solution)/shard_map/ppermute | solution.py:111
  19.1 10.6 %collective-permute-start.4 = (bf16[24,2048]{1,0:T(8,128)(2,1)S(1)}, bf16[24,2048]{1,0:T(8,128)(2,1)S(1)}, u32[]{:S(2)}, u32[]{:S(2)}) collective-permute-start(bf16[24,2048]{1,0:T(8,128)(2,1)S(1)} %get-tuple-element.42), channel_id=1, source_target_pairs={{0,5},{1,4},{2,7},{3,6},{4,1},{5,0},{6,3},{7,2},{8,13},{9,12},{10,... | collective-permute-start | bytes 294920 | tf_op jit(solution)/shard_map/ppermute | solution.py:111
  23.5 8.3 %collective-permute-start.5 = (bf16[24,2048]{1,0:T(8,128)(2,1)S(1)}, bf16[24,2048]{1,0:T(8,128)(2,1)S(1)}, u32[]{:S(2)}, u32[]{:S(2)}) collective-permute-start(bf16[24,2048]{1,0:T(8,128)(2,1)S(1)} %get-tuple-element.43), channel_id=1, source_target_pairs={{0,6},{1,7},{2,4},{3,5},{4,2},{5,3},{6,0},{7,1},{8,14},{9,15},{10,... | collective-permute-start | bytes 294920 | tf_op jit(solution)/shard_map/ppermute | solution.py:111
  29.8 6.5 %collective-permute-start.6 = (bf16[24,2048]{1,0:T(8,128)(2,1)S(1)}, bf16[24,2048]{1,0:T(8,128)(2,1)S(1)}, u32[]{:S(2)}, u32[]{:S(2)}) collective-permute-start(bf16[24,2048]{1,0:T(8,128)(2,1)S(1)} %get-tuple-element.44), channel_id=1, source_target_pairs={{0,7},{1,6},{2,5},{3,4},{4,3},{5,2},{6,1},{7,0},{8,15},{9,14},{10,... | collective-permute-start | bytes 294920 | tf_op jit(solution)/shard_map/ppermute | solution.py:111
  31.8 5.4 %collective-permute-start.7 = (bf16[24,2048]{1,0:T(8,128)(2,1)S(1)}, bf16[24,2048]{1,0:T(8,128)(2,1)S(1)}, u32[]{:S(2)}, u32[]{:S(2)}) collective-permute-start(bf16[24,2048]{1,0:T(8,128)(2,1)S(1)} %get-tuple-element.46), channel_id=1, source_target_pairs={{0,1},{1,0},{2,3},{3,2},{4,5},{5,4},{6,7},{7,6},{8,9},{9,8},{10,11... | collective-permute-start | bytes 294920 | tf_op jit(solution)/shard_map/ppermute | solution.py:111
  36.3 5.4 %collective-permute-start.8 = (bf16[24,2048]{1,0:T(8,128)(2,1)S(1)}, bf16[24,2048]{1,0:T(8,128)(2,1)S(1)}, u32[]{:S(2)}, u32[]{:S(2)}) collective-permute-start(bf16[24,2048]{1,0:T(8,128)(2,1)S(1)} %get-tuple-element.47), channel_id=1, source_target_pairs={{0,2},{1,3},{2,0},{3,1},{4,6},{5,7},{6,4},{7,5},{8,10},{9,11},{10,... | collective-permute-start | bytes 294920 | tf_op jit(solution)/shard_map/ppermute | solution.py:111
  37.2 7.3 %collective-permute-start.9 = (bf16[24,2048]{1,0:T(8,128)(2,1)S(1)}, bf16[24,2048]{1,0:T(8,128)(2,1)S(1)}, u32[]{:S(2)}, u32[]{:S(2)}) collective-permute-start(bf16[24,2048]{1,0:T(8,128)(2,1)S(1)} %get-tuple-element.48), channel_id=1, source_target_pairs={{0,3},{1,2},{2,1},{3,0},{4,7},{5,6},{6,5},{7,4},{8,11},{9,10},{10,... | collective-permute-start | bytes 294920 | tf_op jit(solution)/shard_map/ppermute | solution.py:111
  41.6 8.6 %collective-permute-start.10 = (bf16[24,2048]{1,0:T(8,128)(2,1)S(1)}, bf16[24,2048]{1,0:T(8,128)(2,1)S(1)}, u32[]{:S(2)}, u32[]{:S(2)}) collective-permute-start(bf16[24,2048]{1,0:T(8,128)(2,1)S(1)} %get-tuple-element.49), channel_id=1, source_target_pairs={{0,4},{1,5},{2,6},{3,7},{4,0},{5,1},{6,2},{7,3},{8,12},{9,13},{10,... | collective-permute-start | bytes 294920 | tf_op jit(solution)/shard_map/ppermute | solution.py:111
  44.5 8.1 %collective-permute-start.11 = (bf16[24,2048]{1,0:T(8,128)(2,1)S(1)}, bf16[24,2048]{1,0:T(8,128)(2,1)S(1)}, u32[]{:S(2)}, u32[]{:S(2)}) collective-permute-start(bf16[24,2048]{1,0:T(8,128)(2,1)S(1)} %get-tuple-element.50), channel_id=1, source_target_pairs={{0,5},{1,4},{2,7},{3,6},{4,1},{5,0},{6,3},{7,2},{8,13},{9,12},{10,... | collective-permute-start | bytes 294920 | tf_op jit(solution)/shard_map/ppermute | solution.py:111
  50.2 19.7 %collective-permute-start.19 = (bf16[512,256]{1,0:T(8,128)(2,1)S(1)}, bf16[512,256]{1,0:T(8,128)(2,1)S(1)}, u32[]{:S(2)}, u32[]{:S(2)}) collective-permute-start(bf16[512,256]{1,0:T(8,128)(2,1)S(1)} %bitcast.14), channel_id=1, source_target_pairs={{0,24},{8,16},{16,8},{24,0},{1,25},{9,17},{17,9},{25,1},{2,26},{10... | collective-permute-start | bytes 786440 | tf_op jit(solution)/shard_map/ppermute | solution.py:111
  52.7 6.5 %collective-permute-start.12 = (bf16[24,2048]{1,0:T(8,128)(2,1)S(1)}, bf16[24,2048]{1,0:T(8,128)(2,1)S(1)}, u32[]{:S(2)}, u32[]{:S(2)}) collective-permute-start(bf16[24,2048]{1,0:T(8,128)(2,1)S(1)} %get-tuple-element.51), channel_id=1, source_target_pairs={{0,6},{1,7},{2,4},{3,5},{4,2},{5,3},{6,0},{7,1},{8,14},{9,15},{10,... | collective-permute-start | bytes 294920 | tf_op jit(solution)/shard_map/ppermute | solution.py:111
  59.1 5.8 %collective-permute-start.13 = (bf16[24,2048]{1,0:T(8,128)(2,1)S(1)}, bf16[24,2048]{1,0:T(8,128)(2,1)S(1)}, u32[]{:S(2)}, u32[]{:S(2)}) collective-permute-start(bf16[24,2048]{1,0:T(8,128)(2,1)S(1)} %get-tuple-element.52), channel_id=1, source_target_pairs={{0,7},{1,6},{2,5},{3,4},{4,3},{5,2},{6,1},{7,0},{8,15},{9,14},{10,... | collective-permute-start | bytes 294920 | tf_op jit(solution)/shard_map/ppermute | solution.py:111
  65.0 13.3 %collective-permute-start.18 = (bf16[512,256]{1,0:T(8,128)(2,1)S(1)}, bf16[512,256]{1,0:T(8,128)(2,1)S(1)}, u32[]{:S(2)}, u32[]{:S(2)}) collective-permute-start(bf16[512,256]{1,0:T(8,128)(2,1)S(1)} %bitcast.15), channel_id=1, source_target_pairs={{0,16},{8,24},{16,0},{24,8},{1,17},{9,25},{17,1},{25,9},{2,18},{10... | collective-permute-start | bytes 786440 | tf_op jit(solution)/shard_map/ppermute | solution.py:111
  66.4 11.9 %collective-permute-start.17 = (bf16[512,256]{1,0:T(8,128)(2,1)S(1)}, bf16[512,256]{1,0:T(8,128)(2,1)S(1)}, u32[]{:S(2)}, u32[]{:S(2)}) collective-permute-start(bf16[512,256]{1,0:T(8,128)(2,1)S(1)} %bitcast.16), channel_id=1, source_target_pairs={{0,8},{8,0},{16,24},{24,16},{1,9},{9,1},{17,25},{25,17},{2,10},{10... | collective-permute-start | bytes 786440 | tf_op jit(solution)/shard_map/ppermute | solution.py:111
  67.9 13.5 %collective-permute-start.22 = (bf16[512,256]{1,0:T(8,128)(2,1)S(1)}, bf16[512,256]{1,0:T(8,128)(2,1)S(1)}, u32[]{:S(2)}, u32[]{:S(2)}) collective-permute-start(bf16[512,256]{1,0:T(8,128)(2,1)S(1)} %bitcast.18), channel_id=1, source_target_pairs={{0,24},{8,16},{16,8},{24,0},{1,25},{9,17},{17,9},{25,1},{2,26},{10... | collective-permute-start | bytes 786440 | tf_op jit(solution)/shard_map/ppermute | solution.py:111
  68.5 15.4 %collective-permute-start.21 = (bf16[512,256]{1,0:T(8,128)(2,1)S(1)}, bf16[512,256]{1,0:T(8,128)(2,1)S(1)}, u32[]{:S(2)}, u32[]{:S(2)}) collective-permute-start(bf16[512,256]{1,0:T(8,128)(2,1)S(1)} %bitcast.19), channel_id=1, source_target_pairs={{0,16},{8,24},{16,0},{24,8},{1,17},{9,25},{17,1},{25,9},{2,18},{10... | collective-permute-start | bytes 786440 | tf_op jit(solution)/shard_map/ppermute | solution.py:111
  69.9 15.5 %collective-permute-start.20 = (bf16[512,256]{1,0:T(8,128)(2,1)S(1)}, bf16[512,256]{1,0:T(8,128)(2,1)S(1)}, u32[]{:S(2)}, u32[]{:S(2)}) collective-permute-start(bf16[512,256]{1,0:T(8,128)(2,1)S(1)} %bitcast.20), channel_id=1, source_target_pairs={{0,8},{8,0},{16,24},{24,16},{1,9},{9,1},{17,25},{25,17},{2,10},{10... | collective-permute-start | bytes 786440 | tf_op jit(solution)/shard_map/ppermute | solution.py:111
  90.8 47.4 %copy-start = (f32[512,768]{1,0:T(8,128)S(1)}, f32[512,768]{1,0:T(8,128)}, u32[]{:S(2)}) copy-start(f32[512,768]{1,0:T(8,128)} %get-tuple-element.61.own_ref) | copy-start | bytes 4718596
  90.8 4.4 %collective-permute-start.23 = (bf16[24,2048]{1,0:T(8,128)(2,1)S(1)}, bf16[24,2048]{1,0:T(8,128)(2,1)S(1)}, u32[]{:S(2)}, u32[]{:S(2)}) collective-permute-start(bf16[24,2048]{1,0:T(8,128)(2,1)S(1)} %get-tuple-element.54), channel_id=1, source_target_pairs={{0,1},{1,0},{2,3},{3,2},{4,5},{5,4},{6,7},{7,6},{8,9},{9,8},{10,11... | collective-permute-start | bytes 294920 | tf_op jit(solution)/shard_map/ppermute | solution.py:111
  90.8 6.9 %collective-permute-start.24 = (bf16[24,2048]{1,0:T(8,128)(2,1)S(1)}, bf16[24,2048]{1,0:T(8,128)(2,1)S(1)}, u32[]{:S(2)}, u32[]{:S(2)}) collective-permute-start(bf16[24,2048]{1,0:T(8,128)(2,1)S(1)} %get-tuple-element.55), channel_id=1, source_target_pairs={{0,2},{1,3},{2,0},{3,1},{4,6},{5,7},{6,4},{7,5},{8,10},{9,11},{10,... | collective-permute-start | bytes 294920 | tf_op jit(solution)/shard_map/ppermute | solution.py:111
  90.8 9.3 %collective-permute-start.25 = (bf16[24,2048]{1,0:T(8,128)(2,1)S(1)}, bf16[24,2048]{1,0:T(8,128)(2,1)S(1)}, u32[]{:S(2)}, u32[]{:S(2)}) collective-permute-start(bf16[24,2048]{1,0:T(8,128)(2,1)S(1)} %get-tuple-element.56), channel_id=1, source_target_pairs={{0,3},{1,2},{2,1},{3,0},{4,7},{5,6},{6,5},{7,4},{8,11},{9,10},{10,... | collective-permute-start | bytes 294920 | tf_op jit(solution)/shard_map/ppermute | solution.py:111
  92.6 15.0 %collective-permute-start.26 = (bf16[24,2048]{1,0:T(8,128)(2,1)S(1)}, bf16[24,2048]{1,0:T(8,128)(2,1)S(1)}, u32[]{:S(2)}, u32[]{:S(2)}) collective-permute-start(bf16[24,2048]{1,0:T(8,128)(2,1)S(1)} %get-tuple-element.57), channel_id=1, source_target_pairs={{0,4},{1,5},{2,6},{3,7},{4,0},{5,1},{6,2},{7,3},{8,12},{9,13},{10,... | collective-permute-start | bytes 294920 | tf_op jit(solution)/shard_map/ppermute | solution.py:111
  93.8 14.6 %collective-permute-start.27 = (bf16[24,2048]{1,0:T(8,128)(2,1)S(1)}, bf16[24,2048]{1,0:T(8,128)(2,1)S(1)}, u32[]{:S(2)}, u32[]{:S(2)}) collective-permute-start(bf16[24,2048]{1,0:T(8,128)(2,1)S(1)} %get-tuple-element.58), channel_id=1, source_target_pairs={{0,5},{1,4},{2,7},{3,6},{4,1},{5,0},{6,3},{7,2},{8,13},{9,12},{10,... | collective-permute-start | bytes 294920 | tf_op jit(solution)/shard_map/ppermute | solution.py:111
  95.2 15.5 %collective-permute-start.28 = (bf16[24,2048]{1,0:T(8,128)(2,1)S(1)}, bf16[24,2048]{1,0:T(8,128)(2,1)S(1)}, u32[]{:S(2)}, u32[]{:S(2)}) collective-permute-start(bf16[24,2048]{1,0:T(8,128)(2,1)S(1)} %get-tuple-element.59), channel_id=1, source_target_pairs={{0,6},{1,7},{2,4},{3,5},{4,2},{5,3},{6,0},{7,1},{8,14},{9,15},{10,... | collective-permute-start | bytes 294920 | tf_op jit(solution)/shard_map/ppermute | solution.py:111
  97.6 13.1 %collective-permute-start.29 = (bf16[24,2048]{1,0:T(8,128)(2,1)S(1)}, bf16[24,2048]{1,0:T(8,128)(2,1)S(1)}, u32[]{:S(2)}, u32[]{:S(2)}) collective-permute-start(bf16[24,2048]{1,0:T(8,128)(2,1)S(1)} %get-tuple-element.60), channel_id=1, source_target_pairs={{0,7},{1,6},{2,5},{3,4},{4,3},{5,2},{6,1},{7,0},{8,15},{9,14},{10,... | collective-permute-start | bytes 294920 | tf_op jit(solution)/shard_map/ppermute | solution.py:111
  100.1 20.3 %collective-permute-start.30 = (bf16[512,768]{1,0:T(8,128)(2,1)S(1)}, bf16[512,768]{1,0:T(8,128)(2,1)S(1)}, u32[]{:S(2)}, u32[]{:S(2)}) collective-permute-start(bf16[512,768]{1,0:T(8,128)(2,1)S(1)} %get-tuple-element.62), channel_id=1, source_target_pairs={{0,8},{8,0},{16,24},{24,16},{1,9},{9,1},{17,25},{25,17},{2,10},{10... | collective-permute-start | bytes 2359304 | tf_op jit(solution)/shard_map/ppermute | solution.py:111
  107.6 30.5 %collective-permute-start.31 = (bf16[512,768]{1,0:T(8,128)(2,1)S(1)}, bf16[512,768]{1,0:T(8,128)(2,1)S(1)}, u32[]{:S(2)}, u32[]{:S(2)}) collective-permute-start(bf16[512,768]{1,0:T(8,128)(2,1)S(1)} %get-tuple-element.63), channel_id=1, source_target_pairs={{0,16},{8,24},{16,0},{24,8},{1,17},{9,25},{17,1},{25,9},{2,18},{10... | collective-permute-start | bytes 2359304 | tf_op jit(solution)/shard_map/ppermute | solution.py:111
  108.4 29.7 %collective-permute-start.32 = (bf16[512,768]{1,0:T(8,128)(2,1)}, bf16[512,768]{1,0:T(8,128)(2,1)S(1)}, u32[]{:S(2)}, u32[]{:S(2)}) collective-permute-start(bf16[512,768]{1,0:T(8,128)(2,1)} %get-tuple-element.64), channel_id=1, source_target_pairs={{0,24},{8,16},{16,8},{24,0},{1,25},{9,17},{17,9},{25,1},{2,26},{10... | collective-permute-start | bytes 2359304 | tf_op jit(solution)/shard_map/ppermute | solution.py:111

commit v2 on v0

v2 whole, which is shorter than its diff:
```python
import functools

import jax
import jax.numpy as jnp
from jax import lax
from jax.experimental import pallas as pl
from jax.experimental.pallas import tpu as pltpu
from jax.sharding import PartitionSpec as P

VMEM = pl.BlockSpec(memory_space=pltpu.VMEM)
SMEM = pl.BlockSpec(memory_space=pltpu.SMEM)
HBM = pl.BlockSpec(memory_space=pltpu.HBM)
PARAMS = pltpu.CompilerParams(vmem_limit_bytes=48 * 1024 * 1024)
BF16 = jnp.bfloat16
F32 = jnp.float32


def dot(left, right, left_dim, right_dim):
    return lax.dot_general(
        left, right, (((left_dim,), (right_dim,)), ((), ())), preferred_element_type=F32
    )


def shape(rows, cols, dtype=BF16):
    return jax.ShapeDtypeStruct((rows, cols), dtype)


def call(kernel, outs, scalars, scratch=(), fetched=0):
    def run(*operands):
        placed = len(operands) - scalars - fetched
        return pl.pallas_call(
            kernel,
            out_shape=outs,
            in_specs=[SMEM] * scalars + [VMEM] * placed + [HBM] * fetched,
            out_specs=[VMEM] * len(outs),
            scratch_shapes=list(scratch),
            compiler_params=PARAMS,
        )(*operands)

    return run


def join_kernel(gate_ref, up_ref, down_ref, first_ref, second_ref, sems):
    depth = gate_ref.shape[0]
    half = depth // 2
    moves = (
        (gate_ref, first_ref.at[pl.ds(0, depth)]),
        (up_ref.at[pl.ds(0, half)], first_ref.at[pl.ds(depth, half)]),
        (up_ref.at[pl.ds(half, half)], second_ref.at[pl.ds(0, half)]),
        (down_ref, second_ref.at[pl.ds(half, depth)]),
    )
    loads = [pltpu.make_async_copy(source, into, sems.at[i]) for i, (source, into) in enumerate(moves)]
    for load in loads:
        load.start()
    for load in loads:
        load.wait()


def pack_kernel(capacity, rank_ref, host_ref, route_a, route_b, x_b, dy_b, *refs):
    sources, (pick_ref, *send_refs), (x_a, dy_a, sems) = refs[:2], refs[2:-3], refs[-3:]
    loads = [
        pltpu.make_async_copy(source, into, sems.at[i]) for i, (source, into) in enumerate(zip(sources, (x_a, dy_a)))
    ]
    for load in loads:
        load.start()
    hot = host_ref.shape[0]
    slots = pick_ref.shape[0]
    tokens = route_a.shape[1]
    block = 2 * capacity
    label = lax.broadcasted_iota(jnp.int32, (hot, tokens), 0)
    base = jnp.zeros((hot, tokens), jnp.int32)
    for e in range(hot):
        apart = host_ref[e] ^ rank_ref[0]
        start = jnp.where((apart & 1) == 0, (apart >> 1) * block, -2 * slots)
        base = jnp.where(label == e, start, base)
    earlier = lax.broadcasted_iota(jnp.int32, (tokens, tokens), 0) < lax.broadcasted_iota(
        jnp.int32, (tokens, tokens), 1
    )
    earlier = jnp.where(earlier, 1.0, 0.0).astype(BF16)
    slot = lax.broadcasted_iota(jnp.int32, (slots, tokens), 0)

    def picks(route_ref, offset):
        marked = route_ref[...] == label
        before = dot(jnp.where(marked, 1.0, 0.0).astype(BF16), earlier, 1, 0).astype(jnp.int32)
        position = jnp.sum(jnp.where(marked, before + base, 0), axis=0, keepdims=True) + offset
        return jnp.where(slot == position, 1.0, 0.0).astype(BF16)

    pick_a, pick_b = picks(route_a, 0), picks(route_b, capacity)
    pick_ref[:, :tokens] = pick_a
    pick_ref[:, tokens:] = pick_b
    for at, (a, b) in enumerate(((x_a, x_b), (dy_a, dy_b))):
        loads[at].wait()
        filled = (dot(pick_a, a[...], 1, 0) + dot(pick_b, b[...], 1, 0)).astype(BF16)
        for k, ref in enumerate(send_refs):
            ref[at * block : (at + 1) * block] = filled[k * block : (k + 1) * block]


def main_kernel(parts, own_ref, *refs):
    got, weights = refs[:parts], refs[parts : parts + 8]
    back_refs = refs[parts + 8 : 2 * parts + 8]
    own_term, one_a, one_b, two_a, two_b, three_a, three_b, x_ref, dy_ref = refs[2 * parts + 8 :]
    block = got[0].shape[0] // 2
    depth = weights[0].shape[0] * 2 // 3
    half = depth // 2
    own = own_ref[0]
    for k in range(parts):
        x_ref[k * block : (k + 1) * block] = got[k][:block]
        dy_ref[k * block : (k + 1) * block] = got[k][block:]

    def gate(k):
        return weights[2 * k][:depth]

    def up(k):
        return jnp.concatenate([weights[2 * k][depth:], weights[2 * k + 1][:half]], axis=0)

    def down(k):
        return weights[2 * k + 1][half:]

    columns = [pl.ds(pl.multiple_of((own ^ k) * depth, depth), depth) for k in range(4)]
    gate_act = sum(dot(x_ref[:, columns[k]], gate(k), 1, 0) for k in range(4))
    up_act = sum(dot(x_ref[:, columns[k]], up(k), 1, 0) for k in range(4))
    back_grad = sum(dot(dy_ref[:, columns[k]], down(k), 1, 0) for k in range(4))
    sigmoid_g = jax.nn.sigmoid(gate_act)
    silu_gate = gate_act * sigmoid_g
    hidden = (silu_gate * up_act).astype(BF16)
    grad_gate_h = (back_grad * up_act * sigmoid_g * (1.0 + gate_act * (1.0 - sigmoid_g))).astype(BF16)
    grad_up_h = (back_grad * silu_gate).astype(BF16)
    for k in range(4):
        slot_grad = (dot(grad_gate_h, gate(k), 1, 1) + dot(grad_up_h, up(k), 1, 1)).astype(BF16)
        for j in range(parts):
            back_refs[j][:, columns[k]] = slot_grad[j * block : (j + 1) * block]
    width = hidden.shape[1]
    for k, into in ((3, (three_a, three_b)), (1, (one_a, one_b)), (2, (two_a, two_b)), (0, (own_term,))):
        x_part, dy_part = x_ref[:, columns[k]], dy_ref[:, columns[k]]
        terms = (dot(x_part, grad_gate_h, 0, 0), dot(x_part, grad_up_h, 0, 0), dot(dy_part, hidden, 0, 0))
        rows = depth // len(into)
        for i, term in enumerate(terms):
            for j, ref in enumerate(into):
                ref[:, i * width : (i + 1) * width] = term[j * rows : (j + 1) * rows].astype(ref.dtype)


def sum_kernel(own_ref, one_a, two_a, one_b, two_b, *out_refs):
    width = out_refs[0].shape[1]
    half = one_a.shape[0]
    for i, out_ref in enumerate(out_refs):
        at = slice(i * width, (i + 1) * width)
        out_ref[:half] = own_ref[:half, at] + one_a[:, at].astype(F32) + two_a[:, at].astype(F32)
        out_ref[half:] = own_ref[half:, at] + one_b[:, at].astype(F32) + two_b[:, at].astype(F32)


def unpack_kernel(pick_ref, *refs):
    returned, (mine_ref, other_ref) = refs[:-2], refs[-2:]
    tokens = mine_ref.shape[0]
    block = returned[0].shape[0]
    for at, ref in enumerate((other_ref, mine_ref)):
        half = slice((1 - at) * tokens, (2 - at) * tokens)
        ref[...] = sum(
            dot(pick_ref[k * block : (k + 1) * block, half], part[...], 0, 0) for k, part in enumerate(returned)
        ).astype(BF16)


def shards_by_partner(n_rep, tokens, cotangent, route, host, w_gate, w_up, w_down_t):
    tok_rows, model_width = tokens.shape
    hot = host.shape[0]
    _, depth, width = w_gate.shape
    half = depth // 2
    capacity = (3 * tok_rows + 2 * hot - 1) // (2 * hot)
    slots = hot * capacity
    parts = n_rep // 2
    block = 2 * capacity
    own = lax.axis_index("own").astype(jnp.int32).reshape(1)
    rank = lax.axis_index("rep").astype(jnp.int32).reshape(1)

    def over_own(value, k):
        return lax.ppermute(value, "own", [(i, i ^ k) for i in range(4)])

    def over_rep(value, k):
        return lax.ppermute(value, "rep", [(i, i ^ k) for i in range(n_rep)])

    route = route.reshape(1, tok_rows)
    route_b, tokens_b, cotangent_b = over_rep(route, 1), over_rep(tokens, 1), over_rep(cotangent, 1)

    first, second = call(
        join_kernel, [shape(3 * half, width)] * 2, 0, [pltpu.SemaphoreType.DMA((4,))], 3
    )(w_gate[0], w_up[0], w_down_t[0])
    first_1, second_2 = over_own(first, 1), over_own(second, 2)

    pick, *sent = call(
        functools.partial(pack_kernel, capacity),
        [shape(slots, 2 * tok_rows)] + [shape(2 * block, model_width)] * parts,
        2,
        [pltpu.VMEM((tok_rows, model_width), BF16)] * 2 + [pltpu.SemaphoreType.DMA((2,))],
        2,
    )(rank, host, route, route_b, tokens_b, cotangent_b, tokens, cotangent)
    got = [sent[0]] + [over_rep(sent[k], 2 * k) for k in range(1, parts)]
    first, second, first_1, second_2, pick = lax.optimization_barrier((first, second, first_1, second_2, pick))
    second_1, first_2 = over_own(second, 1), over_own(first, 2)
    first_3, second_3 = over_own(first_1, 2), over_own(second_2, 1)

    piece = [shape(half, 3 * width), shape(half, 3 * width, F32)]
    outs = call(
        functools.partial(main_kernel, parts),
        [shape(block, model_width)] * parts
        + [shape(depth, 3 * width, F32), piece[0], piece[1], piece[1], piece[0], piece[0], piece[0]],
        1,
        [pltpu.VMEM((slots, model_width), BF16)] * 2,
    )(own, *got, first, second, first_1, second_1, first_2, second_2, first_3, second_3)
    back, (own_term, one_a, one_b, two_a, two_b, three_a, three_b) = outs[:parts], outs[parts:]

    far_a, far_b = over_own(three_a, 1), over_own(three_b, 2)
    returned = [back[0]] + [over_rep(back[k], 2 * k) for k in range(1, parts)]
    got_1a, got_2b = over_own(one_a, 1), over_own(two_b, 2)
    got_2a = over_own((two_a + far_a.astype(F32)).astype(BF16), 2)
    got_1b = over_own((one_b + far_b.astype(F32)).astype(BF16), 1)

    mine, other = call(unpack_kernel, [shape(tok_rows, model_width)] * 2, 0)(pick, *returned)
    x_grad = mine + over_rep(other, 1)
    grads = call(sum_kernel, [shape(depth, width, F32)] * 3, 0)(own_term, got_1a, got_2a, got_1b, got_2b)
    return (x_grad, *(grad[None] for grad in grads))


def shards_whole(tokens, cotangent, route, host, w_gate, w_up, w_down_t):
    tok_rows, model_width = tokens.shape
    hot = host.shape[0]
    width = w_gate.shape[2]
    capacity = max(2, (3 * tok_rows + 2 * hot - 1) // (2 * hot))
    slots = hot * capacity
    labels = lax.broadcasted_iota(jnp.int32, (tok_rows, hot), 1)
    target = jnp.sum(jnp.where(route == labels, host[None, :], 0), axis=1)
    marked = (target[:, None] == labels).astype(jnp.int32)
    arrival = jnp.sum(jnp.cumsum(marked, axis=0) * marked, axis=1) - 1
    position = target * capacity + arrival
    pick = (lax.broadcasted_iota(jnp.int32, (slots, tok_rows), 0) == position[None, :]).astype(BF16)

    def exchange(value):
        split = value.astype(BF16).reshape(hot, capacity, model_width)
        return lax.all_to_all(split, "rep", split_axis=0, concat_axis=0, tiled=True).reshape(slots, model_width)

    slot_x, slot_dy = exchange(dot(pick, tokens, 1, 0)), exchange(dot(pick, cotangent, 1, 0))
    gate, up, down = (lax.all_gather(w[0], "own", axis=0, tiled=True) for w in (w_gate, w_up, w_down_t))
    gate_act, up_act, back_grad = dot(slot_x, gate, 1, 0), dot(slot_x, up, 1, 0), dot(slot_dy, down, 1, 0)
    sigmoid_g = jax.nn.sigmoid(gate_act)
    silu_gate = gate_act * sigmoid_g
    hidden = (silu_gate * up_act).astype(BF16)
    grad_gate_h = (back_grad * up_act * sigmoid_g * (1.0 + gate_act * (1.0 - sigmoid_g))).astype(BF16)
    grad_up_h = (back_grad * silu_gate).astype(BF16)
    returned = exchange(dot(grad_gate_h, gate, 1, 1) + dot(grad_up_h, up, 1, 1))
    x_grad = dot(pick, returned, 0, 0).astype(BF16)
    terms = [dot(slot_x, grad_gate_h, 0, 0), dot(slot_x, grad_up_h, 0, 0), dot(slot_dy, hidden, 0, 0)]
    summed = lax.psum_scatter(
        jnp.concatenate(terms, axis=1).astype(BF16), "own", scatter_dimension=0, tiled=True
    ).astype(F32)
    return (x_grad, *(summed[None, :, i * width : (i + 1) * width] for i in range(3)))


def solution(mesh):
    n_own, n_rep = mesh.shape["own"], mesh.shape["rep"]

    def shards(tokens, *rest):
        capacity = (3 * tokens.shape[0] + 2 * n_rep - 1) // (2 * n_rep)
        if n_own == 4 and n_rep & (n_rep - 1) == 0 and capacity % 8 == 0:
            return shards_by_partner(n_rep, tokens, *rest)
        return shards_whole(tokens, *rest)

    return jax.shard_map(
        shards,
        mesh=mesh,
        in_specs=(
            P(("own", "rep"), None),
            P(("own", "rep"), None),
            P(("own", "rep"), None),
            P(),
            P("rep", "own", None),
            P("rep", "own", None),
            P("rep", "own", None),
        ),
        out_specs=(
            P(("own", "rep"), None),
            P("rep", "own", None),
            P("rep", "own", None),
            P("rep", "own", None),
        ),
        check_vma=False,
    )
```

time: 156 us -> 94.9 us (0.61)
  waiting for transfers between devices: 84 us -> 50.8 us
  blocking collectives: 27.1 us -> 0 us
  starting transfers between devices: 8.32 us -> 22.5 us
  between operations: 14 us -> 0.73 us
  Pallas kernels: 0 us -> 11.3 us
  matrix products: 8.19 us -> 0 us
  other arithmetic: 5.85 us -> 2.2 us
  local copies, waits for them, and re-layouts: 8.6 us -> 6.99 us
    ppermute x0 -> x22, waiting for transfers between devices: none -> 50.8 us  [the longest x10 32.1 us: over_rep(): return lax.ppermute(value, 'rep', [(i, i ^ k) for i in range(n_rep)])]
    all_gather x3 -> x0, waiting for transfers between devices: 47.3 us -> none  [the longest x1 26.4 us: shards(): lax.all_gather(down_piece, 'own', axis=0, tiled=True)]
    all_to_all x1 -> x0, blocking collectives: 27.1 us -> none  [shards(): lax.all_to_all(send_x.reshape(hot_count, capacity, model_width), 'rep', s...]
    ppermute x0 -> x22, starting transfers between devices: none -> 22.5 us  [the longest x12 12.6 us: over_own(): return lax.ppermute(value, 'own', [(i, i ^ k) for i in range(4)])]
    all_to_all x2 -> x0, waiting for transfers between devices: 21 us -> none  [the longest x1 21 us: shards(): lax.all_to_all(slot_grad.reshape(hot_count, capacity, model_width), 'rep'...]
    reduce_scatter x1 -> x0, waiting for transfers between devices: 13.7 us -> none  [shards(): lax.psum_scatter(jnp.concatenate([first_contract(slot_x, grad_gate_h), fi...]
    pallas_call x0 -> x5, Pallas kernels: none -> 11.3 us  [run(): pl.pallas_call(kernel, out_shape=outs, in_specs=[SMEM] * scalars + [VMEM]...]
    dot_general x8 -> x0, matrix products: 8.19 us -> none  [the longest x2 1.89 us: times_rows(): lax.dot_general(left, right, (((1,), (1,)), ((), ())), preferred_element_...]
  transfers between devices with their start and end apart: 6 -> 22, of which waited for: 4 -> 7; matrix products, arithmetic and copies ran while one was open for 8% -> 2% of each run, Pallas kernels for 0% -> 5%
where the time goes in v2:
time: 94.9 us; the launch traced here: 94.5 us
  waiting for transfers between devices  50.8 us (54%)
  starting transfers between devices  22.5 us (24%)
  Pallas kernels  11.3 us (12%)
  local copies, waits for them, and re-layouts  6.99 us (7%)
  other arithmetic  2.2 us (2%)
    ppermute x10, waiting for transfers between devices, over_rep(): return lax.ppermute(value, 'rep', [(i, i ^ k) for i in range(n_rep)])  32.1 us
    ppermute x12, waiting for transfers between devices, over_own(): return lax.ppermute(value, 'own', [(i, i ^ k) for i in range(4)])  18.7 us
    ppermute x12, starting transfers between devices, over_own(): return lax.ppermute(value, 'own', [(i, i ^ k) for i in range(4)])  12.6 us
    pallas_call x5, Pallas kernels, run(): pl.pallas_call(kernel, out_shape=outs, in_specs=[SMEM] * scalars + [VMEM]...  11.3 us
    ppermute x10, starting transfers between devices, over_rep(): return lax.ppermute(value, 'rep', [(i, i ^ k) for i in range(n_rep)])  9.94 us
    unnamed x20, local copies, waits for them, and re-layouts  6.99 us
  transfers between devices with their start and end apart: 22, of which 7 were waited for; matrix products, arithmetic and copies ran while one was open for 2% of the time, Pallas kernels for 5%

profile of v2, /device:TPU:0, one launch (start us, length us, event | category | flops | bytes accessed | tf_op | source)
XLA Modules:
  0.0 94.5 jit_solution(5461593692939953509)
XLA Ops:
  0.6 0.5 collective-permute-start.3
  1.1 0.1 collective-permute-start.4
  1.2 0.4 collective-permute-start.2
  1.7 0.0 copy-start.3
  1.7 0.9 %copy-done.3 = bf16[1,512,256]{2,1,0:T(8,128)(2,1)S(1)} copy-done((bf16[1,512,256]{2,1,0:T(8,128)(2,1)S(1)}, bf16[1,512,256]{2,1,0:T(8,128)(2,1)}, u32[]{:S(2)}) %copy-start.3) | copy-done | bytes 262168
  2.6 0.9 %copy-done.4 = bf16[1,512,256]{2,1,0:T(8,128)(2,1)S(1)} copy-done((bf16[1,512,256]{2,1,0:T(8,128)(2,1)S(1)}, bf16[1,512,256]{2,1,0:T(8,128)(2,1)}, u32[]{:S(2)}) %copy-start.4) | copy-done | bytes 262168
  3.6 0.9 %copy-done.5 = bf16[1,512,256]{2,1,0:T(8,128)(2,1)S(1)} copy-done((bf16[1,512,256]{2,1,0:T(8,128)(2,1)S(1)}, bf16[1,512,256]{2,1,0:T(8,128)(2,1)}, u32[]{:S(2)}) %copy-start.5) | copy-done | bytes 262168
  4.5 0.4 shard_map.102
  4.9 2.6 %collective-permute-start = (bf16[768,256]{1,0:T(8,128)(2,1)S(1)}, bf16[768,256]{1,0:T(8,128)(2,1)S(1)}, u32[]{:S(2)}, u32[]{:S(2)}) collective-permute-start(bf16[768,256]{1,0:T(8,128)(2,1)S(1)} %get-tuple-element.40.refs_4_), channel_id=1, source_target_pairs={{0,8},{8,0},{16,24},{24,16},{1,9},{9,1},{17,25},{25,17},{2,10},{10... | collective-permute-start | bytes 1179656 | tf_op jit(solution)/shard_map/ppermute | solution.py:175
  7.6 1.5 %collective-permute-start.1 = (bf16[768,256]{1,0:T(8,128)(2,1)S(1)}, bf16[768,256]{1,0:T(8,128)(2,1)S(1)}, u32[]{:S(2)}, u32[]{:S(2)}) collective-permute-start(bf16[768,256]{1,0:T(8,128)(2,1)S(1)} %get-tuple-element.41.refs_5_), channel_id=1, source_target_pairs={{0,16},{8,24},{16,0},{24,8},{1,17},{9,25},{17,1},{25,9},{2,18},{10... | collective-permute-start | bytes 1179656 | tf_op jit(solution)/shard_map/ppermute | solution.py:175
  9.1 0.0 collective-permute-done.2.route_b
  9.1 0.0 collective-permute-done.3.x_b
  9.1 0.0 collective-permute-done.4.dy_b
  9.1 0.0 copy-start.1
  9.1 1.0 %copy-done.1 = bf16[128,2048]{1,0:T(8,128)(2,1)S(1)} copy-done((bf16[128,2048]{1,0:T(8,128)(2,1)S(1)}, bf16[128,2048]{1,0:T(8,128)(2,1)}, u32[]{:S(2)}) %copy-start.1) | copy-done | bytes 524312
  10.1 1.0 %copy-done.2 = bf16[128,2048]{1,0:T(8,128)(2,1)S(1)} copy-done((bf16[128,2048]{1,0:T(8,128)(2,1)S(1)}, bf16[128,2048]{1,0:T(8,128)(2,1)}, u32[]{:S(2)}) %copy-start.2) | copy-done | bytes 524312
  11.2 0.7 copy-done.6
  11.8 0.7 copy-done.7
  12.5 2.7 %shard_map.103 = (bf16[192,256]{1,0:T(8,128)(2,1)S(1)}, bf16[96,2048]{1,0:T(8,128)(2,1)S(1)}, bf16[96,2048]{1,0:T(8,128)(2,1)S(1)}, bf16[96,2048]{1,0:T(8,128)(2,1)S(1)}, bf16[96,2048]{1,0:T(8,128)(2,1)}) custom-call(s32[1]{0:T(128)} %bitcast.3.rank_ref, s32[8]{0:T(128)S(1)} %copy-done.6, s32[1,128]{1,0:T(1,128)S(1)} %bitcast.13, ...), custom_call_target="tpu_custom_call" | custom-call | tf_op jit(solution)/shard_map/pallas_call | solution.py:31
  15.2 1.6 %collective-permute-start.5 = (bf16[96,2048]{1,0:T(8,128)(2,1)S(1)}, bf16[96,2048]{1,0:T(8,128)(2,1)S(1)}, u32[]{:S(2)}, u32[]{:S(2)}) collective-permute-start(bf16[96,2048]{1,0:T(8,128)(2,1)S(1)} %get-tuple-element.37), channel_id=1, source_target_pairs={{0,2},{1,3},{2,0},{3,1},{4,6},{5,7},{6,4},{7,5},{8,10},{9,11},{10,... | collective-permute-start | bytes 1179656 | tf_op jit(solution)/shard_map/ppermute | solution.py:178
  16.8 2.6 %collective-permute-start.6 = (bf16[96,2048]{1,0:T(8,128)(2,1)S(1)}, bf16[96,2048]{1,0:T(8,128)(2,1)S(1)}, u32[]{:S(2)}, u32[]{:S(2)}) collective-permute-start(bf16[96,2048]{1,0:T(8,128)(2,1)S(1)} %get-tuple-element.38), channel_id=1, source_target_pairs={{0,4},{1,5},{2,6},{3,7},{4,0},{5,1},{6,2},{7,3},{8,12},{9,13},{10,... | collective-permute-start | bytes 1179656 | tf_op jit(solution)/shard_map/ppermute | solution.py:178
  19.4 0.2 collective-permute-start.7
  19.6 0.0 collective-permute-done.refs_6_
  19.6 0.0 collective-permute-done.1.refs_9_
  19.6 0.7 copy-done.9
  20.4 0.6 collective-permute-start.9
  21.0 0.5 collective-permute-start.8
  21.6 12.3 %collective-permute-done.5.refs_1_ = bf16[96,2048]{1,0:T(8,128)(2,1)S(1)} collective-permute-done((bf16[96,2048]{1,0:T(8,128)(2,1)S(1)}, bf16[96,2048]{1,0:T(8,128)(2,1)S(1)}, u32[]{:S(2)}, u32[]{:S(2)}) %collective-permute-start.5) | collective-permute-done | bytes 393248 | tf_op jit(solution)/shard_map/ppermute | solution.py:178
  33.8 0.5 collective-permute-start.10
  34.3 12.3 %collective-permute-done.6.refs_2_ = bf16[96,2048]{1,0:T(8,128)(2,1)S(1)} collective-permute-done((bf16[96,2048]{1,0:T(8,128)(2,1)S(1)}, bf16[96,2048]{1,0:T(8,128)(2,1)S(1)}, u32[]{:S(2)}, u32[]{:S(2)}) %collective-permute-start.6) | collective-permute-done | bytes 393248 | tf_op jit(solution)/shard_map/ppermute | solution.py:178
  46.6 0.5 collective-permute-start.11
  47.1 0.0 collective-permute-done.7.refs_3_
  47.1 0.0 collective-permute-done.9.refs_8_
  47.1 0.0 collective-permute-done.8.refs_7_
  47.1 0.0 collective-permute-done.10.refs_10_
  47.2 9.7 %collective-permute-done.11.refs_11_ = bf16[768,256]{1,0:T(8,128)(2,1)} collective-permute-done((bf16[768,256]{1,0:T(8,128)(2,1)}, bf16[768,256]{1,0:T(8,128)(2,1)}, u32[]{:S(2)}, u32[]{:S(2)}) %collective-permute-start.11) | collective-permute-done | bytes 393248 | tf_op jit(solution)/shard_map/ppermute | solution.py:175
  56.9 5.6 %shard_map.104 = (bf16[48,2048]{1,0:T(8,128)(2,1)S(1)}, bf16[48,2048]{1,0:T(8,128)(2,1)S(1)}, bf16[48,2048]{1,0:T(8,128)(2,1)S(1)}, bf16[48,2048]{1,0:T(8,128)(2...) custom-call(s32[1]{0:T(128)} %bitcast.5.own_ref, ...), custom_call_target="tpu_custom_call" | custom-call | tf_op jit(solution)/shard_map/pallas_call | solution.py:31
  62.5 0.5 collective-permute-start.17
  63.0 0.0 collective-permute-start.12
  63.0 4.2 %collective-permute-start.13 = (bf16[48,2048]{1,0:T(8,128)(2,1)S(1)}, bf16[48,2048]{1,0:T(8,128)(2,1)S(1)}, u32[]{:S(2)}, u32[]{:S(2)}) collective-permute-start(bf16[48,2048]{1,0:T(8,128)(2,1)S(1)} %get-tuple-element.46), channel_id=1, source_target_pairs={{0,4},{1,5},{2,6},{3,7},{4,0},{5,1},{6,2},{7,3},{8,12},{9,13},{10,... | collective-permute-start | bytes 589832 | tf_op jit(solution)/shard_map/ppermute | solution.py:178
  67.3 0.1 collective-permute-start.14
  67.4 0.5 collective-permute-start.19
  67.9 3.6 %collective-permute-done.12.refs_1_ = bf16[48,2048]{1,0:T(8,128)(2,1)S(1)} collective-permute-done((bf16[48,2048]{1,0:T(8,128)(2,1)S(1)}, bf16[48,2048]{1,0:T(8,128)(2,1)S(1)}, u32[]{:S(2)}, u32[]{:S(2)}) %collective-permute-start.12) | collective-permute-done | bytes 196640 | tf_op jit(solution)/shard_map/ppermute | solution.py:178
  71.5 1.5 %collective-permute-start.16 = (bf16[256,768]{1,0:T(8,128)(2,1)S(1)}, bf16[256,768]{1,0:T(8,128)(2,1)S(1)}, u32[]{:S(2)}, u32[]{:S(2)}) collective-permute-start(bf16[256,768]{1,0:T(8,128)(2,1)S(1)} %get-tuple-element.51), channel_id=1, source_target_pairs={{0,8},{8,0},{16,24},{24,16},{1,9},{9,1},{17,25},{25,17},{2,10},{10... | collective-permute-start | bytes 1179656 | tf_op jit(solution)/shard_map/ppermute | solution.py:175
  73.0 4.0 %collective-permute-done.13.refs_2_ = bf16[48,2048]{1,0:T(8,128)(2,1)S(1)} collective-permute-done((bf16[48,2048]{1,0:T(8,128)(2,1)S(1)}, bf16[48,2048]{1,0:T(8,128)(2,1)S(1)}, u32[]{:S(2)}, u32[]{:S(2)}) %collective-permute-start.13) | collective-permute-done | bytes 196640 | tf_op jit(solution)/shard_map/ppermute | solution.py:178
  77.0 0.5 collective-permute-start.21
  77.5 0.0 collective-permute-done.14.refs_3_
  77.5 1.3 %shard_map.105 = (bf16[128,2048]{1,0:T(8,128)(2,1)S(1)}, bf16[128,2048]{1,0:T(8,128)(2,1)S(1)}) custom-call(bf16[192,256]{1,0:T(8,128)(2,1)S(1)} %get-tuple-element.35.pick_ref, bf16[48,2048]{1,0:T(8,128)(2,1)S(1)} %get-tuple-element.44.refs_0_, bf16[48,2048]{1,0:T(8,128)(2,1)S(1)} %collective-permute-done.12.refs_1_, ...), custom_call_target="tpu_custom_call" | custom-call | tf_op jit(solution)/shard_map/pallas_call | solution.py:31
  78.8 0.1 collective-permute-start.15
  78.9 0.0 collective-permute-done.17
  78.9 1.2 %add_convert_fusion.1 = bf16[256,768]{1,0:T(8,128)(2,1)S(1)} fusion(f32[256,768]{1,0:T(8,128)} %get-tuple-element.52, bf16[256,768]{1,0:T(8,128)(2,1)S(1)} %collective-permute-done.17), kind=kLoop, calls=%fused_computation.1 | loop fusion | flops 589824 | bytes 1572864 | tf_op jit(solution)/shard_map/convert_element_type | solution.py:213
  80.1 1.6 %collective-permute-start.18 = (bf16[256,768]{1,0:T(8,128)(2,1)S(1)}, bf16[256,768]{1,0:T(8,128)(2,1)S(1)}, u32[]{:S(2)}, u32[]{:S(2)}) collective-permute-start(bf16[256,768]{1,0:T(8,128)(2,1)S(1)} %add_convert_fusion.1), channel_id=1, source_target_pairs={{0,16},{8,24},{16,0},{24,8},{1,17},{9,25},{17,1},{25,9},{2,18},{10... | collective-permute-start | bytes 1179656 | tf_op jit(solution)/shard_map/ppermute | solution.py:175
  81.7 0.0 collective-permute-done.19
  81.7 0.0 copy-done.8
  81.7 0.1 add_convert_fusion
  81.8 1.6 %collective-permute-start.20 = (bf16[256,768]{1,0:T(8,128)(2,1)S(1)}, bf16[256,768]{1,0:T(8,128)(2,1)S(1)}, u32[]{:S(2)}, u32[]{:S(2)}) collective-permute-start(bf16[256,768]{1,0:T(8,128)(2,1)S(1)} %add_convert_fusion), channel_id=1, source_target_pairs={{0,8},{8,0},{16,24},{24,16},{1,9},{9,1},{17,25},{25,17},{2,10},{10... | collective-permute-start | bytes 1179656 | tf_op jit(solution)/shard_map/ppermute | solution.py:175
  83.3 0.0 collective-permute-done.15
  83.3 0.9 add.9
  84.2 0.0 collective-permute-done.16.one_a
  84.2 2.0 %collective-permute-done.21.two_b = bf16[256,768]{1,0:T(8,128)(2,1)S(1)} collective-permute-done((bf16[256,768]{1,0:T(8,128)(2,1)S(1)}, bf16[256,768]{1,0:T(8,128)(2,1)S(1)}, u32[]{:S(2)}, u32[]{:S(2)}) %collective-permute-start.21) | collective-permute-done | bytes 393248 | tf_op jit(solution)/shard_map/ppermute | solution.py:175
  86.3 6.9 %collective-permute-done.18.two_a = bf16[256,768]{1,0:T(8,128)(2,1)S(1)} collective-permute-done((bf16[256,768]{1,0:T(8,128)(2,1)S(1)}, bf16[256,768]{1,0:T(8,128)(2,1)S(1)}, u32[]{:S(2)}, u32[]{:S(2)}) %collective-permute-start.18) | collective-permute-done | bytes 393248 | tf_op jit(solution)/shard_map/ppermute | solution.py:175
  93.2 0.0 collective-permute-done.20.one_b
  93.2 0.0 copy-done
  93.2 1.3 %shard_map.106 = (f32[512,256]{1,0:T(8,128)}, f32[512,256]{1,0:T(8,128)}, f32[512,256]{1,0:T(8,128)}) custom-call(f32[512,768]{1,0:T(8,128)S(1)} %copy-done, bf16[256,768]{1,0:T(8,128)(2,1)S(1)} %collective-permute-done.16.one_a, bf16[256,768]{1,0:T(8,128)(2,1)S(1)} %collective-permute-done.18.two_a, bf16[256,768]{1,0:T(8,128)(2,1)S(1)} %collective-permute-done.20.one_b, ...), custom_call_target="tpu_custom_call" | custom-call | tf_op jit(solution)/shard_map/pallas_call | solution.py:31
  (8 shorter events, 0.0 us)
Async XLA Ops:
  0.6 8.5 %collective-permute-start.3 = (bf16[128,2048]{1,0:T(8,128)(2,1)}, bf16[128,2048]{1,0:T(8,128)(2,1)S(1)}, u32[]{:S(2)}, u32[]{:S(2)}) collective-permute-start(bf16[128,2048]{1,0:T(8,128)(2,1)} %refs_0_.1), channel_id=1, source_target_pairs={{0,1},{1,0},{2,3},{3,2},{4,5},{5,4},{6,7},{7,6},{8,9},{9,8},{10,11... | collective-permute-start | bytes 1572872 | tf_op jit(solution)/shard_map/ppermute | solution.py:178
  1.1 7.9 %collective-permute-start.4 = (bf16[128,2048]{1,0:T(8,128)(2,1)}, bf16[128,2048]{1,0:T(8,128)(2,1)S(1)}, u32[]{:S(2)}, u32[]{:S(2)}) collective-permute-start(bf16[128,2048]{1,0:T(8,128)(2,1)} %refs_1_.1), channel_id=1, source_target_pairs={{0,1},{1,0},{2,3},{3,2},{4,5},{5,4},{6,7},{7,6},{8,9},{9,8},{10,11... | collective-permute-start | bytes 1572872 | tf_op jit(solution)/shard_map/ppermute | solution.py:178
  1.2 7.9 %collective-permute-start.2 = (s32[1,128]{1,0:T(1,128)}, s32[1,128]{1,0:T(1,128)S(1)}, u32[]{:S(2)}, u32[]{:S(2)}) collective-permute-start(s32[1,128]{1,0:T(1,128)} %bitcast.12), channel_id=1, source_target_pairs={{0,1},{1,0},{2,3},{3,2},{4,5},{5,4},{6,7},{7,6},{8,9},{9,8},{10,11... | collective-permute-start | bytes 1544 | tf_op jit(solution)/shard_map/ppermute | solution.py:178
  1.7 0.9 %copy-start.3 = (bf16[1,512,256]{2,1,0:T(8,128)(2,1)S(1)}, bf16[1,512,256]{2,1,0:T(8,128)(2,1)}, u32[]{:S(2)}) copy-start(bf16[1,512,256]{2,1,0:T(8,128)(2,1)} %param.11) | copy-start | bytes 786436
  2.6 0.9 %copy-start.4 = (bf16[1,512,256]{2,1,0:T(8,128)(2,1)S(1)}, bf16[1,512,256]{2,1,0:T(8,128)(2,1)}, u32[]{:S(2)}) copy-start(bf16[1,512,256]{2,1,0:T(8,128)(2,1)} %param.12) | copy-start | bytes 786436
  3.6 0.9 %copy-start.5 = (bf16[1,512,256]{2,1,0:T(8,128)(2,1)S(1)}, bf16[1,512,256]{2,1,0:T(8,128)(2,1)}, u32[]{:S(2)}) copy-start(bf16[1,512,256]{2,1,0:T(8,128)(2,1)} %param.13) | copy-start | bytes 786436
  4.9 14.7 %collective-permute-start = (bf16[768,256]{1,0:T(8,128)(2,1)S(1)}, bf16[768,256]{1,0:T(8,128)(2,1)S(1)}, u32[]{:S(2)}, u32[]{:S(2)}) collective-permute-start(bf16[768,256]{1,0:T(8,128)(2,1)S(1)} %get-tuple-element.40.refs_4_), channel_id=1, source_target_pairs={{0,8},{8,0},{16,24},{24,16},{1,9},{9,1},{17,25},{25,17},{2,10},{10... | collective-permute-start | bytes 1179656 | tf_op jit(solution)/shard_map/ppermute | solution.py:175
  7.6 12.1 %collective-permute-start.1 = (bf16[768,256]{1,0:T(8,128)(2,1)S(1)}, bf16[768,256]{1,0:T(8,128)(2,1)S(1)}, u32[]{:S(2)}, u32[]{:S(2)}) collective-permute-start(bf16[768,256]{1,0:T(8,128)(2,1)S(1)} %get-tuple-element.41.refs_5_), channel_id=1, source_target_pairs={{0,16},{8,24},{16,0},{24,8},{1,17},{9,25},{17,1},{25,9},{2,18},{10... | collective-permute-start | bytes 1179656 | tf_op jit(solution)/shard_map/ppermute | solution.py:175
  9.1 1.0 %copy-start.1 = (bf16[128,2048]{1,0:T(8,128)(2,1)S(1)}, bf16[128,2048]{1,0:T(8,128)(2,1)}, u32[]{:S(2)}) copy-start(bf16[128,2048]{1,0:T(8,128)(2,1)} %refs_0_.1) | copy-start | bytes 1572868
  10.1 1.0 %copy-start.2 = (bf16[128,2048]{1,0:T(8,128)(2,1)S(1)}, bf16[128,2048]{1,0:T(8,128)(2,1)}, u32[]{:S(2)}) copy-start(bf16[128,2048]{1,0:T(8,128)(2,1)} %refs_1_.1) | copy-start | bytes 1572868
  11.2 0.7 copy-start.6
  11.8 0.7 copy-start.7
  15.2 18.6 %collective-permute-start.5 = (bf16[96,2048]{1,0:T(8,128)(2,1)S(1)}, bf16[96,2048]{1,0:T(8,128)(2,1)S(1)}, u32[]{:S(2)}, u32[]{:S(2)}) collective-permute-start(bf16[96,2048]{1,0:T(8,128)(2,1)S(1)} %get-tuple-element.37), channel_id=1, source_target_pairs={{0,2},{1,3},{2,0},{3,1},{4,6},{5,7},{6,4},{7,5},{8,10},{9,11},{10,... | collective-permute-start | bytes 1179656 | tf_op jit(solution)/shard_map/ppermute | solution.py:178
  16.8 29.8 %collective-permute-start.6 = (bf16[96,2048]{1,0:T(8,128)(2,1)S(1)}, bf16[96,2048]{1,0:T(8,128)(2,1)S(1)}, u32[]{:S(2)}, u32[]{:S(2)}) collective-permute-start(bf16[96,2048]{1,0:T(8,128)(2,1)S(1)} %get-tuple-element.38), channel_id=1, source_target_pairs={{0,4},{1,5},{2,6},{3,7},{4,0},{5,1},{6,2},{7,3},{8,12},{9,13},{10,... | collective-permute-start | bytes 1179656 | tf_op jit(solution)/shard_map/ppermute | solution.py:178
  19.4 27.7 %collective-permute-start.7 = (bf16[96,2048]{1,0:T(8,128)(2,1)}, bf16[96,2048]{1,0:T(8,128)(2,1)S(1)}, u32[]{:S(2)}, u32[]{:S(2)}) collective-permute-start(bf16[96,2048]{1,0:T(8,128)(2,1)} %get-tuple-element.39), channel_id=1, source_target_pairs={{0,6},{1,7},{2,4},{3,5},{4,2},{5,3},{6,0},{7,1},{8,14},{9,15},{10,... | collective-permute-start | bytes 1179656 | tf_op jit(solution)/shard_map/ppermute | solution.py:178
  19.6 0.7 copy-start.9
  20.4 26.8 %collective-permute-start.9 = (bf16[768,256]{1,0:T(8,128)(2,1)S(1)}, bf16[768,256]{1,0:T(8,128)(2,1)S(1)}, u32[]{:S(2)}, u32[]{:S(2)}) collective-permute-start(bf16[768,256]{1,0:T(8,128)(2,1)S(1)} %get-tuple-element.40.refs_4_), channel_id=1, source_target_pairs={{0,16},{8,24},{16,0},{24,8},{1,17},{9,25},{17,1},{25,9},{2,18},{10... | collective-permute-start | bytes 1179656 | tf_op jit(solution)/shard_map/ppermute | solution.py:175
  21.0 26.1 %collective-permute-start.8 = (bf16[768,256]{1,0:T(8,128)(2,1)S(1)}, bf16[768,256]{1,0:T(8,128)(2,1)}, u32[]{:S(2)}, u32[]{:S(2)}) collective-permute-start(bf16[768,256]{1,0:T(8,128)(2,1)S(1)} %get-tuple-element.41.refs_5_), channel_id=1, source_target_pairs={{0,8},{8,0},{16,24},{24,16},{1,9},{9,1},{17,25},{25,17},{2,10},{10... | collective-permute-start | bytes 1179656 | tf_op jit(solution)/shard_map/ppermute | solution.py:175
  33.8 13.3 %collective-permute-start.10 = (bf16[768,256]{1,0:T(8,128)(2,1)S(1)}, bf16[768,256]{1,0:T(8,128)(2,1)}, u32[]{:S(2)}, u32[]{:S(2)}) collective-permute-start(bf16[768,256]{1,0:T(8,128)(2,1)S(1)} %collective-permute-done.refs_6_), channel_id=1, source_target_pairs={{0,16},{8,24},{16,0},{24,8},{1,17},{9,25},{17,1},{25,9},{2,18},{10... | collective-permute-start | bytes 1179656 | tf_op jit(solution)/shard_map/ppermute | solution.py:175
  46.6 10.2 %collective-permute-start.11 = (bf16[768,256]{1,0:T(8,128)(2,1)}, bf16[768,256]{1,0:T(8,128)(2,1)}, u32[]{:S(2)}, u32[]{:S(2)}) collective-permute-start(bf16[768,256]{1,0:T(8,128)(2,1)} %copy-done.9), channel_id=1, source_target_pairs={{0,8},{8,0},{16,24},{24,16},{1,9},{9,1},{17,25},{25,17},{2,10},{10... | collective-permute-start | bytes 1179656 | tf_op jit(solution)/shard_map/ppermute | solution.py:175
  62.5 19.2 %copy-start.8 = (f32[256,768]{1,0:T(8,128)S(1)}, f32[256,768]{1,0:T(8,128)}, u32[]{:S(2)}) copy-start(f32[256,768]{1,0:T(8,128)} %get-tuple-element.54) | copy-start | bytes 2359300
  62.5 16.4 %collective-permute-start.17 = (bf16[256,768]{1,0:T(8,128)(2,1)S(1)}, bf16[256,768]{1,0:T(8,128)(2,1)S(1)}, u32[]{:S(2)}, u32[]{:S(2)}) collective-permute-start(bf16[256,768]{1,0:T(8,128)(2,1)S(1)} %get-tuple-element.53), channel_id=1, source_target_pairs={{0,8},{8,0},{16,24},{24,16},{1,9},{9,1},{17,25},{25,17},{2,10},{10... | collective-permute-start | bytes 1179656 | tf_op jit(solution)/shard_map/ppermute | solution.py:175
  63.0 8.5 %collective-permute-start.12 = (bf16[48,2048]{1,0:T(8,128)(2,1)S(1)}, bf16[48,2048]{1,0:T(8,128)(2,1)S(1)}, u32[]{:S(2)}, u32[]{:S(2)}) collective-permute-start(bf16[48,2048]{1,0:T(8,128)(2,1)S(1)} %get-tuple-element.45), channel_id=1, source_target_pairs={{0,2},{1,3},{2,0},{3,1},{4,6},{5,7},{6,4},{7,5},{8,10},{9,11},{10,... | collective-permute-start | bytes 589832 | tf_op jit(solution)/shard_map/ppermute | solution.py:178
  63.0 14.0 %collective-permute-start.13 = (bf16[48,2048]{1,0:T(8,128)(2,1)S(1)}, bf16[48,2048]{1,0:T(8,128)(2,1)S(1)}, u32[]{:S(2)}, u32[]{:S(2)}) collective-permute-start(bf16[48,2048]{1,0:T(8,128)(2,1)S(1)} %get-tuple-element.46), channel_id=1, source_target_pairs={{0,4},{1,5},{2,6},{3,7},{4,0},{5,1},{6,2},{7,3},{8,12},{9,13},{10,... | collective-permute-start | bytes 589832 | tf_op jit(solution)/shard_map/ppermute | solution.py:178
  67.3 10.2 %collective-permute-start.14 = (bf16[48,2048]{1,0:T(8,128)(2,1)S(1)}, bf16[48,2048]{1,0:T(8,128)(2,1)S(1)}, u32[]{:S(2)}, u32[]{:S(2)}) collective-permute-start(bf16[48,2048]{1,0:T(8,128)(2,1)S(1)} %get-tuple-element.47), channel_id=1, source_target_pairs={{0,6},{1,7},{2,4},{3,5},{4,2},{5,3},{6,0},{7,1},{8,14},{9,15},{10,... | collective-permute-start | bytes 589832 | tf_op jit(solution)/shard_map/ppermute | solution.py:178
  67.4 14.2 %collective-permute-start.19 = (bf16[256,768]{1,0:T(8,128)(2,1)S(1)}, bf16[256,768]{1,0:T(8,128)(2,1)S(1)}, u32[]{:S(2)}, u32[]{:S(2)}) collective-permute-start(bf16[256,768]{1,0:T(8,128)(2,1)S(1)} %get-tuple-element.55), channel_id=1, source_target_pairs={{0,16},{8,24},{16,0},{24,8},{1,17},{9,25},{17,1},{25,9},{2,18},{10... | collective-permute-start | bytes 1179656 | tf_op jit(solution)/shard_map/ppermute | solution.py:175
  71.5 12.7 %collective-permute-start.16 = (bf16[256,768]{1,0:T(8,128)(2,1)S(1)}, bf16[256,768]{1,0:T(8,128)(2,1)S(1)}, u32[]{:S(2)}, u32[]{:S(2)}) collective-permute-start(bf16[256,768]{1,0:T(8,128)(2,1)S(1)} %get-tuple-element.51), channel_id=1, source_target_pairs={{0,8},{8,0},{16,24},{24,16},{1,9},{9,1},{17,25},{25,17},{2,10},{10... | collective-permute-start | bytes 1179656 | tf_op jit(solution)/shard_map/ppermute | solution.py:175
  77.0 9.3 %collective-permute-start.21 = (bf16[256,768]{1,0:T(8,128)(2,1)S(1)}, bf16[256,768]{1,0:T(8,128)(2,1)S(1)}, u32[]{:S(2)}, u32[]{:S(2)}) collective-permute-start(bf16[256,768]{1,0:T(8,128)(2,1)S(1)} %get-tuple-element.56), channel_id=1, source_target_pairs={{0,16},{8,24},{16,0},{24,8},{1,17},{9,25},{17,1},{25,9},{2,18},{10... | collective-permute-start | bytes 1179656 | tf_op jit(solution)/shard_map/ppermute | solution.py:175
  78.8 4.5 %collective-permute-start.15 = (bf16[128,2048]{1,0:T(8,128)(2,1)S(1)}, bf16[128,2048]{1,0:T(8,128)(2,1)S(1)}, u32[]{:S(2)}, u32[]{:S(2)}) collective-permute-start(bf16[128,2048]{1,0:T(8,128)(2,1)S(1)} %get-tuple-element.49), channel_id=1, source_target_pairs={{0,1},{1,0},{2,3},{3,2},{4,5},{5,4},{6,7},{7,6},{8,9},{9,8},{10,11... | collective-permute-start | bytes 1572872 | tf_op jit(solution)/shard_map/ppermute | solution.py:178
  80.1 13.1 %collective-permute-start.18 = (bf16[256,768]{1,0:T(8,128)(2,1)S(1)}, bf16[256,768]{1,0:T(8,128)(2,1)S(1)}, u32[]{:S(2)}, u32[]{:S(2)}) collective-permute-start(bf16[256,768]{1,0:T(8,128)(2,1)S(1)} %add_convert_fusion.1), channel_id=1, source_target_pairs={{0,16},{8,24},{16,0},{24,8},{1,17},{9,25},{17,1},{25,9},{2,18},{10... | collective-permute-start | bytes 1179656 | tf_op jit(solution)/shard_map/ppermute | solution.py:175
  81.7 11.5 %copy-start = (f32[512,768]{1,0:T(8,128)S(1)}, f32[512,768]{1,0:T(8,128)}, u32[]{:S(2)}) copy-start(f32[512,768]{1,0:T(8,128)} %get-tuple-element.50.own_ref) | copy-start | bytes 4718596
  81.8 11.5 %collective-permute-start.20 = (bf16[256,768]{1,0:T(8,128)(2,1)S(1)}, bf16[256,768]{1,0:T(8,128)(2,1)S(1)}, u32[]{:S(2)}, u32[]{:S(2)}) collective-permute-start(bf16[256,768]{1,0:T(8,128)(2,1)S(1)} %add_convert_fusion), channel_id=1, source_target_pairs={{0,8},{8,0},{16,24},{24,16},{1,9},{9,1},{17,25},{25,17},{2,10},{10... | collective-permute-start | bytes 1179656 | tf_op jit(solution)/shard_map/ppermute | solution.py:175

commit v3 on v2

v3 whole, which is shorter than its diff:
```python
import functools

import jax
import jax.numpy as jnp
from jax import lax
from jax.experimental import pallas as pl
from jax.experimental.pallas import tpu as pltpu
from jax.sharding import PartitionSpec as P

VMEM = pl.BlockSpec(memory_space=pltpu.VMEM)
SMEM = pl.BlockSpec(memory_space=pltpu.SMEM)
HBM = pl.BlockSpec(memory_space=pltpu.HBM)
MIB = 1024 * 1024
BF16 = jnp.bfloat16
F32 = jnp.float32


def dot(left, right, left_dim, right_dim):
    return lax.dot_general(
        left, right, (((left_dim,), (right_dim,)), ((), ())), preferred_element_type=F32
    )


def shape(rows, cols, dtype=BF16):
    return jax.ShapeDtypeStruct((rows, cols), dtype)


def call(kernel, outs, scalars=0, scratch=(), fetched=0, room=32):
    def run(*operands):
        placed = len(operands) - scalars - fetched
        moved = sum(value.size * value.dtype.itemsize for value in (*operands, *outs))
        return pl.pallas_call(
            kernel,
            out_shape=outs,
            in_specs=[SMEM] * scalars + [VMEM] * placed + [HBM] * fetched,
            out_specs=[VMEM] * len(outs),
            scratch_shapes=list(scratch),
            cost_estimate=pl.CostEstimate(flops=0, bytes_accessed=moved, transcendentals=0),
            compiler_params=pltpu.CompilerParams(vmem_limit_bytes=room * MIB),
        )(*operands)

    return run


def after(values, *earlier):
    return lax.optimization_barrier((values, earlier))[0]


def join_kernel(gate_ref, up_ref, down_ref, joined_ref, sems):
    depth = gate_ref.shape[0]
    loads = [
        pltpu.make_async_copy(source, joined_ref.at[pl.ds(i * depth, depth)], sems.at[i])
        for i, source in enumerate((gate_ref, up_ref, down_ref))
    ]
    for load in loads:
        load.start()
    for load in loads:
        load.wait()


def pack_kernel(capacity, rank_ref, host_ref, route_a, *refs):
    sources, outs, (route_b, x_a, x_b, dy_a, dy_b, sems) = refs[:5], refs[5:-6], refs[-6:]
    pick_ref, *send_refs = outs
    loads = [
        pltpu.make_async_copy(source, into, sems.at[i])
        for i, (source, into) in enumerate(zip(sources, (route_b, x_a, x_b, dy_a, dy_b)))
    ]
    for load in loads:
        load.start()
    hot = host_ref.shape[0]
    slots = pick_ref.shape[0]
    tokens = route_a.shape[1]
    block = 2 * capacity
    parts = slots // block
    label = lax.broadcasted_iota(jnp.int32, (hot, tokens), 0)
    base = jnp.zeros((hot, tokens), jnp.int32)
    for e in range(hot):
        apart = host_ref[e] ^ rank_ref[0]
        start = jnp.where((apart & 1) == 0, (apart >> 1) * block, -2 * slots)
        base = jnp.where(label == e, start, base)
    earlier = lax.broadcasted_iota(jnp.int32, (tokens, tokens), 0) < lax.broadcasted_iota(
        jnp.int32, (tokens, tokens), 1
    )
    earlier = jnp.where(earlier, 1.0, 0.0).astype(BF16)
    slot = lax.broadcasted_iota(jnp.int32, (slots, tokens), 0)

    def picks(route_ref, offset):
        marked = route_ref[...] == label
        before = dot(jnp.where(marked, 1.0, 0.0).astype(BF16), earlier, 1, 0).astype(jnp.int32)
        position = jnp.sum(jnp.where(marked, before + base, 0), axis=0, keepdims=True) + offset
        return jnp.where(slot == position, 1.0, 0.0).astype(BF16)

    pick_a = picks(route_a, 0)
    loads[0].wait()
    pick_b = picks(route_b, capacity)
    pick_ref[:, :tokens] = pick_a
    pick_ref[:, tokens:] = pick_b
    for at, (a, b) in enumerate(((x_a, x_b), (dy_a, dy_b))):
        loads[1 + 2 * at].wait()
        loads[2 + 2 * at].wait()
        filled = (dot(pick_a, a[...], 1, 0) + dot(pick_b, b[...], 1, 0)).astype(BF16)
        for k in range(parts):
            rows = filled[k * block : (k + 1) * block]
            if k < 2:
                send_refs[k][at * block : (at + 1) * block] = rows
            else:
                send_refs[2 * k - 2 + at][...] = rows


def columns_of(own_ref, depth):
    return [pl.ds(pl.multiple_of((own_ref[0] ^ k) * depth, depth), depth) for k in range(4)]


def spread_kernel(depth, own_ref, *refs):
    got, (x_ref, *piece_refs) = refs[:-5], refs[-5:]
    block = x_ref.shape[0] // len(got)
    columns = columns_of(own_ref, depth)
    for j, ref in enumerate(got):
        rows = slice(j * block, (j + 1) * block)
        x_ref[rows] = ref[:block]
        for k, piece_ref in enumerate(piece_refs):
            piece_ref[rows] = ref[:block, columns[k]]


def weight_rows(weights, k, start, rows):
    if k < 3:
        return weights[k][start : start + rows]
    split = weights[3].shape[0]
    half, start = divmod(start, split)
    return weights[3 + half][start : start + rows]


def act_kernel(*refs):
    own_ref, x_ref, weights, (gate_ref, up_ref) = refs[0], refs[1], refs[2:-2], refs[-2:]
    depth = weights[0].shape[0] // 3
    half = depth // 2
    gate_act = jnp.zeros(gate_ref.shape, F32)
    up_act = jnp.zeros(up_ref.shape, F32)
    for k, cols in enumerate(columns_of(own_ref, depth)):
        x = x_ref[:, cols]
        gate_act += dot(x, weight_rows(weights, k, 0, depth), 1, 0)
        up_act += dot(x[:, :half], weight_rows(weights, k, depth, half), 1, 0)
        up_act += dot(x[:, half:], weight_rows(weights, k, depth + half, half), 1, 0)
    gate_ref[...] = gate_act
    up_ref[...] = up_act


def grad_kernel(parts, own_ref, gate_ref, up_ref, *refs):
    got, weights, outs, dy_ref = refs[:parts], refs[parts : parts + 5], refs[parts + 5 : -1], refs[-1]
    back_refs, own_term, (own_grads, *messages) = outs[:parts], outs[parts], outs[parts + 1 :]
    slots, width = gate_ref.shape
    block = slots // parts
    depth = weights[0].shape[0] // 3
    half = depth // 2
    columns = columns_of(own_ref, depth)
    for j, ref in enumerate(got):
        dy_ref[j * block : (j + 1) * block] = ref[ref.shape[0] - block :]
    back_grad = sum(dot(dy_ref[:, columns[k]], weight_rows(weights, k, 2 * depth, depth), 1, 0) for k in range(4))
    gate_act, up_act = gate_ref[...], up_ref[...]
    sigmoid_g = jax.nn.sigmoid(gate_act)
    silu_gate = gate_act * sigmoid_g
    hidden = (silu_gate * up_act).astype(BF16)
    gate_h = (back_grad * up_act * sigmoid_g * (1.0 + gate_act * (1.0 - sigmoid_g))).astype(BF16)
    up_h = (back_grad * silu_gate).astype(BF16)
    for ref in (own_grads, *messages):
        ref[:slots, :width] = gate_h
        ref[:slots, width:] = up_h
    for k in range(4):
        term = dot(dy_ref[:, columns[k]], hidden, 0, 0)
        if k == 0:
            own_term[...] = term
        else:
            messages[k - 1][slots:, :width] = term[:half].astype(BF16)
            messages[k - 1][slots:, width:] = term[half:].astype(BF16)
    for k in range(4):
        for at in range(2):
            gate_rows = weight_rows(weights, k, at * half, half)
            up_rows = weight_rows(weights, k, depth + at * half, half)
            slot_grad = (dot(gate_h, gate_rows, 1, 1) + dot(up_h, up_rows, 1, 1)).astype(BF16)
            cols = pl.ds(pl.multiple_of((own_ref[0] ^ k) * depth + at * half, half), half)
            for j, back_ref in enumerate(back_refs):
                back_ref[:, cols] = slot_grad[j * block : (j + 1) * block]


def sum_kernel(*refs):
    pieces, messages, own_term, (gate_ref, up_ref, down_ref) = refs[:4], refs[4:8], refs[8], refs[9:]
    slots = pieces[0].shape[0]
    depth, width = gate_ref.shape
    half = depth // 2
    gate_ref[...] = sum(dot(piece[...], got[:slots, :width], 0, 0) for piece, got in zip(pieces, messages))
    up_ref[...] = sum(dot(piece[...], got[:slots, width:], 0, 0) for piece, got in zip(pieces, messages))
    for rows, cols in ((slice(0, half), slice(0, width)), (slice(half, depth), slice(width, 2 * width))):
        down_ref[rows] = own_term[rows] + sum(got[slots:, cols].astype(F32) for got in messages[1:])


def unpack_kernel(pick_ref, *refs):
    returned, (mine_ref, other_ref) = refs[:-2], refs[-2:]
    tokens = mine_ref.shape[0]
    block = returned[0].shape[0]
    for at, ref in enumerate((other_ref, mine_ref)):
        half = slice((1 - at) * tokens, (2 - at) * tokens)
        ref[...] = sum(
            dot(pick_ref[k * block : (k + 1) * block, half], part[...], 0, 0) for k, part in enumerate(returned)
        ).astype(BF16)


def shards_by_partner(n_rep, tokens, cotangent, route, host, w_gate, w_up, w_down_t):
    tok_rows, model_width = tokens.shape
    hot = host.shape[0]
    _, depth, width = w_gate.shape
    capacity = (3 * tok_rows + 2 * hot - 1) // (2 * hot)
    slots = hot * capacity
    parts = n_rep // 2
    block = 2 * capacity
    own = lax.axis_index("own").astype(jnp.int32).reshape(1)
    rank = lax.axis_index("rep").astype(jnp.int32).reshape(1)

    def over_own(value, k):
        return lax.ppermute(value, "own", [(i, i ^ k) for i in range(4)])

    def over_rep(value, k):
        return lax.ppermute(value, "rep", [(i, i ^ k) for i in range(n_rep)])

    route = route.reshape(1, tok_rows)
    route_b, tokens_b, cotangent_b = over_rep(route, 1), over_rep(tokens, 1), over_rep(cotangent, 1)
    joined = call(join_kernel, [shape(3 * depth, width)], 0, [pltpu.SemaphoreType.DMA((3,))], 3, 62)(
        w_gate[0], w_up[0], w_down_t[0]
    )[0]
    joined_1, joined_2 = over_own(joined, 1), over_own(joined, 2)

    token_rows = pltpu.VMEM((tok_rows, model_width), BF16)
    pick, *sent = call(
        functools.partial(pack_kernel, capacity),
        [shape(slots, 2 * tok_rows)]
        + [shape(2 * block, model_width)] * 2
        + [shape(block, model_width)] * (2 * parts - 4),
        2,
        [pltpu.VMEM((1, tok_rows), jnp.int32)] + [token_rows] * 4 + [pltpu.SemaphoreType.DMA((5,))],
        5,
        62,
    )(rank, host, route, route_b, tokens, tokens_b, cotangent, cotangent_b)
    far = range(2, parts)
    near = over_rep(sent[1], 2)
    far_x = [over_rep(sent[2 * k - 2], 2 * k) for k in far]
    (sent_dy, joined_1, joined_2) = after(
        ([sent[2 * k - 1] for k in far], joined_1, joined_2), near, *far_x
    )
    far_dy = [over_rep(value, 2 * k) for k, value in zip(far, sent_dy)]
    split = 3 * depth // 2
    joined_3 = [over_own(joined_1[:split], 2), over_own(joined_2[split:], 1)]

    x, *pieces = call(
        functools.partial(spread_kernel, depth), [shape(slots, model_width)] + [shape(slots, depth)] * 4, 1
    )(own, sent[0], near, *far_x)
    pieces = [pieces[0]] + [over_own(after(pieces[k], *joined_3), k) for k in range(1, 4)]
    weights = [joined, joined_1, joined_2, *joined_3]
    gate_act, up_act = call(act_kernel, [shape(slots, width, F32)] * 2, 1)(own, x, *weights)
    far_dy = after(far_dy, *pieces)
    message = shape(slots + depth // 2, 2 * width)
    outs = call(
        functools.partial(grad_kernel, parts),
        [shape(block, model_width)] * parts
        + [shape(depth, width, F32), shape(slots, 2 * width), message, message, message],
        1,
        [pltpu.VMEM((slots, model_width), BF16)],
    )(own, gate_act, up_act, sent[0], near, *far_dy, *weights)
    back, own_term, grads, messages = outs[:parts], outs[parts], outs[parts + 1], outs[parts + 2 :]
    returned = [over_rep(back[k], 2 * k) for k in range(1, parts)]
    messages = [over_own(messages[k - 1], k) for k in range(1, 4)]

    returned = after(returned, *messages)
    mine, other = call(unpack_kernel, [shape(tok_rows, model_width)] * 2)(pick, back[0], *returned)
    x_grad = mine + over_rep(other, 1)
    out = call(sum_kernel, [shape(depth, width, F32)] * 3)(*pieces, grads, *messages, own_term)
    return (x_grad, *(grad[None] for grad in out))


def shards_whole(tokens, cotangent, route, host, w_gate, w_up, w_down_t):
    tok_rows, model_width = tokens.shape
    hot = host.shape[0]
    width = w_gate.shape[2]
    capacity = max(2, (3 * tok_rows + 2 * hot - 1) // (2 * hot))
    slots = hot * capacity
    labels = lax.broadcasted_iota(jnp.int32, (tok_rows, hot), 1)
    target = jnp.sum(jnp.where(route == labels, host[None, :], 0), axis=1)
    marked = (target[:, None] == labels).astype(jnp.int32)
    arrival = jnp.sum(jnp.cumsum(marked, axis=0) * marked, axis=1) - 1
    position = target * capacity + arrival
    pick = (lax.broadcasted_iota(jnp.int32, (slots, tok_rows), 0) == position[None, :]).astype(BF16)

    def exchange(value):
        split = value.astype(BF16).reshape(hot, capacity, model_width)
        return lax.all_to_all(split, "rep", split_axis=0, concat_axis=0, tiled=True).reshape(slots, model_width)

    slot_x, slot_dy = exchange(dot(pick, tokens, 1, 0)), exchange(dot(pick, cotangent, 1, 0))
    gate, up, down = (lax.all_gather(w[0], "own", axis=0, tiled=True) for w in (w_gate, w_up, w_down_t))
    gate_act, up_act, back_grad = dot(slot_x, gate, 1, 0), dot(slot_x, up, 1, 0), dot(slot_dy, down, 1, 0)
    sigmoid_g = jax.nn.sigmoid(gate_act)
    silu_gate = gate_act * sigmoid_g
    hidden = (silu_gate * up_act).astype(BF16)
    grad_gate_h = (back_grad * up_act * sigmoid_g * (1.0 + gate_act * (1.0 - sigmoid_g))).astype(BF16)
    grad_up_h = (back_grad * silu_gate).astype(BF16)
    returned = exchange(dot(grad_gate_h, gate, 1, 1) + dot(grad_up_h, up, 1, 1))
    x_grad = dot(pick, returned, 0, 0).astype(BF16)
    terms = [dot(slot_x, grad_gate_h, 0, 0), dot(slot_x, grad_up_h, 0, 0), dot(slot_dy, hidden, 0, 0)]
    summed = lax.psum_scatter(
        jnp.concatenate(terms, axis=1).astype(BF16), "own", scatter_dimension=0, tiled=True
    ).astype(F32)
    return (x_grad, *(summed[None, :, i * width : (i + 1) * width] for i in range(3)))


def solution(mesh):
    n_own, n_rep = mesh.shape["own"], mesh.shape["rep"]

    def shards(tokens, *rest):
        capacity = (3 * tokens.shape[0] + 2 * n_rep - 1) // (2 * n_rep)
        if n_own == 4 and n_rep & (n_rep - 1) == 0 and capacity % 8 == 0:
            return shards_by_partner(n_rep, tokens, *rest)
        return shards_whole(tokens, *rest)

    return jax.shard_map(
        shards,
        mesh=mesh,
        in_specs=(
            P(("own", "rep"), None),
            P(("own", "rep"), None),
            P(("own", "rep"), None),
            P(),
            P("rep", "own", None),
            P("rep", "own", None),
            P("rep", "own", None),
        ),
        out_specs=(
            P(("own", "rep"), None),
            P("rep", "own", None),
            P("rep", "own", None),
            P("rep", "own", None),
        ),
        check_vma=False,
    )
```

time: 94.9 us -> 87.2 us (0.919)
  waiting for transfers between devices: 50.8 us -> 42.8 us
  other arithmetic: 2.2 us -> 0.92 us
  local copies, waits for them, and re-layouts: 6.99 us -> 8.08 us
    ppermute x12 -> x10, waiting for transfers between devices: 18.7 us -> 9.4 us  [over_own(): return lax.ppermute(value, 'own', [(i, i ^ k) for i in range(4)])]
    slice x0 -> x2, local copies, waits for them, and re-layouts: none -> 1.54 us  [shards_by_partner(): joined_3 = [over_own(joined_1[:split], 2), over_own(joined_2[split:], 1)]]
    ppermute x10 -> x12, waiting for transfers between devices: 32.1 us -> 33.4 us  [over_rep(): return lax.ppermute(value, 'rep', [(i, i ^ k) for i in range(n_rep)])]
    convert_element_type x2 -> x0, other arithmetic: 1.27 us -> none  [the longest x1 1.2 us: shards_by_partner(): got_2a = over_own((two_a + far_a.astype(F32)).astype(BF16), 2)]
    ppermute x10 -> x12, starting transfers between devices: 9.94 us -> 10.5 us  [over_rep(): return lax.ppermute(value, 'rep', [(i, i ^ k) for i in range(n_rep)])]
    unnamed x20 -> x26, local copies, waits for them, and re-layouts: 6.99 us -> 6.53 us
    ppermute x12 -> x10, starting transfers between devices: 12.6 us -> 12.6 us  [over_own(): return lax.ppermute(value, 'own', [(i, i ^ k) for i in range(4)])]
    pallas_call x5 -> x7, Pallas kernels: 11.3 us -> 11.3 us  [run(): pl.pallas_call(kernel, out_shape=outs, in_specs=[SMEM] * scalars + [VMEM]...]
  transfers between devices with their start and end apart: 22 -> 22, of which waited for: 7 -> 12; matrix products, arithmetic and copies ran while one was open for 2% -> 0% of each run, Pallas kernels for 5% -> 10%
where the time goes in v3:
time: 87.2 us; the launch traced here: 86.9 us
  waiting for transfers between devices  42.8 us (49%)
  starting transfers between devices  23.1 us (26%)
  Pallas kernels  11.3 us (13%)
  local copies, waits for them, and re-layouts  8.08 us (9%)
  other arithmetic  0.92 us (1%)
    ppermute x12, waiting for transfers between devices, over_rep(): return lax.ppermute(value, 'rep', [(i, i ^ k) for i in range(n_rep)])  33.4 us
    ppermute x10, starting transfers between devices, over_own(): return lax.ppermute(value, 'own', [(i, i ^ k) for i in range(4)])  12.6 us
    pallas_call x7, Pallas kernels, run(): pl.pallas_call(kernel, out_shape=outs, in_specs=[SMEM] * scalars + [VMEM]...  11.3 us
    ppermute x12, starting transfers between devices, over_rep(): return lax.ppermute(value, 'rep', [(i, i ^ k) for i in range(n_rep)])  10.5 us
    ppermute x10, waiting for transfers between devices, over_own(): return lax.ppermute(value, 'own', [(i, i ^ k) for i in range(4)])  9.4 us
    unnamed x26, local copies, waits for them, and re-layouts  6.53 us
  transfers between devices with their start and end apart: 22, of which 12 were waited for; matrix products, arithmetic and copies ran while one was open for 0% of the time, Pallas kernels for 10%

profile of v3, /device:TPU:0, one launch (start us, length us, event | category | flops | bytes accessed | tf_op | source)
XLA Modules:
  0.0 86.9 jit_solution(16431075733305945119)
XLA Ops:
  0.6 0.5 collective-permute-start.1
  1.1 0.1 collective-permute-start.2
  1.2 2.0 %shard_map.104.refs_2_.refs_4_ = bf16[1536,256]{1,0:T(8,128)(2,1)} custom-call(bf16[512,256]{1,0:T(8,128)(2,1)} %bitcast.9, bf16[512,256]{1,0:T(8,128)(2,1)} %bitcast.10, bf16[512,256]{1,0:T(8,128)(2,1)} %bitcast.11), custom_call_target="tpu_custom_call" | custom-call | bytes 1572864 | tf_op jit(solution)/shard_map/pallas_call | solution.py:32
  3.3 0.0 copy-start.9
  3.3 3.0 %collective-permute-start.7 = (bf16[1536,256]{1,0:T(8,128)(2,1)}, bf16[1536,256]{1,0:T(8,128)(2,1)S(1)}, u32[]{:S(2)}, u32[]{:S(2)}) collective-permute-start(bf16[1536,256]{1,0:T(8,128)(2,1)} %shard_map.104.refs_2_.refs_4_), channel_id=1, source_target_pairs={{0,16},{8,24},{16,0},{24,8},{1,17},{9,25},{17,1},{25,9},{2,18},{10... | collective-permute-start | bytes 2359304 | tf_op jit(solution)/shard_map/ppermute | solution.py:219
  6.3 1.5 %collective-permute-start.6 = (bf16[1536,256]{1,0:T(8,128)(2,1)}, bf16[1536,256]{1,0:T(8,128)(2,1)S(1)}, u32[]{:S(2)}, u32[]{:S(2)}) collective-permute-start(bf16[1536,256]{1,0:T(8,128)(2,1)} %shard_map.104.refs_2_.refs_4_), channel_id=1, source_target_pairs={{0,8},{8,0},{16,24},{24,16},{1,9},{9,1},{17,25},{25,17},{2,10},{10... | collective-permute-start | bytes 2359304 | tf_op jit(solution)/shard_map/ppermute | solution.py:219
  7.8 0.0 collective-permute-start
  7.8 1.1 %collective-permute-done.refs_0_ = s32[1,128]{1,0:T(1,128)S(1)} collective-permute-done((s32[1,128]{1,0:T(1,128)S(1)}, s32[1,128]{1,0:T(1,128)S(1)}, u32[]{:S(2)}, u32[]{:S(2)}) %collective-permute-start) | collective-permute-done | bytes 544 | tf_op jit(solution)/shard_map/ppermute | solution.py:222
  8.9 0.0 collective-permute-done.1.refs_2_
  8.9 0.0 collective-permute-done.2.refs_4_
  8.9 0.6 copy-done.10
  9.5 4.0 %shard_map.102 = (bf16[192,256]{1,0:T(8,128)(2,1)}, bf16[96,2048]{1,0:T(8,128)(2,1)}, bf16[96,2048]{1,0:T(8,128)(2,1)}, bf16[48,2048]{1,0:T(8,128)(2,1)}, bf16[4...) custom-call(s32[1]{0:T(128)} %bitcast.rank_ref, s32[8]{0:T(128)} %host_ref.1, ...), custom_call_target="tpu_custom_call" | custom-call | bytes 3769380 | tf_op jit(solution)/shard_map/pallas_call | solution.py:32
  13.5 1.6 %collective-permute-start.3 = (bf16[96,2048]{1,0:T(8,128)(2,1)}, bf16[96,2048]{1,0:T(8,128)(2,1)S(1)}, u32[]{:S(2)}, u32[]{:S(2)}) collective-permute-start(bf16[96,2048]{1,0:T(8,128)(2,1)} %get-tuple-element.46), channel_id=1, source_target_pairs={{0,2},{1,3},{2,0},{3,1},{4,6},{5,7},{6,4},{7,5},{8,10},{9,11},{10,... | collective-permute-start | bytes 1179656 | tf_op jit(solution)/shard_map/ppermute | solution.py:222
  15.1 2.6 %collective-permute-start.4 = (bf16[48,2048]{1,0:T(8,128)(2,1)}, bf16[48,2048]{1,0:T(8,128)(2,1)S(1)}, u32[]{:S(2)}, u32[]{:S(2)}) collective-permute-start(bf16[48,2048]{1,0:T(8,128)(2,1)} %get-tuple-element.47), channel_id=1, source_target_pairs={{0,4},{1,5},{2,6},{3,7},{4,0},{5,1},{6,2},{7,3},{8,12},{9,13},{10,... | collective-permute-start | bytes 589832 | tf_op jit(solution)/shard_map/ppermute | solution.py:222
  17.7 0.2 collective-permute-start.5
  17.9 11.2 %collective-permute-done.4.refs_2_ = bf16[48,2048]{1,0:T(8,128)(2,1)S(1)} collective-permute-done((bf16[48,2048]{1,0:T(8,128)(2,1)}, bf16[48,2048]{1,0:T(8,128)(2,1)S(1)}, u32[]{:S(2)}, u32[]{:S(2)}) %collective-permute-start.4) | collective-permute-done | bytes 196640 | tf_op jit(solution)/shard_map/ppermute | solution.py:222
  29.2 0.7 copy-done.4
  29.9 5.7 %collective-permute-done.5.refs_3_ = bf16[48,2048]{1,0:T(8,128)(2,1)S(1)} collective-permute-done((bf16[48,2048]{1,0:T(8,128)(2,1)}, bf16[48,2048]{1,0:T(8,128)(2,1)S(1)}, u32[]{:S(2)}, u32[]{:S(2)}) %collective-permute-start.5) | collective-permute-done | bytes 196640 | tf_op jit(solution)/shard_map/ppermute | solution.py:222
  35.5 0.7 copy-done.6
  36.2 0.0 collective-permute-done.7.refs_4_.refs_6_
  36.2 0.0 collective-permute-done.6.refs_3_.refs_5_
  36.2 0.0 collective-permute-done.3.refs_1_
  36.2 0.0 copy-start.2
  36.3 0.7 copy-done.2
  37.0 0.8 slice.6
  37.8 0.8 slice.7
  38.5 0.5 collective-permute-start.9
  39.1 0.5 collective-permute-start.8
  39.6 1.7 %collective-permute-start.10 = (bf16[48,2048]{1,0:T(8,128)(2,1)S(1)}, bf16[48,2048]{1,0:T(8,128)(2,1)S(1)}, u32[]{:S(2)}, u32[]{:S(2)}) collective-permute-start(bf16[48,2048]{1,0:T(8,128)(2,1)S(1)} %copy-done.12), channel_id=1, source_target_pairs={{0,4},{1,5},{2,6},{3,7},{4,0},{5,1},{6,2},{7,3},{8,12},{9,13},{10,... | collective-permute-start | bytes 589832 | tf_op jit(solution)/shard_map/ppermute | solution.py:222
  41.3 1.3 %collective-permute-start.11 = (bf16[48,2048]{1,0:T(8,128)(2,1)S(1)}, bf16[48,2048]{1,0:T(8,128)(2,1)S(1)}, u32[]{:S(2)}, u32[]{:S(2)}) collective-permute-start(bf16[48,2048]{1,0:T(8,128)(2,1)S(1)} %copy-done.11), channel_id=1, source_target_pairs={{0,6},{1,7},{2,4},{3,5},{4,2},{5,3},{6,0},{7,1},{8,14},{9,15},{10,... | collective-permute-start | bytes 589832 | tf_op jit(solution)/shard_map/ppermute | solution.py:222
  42.6 1.0 %copy-done.1 = bf16[96,2048]{1,0:T(8,128)(2,1)S(1)} copy-done((bf16[96,2048]{1,0:T(8,128)(2,1)S(1)}, bf16[96,2048]{1,0:T(8,128)(2,1)}, u32[]{:S(2)}) %copy-start.1) | copy-done | bytes 393240
  43.6 1.0 %copy-done.3 = bf16[96,2048]{1,0:T(8,128)(2,1)S(1)} copy-done((bf16[96,2048]{1,0:T(8,128)(2,1)S(1)}, bf16[96,2048]{1,0:T(8,128)(2,1)}, u32[]{:S(2)}) %copy-start.3) | copy-done | bytes 393240
  44.6 0.9 %copy-done.5 = bf16[48,2048]{1,0:T(8,128)(2,1)S(1)} copy-done((bf16[48,2048]{1,0:T(8,128)(2,1)S(1)}, bf16[48,2048]{1,0:T(8,128)(2,1)}, u32[]{:S(2)}) %copy-start.5) | copy-done | bytes 196632
  45.5 0.9 %copy-done.7 = bf16[48,2048]{1,0:T(8,128)(2,1)S(1)} copy-done((bf16[48,2048]{1,0:T(8,128)(2,1)S(1)}, bf16[48,2048]{1,0:T(8,128)(2,1)}, u32[]{:S(2)}) %copy-start.7) | copy-done | bytes 196632
  46.5 0.1 shard_map.103
  46.6 2.5 %collective-permute-done.9.refs_6_.refs_8_ = bf16[768,256]{1,0:T(8,128)(2,1)S(1)} collective-permute-done((bf16[768,256]{1,0:T(8,128)(2,1)}, bf16[768,256]{1,0:T(8,128)(2,1)S(1)}, u32[]{:S(2)}, u32[]{:S(2)}) %collective-permute-start.9) | collective-permute-done | bytes 393248 | tf_op jit(solution)/shard_map/ppermute | solution.py:219
  49.1 0.2 collective-permute-done.8.refs_5_.refs_7_
  49.3 1.4 %collective-permute-start.14 = (bf16[192,512]{1,0:T(8,128)(2,1)S(1)}, bf16[192,512]{1,0:T(8,128)(2,1)S(1)}, u32[]{:S(2)}, u32[]{:S(2)}) collective-permute-start(bf16[192,512]{1,0:T(8,128)(2,1)S(1)} %get-tuple-element.64), channel_id=1, source_target_pairs={{0,24},{8,16},{16,8},{24,0},{1,25},{9,17},{17,9},{25,1},{2,26},{10... | collective-permute-start | bytes 589832 | tf_op jit(solution)/shard_map/ppermute | solution.py:219
  50.8 1.5 %collective-permute-start.13 = (bf16[192,512]{1,0:T(8,128)(2,1)S(1)}, bf16[192,512]{1,0:T(8,128)(2,1)S(1)}, u32[]{:S(2)}, u32[]{:S(2)}) collective-permute-start(bf16[192,512]{1,0:T(8,128)(2,1)S(1)} %get-tuple-element.62), channel_id=1, source_target_pairs={{0,16},{8,24},{16,0},{24,8},{1,17},{9,25},{17,1},{25,9},{2,18},{10... | collective-permute-start | bytes 589832 | tf_op jit(solution)/shard_map/ppermute | solution.py:219
  52.3 0.5 collective-permute-start.12
  52.8 0.6 shard_map.105
  53.4 1.2 %collective-permute-done.10.refs_2_ = bf16[48,2048]{1,0:T(8,128)(2,1)S(1)} collective-permute-done((bf16[48,2048]{1,0:T(8,128)(2,1)S(1)}, bf16[48,2048]{1,0:T(8,128)(2,1)S(1)}, u32[]{:S(2)}, u32[]{:S(2)}) %collective-permute-start.10) | collective-permute-done | bytes 196640 | tf_op jit(solution)/shard_map/ppermute | solution.py:222
  54.6 0.0 collective-permute-done.11.refs_3_
  54.6 2.9 %collective-permute-done.14.refs_3_ = bf16[192,512]{1,0:T(8,128)(2,1)S(1)} collective-permute-done((bf16[192,512]{1,0:T(8,128)(2,1)S(1)}, bf16[192,512]{1,0:T(8,128)(2,1)S(1)}, u32[]{:S(2)}, u32[]{:S(2)}) %collective-permute-start.14) | collective-permute-done | bytes 196640 | tf_op jit(solution)/shard_map/ppermute | solution.py:219
  57.5 2.0 %collective-permute-done.13.refs_2_ = bf16[192,512]{1,0:T(8,128)(2,1)S(1)} collective-permute-done((bf16[192,512]{1,0:T(8,128)(2,1)S(1)}, bf16[192,512]{1,0:T(8,128)(2,1)S(1)}, u32[]{:S(2)}, u32[]{:S(2)}) %collective-permute-start.13) | collective-permute-done | bytes 196640 | tf_op jit(solution)/shard_map/ppermute | solution.py:219
  59.5 0.0 collective-permute-done.12.refs_1_
  59.5 1.3 %shard_map.106 = (bf16[48,2048]{1,0:T(8,128)(2,1)S(1)}, bf16[48,2048]{1,0:T(8,128)(2,1)S(1)}, bf16[48,2048]{1,0:T(8,128)(2,1)S(1)}, bf16[48,2048]{1,0:T(8,128)(2...) custom-call(s32[1]{0:T(128)} %bitcast.2.own_ref.refs_0_, ...), custom_call_target="tpu_custom_call" | custom-call | bytes 7602180 | tf_op jit(solution)/shard_map/pallas_call | solution.py:32
  60.8 0.8 collective-permute-start.18
  61.6 1.3 %collective-permute-start.19 = (bf16[448,512]{1,0:T(8,128)(2,1)S(1)}, bf16[448,512]{1,0:T(8,128)(2,1)S(1)}, u32[]{:S(2)}, u32[]{:S(2)}) collective-permute-start(bf16[448,512]{1,0:T(8,128)(2,1)S(1)} %get-tuple-element.72), channel_id=1, source_target_pairs={{0,16},{8,24},{16,0},{24,8},{1,17},{9,25},{17,1},{25,9},{2,18},{10... | collective-permute-start | bytes 1376264 | tf_op jit(solution)/shard_map/ppermute | solution.py:219
  62.9 1.4 %collective-permute-start.20 = (bf16[448,512]{1,0:T(8,128)(2,1)S(1)}, bf16[448,512]{1,0:T(8,128)(2,1)S(1)}, u32[]{:S(2)}, u32[]{:S(2)}) collective-permute-start(bf16[448,512]{1,0:T(8,128)(2,1)S(1)} %get-tuple-element.73), channel_id=1, source_target_pairs={{0,24},{8,16},{16,8},{24,0},{1,25},{9,17},{17,9},{25,1},{2,26},{10... | collective-permute-start | bytes 1376264 | tf_op jit(solution)/shard_map/ppermute | solution.py:219
  64.4 0.0 collective-permute-start.15
  64.4 1.9 %collective-permute-start.16 = (bf16[48,2048]{1,0:T(8,128)(2,1)S(1)}, bf16[48,2048]{1,0:T(8,128)(2,1)S(1)}, u32[]{:S(2)}, u32[]{:S(2)}) collective-permute-start(bf16[48,2048]{1,0:T(8,128)(2,1)S(1)} %get-tuple-element.69), channel_id=1, source_target_pairs={{0,4},{1,5},{2,6},{3,7},{4,0},{5,1},{6,2},{7,3},{8,12},{9,13},{10,... | collective-permute-start | bytes 589832 | tf_op jit(solution)/shard_map/ppermute | solution.py:222
  66.2 7.0 %collective-permute-done.15.refs_1_ = bf16[48,2048]{1,0:T(8,128)(2,1)S(1)} collective-permute-done((bf16[48,2048]{1,0:T(8,128)(2,1)S(1)}, bf16[48,2048]{1,0:T(8,128)(2,1)S(1)}, u32[]{:S(2)}, u32[]{:S(2)}) %collective-permute-start.15) | collective-permute-done | bytes 196640 | tf_op jit(solution)/shard_map/ppermute | solution.py:222
  73.3 0.5 collective-permute-start.17
  73.7 1.1 %collective-permute-done.16.refs_2_ = bf16[48,2048]{1,0:T(8,128)(2,1)S(1)} collective-permute-done((bf16[48,2048]{1,0:T(8,128)(2,1)S(1)}, bf16[48,2048]{1,0:T(8,128)(2,1)S(1)}, u32[]{:S(2)}, u32[]{:S(2)}) %collective-permute-start.16) | collective-permute-done | bytes 196640 | tf_op jit(solution)/shard_map/ppermute | solution.py:222
  74.9 6.0 %collective-permute-done.17.refs_3_ = bf16[48,2048]{1,0:T(8,128)(2,1)S(1)} collective-permute-done((bf16[48,2048]{1,0:T(8,128)(2,1)S(1)}, bf16[48,2048]{1,0:T(8,128)(2,1)S(1)}, u32[]{:S(2)}, u32[]{:S(2)}) %collective-permute-start.17) | collective-permute-done | bytes 196640 | tf_op jit(solution)/shard_map/ppermute | solution.py:222
  80.8 0.0 collective-permute-done.18.refs_5_
  80.8 1.8 %collective-permute-done.19.refs_6_ = bf16[448,512]{1,0:T(8,128)(2,1)S(1)} collective-permute-done((bf16[448,512]{1,0:T(8,128)(2,1)S(1)}, bf16[448,512]{1,0:T(8,128)(2,1)S(1)}, u32[]{:S(2)}, u32[]{:S(2)}) %collective-permute-start.19) | collective-permute-done | bytes 458784 | tf_op jit(solution)/shard_map/ppermute | solution.py:219
  82.6 0.0 collective-permute-done.20.refs_7_
  82.7 1.3 %shard_map.107 = (bf16[128,2048]{1,0:T(8,128)(2,1)S(1)}, bf16[128,2048]{1,0:T(8,128)(2,1)S(1)}) custom-call(bf16[192,256]{1,0:T(8,128)(2,1)S(1)} %copy-done.8, bf16[48,2048]{1,0:T(8,128)(2,1)S(1)} %get-tuple-element.67.refs_0_, bf16[48,2048]{1,0:T(8,128)(2,1)S(1)} %collective-permute-done.15.refs_1_, bf16[48,2048]{1,0:T(8,128)(2,1)S(1)} %collective-permute-done.16.refs_2_, ...), custom_call_target="tpu_custom_call" | custom-call | bytes 1933312 | tf_op jit(solution)/shard_map/pallas_call | solution.py:32
  83.9 0.1 collective-permute-start.21
  84.0 1.9 %shard_map.108 = (f32[512,256]{1,0:T(8,128)}, f32[512,256]{1,0:T(8,128)}, f32[512,256]{1,0:T(8,128)}) custom-call(bf16[192,512]{1,0:T(8,128)(2,1)S(1)} %get-tuple-element.58.refs_0_, bf16[192,512]{1,0:T(8,128)(2,1)S(1)} %collective-permute-done.12.refs_1_, bf16[192,512]{1,0:T(8,128)(2,1)S(1)} %collective-permute-done.13.refs_2_, ...), custom_call_target="tpu_custom_call" | custom-call | bytes 4456448 | tf_op jit(solution)/shard_map/pallas_call | solution.py:32
  85.9 0.0 collective-permute-done.21
  86.0 0.9 %add.3 = bf16[128,2048]{1,0:T(8,128)(2,1)} add(bf16[128,2048]{1,0:T(8,128)(2,1)S(1)} %get-tuple-element.77, bf16[128,2048]{1,0:T(8,128)(2,1)S(1)} %collective-permute-done.21) | non-fusion elementwise | flops 262144 | bytes 1572864 | tf_op jit(solution)/shard_map/add | solution.py:273
  (16 shorter events, 0.0 us)
Async XLA Ops:
  0.6 8.3 %collective-permute-start.1 = (bf16[128,2048]{1,0:T(8,128)(2,1)}, bf16[128,2048]{1,0:T(8,128)(2,1)}, u32[]{:S(2)}, u32[]{:S(2)}) collective-permute-start(bf16[128,2048]{1,0:T(8,128)(2,1)} %refs_1_.1), channel_id=1, source_target_pairs={{0,1},{1,0},{2,3},{3,2},{4,5},{5,4},{6,7},{7,6},{8,9},{9,8},{10,11... | collective-permute-start | bytes 1572872 | tf_op jit(solution)/shard_map/ppermute | solution.py:222
  1.1 7.8 %collective-permute-start.2 = (bf16[128,2048]{1,0:T(8,128)(2,1)}, bf16[128,2048]{1,0:T(8,128)(2,1)}, u32[]{:S(2)}, u32[]{:S(2)}) collective-permute-start(bf16[128,2048]{1,0:T(8,128)(2,1)} %refs_3_.1), channel_id=1, source_target_pairs={{0,1},{1,0},{2,3},{3,2},{4,5},{5,4},{6,7},{7,6},{8,9},{9,8},{10,11... | collective-permute-start | bytes 1572872 | tf_op jit(solution)/shard_map/ppermute | solution.py:222
  3.3 4.5 %copy-start.9 = (s32[128,1]{0,1:T(1,128)S(1)}, s32[128,1]{0,1:T(1,128)}, u32[]{:S(2)}) copy-start(s32[128,1]{0,1:T(1,128)} %param.9) | copy-start | bytes 1540
  3.3 33.0 %collective-permute-start.7 = (bf16[1536,256]{1,0:T(8,128)(2,1)}, bf16[1536,256]{1,0:T(8,128)(2,1)S(1)}, u32[]{:S(2)}, u32[]{:S(2)}) collective-permute-start(bf16[1536,256]{1,0:T(8,128)(2,1)} %shard_map.104.refs_2_.refs_4_), channel_id=1, source_target_pairs={{0,16},{8,24},{16,0},{24,8},{1,17},{9,25},{17,1},{25,9},{2,18},{10... | collective-permute-start | bytes 2359304 | tf_op jit(solution)/shard_map/ppermute | solution.py:219
  6.3 30.0 %collective-permute-start.6 = (bf16[1536,256]{1,0:T(8,128)(2,1)}, bf16[1536,256]{1,0:T(8,128)(2,1)S(1)}, u32[]{:S(2)}, u32[]{:S(2)}) collective-permute-start(bf16[1536,256]{1,0:T(8,128)(2,1)} %shard_map.104.refs_2_.refs_4_), channel_id=1, source_target_pairs={{0,8},{8,0},{16,24},{24,16},{1,9},{9,1},{17,25},{25,17},{2,10},{10... | collective-permute-start | bytes 2359304 | tf_op jit(solution)/shard_map/ppermute | solution.py:219
  7.8 1.1 %collective-permute-start = (s32[1,128]{1,0:T(1,128)S(1)}, s32[1,128]{1,0:T(1,128)S(1)}, u32[]{:S(2)}, u32[]{:S(2)}) collective-permute-start(s32[1,128]{1,0:T(1,128)S(1)} %bitcast.13), channel_id=1, source_target_pairs={{0,1},{1,0},{2,3},{3,2},{4,5},{5,4},{6,7},{7,6},{8,9},{9,8},{10,11... | collective-permute-start | bytes 1544 | tf_op jit(solution)/shard_map/ppermute | solution.py:222
  8.9 0.6 copy-start.10
  13.5 22.7 %collective-permute-start.3 = (bf16[96,2048]{1,0:T(8,128)(2,1)}, bf16[96,2048]{1,0:T(8,128)(2,1)S(1)}, u32[]{:S(2)}, u32[]{:S(2)}) collective-permute-start(bf16[96,2048]{1,0:T(8,128)(2,1)} %get-tuple-element.46), channel_id=1, source_target_pairs={{0,2},{1,3},{2,0},{3,1},{4,6},{5,7},{6,4},{7,5},{8,10},{9,11},{10,... | collective-permute-start | bytes 1179656 | tf_op jit(solution)/shard_map/ppermute | solution.py:222
  15.1 14.0 %collective-permute-start.4 = (bf16[48,2048]{1,0:T(8,128)(2,1)}, bf16[48,2048]{1,0:T(8,128)(2,1)S(1)}, u32[]{:S(2)}, u32[]{:S(2)}) collective-permute-start(bf16[48,2048]{1,0:T(8,128)(2,1)} %get-tuple-element.47), channel_id=1, source_target_pairs={{0,4},{1,5},{2,6},{3,7},{4,0},{5,1},{6,2},{7,3},{8,12},{9,13},{10,... | collective-permute-start | bytes 589832 | tf_op jit(solution)/shard_map/ppermute | solution.py:222
  17.7 17.8 %collective-permute-start.5 = (bf16[48,2048]{1,0:T(8,128)(2,1)}, bf16[48,2048]{1,0:T(8,128)(2,1)S(1)}, u32[]{:S(2)}, u32[]{:S(2)}) collective-permute-start(bf16[48,2048]{1,0:T(8,128)(2,1)} %get-tuple-element.48), channel_id=1, source_target_pairs={{0,6},{1,7},{2,4},{3,5},{4,2},{5,3},{6,0},{7,1},{8,14},{9,15},{10,... | collective-permute-start | bytes 589832 | tf_op jit(solution)/shard_map/ppermute | solution.py:222
  29.2 0.7 copy-start.4
  35.5 0.7 copy-start.6
  36.2 0.7 copy-start.2
  37.8 1.8 %copy-start.12 = (bf16[48,2048]{1,0:T(8,128)(2,1)S(1)}, bf16[48,2048]{1,0:T(8,128)(2,1)}, u32[]{:S(2)}) copy-start(bf16[48,2048]{1,0:T(8,128)(2,1)} %get-tuple-element.56) | copy-start | bytes 589828
  37.8 3.5 %copy-start.11 = (bf16[48,2048]{1,0:T(8,128)(2,1)S(1)}, bf16[48,2048]{1,0:T(8,128)(2,1)}, u32[]{:S(2)}) copy-start(bf16[48,2048]{1,0:T(8,128)(2,1)} %get-tuple-element.57) | copy-start | bytes 589828
  38.5 14.3 %copy-start = (bf16[1536,256]{1,0:T(8,128)(2,1)S(1)}, bf16[1536,256]{1,0:T(8,128)(2,1)}, u32[]{:S(2)}) copy-start(bf16[1536,256]{1,0:T(8,128)(2,1)} %shard_map.104.refs_2_.refs_4_) | copy-start | bytes 2359300
  38.5 10.6 %collective-permute-start.9 = (bf16[768,256]{1,0:T(8,128)(2,1)}, bf16[768,256]{1,0:T(8,128)(2,1)S(1)}, u32[]{:S(2)}, u32[]{:S(2)}) collective-permute-start(bf16[768,256]{1,0:T(8,128)(2,1)} %slice.7), channel_id=1, source_target_pairs={{0,8},{8,0},{16,24},{24,16},{1,9},{9,1},{17,25},{25,17},{2,10},{10... | collective-permute-start | bytes 1179656 | tf_op jit(solution)/shard_map/ppermute | solution.py:219
  39.1 10.3 %collective-permute-start.8 = (bf16[768,256]{1,0:T(8,128)(2,1)}, bf16[768,256]{1,0:T(8,128)(2,1)S(1)}, u32[]{:S(2)}, u32[]{:S(2)}) collective-permute-start(bf16[768,256]{1,0:T(8,128)(2,1)} %slice.6), channel_id=1, source_target_pairs={{0,16},{8,24},{16,0},{24,8},{1,17},{9,25},{17,1},{25,9},{2,18},{10... | collective-permute-start | bytes 1179656 | tf_op jit(solution)/shard_map/ppermute | solution.py:219
  39.6 15.0 %collective-permute-start.10 = (bf16[48,2048]{1,0:T(8,128)(2,1)S(1)}, bf16[48,2048]{1,0:T(8,128)(2,1)S(1)}, u32[]{:S(2)}, u32[]{:S(2)}) collective-permute-start(bf16[48,2048]{1,0:T(8,128)(2,1)S(1)} %copy-done.12), channel_id=1, source_target_pairs={{0,4},{1,5},{2,6},{3,7},{4,0},{5,1},{6,2},{7,3},{8,12},{9,13},{10,... | collective-permute-start | bytes 589832 | tf_op jit(solution)/shard_map/ppermute | solution.py:222
  41.3 13.4 %collective-permute-start.11 = (bf16[48,2048]{1,0:T(8,128)(2,1)S(1)}, bf16[48,2048]{1,0:T(8,128)(2,1)S(1)}, u32[]{:S(2)}, u32[]{:S(2)}) collective-permute-start(bf16[48,2048]{1,0:T(8,128)(2,1)S(1)} %copy-done.11), channel_id=1, source_target_pairs={{0,6},{1,7},{2,4},{3,5},{4,2},{5,3},{6,0},{7,1},{8,14},{9,15},{10,... | collective-permute-start | bytes 589832 | tf_op jit(solution)/shard_map/ppermute | solution.py:222
  42.6 1.0 %copy-start.1 = (bf16[96,2048]{1,0:T(8,128)(2,1)S(1)}, bf16[96,2048]{1,0:T(8,128)(2,1)}, u32[]{:S(2)}) copy-start(bf16[96,2048]{1,0:T(8,128)(2,1)} %get-tuple-element.45.refs_0_) | copy-start | bytes 1179652
  43.6 1.0 %copy-start.3 = (bf16[96,2048]{1,0:T(8,128)(2,1)S(1)}, bf16[96,2048]{1,0:T(8,128)(2,1)}, u32[]{:S(2)}) copy-start(bf16[96,2048]{1,0:T(8,128)(2,1)} %copy-done.2) | copy-start | bytes 1179652
  44.6 0.9 %copy-start.5 = (bf16[48,2048]{1,0:T(8,128)(2,1)S(1)}, bf16[48,2048]{1,0:T(8,128)(2,1)}, u32[]{:S(2)}) copy-start(bf16[48,2048]{1,0:T(8,128)(2,1)} %copy-done.4) | copy-start | bytes 589828
  45.5 0.9 %copy-start.7 = (bf16[48,2048]{1,0:T(8,128)(2,1)S(1)}, bf16[48,2048]{1,0:T(8,128)(2,1)}, u32[]{:S(2)}) copy-start(bf16[48,2048]{1,0:T(8,128)(2,1)} %copy-done.6) | copy-start | bytes 589828
  49.3 8.2 %collective-permute-start.14 = (bf16[192,512]{1,0:T(8,128)(2,1)S(1)}, bf16[192,512]{1,0:T(8,128)(2,1)S(1)}, u32[]{:S(2)}, u32[]{:S(2)}) collective-permute-start(bf16[192,512]{1,0:T(8,128)(2,1)S(1)} %get-tuple-element.64), channel_id=1, source_target_pairs={{0,24},{8,16},{16,8},{24,0},{1,25},{9,17},{17,9},{25,1},{2,26},{10... | collective-permute-start | bytes 589832 | tf_op jit(solution)/shard_map/ppermute | solution.py:219
  50.8 8.7 %collective-permute-start.13 = (bf16[192,512]{1,0:T(8,128)(2,1)S(1)}, bf16[192,512]{1,0:T(8,128)(2,1)S(1)}, u32[]{:S(2)}, u32[]{:S(2)}) collective-permute-start(bf16[192,512]{1,0:T(8,128)(2,1)S(1)} %get-tuple-element.62), channel_id=1, source_target_pairs={{0,16},{8,24},{16,0},{24,8},{1,17},{9,25},{17,1},{25,9},{2,18},{10... | collective-permute-start | bytes 589832 | tf_op jit(solution)/shard_map/ppermute | solution.py:219
  52.3 7.1 %collective-permute-start.12 = (bf16[192,512]{1,0:T(8,128)(2,1)S(1)}, bf16[192,512]{1,0:T(8,128)(2,1)S(1)}, u32[]{:S(2)}, u32[]{:S(2)}) collective-permute-start(bf16[192,512]{1,0:T(8,128)(2,1)S(1)} %get-tuple-element.60), channel_id=1, source_target_pairs={{0,8},{8,0},{16,24},{24,16},{1,9},{9,1},{17,25},{25,17},{2,10},{10... | collective-permute-start | bytes 589832 | tf_op jit(solution)/shard_map/ppermute | solution.py:219
  59.5 23.2 %copy-start.8 = (bf16[192,256]{1,0:T(8,128)(2,1)S(1)}, bf16[192,256]{1,0:T(8,128)(2,1)}, u32[]{:S(2)}) copy-start(bf16[192,256]{1,0:T(8,128)(2,1)} %get-tuple-element.44.pick_ref) | copy-start | bytes 294916
  60.8 20.0 %collective-permute-start.18 = (bf16[448,512]{1,0:T(8,128)(2,1)S(1)}, bf16[448,512]{1,0:T(8,128)(2,1)S(1)}, u32[]{:S(2)}, u32[]{:S(2)}) collective-permute-start(bf16[448,512]{1,0:T(8,128)(2,1)S(1)} %get-tuple-element.71), channel_id=1, source_target_pairs={{0,8},{8,0},{16,24},{24,16},{1,9},{9,1},{17,25},{25,17},{2,10},{10... | collective-permute-start | bytes 1376264 | tf_op jit(solution)/shard_map/ppermute | solution.py:219
  61.6 21.0 %collective-permute-start.19 = (bf16[448,512]{1,0:T(8,128)(2,1)S(1)}, bf16[448,512]{1,0:T(8,128)(2,1)S(1)}, u32[]{:S(2)}, u32[]{:S(2)}) collective-permute-start(bf16[448,512]{1,0:T(8,128)(2,1)S(1)} %get-tuple-element.72), channel_id=1, source_target_pairs={{0,16},{8,24},{16,0},{24,8},{1,17},{9,25},{17,1},{25,9},{2,18},{10... | collective-permute-start | bytes 1376264 | tf_op jit(solution)/shard_map/ppermute | solution.py:219
  62.9 19.7 %collective-permute-start.20 = (bf16[448,512]{1,0:T(8,128)(2,1)S(1)}, bf16[448,512]{1,0:T(8,128)(2,1)S(1)}, u32[]{:S(2)}, u32[]{:S(2)}) collective-permute-start(bf16[448,512]{1,0:T(8,128)(2,1)S(1)} %get-tuple-element.73), channel_id=1, source_target_pairs={{0,24},{8,16},{16,8},{24,0},{1,25},{9,17},{17,9},{25,1},{2,26},{10... | collective-permute-start | bytes 1376264 | tf_op jit(solution)/shard_map/ppermute | solution.py:219
  64.4 8.9 %collective-permute-start.15 = (bf16[48,2048]{1,0:T(8,128)(2,1)S(1)}, bf16[48,2048]{1,0:T(8,128)(2,1)S(1)}, u32[]{:S(2)}, u32[]{:S(2)}) collective-permute-start(bf16[48,2048]{1,0:T(8,128)(2,1)S(1)} %get-tuple-element.68), channel_id=1, source_target_pairs={{0,2},{1,3},{2,0},{3,1},{4,6},{5,7},{6,4},{7,5},{8,10},{9,11},{10,... | collective-permute-start | bytes 589832 | tf_op jit(solution)/shard_map/ppermute | solution.py:222
  64.4 10.5 %collective-permute-start.16 = (bf16[48,2048]{1,0:T(8,128)(2,1)S(1)}, bf16[48,2048]{1,0:T(8,128)(2,1)S(1)}, u32[]{:S(2)}, u32[]{:S(2)}) collective-permute-start(bf16[48,2048]{1,0:T(8,128)(2,1)S(1)} %get-tuple-element.69), channel_id=1, source_target_pairs={{0,4},{1,5},{2,6},{3,7},{4,0},{5,1},{6,2},{7,3},{8,12},{9,13},{10,... | collective-permute-start | bytes 589832 | tf_op jit(solution)/shard_map/ppermute | solution.py:222
  73.3 7.6 %collective-permute-start.17 = (bf16[48,2048]{1,0:T(8,128)(2,1)S(1)}, bf16[48,2048]{1,0:T(8,128)(2,1)S(1)}, u32[]{:S(2)}, u32[]{:S(2)}) collective-permute-start(bf16[48,2048]{1,0:T(8,128)(2,1)S(1)} %get-tuple-element.70), channel_id=1, source_target_pairs={{0,6},{1,7},{2,4},{3,5},{4,2},{5,3},{6,0},{7,1},{8,14},{9,15},{10,... | collective-permute-start | bytes 589832 | tf_op jit(solution)/shard_map/ppermute | solution.py:222
  83.9 2.0 %collective-permute-start.21 = (bf16[128,2048]{1,0:T(8,128)(2,1)S(1)}, bf16[128,2048]{1,0:T(8,128)(2,1)S(1)}, u32[]{:S(2)}, u32[]{:S(2)}) collective-permute-start(bf16[128,2048]{1,0:T(8,128)(2,1)S(1)} %get-tuple-element.78), channel_id=1, source_target_pairs={{0,1},{1,0},{2,3},{3,2},{4,5},{5,4},{6,7},{7,6},{8,9},{9,8},{10,11... | collective-permute-start | bytes 1572872 | tf_op jit(solution)/shard_map/ppermute | solution.py:222

commit v4 on v3

--- a/solution.py
+++ b/solution.py
@@ -10,6 +10,7 @@
 VMEM = pl.BlockSpec(memory_space=pltpu.VMEM)
 SMEM = pl.BlockSpec(memory_space=pltpu.SMEM)
 HBM = pl.BlockSpec(memory_space=pltpu.HBM)
+ANY = pl.BlockSpec(memory_space=pl.ANY)
 MIB = 1024 * 1024
 BF16 = jnp.bfloat16
 F32 = jnp.float32
@@ -25,51 +26,72 @@
     return jax.ShapeDtypeStruct((rows, cols), dtype)
 
 
-def call(kernel, outs, scalars=0, scratch=(), fetched=0, room=32):
+def call(kernel, outs, scalars=0, scratch=(), fetched=0, room=32, earlier=(), stored=()):
+    earlier = list(earlier)
+
+    def body(*refs):
+        inputs = len(refs) - len(outs) - len(scratch)
+        kernel(*refs[: inputs - len(earlier)], *refs[inputs:])
+
     def run(*operands):
         placed = len(operands) - scalars - fetched
         moved = sum(value.size * value.dtype.itemsize for value in (*operands, *outs))
         return pl.pallas_call(
-            kernel,
+            body,
             out_shape=outs,
-            in_specs=[SMEM] * scalars + [VMEM] * placed + [HBM] * fetched,
-            out_specs=[VMEM] * len(outs),
+            in_specs=[SMEM] * scalars + [VMEM] * placed + [HBM] * fetched + [ANY] * len(earlier),
+            out_specs=[HBM if i in stored else VMEM for i in range(len(outs))],
             scratch_shapes=list(scratch),
             cost_estimate=pl.CostEstimate(flops=0, bytes_accessed=moved, transcendentals=0),
             compiler_params=pltpu.CompilerParams(vmem_limit_bytes=room * MIB),
-        )(*operands)
+        )(*operands, *earlier)
 
     return run
 
 
 def after(values, *earlier):
-    return lax.optimization_barrier((values, earlier))[0]
+    return pl.pallas_call(
+        lambda *refs: None,
+        out_shape=[shape(*value.shape, value.dtype) for value in values],
+        in_specs=[HBM] * len(values) + [ANY] * len(earlier),
+        out_specs=[HBM] * len(values),
+        input_output_aliases={i: i for i in range(len(values))},
+        compiler_params=pltpu.CompilerParams(vmem_limit_bytes=MIB),
+    )(*values, *earlier)
+
+
+def start_copies(pairs, sems):
+    copies = [pltpu.make_async_copy(source, into, sems.at[i]) for i, (source, into) in enumerate(pairs)]
+    for copy in copies:
+        copy.start()
+    return copies
 
 
 def join_kernel(gate_ref, up_ref, down_ref, joined_ref, sems):
     depth = gate_ref.shape[0]
-    loads = [
-        pltpu.make_async_copy(source, joined_ref.at[pl.ds(i * depth, depth)], sems.at[i])
-        for i, source in enumerate((gate_ref, up_ref, down_ref))
-    ]
-    for load in loads:
-        load.start()
-    for load in loads:
-        load.wait()
+    rows = depth // 4
+    copies = start_copies(
+        [
+            (source.at[pl.ds(at * rows, rows)], joined_ref.at[pl.ds(i * depth + at * rows, rows)])
+            for i, source in enumerate((gate_ref, up_ref, down_ref))
+            for at in range(4)
+        ],
+        sems,
+    )
+    for copy in copies:
+        copy.wait()
 
 
 def pack_kernel(capacity, rank_ref, host_ref, route_a, *refs):
-    sources, outs, (route_b, x_a, x_b, dy_a, dy_b, sems) = refs[:5], refs[5:-6], refs[-6:]
+    sources, outs, (route_b, x, dy, filled_x, filled_dy, sems, out_sems) = refs[:5], refs[5:-7], refs[-7:]
     pick_ref, *send_refs = outs
-    loads = [
-        pltpu.make_async_copy(source, into, sems.at[i])
-        for i, (source, into) in enumerate(zip(sources, (route_b, x_a, x_b, dy_a, dy_b)))
-    ]
-    for load in loads:
-        load.start()
+    tokens = route_a.shape[1]
+    own_rows, other_rows = pl.ds(0, tokens), pl.ds(tokens, tokens)
+    loads = start_copies(
+        zip(sources, (route_b, x.at[own_rows], x.at[other_rows], dy.at[own_rows], dy.at[other_rows])), sems
+    )
     hot = host_ref.shape[0]
     slots = pick_ref.shape[0]
-    tokens = route_a.shape[1]
     block = 2 * capacity
     parts = slots // block
     label = lax.broadcasted_iota(jnp.int32, (hot, tokens), 0)
@@ -90,21 +112,21 @@
         position = jnp.sum(jnp.where(marked, before + base, 0), axis=0, keepdims=True) + offset
         return jnp.where(slot == position, 1.0, 0.0).astype(BF16)
 
-    pick_a = picks(route_a, 0)
+    pick_ref[:, :tokens] = picks(route_a, 0)
     loads[0].wait()
-    pick_b = picks(route_b, capacity)
-    pick_ref[:, :tokens] = pick_a
-    pick_ref[:, tokens:] = pick_b
-    for at, (a, b) in enumerate(((x_a, x_b), (dy_a, dy_b))):
+    pick_ref[:, tokens:] = picks(route_b, capacity)
+    stores = []
+    for at, (rows, filled) in enumerate(((x, filled_x), (dy, filled_dy))):
         loads[1 + 2 * at].wait()
         loads[2 + 2 * at].wait()
-        filled = (dot(pick_a, a[...], 1, 0) + dot(pick_b, b[...], 1, 0)).astype(BF16)
-        for k in range(parts):
-            rows = filled[k * block : (k + 1) * block]
-            if k < 2:
-                send_refs[k][at * block : (at + 1) * block] = rows
-            else:
-                send_refs[2 * k - 2 + at][...] = rows
+        filled[...] = dot(pick_ref[...], rows[...], 1, 0).astype(BF16)
+        targets = [ref.at[pl.ds(at * block, block)] for ref in send_refs[:2]] + send_refs[2 + at :: 2]
+        stores += start_copies(
+            [(filled.at[pl.ds(k * block, block)], target) for k, target in enumerate(targets)],
+            out_sems.at[at],
+        )
+    for store in stores:
+        store.wait()
 
 
 def columns_of(own_ref, depth):
@@ -130,48 +152,17 @@
     return weights[3 + half][start : start + rows]
 
 
-def act_kernel(*refs):
-    own_ref, x_ref, weights, (gate_ref, up_ref) = refs[0], refs[1], refs[2:-2], refs[-2:]
+def hidden_grads(gate_act, up_act, back_grad):
+    sigmoid_g = jax.nn.sigmoid(gate_act)
+    silu_gate = gate_act * sigmoid_g
+    gate_h = back_grad * up_act * sigmoid_g * (1.0 + gate_act * (1.0 - sigmoid_g))
+    return (silu_gate * up_act).astype(BF16), gate_h.astype(BF16), (back_grad * silu_gate).astype(BF16)
+
+
+def back_columns(own_ref, weights, gate_h, up_h, back_refs):
     depth = weights[0].shape[0] // 3
     half = depth // 2
-    gate_act = jnp.zeros(gate_ref.shape, F32)
-    up_act = jnp.zeros(up_ref.shape, F32)
-    for k, cols in enumerate(columns_of(own_ref, depth)):
-        x = x_ref[:, cols]
-        gate_act += dot(x, weight_rows(weights, k, 0, depth), 1, 0)
-        up_act += dot(x[:, :half], weight_rows(weights, k, depth, half), 1, 0)
-        up_act += dot(x[:, half:], weight_rows(weights, k, depth + half, half), 1, 0)
-    gate_ref[...] = gate_act
-    up_ref[...] = up_act
-
-
-def grad_kernel(parts, own_ref, gate_ref, up_ref, *refs):
-    got, weights, outs, dy_ref = refs[:parts], refs[parts : parts + 5], refs[parts + 5 : -1], refs[-1]
-    back_refs, own_term, (own_grads, *messages) = outs[:parts], outs[parts], outs[parts + 1 :]
-    slots, width = gate_ref.shape
-    block = slots // parts
-    depth = weights[0].shape[0] // 3
-    half = depth // 2
-    columns = columns_of(own_ref, depth)
-    for j, ref in enumerate(got):
-        dy_ref[j * block : (j + 1) * block] = ref[ref.shape[0] - block :]
-    back_grad = sum(dot(dy_ref[:, columns[k]], weight_rows(weights, k, 2 * depth, depth), 1, 0) for k in range(4))
-    gate_act, up_act = gate_ref[...], up_ref[...]
-    sigmoid_g = jax.nn.sigmoid(gate_act)
-    silu_gate = gate_act * sigmoid_g
-    hidden = (silu_gate * up_act).astype(BF16)
-    gate_h = (back_grad * up_act * sigmoid_g * (1.0 + gate_act * (1.0 - sigmoid_g))).astype(BF16)
-    up_h = (back_grad * silu_gate).astype(BF16)
-    for ref in (own_grads, *messages):
-        ref[:slots, :width] = gate_h
-        ref[:slots, width:] = up_h
-    for k in range(4):
-        term = dot(dy_ref[:, columns[k]], hidden, 0, 0)
-        if k == 0:
-            own_term[...] = term
-        else:
-            messages[k - 1][slots:, :width] = term[:half].astype(BF16)
-            messages[k - 1][slots:, width:] = term[half:].astype(BF16)
+    block = back_refs[0].shape[0]
     for k in range(4):
         for at in range(2):
             gate_rows = weight_rows(weights, k, at * half, half)
@@ -180,6 +171,64 @@
             cols = pl.ds(pl.multiple_of((own_ref[0] ^ k) * depth + at * half, half), half)
             for j, back_ref in enumerate(back_refs):
                 back_ref[:, cols] = slot_grad[j * block : (j + 1) * block]
+
+
+def near_kernel(own_ref, x_ref, *refs):
+    got, weights, outs, dy_ref = refs[:2], refs[2:7], refs[7:-1], refs[-1]
+    gate_ref, up_ref, grads_ref, hidden_ref, *back_refs = outs
+    near, width = hidden_ref.shape
+    block = near // 2
+    depth = weights[0].shape[0] // 3
+    half = depth // 2
+    gate_act = jnp.zeros((x_ref.shape[0], width), F32)
+    up_act = jnp.zeros((x_ref.shape[0], width), F32)
+    back_grad = jnp.zeros((near, width), F32)
+    for j, ref in enumerate(got):
+        dy_ref[j * block : (j + 1) * block] = ref[block:]
+    for k, cols in enumerate(columns_of(own_ref, depth)):
+        x = x_ref[:, cols]
+        gate_act += dot(x, weight_rows(weights, k, 0, depth), 1, 0)
+        up_act += dot(x[:, :half], weight_rows(weights, k, depth, half), 1, 0)
+        up_act += dot(x[:, half:], weight_rows(weights, k, depth + half, half), 1, 0)
+        back_grad += dot(dy_ref[:, cols], weight_rows(weights, k, 2 * depth, depth), 1, 0)
+    gate_ref[...] = gate_act[near:]
+    up_ref[...] = up_act[near:]
+    hidden, gate_h, up_h = hidden_grads(gate_act[:near], up_act[:near], back_grad)
+    hidden_ref[...] = hidden
+    grads_ref[:, :width] = gate_h
+    grads_ref[:, width:] = up_h
+    back_columns(own_ref, weights, gate_h, up_h, back_refs)
+
+
+def far_kernel(own_ref, gate_ref, up_ref, near_grads, near_hidden, *refs):
+    got, weights, outs, (dy_ref, hidden_ref) = refs[:4], refs[4:9], refs[9:-2], refs[-2:]
+    back_refs, own_term, (own_grads, *messages) = outs[:2], outs[2], outs[3:]
+    near, width = near_hidden.shape
+    slots = dy_ref.shape[0]
+    block = near // 2
+    depth = weights[0].shape[0] // 3
+    half = depth // 2
+    columns = columns_of(own_ref, depth)
+    for j, ref in enumerate(got):
+        dy_ref[j * block : (j + 1) * block] = ref[ref.shape[0] - block :]
+    back_grad = sum(
+        dot(dy_ref[near:, columns[k]], weight_rows(weights, k, 2 * depth, depth), 1, 0) for k in range(4)
+    )
+    hidden, gate_h, up_h = hidden_grads(gate_ref[...], up_ref[...], back_grad)
+    hidden_ref[:near] = near_hidden[...]
+    hidden_ref[near:] = hidden
+    for ref in (own_grads, *messages):
+        ref[:near] = near_grads[...]
+        ref[near:slots, :width] = gate_h
+        ref[near:slots, width:] = up_h
+    for k in range(4):
+        term = dot(dy_ref[:, columns[k]], hidden_ref[...], 0, 0)
+        if k == 0:
+            own_term[...] = term
+        else:
+            messages[k - 1][slots:, :width] = term[:half].astype(BF16)
+            messages[k - 1][slots:, width:] = term[half:].astype(BF16)
+    back_columns(own_ref, weights, gate_h, up_h, back_refs)
 
 
 def sum_kernel(*refs):
@@ -223,53 +272,62 @@
 
     route = route.reshape(1, tok_rows)
     route_b, tokens_b, cotangent_b = over_rep(route, 1), over_rep(tokens, 1), over_rep(cotangent, 1)
-    joined = call(join_kernel, [shape(3 * depth, width)], 0, [pltpu.SemaphoreType.DMA((3,))], 3, 62)(
-        w_gate[0], w_up[0], w_down_t[0]
-    )[0]
-    joined_1, joined_2 = over_own(joined, 1), over_own(joined, 2)
-
-    token_rows = pltpu.VMEM((tok_rows, model_width), BF16)
+    joined = call(
+        join_kernel, [shape(3 * depth, width)], 0, [pltpu.SemaphoreType.DMA((12,))], 3, 62, (), [0]
+    )(w_gate[0], w_up[0], w_down_t[0])[0]
+
+    token_rows = pltpu.VMEM((2 * tok_rows, model_width), BF16)
+    slot_rows = pltpu.VMEM((slots, model_width), BF16)
+    dma = pltpu.SemaphoreType.DMA
     pick, *sent = call(
         functools.partial(pack_kernel, capacity),
-        [shape(slots, 2 * tok_rows)]
-        + [shape(2 * block, model_width)] * 2
-        + [shape(block, model_width)] * (2 * parts - 4),
+        [shape(slots, 2 * tok_rows)] + [shape(2 * block, model_width)] * 2 + [shape(block, model_width)] * 4,
         2,
-        [pltpu.VMEM((1, tok_rows), jnp.int32)] + [token_rows] * 4 + [pltpu.SemaphoreType.DMA((5,))],
+        [pltpu.VMEM((1, tok_rows), jnp.int32)]
+        + [token_rows, token_rows, slot_rows, slot_rows, dma((5,)), dma((2, parts))],
         5,
         62,
+        (),
+        range(1, 7),
     )(rank, host, route, route_b, tokens, tokens_b, cotangent, cotangent_b)
-    far = range(2, parts)
     near = over_rep(sent[1], 2)
-    far_x = [over_rep(sent[2 * k - 2], 2 * k) for k in far]
-    (sent_dy, joined_1, joined_2) = after(
-        ([sent[2 * k - 1] for k in far], joined_1, joined_2), near, *far_x
-    )
-    far_dy = [over_rep(value, 2 * k) for k, value in zip(far, sent_dy)]
+    far_x = [over_rep(sent[2], 4), over_rep(sent[4], 6)]
+    joined = after([joined], pick)[0]
+    joined_1, joined_2 = over_own(joined, 1), over_own(joined, 2)
     split = 3 * depth // 2
-    joined_3 = [over_own(joined_1[:split], 2), over_own(joined_2[split:], 1)]
+    *far_dy, onward_1, onward_2 = after([sent[3], sent[5], joined_1[:split], joined_2[split:]], *far_x)
+    far_dy = [over_rep(far_dy[0], 4), over_rep(far_dy[1], 6)]
+    joined_3 = [over_own(onward_1, 2), over_own(onward_2, 1)]
+    weights = [joined, joined_1, joined_2, *joined_3]
 
     x, *pieces = call(
-        functools.partial(spread_kernel, depth), [shape(slots, model_width)] + [shape(slots, depth)] * 4, 1
+        functools.partial(spread_kernel, depth),
+        [shape(slots, model_width)] + [shape(slots, depth)] * 4,
+        1,
+        earlier=joined_3,
     )(own, sent[0], near, *far_x)
-    pieces = [pieces[0]] + [over_own(after(pieces[k], *joined_3), k) for k in range(1, 4)]
-    weights = [joined, joined_1, joined_2, *joined_3]
-    gate_act, up_act = call(act_kernel, [shape(slots, width, F32)] * 2, 1)(own, x, *weights)
-    far_dy = after(far_dy, *pieces)
+    pieces = [pieces[0]] + [over_own(pieces[k], k) for k in range(1, 4)]
+    acts = shape(block * 2, width, F32)
+    gate_act, up_act, near_grads, near_hidden, *back = call(
+        near_kernel,
+        [acts, acts, shape(2 * block, 2 * width), shape(2 * block, width)] + [shape(block, model_width)] * 2,
+        1,
+        [pltpu.VMEM((2 * block, model_width), BF16)],
+    )(own, x, sent[0], near, *weights)
+    returned = [back[0], over_rep(back[1], 2)]
     message = shape(slots + depth // 2, 2 * width)
-    outs = call(
-        functools.partial(grad_kernel, parts),
-        [shape(block, model_width)] * parts
+    *back, own_term, grads, message_1, message_2, message_3 = call(
+        far_kernel,
+        [shape(block, model_width)] * 2
         + [shape(depth, width, F32), shape(slots, 2 * width), message, message, message],
         1,
-        [pltpu.VMEM((slots, model_width), BF16)],
-    )(own, gate_act, up_act, sent[0], near, *far_dy, *weights)
-    back, own_term, grads, messages = outs[:parts], outs[parts], outs[parts + 1], outs[parts + 2 :]
-    returned = [over_rep(back[k], 2 * k) for k in range(1, parts)]
-    messages = [over_own(messages[k - 1], k) for k in range(1, 4)]
-
-    returned = after(returned, *messages)
-    mine, other = call(unpack_kernel, [shape(tok_rows, model_width)] * 2)(pick, back[0], *returned)
+        [pltpu.VMEM((slots, model_width), BF16), pltpu.VMEM((slots, width), BF16)],
+        earlier=[*pieces[1:], returned[1]],
+    )(own, gate_act, up_act, near_grads, near_hidden, sent[0], near, *far_dy, *weights)
+    returned += [over_rep(back[0], 4), over_rep(back[1], 6)]
+    messages = [over_own(message_1, 1), over_own(message_2, 2), over_own(message_3, 3)]
+
+    mine, other = call(unpack_kernel, [shape(tok_rows, model_width)] * 2, earlier=messages)(pick, *returned)
     x_grad = mine + over_rep(other, 1)
     out = call(sum_kernel, [shape(depth, width, F32)] * 3)(*pieces, grads, *messages, own_term)
     return (x_grad, *(grad[None] for grad in out))
@@ -314,7 +372,7 @@
 
     def shards(tokens, *rest):
         capacity = (3 * tokens.shape[0] + 2 * n_rep - 1) // (2 * n_rep)
-        if n_own == 4 and n_rep & (n_rep - 1) == 0 and capacity % 8 == 0:
+        if n_own == 4 and n_rep == 8 and capacity % 8 == 0:
             return shards_by_partner(n_rep, tokens, *rest)
         return shards_whole(tokens, *rest)
 

time: 87.2 us -> 114 us (1.31)
  Pallas kernels: 11.3 us -> 37.9 us
  starting transfers between devices: 23.1 us -> 27.9 us
  waiting for transfers between devices: 42.8 us -> 40.3 us
  local copies, waits for them, and re-layouts: 8.08 us -> 5.73 us
    pallas_call x7 -> x9, Pallas kernels: 11.3 us -> 37.9 us  [the longest x7 37.9 us: run(): pl.pallas_call(body, out_shape=outs, in_specs=[SMEM] * scalars + [VMEM] *...]
    ppermute x12, waiting for transfers between devices: 33.4 us -> 12.3 us  [over_rep(): return lax.ppermute(value, 'rep', [(i, i ^ k) for i in range(n_rep)])]
    ppermute x10, waiting for transfers between devices: 9.4 us -> 28 us  [over_own(): return lax.ppermute(value, 'own', [(i, i ^ k) for i in range(4)])]
    ppermute x12, starting transfers between devices: 10.5 us -> 14.2 us  [over_rep(): return lax.ppermute(value, 'rep', [(i, i ^ k) for i in range(n_rep)])]
    unnamed x26 -> x28, local copies, waits for them, and re-layouts: 6.53 us -> 4.19 us
  transfers between devices with their start and end apart: 22 -> 22, of which waited for: 12 -> 9; matrix products, arithmetic and copies ran while one was open for 0% -> 1% of each run, Pallas kernels for 10% -> 26%
where the time goes in v4:
time: 114 us
  waiting for transfers between devices  40.3 us (35%)
  Pallas kernels  37.9 us (33%)
  starting transfers between devices  27.9 us (24%)
  local copies, waits for them, and re-layouts  5.73 us (5%)
    pallas_call x7, Pallas kernels, run(): pl.pallas_call(body, out_shape=outs, in_specs=[SMEM] * scalars + [VMEM] *...  37.9 us
    ppermute x10, waiting for transfers between devices, over_own(): return lax.ppermute(value, 'own', [(i, i ^ k) for i in range(4)])  28 us
    ppermute x12, starting transfers between devices, over_rep(): return lax.ppermute(value, 'rep', [(i, i ^ k) for i in range(n_rep)])  14.2 us
    ppermute x10, starting transfers between devices, over_own(): return lax.ppermute(value, 'own', [(i, i ^ k) for i in range(4)])  13.6 us
    ppermute x12, waiting for transfers between devices, over_rep(): return lax.ppermute(value, 'rep', [(i, i ^ k) for i in range(n_rep)])  12.3 us
    unnamed x28, local copies, waits for them, and re-layouts  4.19 us
  transfers between devices with their start and end apart: 22, of which 9 were waited for; matrix products, arithmetic and copies ran while one was open for 1% of the time, Pallas kernels for 26%

profile of v4, /device:TPU:0, one launch (start us, length us, event | category | flops | bytes accessed | tf_op | source)
XLA Modules:
  0.0 113.5 jit_solution(17531181428274513975)
XLA Ops:
  0.6 0.0 copy-start.10
  0.6 0.5 collective-permute-start.1
  1.2 0.1 collective-permute-start.2
  1.2 0.0 copy-done.10
  1.3 0.5 collective-permute-start
  1.7 25.0 %shard_map.103.refs_0_ = bf16[1536,256]{1,0:T(8,128)(2,1)} custom-call(bf16[512,256]{1,0:T(8,128)(2,1)} %bitcast.9, bf16[512,256]{1,0:T(8,128)(2,1)} %bitcast.10, bf16[512,256]{1,0:T(8,128)(2,1)} %bitcast.11), custom_call_target="tpu_custom_call" | custom-call | bytes 1572864 | tf_op jit(solution)/shard_map/pallas_call | solution.py:39
  26.8 0.0 collective-permute-done.refs_3_
  26.8 0.0 collective-permute-done.1.refs_5_
  26.8 0.0 copy-start.8
  26.8 0.0 collective-permute-done.2.refs_7_
  26.8 0.0 copy-start.9
  26.8 0.5 copy-done.11
  27.4 0.2 copy-done.8
  27.6 0.2 copy-done.9
  27.8 4.4 %shard_map.102 = (bf16[192,256]{1,0:T(8,128)(2,1)}, bf16[96,2048]{1,0:T(8,128)(2,1)}, bf16[96,2048]{1,0:T(8,128)(2,1)}, bf16[48,2048]{1,0:T(8,128)(2,1)}, bf16[4...) custom-call(s32[1]{0:T(128)} %bitcast.refs_0_, s32[8]{0:T(128)} %refs_1_.1, ...), custom_call_target="tpu_custom_call" | custom-call | bytes 3769380 | tf_op jit(solution)/shard_map/pallas_call | solution.py:39
  32.2 0.9 copy-done.4
  33.1 2.5 %collective-permute-start.7 = (bf16[1536,256]{1,0:T(8,128)(2,1)S(1)}, bf16[1536,256]{1,0:T(8,128)(2,1)S(1)}, u32[]{:S(2)}, u32[]{:S(2)}) collective-permute-start(bf16[1536,256]{1,0:T(8,128)(2,1)S(1)} %shard_map.104.refs_4_.refs_9_), channel_id=1, source_target_pairs={{0,16},{8,24},{16,0},{24,8},{1,17},{9,25},{17,1},{25,9},{2,18},{10... | collective-permute-start | bytes 2359304 | tf_op jit(solution)/shard_map/ppermute | solution.py:268
  35.6 1.5 %collective-permute-start.6 = (bf16[1536,256]{1,0:T(8,128)(2,1)S(1)}, bf16[1536,256]{1,0:T(8,128)(2,1)S(1)}, u32[]{:S(2)}, u32[]{:S(2)}) collective-permute-start(bf16[1536,256]{1,0:T(8,128)(2,1)S(1)} %shard_map.104.refs_4_.refs_9_), channel_id=1, source_target_pairs={{0,8},{8,0},{16,24},{24,16},{1,9},{9,1},{17,25},{25,17},{2,10},{10... | collective-permute-start | bytes 2359304 | tf_op jit(solution)/shard_map/ppermute | solution.py:268
  37.1 2.6 %collective-permute-start.4 = (bf16[48,2048]{1,0:T(8,128)(2,1)S(1)}, bf16[48,2048]{1,0:T(8,128)(2,1)S(1)}, u32[]{:S(2)}, u32[]{:S(2)}) collective-permute-start(bf16[48,2048]{1,0:T(8,128)(2,1)S(1)} %copy-done.13), channel_id=1, source_target_pairs={{0,4},{1,5},{2,6},{3,7},{4,0},{5,1},{6,2},{7,3},{8,12},{9,13},{10,... | collective-permute-start | bytes 589832 | tf_op jit(solution)/shard_map/ppermute | solution.py:271
  39.7 1.4 %collective-permute-start.5 = (bf16[48,2048]{1,0:T(8,128)(2,1)S(1)}, bf16[48,2048]{1,0:T(8,128)(2,1)S(1)}, u32[]{:S(2)}, u32[]{:S(2)}) collective-permute-start(bf16[48,2048]{1,0:T(8,128)(2,1)S(1)} %copy-done.12), channel_id=1, source_target_pairs={{0,6},{1,7},{2,4},{3,5},{4,2},{5,3},{6,0},{7,1},{8,14},{9,15},{10,... | collective-permute-start | bytes 589832 | tf_op jit(solution)/shard_map/ppermute | solution.py:271
  41.1 0.2 collective-permute-start.3
  41.3 12.5 %collective-permute-done.7.refs_6_.refs_11_ = bf16[1536,256]{1,0:T(8,128)(2,1)S(1)} collective-permute-done((bf16[1536,256]{1,0:T(8,128)(2,1)S(1)}, bf16[1536,256]{1,0:T(8,128)(2,1)S(1)}, u32[]{:S(2)}, u32[]{:S(2)}) %collective-permute-start.7) | collective-permute-done | bytes 786464 | tf_op jit(solution)/shard_map/ppermute | solution.py:268
  53.8 0.8 slice.9.refs_3_
  54.6 0.7 collective-permute-done.6.refs_5_.refs_10_
  55.3 0.8 slice.8.refs_2_
  56.1 0.0 collective-permute-done.4.refs_4_.refs_3_
  56.1 0.0 collective-permute-done.5.refs_5_.refs_4_
  56.1 0.0 copy-start.1
  56.1 0.7 copy-done.2
  56.8 0.7 copy-done.7
  57.5 1.1 collective-permute-start.8
  58.5 1.5 %collective-permute-start.9 = (bf16[768,256]{1,0:T(8,128)(2,1)}, bf16[768,256]{1,0:T(8,128)(2,1)}, u32[]{:S(2)}, u32[]{:S(2)}) collective-permute-start(bf16[768,256]{1,0:T(8,128)(2,1)} %get-tuple-element.46), channel_id=1, source_target_pairs={{0,8},{8,0},{16,24},{24,16},{1,9},{9,1},{17,25},{25,17},{2,10},{10... | collective-permute-start | bytes 1179656 | tf_op jit(solution)/shard_map/ppermute | solution.py:268
  60.0 2.9 %collective-permute-start.11 = (bf16[48,2048]{1,0:T(8,128)(2,1)}, bf16[48,2048]{1,0:T(8,128)(2,1)}, u32[]{:S(2)}, u32[]{:S(2)}) collective-permute-start(bf16[48,2048]{1,0:T(8,128)(2,1)} %get-tuple-element.54), channel_id=1, source_target_pairs={{0,4},{1,5},{2,6},{3,7},{4,0},{5,1},{6,2},{7,3},{8,12},{9,13},{10,... | collective-permute-start | bytes 589832 | tf_op jit(solution)/shard_map/ppermute | solution.py:271
  62.9 1.0 collective-permute-start.12
  63.9 0.0 collective-permute-done.3.refs_2_.refs_3_.refs_6_
  63.9 4.2 %collective-permute-done.8.refs_5_.refs_7_.refs_12_ = bf16[768,256]{1,0:T(8,128)(2,1)} collective-permute-done((bf16[768,256]{1,0:T(8,128)(2,1)}, bf16[768,256]{1,0:T(8,128)(2,1)}, u32[]{:S(2)}, u32[]{:S(2)}) %collective-permute-start.8) | collective-permute-done | bytes 393248 | tf_op jit(solution)/shard_map/ppermute | solution.py:268
  68.2 1.1 collective-permute-done.9.refs_6_.refs_8_.refs_13_
  69.3 0.9 copy-done.3
  70.2 0.1 shard_map.106
  70.3 2.8 %shard_map.107 = (f32[96,256]{1,0:T(8,128)S(1)}, f32[96,256]{1,0:T(8,128)S(1)}, bf16[96,512]{1,0:T(8,128)(2,1)S(1)}, bf16[96,256]{1,0:T(8,128)(2,1)S(1)}, bf16[4...) custom-call(s32[1]{0:T(128)} %bitcast.2.refs_0_, bf16[192,2048]{1,0:T(8,128)(2,1)S(1)} %get-tuple-element.47.refs_1_, ...), custom_call_target="tpu_custom_call" | custom-call | bytes 5455876 | tf_op jit(solution)/shard_map/pallas_call | solution.py:39
  73.1 1.9 %collective-permute-start.10 = (bf16[48,2048]{1,0:T(8,128)(2,1)S(1)}, bf16[48,2048]{1,0:T(8,128)(2,1)S(1)}, u32[]{:S(2)}, u32[]{:S(2)}) collective-permute-start(bf16[48,2048]{1,0:T(8,128)(2,1)S(1)} %get-tuple-element.49), channel_id=1, source_target_pairs={{0,2},{1,3},{2,0},{3,1},{4,6},{5,7},{6,4},{7,5},{8,10},{9,11},{10,... | collective-permute-start | bytes 589832 | tf_op jit(solution)/shard_map/ppermute | solution.py:271
  75.0 1.3 %collective-permute-start.13 = (bf16[192,512]{1,0:T(8,128)(2,1)S(1)}, bf16[192,512]{1,0:T(8,128)(2,1)S(1)}, u32[]{:S(2)}, u32[]{:S(2)}) collective-permute-start(bf16[192,512]{1,0:T(8,128)(2,1)S(1)} %get-tuple-element.56), channel_id=1, source_target_pairs={{0,8},{8,0},{16,24},{24,16},{1,9},{9,1},{17,25},{25,17},{2,10},{10... | collective-permute-start | bytes 589832 | tf_op jit(solution)/shard_map/ppermute | solution.py:268
  76.2 0.8 collective-permute-start.14
  77.0 0.0 collective-permute-done.11.refs_7_
  77.0 1.4 %collective-permute-start.15 = (bf16[192,512]{1,0:T(8,128)(2,1)S(1)}, bf16[192,512]{1,0:T(8,128)(2,1)S(1)}, u32[]{:S(2)}, u32[]{:S(2)}) collective-permute-start(bf16[192,512]{1,0:T(8,128)(2,1)S(1)} %get-tuple-element.58), channel_id=1, source_target_pairs={{0,24},{8,16},{16,8},{24,0},{1,25},{9,17},{17,9},{25,1},{2,26},{10... | collective-permute-start | bytes 589832 | tf_op jit(solution)/shard_map/ppermute | solution.py:268
  78.5 0.0 collective-permute-done.12.refs_8_
  78.5 1.8 %collective-permute-done.10.refs_17_.refs_2_ = bf16[48,2048]{1,0:T(8,128)(2,1)S(1)} collective-permute-done((bf16[48,2048]{1,0:T(8,128)(2,1)S(1)}, bf16[48,2048]{1,0:T(8,128)(2,1)S(1)}, u32[]{:S(2)}, u32[]{:S(2)}) %collective-permute-start.10) | collective-permute-done | bytes 196640 | tf_op jit(solution)/shard_map/ppermute | solution.py:271
  80.3 1.9 %collective-permute-done.13.refs_14_.refs_1_ = bf16[192,512]{1,0:T(8,128)(2,1)S(1)} collective-permute-done((bf16[192,512]{1,0:T(8,128)(2,1)S(1)}, bf16[192,512]{1,0:T(8,128)(2,1)S(1)}, u32[]{:S(2)}, u32[]{:S(2)}) %collective-permute-start.13) | collective-permute-done | bytes 196640 | tf_op jit(solution)/shard_map/ppermute | solution.py:268
  82.2 3.5 %collective-permute-done.14.refs_15_.refs_2_ = bf16[192,512]{1,0:T(8,128)(2,1)S(1)} collective-permute-done((bf16[192,512]{1,0:T(8,128)(2,1)S(1)}, bf16[192,512]{1,0:T(8,128)(2,1)S(1)}, u32[]{:S(2)}, u32[]{:S(2)}) %collective-permute-start.14) | collective-permute-done | bytes 196640 | tf_op jit(solution)/shard_map/ppermute | solution.py:268
  85.7 0.0 collective-permute-done.15.refs_16_.refs_3_
  85.7 2.4 %shard_map.108 = (bf16[48,2048]{1,0:T(8,128)(2,1)S(1)}, bf16[48,2048]{1,0:T(8,128)(2,1)S(1)}, f32[512,256]{1,0:T(8,128)S(1)}, bf16[192,512]{1,0:T(8,128)(2,1)S(1...) custom-call(s32[1]{0:T(128)} %bitcast.2.refs_0_, ...), custom_call_target="tpu_custom_call" | custom-call | bytes 7159812 | tf_op jit(solution)/shard_map/pallas_call | solution.py:39
  88.2 1.2 %collective-permute-start.18 = (bf16[448,512]{1,0:T(8,128)(2,1)S(1)}, bf16[448,512]{1,0:T(8,128)(2,1)S(1)}, u32[]{:S(2)}, u32[]{:S(2)}) collective-permute-start(bf16[448,512]{1,0:T(8,128)(2,1)S(1)} %get-tuple-element.61), channel_id=1, source_target_pairs={{0,8},{8,0},{16,24},{24,16},{1,9},{9,1},{17,25},{25,17},{2,10},{10... | collective-permute-start | bytes 1376264 | tf_op jit(solution)/shard_map/ppermute | solution.py:268
  89.4 1.5 %collective-permute-start.19 = (bf16[448,512]{1,0:T(8,128)(2,1)S(1)}, bf16[448,512]{1,0:T(8,128)(2,1)S(1)}, u32[]{:S(2)}, u32[]{:S(2)}) collective-permute-start(bf16[448,512]{1,0:T(8,128)(2,1)S(1)} %get-tuple-element.62), channel_id=1, source_target_pairs={{0,16},{8,24},{16,0},{24,8},{1,17},{9,25},{17,1},{25,9},{2,18},{10... | collective-permute-start | bytes 1376264 | tf_op jit(solution)/shard_map/ppermute | solution.py:268
  90.9 0.8 collective-permute-start.20
  91.7 2.5 %collective-permute-start.16 = (bf16[48,2048]{1,0:T(8,128)(2,1)S(1)}, bf16[48,2048]{1,0:T(8,128)(2,1)S(1)}, u32[]{:S(2)}, u32[]{:S(2)}) collective-permute-start(bf16[48,2048]{1,0:T(8,128)(2,1)S(1)} %get-tuple-element.59), channel_id=1, source_target_pairs={{0,4},{1,5},{2,6},{3,7},{4,0},{5,1},{6,2},{7,3},{8,12},{9,13},{10,... | collective-permute-start | bytes 589832 | tf_op jit(solution)/shard_map/ppermute | solution.py:271
  94.2 0.7 collective-permute-start.17
  94.9 10.4 %collective-permute-done.16.refs_3_ = bf16[48,2048]{1,0:T(8,128)(2,1)S(1)} collective-permute-done((bf16[48,2048]{1,0:T(8,128)(2,1)S(1)}, bf16[48,2048]{1,0:T(8,128)(2,1)S(1)}, u32[]{:S(2)}, u32[]{:S(2)}) %collective-permute-start.16) | collective-permute-done | bytes 196640 | tf_op jit(solution)/shard_map/ppermute | solution.py:271
  105.3 0.0 collective-permute-done.17.refs_4_
  105.3 4.0 %collective-permute-done.19.refs_6_ = bf16[448,512]{1,0:T(8,128)(2,1)S(1)} collective-permute-done((bf16[448,512]{1,0:T(8,128)(2,1)S(1)}, bf16[448,512]{1,0:T(8,128)(2,1)S(1)}, u32[]{:S(2)}, u32[]{:S(2)}) %collective-permute-start.19) | collective-permute-done | bytes 458784 | tf_op jit(solution)/shard_map/ppermute | solution.py:268
  109.3 0.0 collective-permute-done.20.refs_7_
  109.3 1.3 %shard_map.109 = (bf16[128,2048]{1,0:T(8,128)(2,1)S(1)}, bf16[128,2048]{1,0:T(8,128)(2,1)S(1)}) custom-call(bf16[192,256]{1,0:T(8,128)(2,1)S(1)} %copy-done.5, bf16[48,2048]{1,0:T(8,128)(2,1)S(1)} %get-tuple-element.48.refs_1_, bf16[48,2048]{1,0:T(8,128)(2,1)S(1)} %collective-permute-done.10.refs_17_.refs_2_, ...), custom_call_target="tpu_custom_call" | custom-call | bytes 1933312 | tf_op jit(solution)/shard_map/pallas_call | solution.py:39
  110.6 0.1 collective-permute-start.21
  110.6 1.9 %shard_map.110 = (f32[512,256]{1,0:T(8,128)}, f32[512,256]{1,0:T(8,128)}, f32[512,256]{1,0:T(8,128)}) custom-call(bf16[192,512]{1,0:T(8,128)(2,1)S(1)} %get-tuple-element.66.refs_0_, bf16[192,512]{1,0:T(8,128)(2,1)S(1)} %collective-permute-done.13.refs_14_.refs_1_, bf16[192,512]{1,0:T(8,128)(2,1)S(1)} %collective-permute-done.14.refs_15_.refs_2_, ...), custom_call_target="tpu_custom_call" | custom-call | bytes 4456448 | tf_op jit(solution)/shard_map/pallas_call | solution.py:39
  112.6 0.9 add.3
  (20 shorter events, 0.0 us)
Async XLA Ops:
  0.6 0.7 copy-start.10
  0.6 26.2 %collective-permute-start.1 = (bf16[128,2048]{1,0:T(8,128)(2,1)}, bf16[128,2048]{1,0:T(8,128)(2,1)S(1)}, u32[]{:S(2)}, u32[]{:S(2)}) collective-permute-start(bf16[128,2048]{1,0:T(8,128)(2,1)} %refs_4_.1), channel_id=1, source_target_pairs={{0,1},{1,0},{2,3},{3,2},{4,5},{5,4},{6,7},{7,6},{8,9},{9,8},{10,11... | collective-permute-start | bytes 1572872 | tf_op jit(solution)/shard_map/ppermute | solution.py:271
  1.2 25.7 %collective-permute-start.2 = (bf16[128,2048]{1,0:T(8,128)(2,1)}, bf16[128,2048]{1,0:T(8,128)(2,1)S(1)}, u32[]{:S(2)}, u32[]{:S(2)}) collective-permute-start(bf16[128,2048]{1,0:T(8,128)(2,1)} %refs_6_.1), channel_id=1, source_target_pairs={{0,1},{1,0},{2,3},{3,2},{4,5},{5,4},{6,7},{7,6},{8,9},{9,8},{10,11... | collective-permute-start | bytes 1572872 | tf_op jit(solution)/shard_map/ppermute | solution.py:271
  1.3 25.5 %collective-permute-start = (s32[1,128]{1,0:T(1,128)S(1)}, s32[1,128]{1,0:T(1,128)S(1)}, u32[]{:S(2)}, u32[]{:S(2)}) collective-permute-start(s32[1,128]{1,0:T(1,128)S(1)} %bitcast.13), channel_id=1, source_target_pairs={{0,1},{1,0},{2,3},{3,2},{4,5},{5,4},{6,7},{7,6},{8,9},{9,8},{10,11... | collective-permute-start | bytes 1544 | tf_op jit(solution)/shard_map/ppermute | solution.py:271
  26.8 0.6 copy-start.11
  26.8 0.8 copy-start.8
  26.8 0.9 copy-start.9
  27.8 4.4 %copy-start = (bf16[1536,256]{1,0:T(8,128)(2,1)S(1)}, bf16[1536,256]{1,0:T(8,128)(2,1)}, u32[]{:S(2)}) copy-start(bf16[1536,256]{1,0:T(8,128)(2,1)} %shard_map.103.refs_0_) | copy-start | bytes 2359300
  32.2 0.9 copy-start.4
  33.1 4.0 %copy-start.13 = (bf16[48,2048]{1,0:T(8,128)(2,1)S(1)}, bf16[48,2048]{1,0:T(8,128)(2,1)}, u32[]{:S(2)}) copy-start(bf16[48,2048]{1,0:T(8,128)(2,1)} %get-tuple-element.41) | copy-start | bytes 589828
  33.1 6.6 %copy-start.12 = (bf16[48,2048]{1,0:T(8,128)(2,1)S(1)}, bf16[48,2048]{1,0:T(8,128)(2,1)}, u32[]{:S(2)}) copy-start(bf16[48,2048]{1,0:T(8,128)(2,1)} %get-tuple-element.42) | copy-start | bytes 589828
  33.1 20.7 %collective-permute-start.7 = (bf16[1536,256]{1,0:T(8,128)(2,1)S(1)}, bf16[1536,256]{1,0:T(8,128)(2,1)S(1)}, u32[]{:S(2)}, u32[]{:S(2)}) collective-permute-start(bf16[1536,256]{1,0:T(8,128)(2,1)S(1)} %shard_map.104.refs_4_.refs_9_), channel_id=1, source_target_pairs={{0,16},{8,24},{16,0},{24,8},{1,17},{9,25},{17,1},{25,9},{2,18},{10... | collective-permute-start | bytes 2359304 | tf_op jit(solution)/shard_map/ppermute | solution.py:268
  35.6 19.7 %collective-permute-start.6 = (bf16[1536,256]{1,0:T(8,128)(2,1)S(1)}, bf16[1536,256]{1,0:T(8,128)(2,1)S(1)}, u32[]{:S(2)}, u32[]{:S(2)}) collective-permute-start(bf16[1536,256]{1,0:T(8,128)(2,1)S(1)} %shard_map.104.refs_4_.refs_9_), channel_id=1, source_target_pairs={{0,8},{8,0},{16,24},{24,16},{1,9},{9,1},{17,25},{25,17},{2,10},{10... | collective-permute-start | bytes 2359304 | tf_op jit(solution)/shard_map/ppermute | solution.py:268
  37.1 18.9 %collective-permute-start.4 = (bf16[48,2048]{1,0:T(8,128)(2,1)S(1)}, bf16[48,2048]{1,0:T(8,128)(2,1)S(1)}, u32[]{:S(2)}, u32[]{:S(2)}) collective-permute-start(bf16[48,2048]{1,0:T(8,128)(2,1)S(1)} %copy-done.13), channel_id=1, source_target_pairs={{0,4},{1,5},{2,6},{3,7},{4,0},{5,1},{6,2},{7,3},{8,12},{9,13},{10,... | collective-permute-start | bytes 589832 | tf_op jit(solution)/shard_map/ppermute | solution.py:271
  39.7 16.4 %collective-permute-start.5 = (bf16[48,2048]{1,0:T(8,128)(2,1)S(1)}, bf16[48,2048]{1,0:T(8,128)(2,1)S(1)}, u32[]{:S(2)}, u32[]{:S(2)}) collective-permute-start(bf16[48,2048]{1,0:T(8,128)(2,1)S(1)} %copy-done.12), channel_id=1, source_target_pairs={{0,6},{1,7},{2,4},{3,5},{4,2},{5,3},{6,0},{7,1},{8,14},{9,15},{10,... | collective-permute-start | bytes 589832 | tf_op jit(solution)/shard_map/ppermute | solution.py:271
  41.1 22.9 %collective-permute-start.3 = (bf16[96,2048]{1,0:T(8,128)(2,1)}, bf16[96,2048]{1,0:T(8,128)(2,1)S(1)}, u32[]{:S(2)}, u32[]{:S(2)}) collective-permute-start(bf16[96,2048]{1,0:T(8,128)(2,1)} %get-tuple-element.40), channel_id=1, source_target_pairs={{0,2},{1,3},{2,0},{3,1},{4,6},{5,7},{6,4},{7,5},{8,10},{9,11},{10,... | collective-permute-start | bytes 1179656 | tf_op jit(solution)/shard_map/ppermute | solution.py:271
  54.6 1.5 %copy-start.6 = (bf16[48,2048]{1,0:T(8,128)(2,1)S(1)}, bf16[48,2048]{1,0:T(8,128)(2,1)}, u32[]{:S(2)}) copy-start(bf16[48,2048]{1,0:T(8,128)(2,1)} %get-tuple-element.44.refs_1_) | copy-start | bytes 589828
  56.1 0.7 copy-start.2
  56.1 13.2 %copy-start.1 = (bf16[96,2048]{1,0:T(8,128)(2,1)S(1)}, bf16[96,2048]{1,0:T(8,128)(2,1)}, u32[]{:S(2)}) copy-start(bf16[96,2048]{1,0:T(8,128)(2,1)} %get-tuple-element.39.refs_1_.refs_2_.refs_5_) | copy-start | bytes 1179652
  56.7 0.7 copy-start.7
  57.5 10.7 %collective-permute-start.8 = (bf16[768,256]{1,0:T(8,128)(2,1)}, bf16[768,256]{1,0:T(8,128)(2,1)}, u32[]{:S(2)}, u32[]{:S(2)}) collective-permute-start(bf16[768,256]{1,0:T(8,128)(2,1)} %get-tuple-element.45), channel_id=1, source_target_pairs={{0,16},{8,24},{16,0},{24,8},{1,17},{9,25},{17,1},{25,9},{2,18},{10... | collective-permute-start | bytes 1179656 | tf_op jit(solution)/shard_map/ppermute | solution.py:268
  58.5 10.8 %collective-permute-start.9 = (bf16[768,256]{1,0:T(8,128)(2,1)}, bf16[768,256]{1,0:T(8,128)(2,1)}, u32[]{:S(2)}, u32[]{:S(2)}) collective-permute-start(bf16[768,256]{1,0:T(8,128)(2,1)} %get-tuple-element.46), channel_id=1, source_target_pairs={{0,8},{8,0},{16,24},{24,16},{1,9},{9,1},{17,25},{25,17},{2,10},{10... | collective-permute-start | bytes 1179656 | tf_op jit(solution)/shard_map/ppermute | solution.py:268
  60.0 17.0 %collective-permute-start.11 = (bf16[48,2048]{1,0:T(8,128)(2,1)}, bf16[48,2048]{1,0:T(8,128)(2,1)}, u32[]{:S(2)}, u32[]{:S(2)}) collective-permute-start(bf16[48,2048]{1,0:T(8,128)(2,1)} %get-tuple-element.54), channel_id=1, source_target_pairs={{0,4},{1,5},{2,6},{3,7},{4,0},{5,1},{6,2},{7,3},{8,12},{9,13},{10,... | collective-permute-start | bytes 589832 | tf_op jit(solution)/shard_map/ppermute | solution.py:271
  62.9 15.6 %collective-permute-start.12 = (bf16[48,2048]{1,0:T(8,128)(2,1)}, bf16[48,2048]{1,0:T(8,128)(2,1)S(1)}, u32[]{:S(2)}, u32[]{:S(2)}) collective-permute-start(bf16[48,2048]{1,0:T(8,128)(2,1)} %copy-done.7), channel_id=1, source_target_pairs={{0,6},{1,7},{2,4},{3,5},{4,2},{5,3},{6,0},{7,1},{8,14},{9,15},{10,... | collective-permute-start | bytes 589832 | tf_op jit(solution)/shard_map/ppermute | solution.py:271
  69.3 0.9 copy-start.3
  73.1 7.2 %collective-permute-start.10 = (bf16[48,2048]{1,0:T(8,128)(2,1)S(1)}, bf16[48,2048]{1,0:T(8,128)(2,1)S(1)}, u32[]{:S(2)}, u32[]{:S(2)}) collective-permute-start(bf16[48,2048]{1,0:T(8,128)(2,1)S(1)} %get-tuple-element.49), channel_id=1, source_target_pairs={{0,2},{1,3},{2,0},{3,1},{4,6},{5,7},{6,4},{7,5},{8,10},{9,11},{10,... | collective-permute-start | bytes 589832 | tf_op jit(solution)/shard_map/ppermute | solution.py:271
  75.0 7.2 %collective-permute-start.13 = (bf16[192,512]{1,0:T(8,128)(2,1)S(1)}, bf16[192,512]{1,0:T(8,128)(2,1)S(1)}, u32[]{:S(2)}, u32[]{:S(2)}) collective-permute-start(bf16[192,512]{1,0:T(8,128)(2,1)S(1)} %get-tuple-element.56), channel_id=1, source_target_pairs={{0,8},{8,0},{16,24},{24,16},{1,9},{9,1},{17,25},{25,17},{2,10},{10... | collective-permute-start | bytes 589832 | tf_op jit(solution)/shard_map/ppermute | solution.py:268
  76.2 9.5 %collective-permute-start.14 = (bf16[192,512]{1,0:T(8,128)(2,1)S(1)}, bf16[192,512]{1,0:T(8,128)(2,1)S(1)}, u32[]{:S(2)}, u32[]{:S(2)}) collective-permute-start(bf16[192,512]{1,0:T(8,128)(2,1)S(1)} %get-tuple-element.57), channel_id=1, source_target_pairs={{0,16},{8,24},{16,0},{24,8},{1,17},{9,25},{17,1},{25,9},{2,18},{10... | collective-permute-start | bytes 589832 | tf_op jit(solution)/shard_map/ppermute | solution.py:268
  77.0 8.7 %collective-permute-start.15 = (bf16[192,512]{1,0:T(8,128)(2,1)S(1)}, bf16[192,512]{1,0:T(8,128)(2,1)S(1)}, u32[]{:S(2)}, u32[]{:S(2)}) collective-permute-start(bf16[192,512]{1,0:T(8,128)(2,1)S(1)} %get-tuple-element.58), channel_id=1, source_target_pairs={{0,24},{8,16},{16,8},{24,0},{1,25},{9,17},{17,9},{25,1},{2,26},{10... | collective-permute-start | bytes 589832 | tf_op jit(solution)/shard_map/ppermute | solution.py:268
  85.7 23.6 %copy-start.5 = (bf16[192,256]{1,0:T(8,128)(2,1)S(1)}, bf16[192,256]{1,0:T(8,128)(2,1)}, u32[]{:S(2)}) copy-start(bf16[192,256]{1,0:T(8,128)(2,1)} %get-tuple-element.38.refs_1_.refs_0_) | copy-start | bytes 294916
  88.2 17.1 %collective-permute-start.18 = (bf16[448,512]{1,0:T(8,128)(2,1)S(1)}, bf16[448,512]{1,0:T(8,128)(2,1)S(1)}, u32[]{:S(2)}, u32[]{:S(2)}) collective-permute-start(bf16[448,512]{1,0:T(8,128)(2,1)S(1)} %get-tuple-element.61), channel_id=1, source_target_pairs={{0,8},{8,0},{16,24},{24,16},{1,9},{9,1},{17,25},{25,17},{2,10},{10... | collective-permute-start | bytes 1376264 | tf_op jit(solution)/shard_map/ppermute | solution.py:268
  89.4 19.9 %collective-permute-start.19 = (bf16[448,512]{1,0:T(8,128)(2,1)S(1)}, bf16[448,512]{1,0:T(8,128)(2,1)S(1)}, u32[]{:S(2)}, u32[]{:S(2)}) collective-permute-start(bf16[448,512]{1,0:T(8,128)(2,1)S(1)} %get-tuple-element.62), channel_id=1, source_target_pairs={{0,16},{8,24},{16,0},{24,8},{1,17},{9,25},{17,1},{25,9},{2,18},{10... | collective-permute-start | bytes 1376264 | tf_op jit(solution)/shard_map/ppermute | solution.py:268
  90.9 18.4 %collective-permute-start.20 = (bf16[448,512]{1,0:T(8,128)(2,1)S(1)}, bf16[448,512]{1,0:T(8,128)(2,1)S(1)}, u32[]{:S(2)}, u32[]{:S(2)}) collective-permute-start(bf16[448,512]{1,0:T(8,128)(2,1)S(1)} %get-tuple-element.63), channel_id=1, source_target_pairs={{0,24},{8,16},{16,8},{24,0},{1,25},{9,17},{17,9},{25,1},{2,26},{10... | collective-permute-start | bytes 1376264 | tf_op jit(solution)/shard_map/ppermute | solution.py:268
  91.7 13.5 %collective-permute-start.16 = (bf16[48,2048]{1,0:T(8,128)(2,1)S(1)}, bf16[48,2048]{1,0:T(8,128)(2,1)S(1)}, u32[]{:S(2)}, u32[]{:S(2)}) collective-permute-start(bf16[48,2048]{1,0:T(8,128)(2,1)S(1)} %get-tuple-element.59), channel_id=1, source_target_pairs={{0,4},{1,5},{2,6},{3,7},{4,0},{5,1},{6,2},{7,3},{8,12},{9,13},{10,... | collective-permute-start | bytes 589832 | tf_op jit(solution)/shard_map/ppermute | solution.py:271
  94.2 11.1 %collective-permute-start.17 = (bf16[48,2048]{1,0:T(8,128)(2,1)S(1)}, bf16[48,2048]{1,0:T(8,128)(2,1)S(1)}, u32[]{:S(2)}, u32[]{:S(2)}) collective-permute-start(bf16[48,2048]{1,0:T(8,128)(2,1)S(1)} %get-tuple-element.60), channel_id=1, source_target_pairs={{0,6},{1,7},{2,4},{3,5},{4,2},{5,3},{6,0},{7,1},{8,14},{9,15},{10,... | collective-permute-start | bytes 589832 | tf_op jit(solution)/shard_map/ppermute | solution.py:271
  110.6 2.0 %collective-permute-start.21 = (bf16[128,2048]{1,0:T(8,128)(2,1)S(1)}, bf16[128,2048]{1,0:T(8,128)(2,1)S(1)}, u32[]{:S(2)}, u32[]{:S(2)}) collective-permute-start(bf16[128,2048]{1,0:T(8,128)(2,1)S(1)} %get-tuple-element.65), channel_id=1, source_target_pairs={{0,1},{1,0},{2,3},{3,2},{4,5},{5,4},{6,7},{7,6},{8,9},{9,8},{10,11... | collective-permute-start | bytes 1572872 | tf_op jit(solution)/shard_map/ppermute | solution.py:271

commit v5 on v4

v5 whole, which is shorter than its diff:
```python
import functools

import jax
import jax.numpy as jnp
from jax import lax
from jax.experimental import pallas as pl
from jax.experimental.pallas import tpu as pltpu
from jax.sharding import PartitionSpec as P

VMEM = pl.BlockSpec(memory_space=pltpu.VMEM)
SMEM = pl.BlockSpec(memory_space=pltpu.SMEM)
HBM = pl.BlockSpec(memory_space=pltpu.HBM)
ANY = pl.BlockSpec(memory_space=pl.ANY)
MIB = 1024 * 1024
BF16 = jnp.bfloat16
F32 = jnp.float32


def dot(left, right, left_dim, right_dim):
    return lax.dot_general(
        left, right, (((left_dim,), (right_dim,)), ((), ())), preferred_element_type=F32
    )


def shape(rows, cols, dtype=BF16):
    return jax.ShapeDtypeStruct((rows, cols), dtype)


def call(kernel, outs, scalars=0, scratch=(), fetched=0, room=32, earlier=(), stored=()):
    earlier = list(earlier)

    def body(*refs):
        inputs = len(refs) - len(outs) - len(scratch)
        kernel(*refs[: inputs - len(earlier)], *refs[inputs:])

    def run(*operands):
        placed = len(operands) - scalars - fetched
        moved = sum(value.size * value.dtype.itemsize for value in (*operands, *outs))
        return pl.pallas_call(
            body,
            out_shape=outs,
            in_specs=[SMEM] * scalars + [VMEM] * placed + [HBM] * fetched + [ANY] * len(earlier),
            out_specs=[HBM if i in stored else VMEM for i in range(len(outs))],
            scratch_shapes=list(scratch),
            cost_estimate=pl.CostEstimate(flops=0, bytes_accessed=moved, transcendentals=0),
            compiler_params=pltpu.CompilerParams(vmem_limit_bytes=room * MIB),
        )(*operands, *earlier)

    return run


def after(values, *earlier):
    return pl.pallas_call(
        lambda *refs: None,
        out_shape=[shape(*value.shape, value.dtype) for value in values],
        in_specs=[ANY] * (len(values) + len(earlier)),
        out_specs=[ANY] * len(values),
        input_output_aliases={i: i for i in range(len(values))},
        compiler_params=pltpu.CompilerParams(vmem_limit_bytes=MIB),
    )(*values, *earlier)


def start_copies(pairs, sems):
    copies = [pltpu.make_async_copy(source, into, sems.at[i]) for i, (source, into) in enumerate(pairs)]
    for copy in copies:
        copy.start()
    return copies


def pack_kernel(capacity, rank_ref, host_ref, route_a, *refs):
    sources, outs, (route_b, x, filled, weights, sems, out_sems) = refs[:6], refs[6:-6], refs[-6:]
    pick_ref, joined_ref, *send_refs = outs
    tokens = route_a.shape[1]
    width = weights.shape[1] // 3
    loads = start_copies(
        zip(
            sources,
            (route_b, x.at[pl.ds(0, tokens)], x.at[pl.ds(tokens, tokens)])
            + tuple(weights.at[:, pl.ds(i * width, width)] for i in range(3)),
        ),
        sems,
    )
    hot = host_ref.shape[0]
    slots = pick_ref.shape[0]
    block = 2 * capacity
    label = lax.broadcasted_iota(jnp.int32, (hot, tokens), 0)
    base = jnp.zeros((hot, tokens), jnp.int32)
    for e in range(hot):
        apart = host_ref[e] ^ rank_ref[0]
        start = jnp.where((apart & 1) == 0, (apart >> 1) * block, -2 * slots)
        base = jnp.where(label == e, start, base)
    earlier = lax.broadcasted_iota(jnp.int32, (tokens, tokens), 0) < lax.broadcasted_iota(
        jnp.int32, (tokens, tokens), 1
    )
    earlier = jnp.where(earlier, 1.0, 0.0).astype(BF16)
    slot = lax.broadcasted_iota(jnp.int32, (slots, tokens), 0)

    def picks(route_ref, offset):
        marked = route_ref[...] == label
        before = dot(jnp.where(marked, 1.0, 0.0).astype(BF16), earlier, 1, 0).astype(jnp.int32)
        position = jnp.sum(jnp.where(marked, before + base, 0), axis=0, keepdims=True) + offset
        return jnp.where(slot == position, 1.0, 0.0).astype(BF16)

    pick_ref[:, :tokens] = picks(route_a, 0)
    loads[0].wait()
    pick_ref[:, tokens:] = picks(route_b, capacity)
    loads[1].wait()
    loads[2].wait()
    filled[...] = dot(pick_ref[...], x[...], 1, 0).astype(BF16)
    for load in loads[3:]:
        load.wait()
    stores = start_copies(
        [(filled.at[pl.ds(k * block, block)], ref) for k, ref in enumerate(send_refs)] + [(weights, joined_ref)],
        out_sems,
    )
    for store in stores:
        store.wait()


def pack_more_kernel(pick_ref, *refs):
    sources, send_refs, (rows, filled, sems, out_sems) = refs[:2], refs[2:-4], refs[-4:]
    tokens = sources[0].shape[0]
    block = send_refs[0].shape[0]
    loads = start_copies(zip(sources, (rows.at[pl.ds(0, tokens)], rows.at[pl.ds(tokens, tokens)])), sems)
    for load in loads:
        load.wait()
    filled[...] = dot(pick_ref[...], rows[...], 1, 0).astype(BF16)
    stores = start_copies(
        [(filled.at[pl.ds(k * block, block)], ref) for k, ref in enumerate(send_refs)], out_sems
    )
    for store in stores:
        store.wait()


def weight_parts(own_ref, weights):
    depth = weights[0].shape[0]
    half = depth // 2
    for k, ref in enumerate(weights):
        partner, start = (k, 0) if k < 3 else (3, (k - 3) * half)
        yield pl.ds(pl.multiple_of((own_ref[0] ^ partner) * depth + start, half), ref.shape[0]), ref


def columns_of(own_ref, depth):
    return [pl.ds(pl.multiple_of((own_ref[0] ^ k) * depth, depth), depth) for k in range(4)]


def spread_kernel(own_ref, *refs):
    got, (x_ref, *piece_refs) = refs[:-5], refs[-5:]
    block = got[0].shape[0]
    columns = columns_of(own_ref, piece_refs[0].shape[1])
    for j, ref in enumerate(got):
        rows = slice(j * block, (j + 1) * block)
        x_ref[rows] = ref[...]
        for k, piece_ref in enumerate(piece_refs):
            piece_ref[rows] = ref[:, columns[k]]


def act_kernel(own_ref, x_ref, *refs):
    weights, acts_ref = refs[:-1], refs[-1]
    both = acts_ref.shape[1]
    acts_ref[...] = sum(dot(x_ref[:, cols], ref[:, :both], 1, 0) for cols, ref in weight_parts(own_ref, weights))


def grad_kernel(parts, own_ref, acts_ref, *refs):
    got, weights, outs, dy_ref = refs[:parts], refs[parts : parts + 5], refs[parts + 5 : -1], refs[-1]
    back_refs, own_term, (own_grads, *messages) = outs[:parts], outs[parts], outs[parts + 1 :]
    slots, both = acts_ref.shape
    width = both // 2
    block = slots // parts
    depth = weights[0].shape[0]
    half = depth // 2
    for j, ref in enumerate(got):
        dy_ref[j * block : (j + 1) * block] = ref[...]
    back_grad = sum(dot(dy_ref[:, cols], ref[:, both:], 1, 0) for cols, ref in weight_parts(own_ref, weights))
    gate_act, up_act = acts_ref[:, :width], acts_ref[:, width:]
    sigmoid_g = jax.nn.sigmoid(gate_act)
    silu_gate = gate_act * sigmoid_g
    hidden = (silu_gate * up_act).astype(BF16)
    gate_h = back_grad * up_act * sigmoid_g * (1.0 + gate_act * (1.0 - sigmoid_g))
    own_grads[:, :width] = gate_h.astype(BF16)
    own_grads[:, width:] = (back_grad * silu_gate).astype(BF16)
    grads = own_grads[...]
    for k, cols in enumerate(columns_of(own_ref, depth)):
        term = dot(dy_ref[:, cols], hidden, 0, 0)
        if k == 0:
            own_term[...] = term
        else:
            messages[k - 1][:slots] = grads
            messages[k - 1][slots:, :width] = term[:half].astype(BF16)
            messages[k - 1][slots:, width:] = term[half:].astype(BF16)
    for cols, ref in weight_parts(own_ref, weights):
        slot_grad = dot(grads, ref[:, :both], 1, 1).astype(BF16)
        for j, back_ref in enumerate(back_refs):
            back_ref[:, cols] = slot_grad[j * block : (j + 1) * block]


def sum_kernel(*refs):
    pieces, messages, own_term, (gate_ref, up_ref, down_ref) = refs[:4], refs[4:8], refs[8], refs[9:]
    slots = pieces[0].shape[0]
    depth, width = gate_ref.shape
    half = depth // 2
    total = sum(dot(piece[...], got[:slots], 0, 0) for piece, got in zip(pieces, messages))
    gate_ref[...] = total[:, :width]
    up_ref[...] = total[:, width:]
    for rows, cols in ((slice(0, half), slice(0, width)), (slice(half, depth), slice(width, 2 * width))):
        down_ref[rows] = own_term[rows] + sum(got[slots:, cols].astype(F32) for got in messages[1:])


def unpack_kernel(pick_ref, *refs):
    returned, (mine_ref, other_ref) = refs[:-2], refs[-2:]
    tokens = mine_ref.shape[0]
    block = returned[0].shape[0]
    for at, ref in enumerate((other_ref, mine_ref)):
        half = slice((1 - at) * tokens, (2 - at) * tokens)
        ref[...] = sum(
            dot(pick_ref[k * block : (k + 1) * block, half], part[...], 0, 0) for k, part in enumerate(returned)
        ).astype(BF16)


def shards_by_partner(n_rep, tokens, cotangent, route, host, w_gate, w_up, w_down_t):
    tok_rows, model_width = tokens.shape
    hot = host.shape[0]
    _, depth, width = w_gate.shape
    capacity = (3 * tok_rows + 2 * hot - 1) // (2 * hot)
    slots = hot * capacity
    parts = n_rep // 2
    block = 2 * capacity
    own = lax.axis_index("own").astype(jnp.int32).reshape(1)
    rank = lax.axis_index("rep").astype(jnp.int32).reshape(1)

    def over_own(value, k):
        return lax.ppermute(value, "own", [(i, i ^ k) for i in range(4)])

    def over_rep(value, k):
        return lax.ppermute(value, "rep", [(i, i ^ k) for i in range(n_rep)])

    route = route.reshape(1, tok_rows)
    route_b, tokens_b, cotangent_b = over_rep(route, 1), over_rep(tokens, 1), over_rep(cotangent, 1)
    token_rows = pltpu.VMEM((2 * tok_rows, model_width), BF16)
    slot_rows = pltpu.VMEM((slots, model_width), BF16)
    dma = pltpu.SemaphoreType.DMA
    pick, joined, *sent_x = call(
        functools.partial(pack_kernel, capacity),
        [shape(slots, 2 * tok_rows), shape(depth, 3 * width)] + [shape(block, model_width)] * parts,
        2,
        [pltpu.VMEM((1, tok_rows), jnp.int32), token_rows, slot_rows, pltpu.VMEM((depth, 3 * width), BF16)]
        + [dma((6,)), dma((parts + 1,))],
        6,
        62,
        [cotangent_b],
        range(1, 2 + parts),
    )(rank, host, route, route_b, tokens, tokens_b, w_gate[0], w_up[0], w_down_t[0])
    got_x = [over_rep(sent_x[k], 2 * k) for k in range(1, parts)]
    joined_1, joined_2 = over_own(joined, 1), over_own(joined, 2)
    sent_dy = call(
        pack_more_kernel,
        [shape(block, model_width)] * parts,
        0,
        [token_rows, slot_rows, dma((2,)), dma((parts,))],
        2,
        62,
        (),
        range(parts),
    )(pick, cotangent, cotangent_b)
    *far_dy, onward_1, onward_2 = after(
        [*sent_dy[1:], joined_1[: depth // 2], joined_2[depth // 2 :]], *got_x
    )
    got_dy = [over_rep(far_dy[k - 1], 2 * k) for k in range(1, parts)]
    joined_3 = [over_own(onward_1, 2), over_own(onward_2, 1)]
    weights = [joined, joined_1, joined_2, *joined_3]

    x, *pieces = call(
        spread_kernel, [shape(slots, model_width)] + [shape(slots, depth)] * 4, 1, earlier=joined_3
    )(own, sent_x[0], *got_x)
    pieces = [pieces[0]] + [over_own(pieces[k], k) for k in range(1, 4)]
    acts = call(act_kernel, [shape(slots, 2 * width, F32)], 1)(own, x, *weights)[0]
    message = shape(slots + depth // 2, 2 * width)
    outs = call(
        functools.partial(grad_kernel, parts),
        [shape(block, model_width)] * parts
        + [shape(depth, width, F32), shape(slots, 2 * width), message, message, message],
        1,
        [slot_rows],
        earlier=pieces[1:],
    )(own, acts, sent_dy[0], *got_dy, *weights)
    back, own_term, grads, messages = outs[:parts], outs[parts], outs[parts + 1], outs[parts + 2 :]
    returned = [back[0]] + [over_rep(back[k], 2 * k) for k in range(1, parts)]
    messages = [over_own(messages[k - 1], k) for k in range(1, 4)]

    mine, other = call(unpack_kernel, [shape(tok_rows, model_width)] * 2, earlier=messages)(pick, *returned)
    x_grad = mine + over_rep(other, 1)
    out = call(sum_kernel, [shape(depth, width, F32)] * 3)(*pieces, grads, *messages, own_term)
    return (x_grad, *(grad[None] for grad in out))


def shards_whole(tokens, cotangent, route, host, w_gate, w_up, w_down_t):
    tok_rows, model_width = tokens.shape
    hot = host.shape[0]
    width = w_gate.shape[2]
    capacity = max(2, (3 * tok_rows + 2 * hot - 1) // (2 * hot))
    slots = hot * capacity
    labels = lax.broadcasted_iota(jnp.int32, (tok_rows, hot), 1)
    target = jnp.sum(jnp.where(route == labels, host[None, :], 0), axis=1)
    marked = (target[:, None] == labels).astype(jnp.int32)
    arrival = jnp.sum(jnp.cumsum(marked, axis=0) * marked, axis=1) - 1
    position = target * capacity + arrival
    pick = (lax.broadcasted_iota(jnp.int32, (slots, tok_rows), 0) == position[None, :]).astype(BF16)

    def exchange(value):
        split = value.astype(BF16).reshape(hot, capacity, model_width)
        return lax.all_to_all(split, "rep", split_axis=0, concat_axis=0, tiled=True).reshape(slots, model_width)

    slot_x, slot_dy = exchange(dot(pick, tokens, 1, 0)), exchange(dot(pick, cotangent, 1, 0))
    gate, up, down = (lax.all_gather(w[0], "own", axis=0, tiled=True) for w in (w_gate, w_up, w_down_t))
    gate_act, up_act, back_grad = dot(slot_x, gate, 1, 0), dot(slot_x, up, 1, 0), dot(slot_dy, down, 1, 0)
    sigmoid_g = jax.nn.sigmoid(gate_act)
    silu_gate = gate_act * sigmoid_g
    hidden = (silu_gate * up_act).astype(BF16)
    grad_gate_h = (back_grad * up_act * sigmoid_g * (1.0 + gate_act * (1.0 - sigmoid_g))).astype(BF16)
    grad_up_h = (back_grad * silu_gate).astype(BF16)
    returned = exchange(dot(grad_gate_h, gate, 1, 1) + dot(grad_up_h, up, 1, 1))
    x_grad = dot(pick, returned, 0, 0).astype(BF16)
    terms = [dot(slot_x, grad_gate_h, 0, 0), dot(slot_x, grad_up_h, 0, 0), dot(slot_dy, hidden, 0, 0)]
    summed = lax.psum_scatter(
        jnp.concatenate(terms, axis=1).astype(BF16), "own", scatter_dimension=0, tiled=True
    ).astype(F32)
    return (x_grad, *(summed[None, :, i * width : (i + 1) * width] for i in range(3)))


def solution(mesh):
    n_own, n_rep = mesh.shape["own"], mesh.shape["rep"]

    def shards(tokens, *rest):
        capacity = (3 * tokens.shape[0] + 2 * n_rep - 1) // (2 * n_rep)
        if n_own == 4 and n_rep == 8 and capacity % 8 == 0:
            return shards_by_partner(n_rep, tokens, *rest)
        return shards_whole(tokens, *rest)

    return jax.shard_map(
        shards,
        mesh=mesh,
        in_specs=(
            P(("own", "rep"), None),
            P(("own", "rep"), None),
            P(("own", "rep"), None),
            P(),
            P("rep", "own", None),
            P("rep", "own", None),
            P("rep", "own", None),
        ),
        out_specs=(
            P(("own", "rep"), None),
            P("rep", "own", None),
            P("rep", "own", None),
            P("rep", "own", None),
        ),
        check_vma=False,
    )
```

time: 114 us -> 81.7 us (0.72)
  Pallas kernels: 37.9 us -> 14.7 us
  waiting for transfers between devices: 40.3 us -> 29.8 us
  starting transfers between devices: 27.9 us -> 33.3 us
  local copies, waits for them, and re-layouts: 5.73 us -> 1.86 us
    pallas_call x7, Pallas kernels: 37.9 us -> 14.7 us  [run(): pl.pallas_call(body, out_shape=outs, in_specs=[SMEM] * scalars + [VMEM] *...]
    ppermute x10, waiting for transfers between devices: 28 us -> 17 us  [over_own(): return lax.ppermute(value, 'own', [(i, i ^ k) for i in range(4)])]
    ppermute x12 -> x13, starting transfers between devices: 14.2 us -> 19.9 us  [over_rep(): return lax.ppermute(value, 'rep', [(i, i ^ k) for i in range(n_rep)])]
    unnamed x28 -> x24, local copies, waits for them, and re-layouts: 4.19 us -> 1.8 us
    slice x2, local copies, waits for them, and re-layouts: 1.54 us -> 0.05 us  [the longest x1 0.03 us: shards_by_partner(): joined_2[depth // 2:]]
    ppermute x12 -> x13, waiting for transfers between devices: 12.3 us -> 12.9 us  [over_rep(): return lax.ppermute(value, 'rep', [(i, i ^ k) for i in range(n_rep)])]
  transfers between devices with their start and end apart: 22 -> 23, of which waited for: 9 -> 13; matrix products, arithmetic and copies ran while one was open for 1% -> 0% of each run, Pallas kernels for 26% -> 9%
where the time goes in v5:
time: 81.7 us; the launch traced here: 81.4 us
  starting transfers between devices  33.3 us (41%)
  waiting for transfers between devices  29.8 us (36%)
  Pallas kernels  14.7 us (18%)
  local copies, waits for them, and re-layouts  1.86 us (2%)
  other arithmetic  0.92 us (1%)
    ppermute x13, starting transfers between devices, over_rep(): return lax.ppermute(value, 'rep', [(i, i ^ k) for i in range(n_rep)])  19.9 us
    ppermute x10, waiting for transfers between devices, over_own(): return lax.ppermute(value, 'own', [(i, i ^ k) for i in range(4)])  17 us
    pallas_call x7, Pallas kernels, run(): pl.pallas_call(body, out_shape=outs, in_specs=[SMEM] * scalars + [VMEM] *...  14.7 us
    ppermute x10, starting transfers between devices, over_own(): return lax.ppermute(value, 'own', [(i, i ^ k) for i in range(4)])  13.4 us
    ppermute x13, waiting for transfers between devices, over_rep(): return lax.ppermute(value, 'rep', [(i, i ^ k) for i in range(n_rep)])  12.9 us
    unnamed x24, local copies, waits for them, and re-layouts  1.8 us
  transfers between devices with their start and end apart: 23, of which 13 were waited for; matrix products, arithmetic and copies ran while one was open for 0% of the time, Pallas kernels for 9%

profile of v5, /device:TPU:0, one launch (start us, length us, event | category | flops | bytes accessed | tf_op | source)
XLA Modules:
  0.0 81.4 jit_solution(11149814850449679918)
XLA Ops:
  0.6 0.0 copy-start.10
  0.6 0.5 collective-permute-start.1
  1.2 0.1 collective-permute-start.2
  1.2 0.0 copy-done.10
  1.3 0.5 collective-permute-start
  1.7 1.0 %collective-permute-done.refs_3_ = s32[1,128]{1,0:T(1,128)S(1)} collective-permute-done((s32[1,128]{1,0:T(1,128)S(1)}, s32[1,128]{1,0:T(1,128)S(1)}, u32[]{:S(2)}, u32[]{:S(2)}) %collective-permute-start) | collective-permute-done | bytes 544 | tf_op jit(solution)/shard_map/ppermute | solution.py:235
  2.7 0.2 collective-permute-done.1.refs_5_
  2.9 0.7 collective-permute-done.2.refs_9_.refs_2_
  3.7 0.0 copy-done.11
  3.7 0.0 copy-done.9
  3.7 0.8 copy-done.8
  4.5 4.1 %shard_map.102 = (bf16[192,256]{1,0:T(8,128)(2,1)}, bf16[512,768]{1,0:T(8,128)(2,1)}, bf16[48,2048]{1,0:T(8,128)(2,1)}, bf16[48,2048]{1,0:T(8,128)(2,1)}, bf16[4...) custom-call(s32[1]{0:T(128)} %bitcast.refs_0_, s32[8]{0:T(128)} %refs_1_.2, s32[1,128]{1,0:T(1,128)} %bitcast.12, ...), custom_call_target="tpu_custom_call" | custom-call | bytes 3507236 | tf_op jit(solution)/shard_map/pallas_call | solution.py:39
  8.6 3.0 %collective-permute-start.7 = (bf16[512,768]{1,0:T(8,128)(2,1)}, bf16[512,768]{1,0:T(8,128)(2,1)S(1)}, u32[]{:S(2)}, u32[]{:S(2)}) collective-permute-start(bf16[512,768]{1,0:T(8,128)(2,1)} %get-tuple-element.46.refs_2_.refs_6_), channel_id=1, source_target_pairs={{0,16},{8,24},{16,0},{24,8},{1,17},{9,25},{17,1},{25,9},{2,18},{10... | collective-permute-start | bytes 2359304 | tf_op jit(solution)/shard_map/ppermute | solution.py:232
  11.5 1.5 %collective-permute-start.6 = (bf16[512,768]{1,0:T(8,128)(2,1)}, bf16[512,768]{1,0:T(8,128)(2,1)S(1)}, u32[]{:S(2)}, u32[]{:S(2)}) collective-permute-start(bf16[512,768]{1,0:T(8,128)(2,1)} %get-tuple-element.46.refs_2_.refs_6_), channel_id=1, source_target_pairs={{0,8},{8,0},{16,24},{24,16},{1,9},{9,1},{17,25},{25,17},{2,10},{10... | collective-permute-start | bytes 2359304 | tf_op jit(solution)/shard_map/ppermute | solution.py:232
  13.0 1.6 %collective-permute-start.3 = (bf16[48,2048]{1,0:T(8,128)(2,1)}, bf16[48,2048]{1,0:T(8,128)(2,1)S(1)}, u32[]{:S(2)}, u32[]{:S(2)}) collective-permute-start(bf16[48,2048]{1,0:T(8,128)(2,1)} %get-tuple-element.40), channel_id=1, source_target_pairs={{0,2},{1,3},{2,0},{3,1},{4,6},{5,7},{6,4},{7,5},{8,10},{9,11},{10,... | collective-permute-start | bytes 589832 | tf_op jit(solution)/shard_map/ppermute | solution.py:235
  14.6 2.6 %collective-permute-start.4 = (bf16[48,2048]{1,0:T(8,128)(2,1)}, bf16[48,2048]{1,0:T(8,128)(2,1)S(1)}, u32[]{:S(2)}, u32[]{:S(2)}) collective-permute-start(bf16[48,2048]{1,0:T(8,128)(2,1)} %get-tuple-element.41), channel_id=1, source_target_pairs={{0,4},{1,5},{2,6},{3,7},{4,0},{5,1},{6,2},{7,3},{8,12},{9,13},{10,... | collective-permute-start | bytes 589832 | tf_op jit(solution)/shard_map/ppermute | solution.py:235
  17.2 0.2 collective-permute-start.5
  17.4 3.4 %shard_map.103 = (bf16[48,2048]{1,0:T(8,128)(2,1)}, bf16[48,2048]{1,0:T(8,128)(2,1)}, bf16[48,2048]{1,0:T(8,128)(2,1)}, bf16[48,2048]{1,0:T(8,128)(2,1)}) custom-call(bf16[192,256]{1,0:T(8,128)(2,1)} %get-tuple-element.38.refs_0_, bf16[128,2048]{1,0:T(8,128)(2,1)} %refs_1_.3, bf16[128,2048]{1,0:T(8,128)(2,1)} %copy-done.8), custom_call_target="tpu_custom_call" | custom-call | bytes 1933312 | tf_op jit(solution)/shard_map/pallas_call | solution.py:39
  20.8 8.8 %collective-permute-done.7.refs_4_.refs_8_ = bf16[512,768]{1,0:T(8,128)(2,1)S(1)} collective-permute-done((bf16[512,768]{1,0:T(8,128)(2,1)}, bf16[512,768]{1,0:T(8,128)(2,1)S(1)}, u32[]{:S(2)}, u32[]{:S(2)}) %collective-permute-start.7) | collective-permute-done | bytes 786464 | tf_op jit(solution)/shard_map/ppermute | solution.py:232
  29.6 1.4 %collective-permute-done.6.refs_3_.refs_7_ = bf16[512,768]{1,0:T(8,128)(2,1)S(1)} collective-permute-done((bf16[512,768]{1,0:T(8,128)(2,1)}, bf16[512,768]{1,0:T(8,128)(2,1)S(1)}, u32[]{:S(2)}, u32[]{:S(2)}) %collective-permute-start.6) | collective-permute-done | bytes 786464 | tf_op jit(solution)/shard_map/ppermute | solution.py:232
  31.1 0.0 collective-permute-done.3.refs_5_.refs_2_
  31.1 0.9 %collective-permute-done.4.refs_6_.refs_3_ = bf16[48,2048]{1,0:T(8,128)(2,1)S(1)} collective-permute-done((bf16[48,2048]{1,0:T(8,128)(2,1)}, bf16[48,2048]{1,0:T(8,128)(2,1)S(1)}, u32[]{:S(2)}, u32[]{:S(2)}) %collective-permute-start.4) | collective-permute-done | bytes 196640 | tf_op jit(solution)/shard_map/ppermute | solution.py:235
  32.0 0.0 collective-permute-done.5.refs_7_.refs_4_
  32.0 0.0 copy-start.5
  32.0 0.0 copy-start.7
  32.0 0.6 collective-permute-start.8
  32.6 1.3 %collective-permute-start.9 = (bf16[256,768]{1,0:T(8,128)(2,1)S(1)}, bf16[256,768]{1,0:T(8,128)(2,1)S(1)}, u32[]{:S(2)}, u32[]{:S(2)}) collective-permute-start(bf16[256,768]{1,0:T(8,128)(2,1)S(1)} %get-tuple-element.48), channel_id=1, source_target_pairs={{0,8},{8,0},{16,24},{24,16},{1,9},{9,1},{17,25},{25,17},{2,10},{10... | collective-permute-start | bytes 1179656 | tf_op jit(solution)/shard_map/ppermute | solution.py:232
  33.9 0.0 copy-done.5
  33.9 2.4 %collective-permute-start.10 = (bf16[48,2048]{1,0:T(8,128)(2,1)}, bf16[48,2048]{1,0:T(8,128)(2,1)}, u32[]{:S(2)}, u32[]{:S(2)}) collective-permute-start(bf16[48,2048]{1,0:T(8,128)(2,1)} %get-tuple-element.51), channel_id=1, source_target_pairs={{0,2},{1,3},{2,0},{3,1},{4,6},{5,7},{6,4},{7,5},{8,10},{9,11},{10,... | collective-permute-start | bytes 589832 | tf_op jit(solution)/shard_map/ppermute | solution.py:235
  36.3 1.7 %collective-permute-start.11 = (bf16[48,2048]{1,0:T(8,128)(2,1)}, bf16[48,2048]{1,0:T(8,128)(2,1)S(1)}, u32[]{:S(2)}, u32[]{:S(2)}) collective-permute-start(bf16[48,2048]{1,0:T(8,128)(2,1)} %copy-done.5), channel_id=1, source_target_pairs={{0,4},{1,5},{2,6},{3,7},{4,0},{5,1},{6,2},{7,3},{8,12},{9,13},{10,... | collective-permute-start | bytes 589832 | tf_op jit(solution)/shard_map/ppermute | solution.py:235
  38.1 0.7 collective-permute-start.12
  38.8 2.6 %collective-permute-done.8.refs_5_.refs_9_ = bf16[256,768]{1,0:T(8,128)(2,1)S(1)} collective-permute-done((bf16[256,768]{1,0:T(8,128)(2,1)S(1)}, bf16[256,768]{1,0:T(8,128)(2,1)S(1)}, u32[]{:S(2)}, u32[]{:S(2)}) %collective-permute-start.8) | collective-permute-done | bytes 393248 | tf_op jit(solution)/shard_map/ppermute | solution.py:232
  41.4 1.1 %collective-permute-done.9.refs_6_.refs_10_ = bf16[256,768]{1,0:T(8,128)(2,1)S(1)} collective-permute-done((bf16[256,768]{1,0:T(8,128)(2,1)S(1)}, bf16[256,768]{1,0:T(8,128)(2,1)S(1)}, u32[]{:S(2)}, u32[]{:S(2)}) %collective-permute-start.9) | collective-permute-done | bytes 393248 | tf_op jit(solution)/shard_map/ppermute | solution.py:232
  42.5 0.9 %copy-done.3 = bf16[48,2048]{1,0:T(8,128)(2,1)S(1)} copy-done((bf16[48,2048]{1,0:T(8,128)(2,1)S(1)}, bf16[48,2048]{1,0:T(8,128)(2,1)}, u32[]{:S(2)}) %copy-start.3) | copy-done | bytes 196632
  43.5 1.1 %shard_map.105 = (bf16[192,2048]{1,0:T(8,128)(2,1)S(1)}, bf16[192,512]{1,0:T(8,128)(2,1)S(1)}, bf16[192,512]{1,0:T(8,128)(2,1)S(1)}, bf16[192,512]{1,0:T(8,128)(2,1)S(1)}, bf16[192,512]{1,0:T(8,128)(2,1)S(1)}) custom-call(s32[1]{0:T(128)} %bitcast.5.refs_0_, bf16[48,2048]{1,0:T(8,128)(2,1)S(1)} %copy-done.3, ...), custom_call_target="tpu_custom_call" | custom-call | bytes 2359300 | tf_op jit(solution)/shard_map/pallas_call | solution.py:39
  44.6 1.5 %collective-permute-start.13 = (bf16[192,512]{1,0:T(8,128)(2,1)S(1)}, bf16[192,512]{1,0:T(8,128)(2,1)S(1)}, u32[]{:S(2)}, u32[]{:S(2)}) collective-permute-start(bf16[192,512]{1,0:T(8,128)(2,1)S(1)} %get-tuple-element.54), channel_id=1, source_target_pairs={{0,8},{8,0},{16,24},{24,16},{1,9},{9,1},{17,25},{25,17},{2,10},{10... | collective-permute-start | bytes 589832 | tf_op jit(solution)/shard_map/ppermute | solution.py:232
  46.0 0.6 collective-permute-start.14
  46.6 0.0 collective-permute-done.10.refs_3_
  46.6 1.5 %collective-permute-start.15 = (bf16[192,512]{1,0:T(8,128)(2,1)S(1)}, bf16[192,512]{1,0:T(8,128)(2,1)S(1)}, u32[]{:S(2)}, u32[]{:S(2)}) collective-permute-start(bf16[192,512]{1,0:T(8,128)(2,1)S(1)} %get-tuple-element.56), channel_id=1, source_target_pairs={{0,24},{8,16},{16,8},{24,0},{1,25},{9,17},{17,9},{25,1},{2,26},{10... | collective-permute-start | bytes 589832 | tf_op jit(solution)/shard_map/ppermute | solution.py:232
  48.1 0.6 shard_map.106.refs_1_
  48.7 3.8 %collective-permute-done.11.refs_4_ = bf16[48,2048]{1,0:T(8,128)(2,1)S(1)} collective-permute-done((bf16[48,2048]{1,0:T(8,128)(2,1)}, bf16[48,2048]{1,0:T(8,128)(2,1)S(1)}, u32[]{:S(2)}, u32[]{:S(2)}) %collective-permute-start.11) | collective-permute-done | bytes 196640 | tf_op jit(solution)/shard_map/ppermute | solution.py:235
  52.5 0.0 collective-permute-done.12.refs_5_
  52.5 0.0 collective-permute-done.13.refs_11_.refs_1_
  52.5 2.4 %collective-permute-done.14.refs_12_.refs_2_ = bf16[192,512]{1,0:T(8,128)(2,1)S(1)} collective-permute-done((bf16[192,512]{1,0:T(8,128)(2,1)S(1)}, bf16[192,512]{1,0:T(8,128)(2,1)S(1)}, u32[]{:S(2)}, u32[]{:S(2)}) %collective-permute-start.14) | collective-permute-done | bytes 196640 | tf_op jit(solution)/shard_map/ppermute | solution.py:232
  55.0 0.0 collective-permute-done.15.refs_13_.refs_3_
  55.0 2.3 %shard_map.107 = (bf16[48,2048]{1,0:T(8,128)(2,1)S(1)}, bf16[48,2048]{1,0:T(8,128)(2,1)S(1)}, bf16[48,2048]{1,0:T(8,128)(2,1)S(1)}, bf16[48,2048]{1,0:T(8,128)(2...) custom-call(s32[1]{0:T(128)} %bitcast.5.refs_0_, ...), custom_call_target="tpu_custom_call" | custom-call | bytes 7208964 | tf_op jit(solution)/shard_map/pallas_call | solution.py:39
  57.3 0.6 collective-permute-start.19
  57.9 1.2 %collective-permute-start.20 = (bf16[448,512]{1,0:T(8,128)(2,1)S(1)}, bf16[448,512]{1,0:T(8,128)(2,1)S(1)}, u32[]{:S(2)}, u32[]{:S(2)}) collective-permute-start(bf16[448,512]{1,0:T(8,128)(2,1)S(1)} %get-tuple-element.62), channel_id=1, source_target_pairs={{0,16},{8,24},{16,0},{24,8},{1,17},{9,25},{17,1},{25,9},{2,18},{10... | collective-permute-start | bytes 1376264 | tf_op jit(solution)/shard_map/ppermute | solution.py:232
  59.1 1.8 %collective-permute-start.21 = (bf16[448,512]{1,0:T(8,128)(2,1)S(1)}, bf16[448,512]{1,0:T(8,128)(2,1)S(1)}, u32[]{:S(2)}, u32[]{:S(2)}) collective-permute-start(bf16[448,512]{1,0:T(8,128)(2,1)S(1)} %get-tuple-element.63), channel_id=1, source_target_pairs={{0,24},{8,16},{16,8},{24,0},{1,25},{9,17},{17,9},{25,1},{2,26},{10... | collective-permute-start | bytes 1376264 | tf_op jit(solution)/shard_map/ppermute | solution.py:232
  60.9 1.3 %collective-permute-start.16 = (bf16[48,2048]{1,0:T(8,128)(2,1)S(1)}, bf16[48,2048]{1,0:T(8,128)(2,1)S(1)}, u32[]{:S(2)}, u32[]{:S(2)}) collective-permute-start(bf16[48,2048]{1,0:T(8,128)(2,1)S(1)} %get-tuple-element.58), channel_id=1, source_target_pairs={{0,2},{1,3},{2,0},{3,1},{4,6},{5,7},{6,4},{7,5},{8,10},{9,11},{10,... | collective-permute-start | bytes 589832 | tf_op jit(solution)/shard_map/ppermute | solution.py:235
  62.2 2.8 %collective-permute-start.17 = (bf16[48,2048]{1,0:T(8,128)(2,1)S(1)}, bf16[48,2048]{1,0:T(8,128)(2,1)S(1)}, u32[]{:S(2)}, u32[]{:S(2)}) collective-permute-start(bf16[48,2048]{1,0:T(8,128)(2,1)S(1)} %get-tuple-element.59), channel_id=1, source_target_pairs={{0,4},{1,5},{2,6},{3,7},{4,0},{5,1},{6,2},{7,3},{8,12},{9,13},{10,... | collective-permute-start | bytes 589832 | tf_op jit(solution)/shard_map/ppermute | solution.py:235
  65.0 2.4 %collective-permute-done.16.refs_2_ = bf16[48,2048]{1,0:T(8,128)(2,1)S(1)} collective-permute-done((bf16[48,2048]{1,0:T(8,128)(2,1)S(1)}, bf16[48,2048]{1,0:T(8,128)(2,1)S(1)}, u32[]{:S(2)}, u32[]{:S(2)}) %collective-permute-start.16) | collective-permute-done | bytes 196640 | tf_op jit(solution)/shard_map/ppermute | solution.py:235
  67.5 5.3 %collective-permute-start.18 = (bf16[48,2048]{1,0:T(8,128)(2,1)S(1)}, bf16[48,2048]{1,0:T(8,128)(2,1)S(1)}, u32[]{:S(2)}, u32[]{:S(2)}) collective-permute-start(bf16[48,2048]{1,0:T(8,128)(2,1)S(1)} %get-tuple-element.60), channel_id=1, source_target_pairs={{0,6},{1,7},{2,4},{3,5},{4,2},{5,3},{6,0},{7,1},{8,14},{9,15},{10,... | collective-permute-start | bytes 589832 | tf_op jit(solution)/shard_map/ppermute | solution.py:235
  72.8 3.8 %collective-permute-done.17.refs_3_ = bf16[48,2048]{1,0:T(8,128)(2,1)S(1)} collective-permute-done((bf16[48,2048]{1,0:T(8,128)(2,1)S(1)}, bf16[48,2048]{1,0:T(8,128)(2,1)S(1)}, u32[]{:S(2)}, u32[]{:S(2)}) %collective-permute-start.17) | collective-permute-done | bytes 196640 | tf_op jit(solution)/shard_map/ppermute | solution.py:235
  76.6 0.0 collective-permute-done.18.refs_4_
  76.6 0.0 collective-permute-done.19.refs_5_
  76.6 0.0 collective-permute-done.20.refs_6_
  76.6 0.6 collective-permute-done.21.refs_7_
  77.2 0.0 copy-done.1
  77.2 1.3 %shard_map.108 = (bf16[128,2048]{1,0:T(8,128)(2,1)S(1)}, bf16[128,2048]{1,0:T(8,128)(2,1)S(1)}) custom-call(bf16[192,256]{1,0:T(8,128)(2,1)S(1)} %copy-done.1, bf16[48,2048]{1,0:T(8,128)(2,1)S(1)} %get-tuple-element.57.refs_1_, bf16[48,2048]{1,0:T(8,128)(2,1)S(1)} %collective-permute-done.16.refs_2_, bf16[48,2048]{1,0:T(8,128)(2,1)S(1)} %collective-permute-done.17.refs_3_, ...), custom_call_target="tpu_custom_call" | custom-call | bytes 1933312 | tf_op jit(solution)/shard_map/pallas_call | solution.py:39
  78.5 0.1 collective-permute-start.22
  78.6 1.9 %shard_map.109 = (f32[512,256]{1,0:T(8,128)}, f32[512,256]{1,0:T(8,128)}, f32[512,256]{1,0:T(8,128)}) custom-call(bf16[192,512]{1,0:T(8,128)(2,1)S(1)} %get-tuple-element.66.refs_0_, bf16[192,512]{1,0:T(8,128)(2,1)S(1)} %collective-permute-done.13.refs_11_.refs_1_, bf16[192,512]{1,0:T(8,128)(2,1)S(1)} %collective-permute-done.14.refs_12_.refs_2_, ...), custom_call_target="tpu_custom_call" | custom-call | bytes 4456448 | tf_op jit(solution)/shard_map/pallas_call | solution.py:39
  80.5 0.0 collective-permute-done.22
  80.5 0.9 %add.3 = bf16[128,2048]{1,0:T(8,128)(2,1)} add(bf16[128,2048]{1,0:T(8,128)(2,1)S(1)} %get-tuple-element.64, bf16[128,2048]{1,0:T(8,128)(2,1)S(1)} %collective-permute-done.22) | non-fusion elementwise | flops 262144 | bytes 1572864 | tf_op jit(solution)/shard_map/add | solution.py:291
  (17 shorter events, 0.1 us)
Async XLA Ops:
  0.6 0.7 copy-start.10
  0.6 2.3 %collective-permute-start.1 = (bf16[128,2048]{1,0:T(8,128)(2,1)}, bf16[128,2048]{1,0:T(8,128)(2,1)S(1)}, u32[]{:S(2)}, u32[]{:S(2)}) collective-permute-start(bf16[128,2048]{1,0:T(8,128)(2,1)} %refs_4_.1), channel_id=1, source_target_pairs={{0,1},{1,0},{2,3},{3,2},{4,5},{5,4},{6,7},{7,6},{8,9},{9,8},{10,11... | collective-permute-start | bytes 1572872 | tf_op jit(solution)/shard_map/ppermute | solution.py:235
  1.2 2.5 %collective-permute-start.2 = (bf16[128,2048]{1,0:T(8,128)(2,1)}, bf16[128,2048]{1,0:T(8,128)(2,1)S(1)}, u32[]{:S(2)}, u32[]{:S(2)}) collective-permute-start(bf16[128,2048]{1,0:T(8,128)(2,1)} %refs_1_.3), channel_id=1, source_target_pairs={{0,1},{1,0},{2,3},{3,2},{4,5},{5,4},{6,7},{7,6},{8,9},{9,8},{10,11... | collective-permute-start | bytes 1572872 | tf_op jit(solution)/shard_map/ppermute | solution.py:235
  1.3 1.4 %collective-permute-start = (s32[1,128]{1,0:T(1,128)S(1)}, s32[1,128]{1,0:T(1,128)S(1)}, u32[]{:S(2)}, u32[]{:S(2)}) collective-permute-start(s32[1,128]{1,0:T(1,128)S(1)} %bitcast.13), channel_id=1, source_target_pairs={{0,1},{1,0},{2,3},{3,2},{4,5},{5,4},{6,7},{7,6},{8,9},{9,8},{10,11... | collective-permute-start | bytes 1544 | tf_op jit(solution)/shard_map/ppermute | solution.py:235
  2.7 1.0 %copy-start.11 = (s32[1,128]{1,0:T(1,128)}, s32[1,128]{1,0:T(1,128)S(1)}, u32[]{:S(2)}) copy-start(s32[1,128]{1,0:T(1,128)S(1)} %collective-permute-done.refs_3_) | copy-start | bytes 1540
  2.9 0.8 copy-start.9
  3.7 0.8 copy-start.8
  8.6 21.0 %collective-permute-start.7 = (bf16[512,768]{1,0:T(8,128)(2,1)}, bf16[512,768]{1,0:T(8,128)(2,1)S(1)}, u32[]{:S(2)}, u32[]{:S(2)}) collective-permute-start(bf16[512,768]{1,0:T(8,128)(2,1)} %get-tuple-element.46.refs_2_.refs_6_), channel_id=1, source_target_pairs={{0,16},{8,24},{16,0},{24,8},{1,17},{9,25},{17,1},{25,9},{2,18},{10... | collective-permute-start | bytes 2359304 | tf_op jit(solution)/shard_map/ppermute | solution.py:232
  11.5 19.5 %collective-permute-start.6 = (bf16[512,768]{1,0:T(8,128)(2,1)}, bf16[512,768]{1,0:T(8,128)(2,1)S(1)}, u32[]{:S(2)}, u32[]{:S(2)}) collective-permute-start(bf16[512,768]{1,0:T(8,128)(2,1)} %get-tuple-element.46.refs_2_.refs_6_), channel_id=1, source_target_pairs={{0,8},{8,0},{16,24},{24,16},{1,9},{9,1},{17,25},{25,17},{2,10},{10... | collective-permute-start | bytes 2359304 | tf_op jit(solution)/shard_map/ppermute | solution.py:232
  13.0 18.1 %collective-permute-start.3 = (bf16[48,2048]{1,0:T(8,128)(2,1)}, bf16[48,2048]{1,0:T(8,128)(2,1)S(1)}, u32[]{:S(2)}, u32[]{:S(2)}) collective-permute-start(bf16[48,2048]{1,0:T(8,128)(2,1)} %get-tuple-element.40), channel_id=1, source_target_pairs={{0,2},{1,3},{2,0},{3,1},{4,6},{5,7},{6,4},{7,5},{8,10},{9,11},{10,... | collective-permute-start | bytes 589832 | tf_op jit(solution)/shard_map/ppermute | solution.py:235
  14.6 17.4 %collective-permute-start.4 = (bf16[48,2048]{1,0:T(8,128)(2,1)}, bf16[48,2048]{1,0:T(8,128)(2,1)S(1)}, u32[]{:S(2)}, u32[]{:S(2)}) collective-permute-start(bf16[48,2048]{1,0:T(8,128)(2,1)} %get-tuple-element.41), channel_id=1, source_target_pairs={{0,4},{1,5},{2,6},{3,7},{4,0},{5,1},{6,2},{7,3},{8,12},{9,13},{10,... | collective-permute-start | bytes 589832 | tf_op jit(solution)/shard_map/ppermute | solution.py:235
  17.2 14.8 %collective-permute-start.5 = (bf16[48,2048]{1,0:T(8,128)(2,1)}, bf16[48,2048]{1,0:T(8,128)(2,1)}, u32[]{:S(2)}, u32[]{:S(2)}) collective-permute-start(bf16[48,2048]{1,0:T(8,128)(2,1)} %get-tuple-element.42), channel_id=1, source_target_pairs={{0,6},{1,7},{2,4},{3,5},{4,2},{5,3},{6,0},{7,1},{8,14},{9,15},{10,... | collective-permute-start | bytes 589832 | tf_op jit(solution)/shard_map/ppermute | solution.py:235
  29.6 2.4 %copy-start.4 = (bf16[48,2048]{1,0:T(8,128)(2,1)S(1)}, bf16[48,2048]{1,0:T(8,128)(2,1)}, u32[]{:S(2)}) copy-start(bf16[48,2048]{1,0:T(8,128)(2,1)} %get-tuple-element.44.refs_1_) | copy-start | bytes 589828
  29.6 2.4 %copy-start.6 = (bf16[48,2048]{1,0:T(8,128)(2,1)S(1)}, bf16[48,2048]{1,0:T(8,128)(2,1)}, u32[]{:S(2)}) copy-start(bf16[48,2048]{1,0:T(8,128)(2,1)} %get-tuple-element.45.refs_2_) | copy-start | bytes 589828
  32.0 1.9 %copy-start.5 = (bf16[48,2048]{1,0:T(8,128)(2,1)}, bf16[48,2048]{1,0:T(8,128)(2,1)S(1)}, u32[]{:S(2)}) copy-start(bf16[48,2048]{1,0:T(8,128)(2,1)S(1)} %get-tuple-element.52) | copy-start | bytes 589828
  32.0 1.9 %copy-start.7 = (bf16[48,2048]{1,0:T(8,128)(2,1)}, bf16[48,2048]{1,0:T(8,128)(2,1)S(1)}, u32[]{:S(2)}) copy-start(bf16[48,2048]{1,0:T(8,128)(2,1)S(1)} %get-tuple-element.53) | copy-start | bytes 589828
  32.0 9.4 %collective-permute-start.8 = (bf16[256,768]{1,0:T(8,128)(2,1)S(1)}, bf16[256,768]{1,0:T(8,128)(2,1)S(1)}, u32[]{:S(2)}, u32[]{:S(2)}) collective-permute-start(bf16[256,768]{1,0:T(8,128)(2,1)S(1)} %get-tuple-element.47), channel_id=1, source_target_pairs={{0,16},{8,24},{16,0},{24,8},{1,17},{9,25},{17,1},{25,9},{2,18},{10... | collective-permute-start | bytes 1179656 | tf_op jit(solution)/shard_map/ppermute | solution.py:232
  32.6 9.9 %collective-permute-start.9 = (bf16[256,768]{1,0:T(8,128)(2,1)S(1)}, bf16[256,768]{1,0:T(8,128)(2,1)S(1)}, u32[]{:S(2)}, u32[]{:S(2)}) collective-permute-start(bf16[256,768]{1,0:T(8,128)(2,1)S(1)} %get-tuple-element.48), channel_id=1, source_target_pairs={{0,8},{8,0},{16,24},{24,16},{1,9},{9,1},{17,25},{25,17},{2,10},{10... | collective-permute-start | bytes 1179656 | tf_op jit(solution)/shard_map/ppermute | solution.py:232
  33.9 12.8 %collective-permute-start.10 = (bf16[48,2048]{1,0:T(8,128)(2,1)}, bf16[48,2048]{1,0:T(8,128)(2,1)}, u32[]{:S(2)}, u32[]{:S(2)}) collective-permute-start(bf16[48,2048]{1,0:T(8,128)(2,1)} %get-tuple-element.51), channel_id=1, source_target_pairs={{0,2},{1,3},{2,0},{3,1},{4,6},{5,7},{6,4},{7,5},{8,10},{9,11},{10,... | collective-permute-start | bytes 589832 | tf_op jit(solution)/shard_map/ppermute | solution.py:235
  36.3 16.2 %collective-permute-start.11 = (bf16[48,2048]{1,0:T(8,128)(2,1)}, bf16[48,2048]{1,0:T(8,128)(2,1)S(1)}, u32[]{:S(2)}, u32[]{:S(2)}) collective-permute-start(bf16[48,2048]{1,0:T(8,128)(2,1)} %copy-done.5), channel_id=1, source_target_pairs={{0,4},{1,5},{2,6},{3,7},{4,0},{5,1},{6,2},{7,3},{8,12},{9,13},{10,... | collective-permute-start | bytes 589832 | tf_op jit(solution)/shard_map/ppermute | solution.py:235
  38.1 14.5 %collective-permute-start.12 = (bf16[48,2048]{1,0:T(8,128)(2,1)}, bf16[48,2048]{1,0:T(8,128)(2,1)S(1)}, u32[]{:S(2)}, u32[]{:S(2)}) collective-permute-start(bf16[48,2048]{1,0:T(8,128)(2,1)} %copy-done.7), channel_id=1, source_target_pairs={{0,6},{1,7},{2,4},{3,5},{4,2},{5,3},{6,0},{7,1},{8,14},{9,15},{10,... | collective-permute-start | bytes 589832 | tf_op jit(solution)/shard_map/ppermute | solution.py:235
  42.5 0.9 %copy-start.3 = (bf16[48,2048]{1,0:T(8,128)(2,1)S(1)}, bf16[48,2048]{1,0:T(8,128)(2,1)}, u32[]{:S(2)}) copy-start(bf16[48,2048]{1,0:T(8,128)(2,1)} %get-tuple-element.39.refs_1_) | copy-start | bytes 589828
  43.5 4.7 %copy-start = (bf16[512,768]{1,0:T(8,128)(2,1)S(1)}, bf16[512,768]{1,0:T(8,128)(2,1)}, u32[]{:S(2)}) copy-start(bf16[512,768]{1,0:T(8,128)(2,1)} %get-tuple-element.46.refs_2_.refs_6_) | copy-start | bytes 2359300
  44.6 8.0 %collective-permute-start.13 = (bf16[192,512]{1,0:T(8,128)(2,1)S(1)}, bf16[192,512]{1,0:T(8,128)(2,1)S(1)}, u32[]{:S(2)}, u32[]{:S(2)}) collective-permute-start(bf16[192,512]{1,0:T(8,128)(2,1)S(1)} %get-tuple-element.54), channel_id=1, source_target_pairs={{0,8},{8,0},{16,24},{24,16},{1,9},{9,1},{17,25},{25,17},{2,10},{10... | collective-permute-start | bytes 589832 | tf_op jit(solution)/shard_map/ppermute | solution.py:232
  46.0 9.0 %collective-permute-start.14 = (bf16[192,512]{1,0:T(8,128)(2,1)S(1)}, bf16[192,512]{1,0:T(8,128)(2,1)S(1)}, u32[]{:S(2)}, u32[]{:S(2)}) collective-permute-start(bf16[192,512]{1,0:T(8,128)(2,1)S(1)} %get-tuple-element.55), channel_id=1, source_target_pairs={{0,16},{8,24},{16,0},{24,8},{1,17},{9,25},{17,1},{25,9},{2,18},{10... | collective-permute-start | bytes 589832 | tf_op jit(solution)/shard_map/ppermute | solution.py:232
  46.6 8.3 %collective-permute-start.15 = (bf16[192,512]{1,0:T(8,128)(2,1)S(1)}, bf16[192,512]{1,0:T(8,128)(2,1)S(1)}, u32[]{:S(2)}, u32[]{:S(2)}) collective-permute-start(bf16[192,512]{1,0:T(8,128)(2,1)S(1)} %get-tuple-element.56), channel_id=1, source_target_pairs={{0,24},{8,16},{16,8},{24,0},{1,25},{9,17},{17,9},{25,1},{2,26},{10... | collective-permute-start | bytes 589832 | tf_op jit(solution)/shard_map/ppermute | solution.py:232
  48.1 6.9 %copy-start.2 = (bf16[48,2048]{1,0:T(8,128)(2,1)S(1)}, bf16[48,2048]{1,0:T(8,128)(2,1)}, u32[]{:S(2)}) copy-start(bf16[48,2048]{1,0:T(8,128)(2,1)} %get-tuple-element.50.refs_2_) | copy-start | bytes 589828
  55.0 22.2 %copy-start.1 = (bf16[192,256]{1,0:T(8,128)(2,1)S(1)}, bf16[192,256]{1,0:T(8,128)(2,1)}, u32[]{:S(2)}) copy-start(bf16[192,256]{1,0:T(8,128)(2,1)} %get-tuple-element.38.refs_0_) | copy-start | bytes 294916
  57.3 19.3 %collective-permute-start.19 = (bf16[448,512]{1,0:T(8,128)(2,1)S(1)}, bf16[448,512]{1,0:T(8,128)(2,1)S(1)}, u32[]{:S(2)}, u32[]{:S(2)}) collective-permute-start(bf16[448,512]{1,0:T(8,128)(2,1)S(1)} %get-tuple-element.61), channel_id=1, source_target_pairs={{0,8},{8,0},{16,24},{24,16},{1,9},{9,1},{17,25},{25,17},{2,10},{10... | collective-permute-start | bytes 1376264 | tf_op jit(solution)/shard_map/ppermute | solution.py:232
  57.9 18.7 %collective-permute-start.20 = (bf16[448,512]{1,0:T(8,128)(2,1)S(1)}, bf16[448,512]{1,0:T(8,128)(2,1)S(1)}, u32[]{:S(2)}, u32[]{:S(2)}) collective-permute-start(bf16[448,512]{1,0:T(8,128)(2,1)S(1)} %get-tuple-element.62), channel_id=1, source_target_pairs={{0,16},{8,24},{16,0},{24,8},{1,17},{9,25},{17,1},{25,9},{2,18},{10... | collective-permute-start | bytes 1376264 | tf_op jit(solution)/shard_map/ppermute | solution.py:232
  59.1 18.1 %collective-permute-start.21 = (bf16[448,512]{1,0:T(8,128)(2,1)S(1)}, bf16[448,512]{1,0:T(8,128)(2,1)S(1)}, u32[]{:S(2)}, u32[]{:S(2)}) collective-permute-start(bf16[448,512]{1,0:T(8,128)(2,1)S(1)} %get-tuple-element.63), channel_id=1, source_target_pairs={{0,24},{8,16},{16,8},{24,0},{1,25},{9,17},{17,9},{25,1},{2,26},{10... | collective-permute-start | bytes 1376264 | tf_op jit(solution)/shard_map/ppermute | solution.py:232
  60.9 6.6 %collective-permute-start.16 = (bf16[48,2048]{1,0:T(8,128)(2,1)S(1)}, bf16[48,2048]{1,0:T(8,128)(2,1)S(1)}, u32[]{:S(2)}, u32[]{:S(2)}) collective-permute-start(bf16[48,2048]{1,0:T(8,128)(2,1)S(1)} %get-tuple-element.58), channel_id=1, source_target_pairs={{0,2},{1,3},{2,0},{3,1},{4,6},{5,7},{6,4},{7,5},{8,10},{9,11},{10,... | collective-permute-start | bytes 589832 | tf_op jit(solution)/shard_map/ppermute | solution.py:235
  62.2 14.4 %collective-permute-start.17 = (bf16[48,2048]{1,0:T(8,128)(2,1)S(1)}, bf16[48,2048]{1,0:T(8,128)(2,1)S(1)}, u32[]{:S(2)}, u32[]{:S(2)}) collective-permute-start(bf16[48,2048]{1,0:T(8,128)(2,1)S(1)} %get-tuple-element.59), channel_id=1, source_target_pairs={{0,4},{1,5},{2,6},{3,7},{4,0},{5,1},{6,2},{7,3},{8,12},{9,13},{10,... | collective-permute-start | bytes 589832 | tf_op jit(solution)/shard_map/ppermute | solution.py:235
  67.5 9.1 %collective-permute-start.18 = (bf16[48,2048]{1,0:T(8,128)(2,1)S(1)}, bf16[48,2048]{1,0:T(8,128)(2,1)S(1)}, u32[]{:S(2)}, u32[]{:S(2)}) collective-permute-start(bf16[48,2048]{1,0:T(8,128)(2,1)S(1)} %get-tuple-element.60), channel_id=1, source_target_pairs={{0,6},{1,7},{2,4},{3,5},{4,2},{5,3},{6,0},{7,1},{8,14},{9,15},{10,... | collective-permute-start | bytes 589832 | tf_op jit(solution)/shard_map/ppermute | solution.py:235
  78.5 2.0 %collective-permute-start.22 = (bf16[128,2048]{1,0:T(8,128)(2,1)S(1)}, bf16[128,2048]{1,0:T(8,128)(2,1)S(1)}, u32[]{:S(2)}, u32[]{:S(2)}) collective-permute-start(bf16[128,2048]{1,0:T(8,128)(2,1)S(1)} %get-tuple-element.65), channel_id=1, source_target_pairs={{0,1},{1,0},{2,3},{3,2},{4,5},{5,4},{6,7},{7,6},{8,9},{9,8},{10,11... | collective-permute-start | bytes 1572872 | tf_op jit(solution)/shard_map/ppermute | solution.py:235

commit v6 on v5

v6 whole, which is shorter than its diff:
```python
import functools

import jax
import jax.numpy as jnp
from jax import lax
from jax.experimental import pallas as pl
from jax.experimental.pallas import tpu as pltpu
from jax.sharding import PartitionSpec as P

VMEM = pl.BlockSpec(memory_space=pltpu.VMEM)
SMEM = pl.BlockSpec(memory_space=pltpu.SMEM)
HBM = pl.BlockSpec(memory_space=pltpu.HBM)
ANY = pl.BlockSpec(memory_space=pl.ANY)
MIB = 1024 * 1024
BF16 = jnp.bfloat16
F32 = jnp.float32


def dot(left, right, left_dim, right_dim):
    return lax.dot_general(
        left, right, (((left_dim,), (right_dim,)), ((), ())), preferred_element_type=F32
    )


def shape(rows, cols, dtype=BF16):
    return jax.ShapeDtypeStruct((rows, cols), dtype)


def call(kernel, outs, scalars=0, scratch=(), fetched=0, room=32, earlier=(), stored=()):
    earlier = list(earlier)

    def body(*refs):
        inputs = len(refs) - len(outs) - len(scratch)
        kernel(*refs[: inputs - len(earlier)], *refs[inputs:])

    def run(*operands):
        placed = len(operands) - scalars - fetched
        moved = sum(value.size * value.dtype.itemsize for value in (*operands, *outs))
        return pl.pallas_call(
            body,
            out_shape=outs,
            in_specs=[SMEM] * scalars + [VMEM] * placed + [HBM] * fetched + [ANY] * len(earlier),
            out_specs=[HBM if i in stored else VMEM for i in range(len(outs))],
            scratch_shapes=list(scratch),
            cost_estimate=pl.CostEstimate(flops=0, bytes_accessed=moved, transcendentals=0),
            compiler_params=pltpu.CompilerParams(vmem_limit_bytes=room * MIB),
        )(*operands, *earlier)

    return run


def after(values, *earlier):
    return pl.pallas_call(
        lambda *refs: None,
        out_shape=[shape(*value.shape, value.dtype) for value in values],
        in_specs=[ANY] * (len(values) + len(earlier)),
        out_specs=[ANY] * len(values),
        input_output_aliases={i: i for i in range(len(values))},
        compiler_params=pltpu.CompilerParams(vmem_limit_bytes=MIB),
    )(*values, *earlier)


def start_copies(pairs, sems):
    copies = [pltpu.make_async_copy(source, into, sems.at[i]) for i, (source, into) in enumerate(pairs)]
    for copy in copies:
        copy.start()
    return copies


def picks(capacity, offset, rank_ref, host_ref, route_ref, slots):
    hot = host_ref.shape[0]
    tokens = route_ref.shape[1]
    label = lax.broadcasted_iota(jnp.int32, (hot, tokens), 0)
    base = jnp.zeros((hot, tokens), jnp.int32)
    for e in range(hot):
        apart = host_ref[e] ^ rank_ref[0]
        start = jnp.where((apart & 1) == 0, (apart >> 1) * (2 * capacity), -2 * slots)
        base = jnp.where(label == e, start, base)
    earlier = lax.broadcasted_iota(jnp.int32, (tokens, tokens), 0) < lax.broadcasted_iota(
        jnp.int32, (tokens, tokens), 1
    )
    marked = route_ref[...] == label
    before = dot(jnp.where(marked, 1.0, 0.0).astype(BF16), jnp.where(earlier, 1.0, 0.0).astype(BF16), 1, 0)
    position = jnp.sum(jnp.where(marked, before.astype(jnp.int32) + base, 0), axis=0, keepdims=True) + offset
    slot = lax.broadcasted_iota(jnp.int32, (slots, tokens), 0)
    return jnp.where(slot == position, 1.0, 0.0).astype(BF16)


def pack_own_kernel(capacity, rank_ref, host_ref, route_ref, *refs):
    sources, (pick_ref, filled_ref, joined_ref), (x, dy, filled, weights, sems, out_sems) = refs[:5], refs[5:8], refs[8:]
    width = weights.shape[1] // 3
    slots = pick_ref.shape[0]
    near = slice(2 * capacity, 4 * capacity)
    loads = start_copies(
        zip(sources, (x, dy) + tuple(weights.at[:, pl.ds(i * width, width)] for i in range(3))), sems
    )
    pick_ref[...] = picks(capacity, 0, rank_ref, host_ref, route_ref, slots)
    for load in loads[2:]:
        load.wait()
    stores = start_copies([(weights, joined_ref)], out_sems.at[0])
    loads[0].wait()
    filled[:slots] = dot(pick_ref[...], x[...], 1, 0).astype(BF16)
    loads[1].wait()
    filled[slots:] = dot(pick_ref[near], dy[...], 1, 0).astype(BF16)
    stores += start_copies([(filled, filled_ref)], out_sems.at[1])
    for store in stores:
        store.wait()


def pack_kernel(capacity, rank_ref, host_ref, route_ref, pick_own, filled_ref, x_ref, dy_ref, *refs):
    pick_ref, *send_refs = refs
    slots, tokens = pick_own.shape
    block = 2 * capacity
    near = slice(block, 2 * block)
    pick = picks(capacity, capacity, rank_ref, host_ref, route_ref, slots)
    pick_ref[:, :tokens] = pick_own[...]
    pick_ref[:, tokens:] = pick
    filled = (dot(pick, x_ref[...], 1, 0) + filled_ref[:slots].astype(F32)).astype(BF16)
    for k, ref in enumerate(send_refs):
        ref[:block] = filled[k * block : (k + 1) * block]
    send_refs[1][block:] = (
        dot(pick_ref[near, tokens:], dy_ref[...], 1, 0) + filled_ref[slots:].astype(F32)
    ).astype(BF16)


def pack_more_kernel(pick_ref, own_ref, other_ref, *send_refs):
    tokens = own_ref.shape[0]
    block = send_refs[0].shape[0]
    filled = (
        dot(pick_ref[:, :tokens], own_ref[...], 1, 0) + dot(pick_ref[:, tokens:], other_ref[...], 1, 0)
    ).astype(BF16)
    for k, ref in zip((0, 2, 3), send_refs):
        ref[...] = filled[k * block : (k + 1) * block]


def columns_of(own_ref, depth):
    return [pl.ds(pl.multiple_of((own_ref[0] ^ k) * depth, depth), depth) for k in range(4)]


def onward_parts(own_ref, onward):
    for at, ref in enumerate(onward):
        half = ref.shape[1] // 2
        quarter = half // 2
        start = ((own_ref[0] ^ 3) * 2 + at) * half
        both = pl.ds(pl.multiple_of(start, half), half), ref[:half]
        downs = [
            (
                pl.ds(pl.multiple_of(start + i * quarter, quarter), quarter),
                ref[half : half + quarter, i * half : (i + 1) * half],
            )
            for i in range(2)
        ]
        yield both, downs


def spread_kernel(own_ref, *refs):
    got, (joined_1, joined_2), (x_ref, piece_0, piece_3, onward_1, onward_2) = refs[:4], refs[4:6], refs[6:]
    slots, depth = piece_0.shape
    block = slots // 4
    half, quarter = depth // 2, depth // 4
    columns = columns_of(own_ref, depth)
    for j, ref in enumerate(got):
        rows = pl.ds(j * block, block)
        x_ref[rows] = ref[:block]
        for into, cols in zip(
            (piece_0, onward_1.at[pl.ds(half + quarter, slots)], onward_2.at[pl.ds(half + quarter, slots)], piece_3),
            columns,
        ):
            into[rows] = ref[:block, cols]
    for joined, start, into in ((joined_2, half, onward_1), (joined_1, 0, onward_2)):
        into[:half] = joined[start : start + half, :depth]
        into[half : half + quarter, :half] = joined[start : start + quarter, depth:]
        into[half : half + quarter, half:] = joined[start + quarter : start + half, depth:]


def act_kernel(own_ref, x_ref, *refs):
    weights, acts_ref = refs[:-1], refs[-1]
    both = acts_ref.shape[1]
    columns = columns_of(own_ref, weights[0].shape[0])
    acts_ref[...] = sum(dot(x_ref[:, cols], ref[:, :both], 1, 0) for cols, ref in zip(columns, weights))


def grad_kernel(own_ref, acts_ref, x_ref, *refs):
    got, weights, onward, outs, dy_ref = refs[:4], refs[4:7], refs[7:9], refs[9:-1], refs[-1]
    back_refs, own_term, (own_grads, *messages) = outs[:4], outs[4], outs[5:]
    slots, both = acts_ref.shape
    width = both // 2
    block = slots // 4
    depth = weights[0].shape[0]
    half = depth // 2
    columns = columns_of(own_ref, depth)
    for j, ref in enumerate(got):
        dy_ref[j * block : (j + 1) * block] = ref[ref.shape[0] - block :]
    acts = acts_ref[...]
    back_grad = sum(dot(dy_ref[:, cols], ref[:, both:], 1, 0) for cols, ref in zip(columns, weights))
    for (cols, rows), downs in onward_parts(own_ref, onward):
        acts += dot(x_ref[:, cols], rows, 1, 0)
        for cols, rows in downs:
            back_grad += dot(dy_ref[:, cols], rows, 1, 0)
    gate_act, up_act = acts[:, :width], acts[:, width:]
    sigmoid_g = jax.nn.sigmoid(gate_act)
    silu_gate = gate_act * sigmoid_g
    hidden = (silu_gate * up_act).astype(BF16)
    gate_h = back_grad * up_act * sigmoid_g * (1.0 + gate_act * (1.0 - sigmoid_g))
    own_grads[:, :width] = gate_h.astype(BF16)
    own_grads[:, width:] = (back_grad * silu_gate).astype(BF16)
    grads = own_grads[...]
    for k, cols in enumerate(columns):
        term = dot(dy_ref[:, cols], hidden, 0, 0)
        if k == 0:
            own_term[...] = term
        else:
            messages[k - 1][:slots] = grads
            messages[k - 1][slots:, :width] = term[:half].astype(BF16)
            messages[k - 1][slots:, width:] = term[half:].astype(BF16)
    pairs = [(cols, ref[:, :both]) for cols, ref in zip(columns, weights)]
    for cols, rows in pairs + [part for part, _ in onward_parts(own_ref, onward)]:
        slot_grad = dot(grads, rows, 1, 1).astype(BF16)
        for j, back_ref in enumerate(back_refs):
            back_ref[:, cols] = slot_grad[j * block : (j + 1) * block]


def sum_kernel(*refs):
    pieces, messages, own_term, (gate_ref, up_ref, down_ref) = refs[:4], refs[4:8], refs[8], refs[9:]
    slots = pieces[0].shape[0]
    depth, width = gate_ref.shape
    half = depth // 2
    total = sum(dot(piece[-slots:], got[:slots], 0, 0) for piece, got in zip(pieces, messages))
    gate_ref[...] = total[:, :width]
    up_ref[...] = total[:, width:]
    for rows, cols in ((slice(0, half), slice(0, width)), (slice(half, depth), slice(width, 2 * width))):
        down_ref[rows] = own_term[rows] + sum(got[slots:, cols].astype(F32) for got in messages[1:])


def unpack_kernel(pick_ref, *refs):
    returned, (mine_ref, other_ref, rows_ref) = refs[:-3], refs[-3:]
    tokens = mine_ref.shape[0]
    block = returned[0].shape[0]
    for k, ref in enumerate(returned):
        rows_ref[k * block : (k + 1) * block] = ref[...]
    both = dot(pick_ref[...], rows_ref[...], 0, 0).astype(BF16)
    mine_ref[...] = both[:tokens]
    other_ref[...] = both[tokens:]


def shards_by_partner(n_rep, tokens, cotangent, route, host, w_gate, w_up, w_down_t):
    tok_rows, model_width = tokens.shape
    hot = host.shape[0]
    _, depth, width = w_gate.shape
    capacity = (3 * tok_rows + 2 * hot - 1) // (2 * hot)
    slots = hot * capacity
    parts = n_rep // 2
    block = 2 * capacity
    own = lax.axis_index("own").astype(jnp.int32).reshape(1)
    rank = lax.axis_index("rep").astype(jnp.int32).reshape(1)

    def over_own(value, k):
        return lax.ppermute(value, "own", [(i, i ^ k) for i in range(4)])

    def over_rep(value, k):
        return lax.ppermute(value, "rep", [(i, i ^ k) for i in range(n_rep)])

    route = route.reshape(1, tok_rows)
    route_b, tokens_b, cotangent_b = over_rep(route, 1), over_rep(tokens, 1), over_rep(cotangent, 1)
    token_rows = pltpu.VMEM((tok_rows, model_width), BF16)
    slot_rows = pltpu.VMEM((slots, model_width), BF16)
    dma = pltpu.SemaphoreType.DMA
    pick, filled, joined = call(
        functools.partial(pack_own_kernel, capacity),
        [shape(slots, tok_rows), shape(slots + block, model_width), shape(depth, 3 * width)],
        2,
        [token_rows, token_rows, pltpu.VMEM((slots + block, model_width), BF16), pltpu.VMEM((depth, 3 * width), BF16)]
        + [dma((5,)), dma((2, 1))],
        5,
        62,
        (),
        (1, 2),
    )(rank, host, route, tokens, cotangent, w_gate[0], w_up[0], w_down_t[0])
    joined_1, joined_2 = over_own(joined, 1), over_own(joined, 2)
    pick, own_x, near, far_xa, far_xb = call(
        functools.partial(pack_kernel, capacity),
        [shape(slots, 2 * tok_rows), shape(block, model_width), shape(2 * block, model_width)]
        + [shape(block, model_width)] * 2,
        2,
    )(rank, host, route_b, pick, filled, tokens_b, cotangent_b)
    near, far_xa, far_xb = over_rep(near, 2), over_rep(far_xa, 4), over_rep(far_xb, 6)
    own_dy, far_a, far_b = call(pack_more_kernel, [shape(block, model_width)] * 3)(pick, cotangent, cotangent_b)

    onward = shape(depth // 2 + depth // 4 + slots, depth)
    x, piece_0, piece_3, onward_1, onward_2 = call(
        spread_kernel,
        [shape(slots, model_width), shape(slots, depth), shape(slots, depth), onward, onward],
        1,
        earlier=[own_dy],
    )(own, own_x, near, far_xa, far_xb, joined_1, joined_2)
    far_a, far_b = after([far_a, far_b], piece_0)
    far_a, far_b = over_rep(far_a, 4), over_rep(far_b, 6)
    onward_1, onward_2, piece_3 = over_own(onward_1, 1), over_own(onward_2, 2), over_own(piece_3, 3)
    weights = [joined, joined_1, joined_2]
    acts = call(act_kernel, [shape(slots, 2 * width, F32)], 1)(own, x, *weights)[0]

    message = shape(slots + depth // 2, 2 * width)
    *back, own_term, grads, message_1, message_2, message_3 = call(
        grad_kernel,
        [shape(block, model_width)] * parts
        + [shape(depth, width, F32), shape(slots, 2 * width), message, message, message],
        1,
        [slot_rows],
        earlier=[piece_3],
    )(own, acts, x, own_dy, near, far_a, far_b, *weights, onward_2, onward_1)
    returned = [back[0]] + [over_rep(back[k], 2 * k) for k in range(1, parts)]
    messages = [over_own(message_1, 1), over_own(message_2, 2), over_own(message_3, 3)]

    mine, other = call(unpack_kernel, [shape(tok_rows, model_width)] * 2, 0, [slot_rows], earlier=messages)(
        pick, *returned
    )
    x_grad = mine + over_rep(other, 1)
    out = call(sum_kernel, [shape(depth, width, F32)] * 3)(
        piece_0, onward_1, onward_2, piece_3, grads, *messages, own_term
    )
    return (x_grad, *(grad[None] for grad in out))


def shards_whole(tokens, cotangent, route, host, w_gate, w_up, w_down_t):
    tok_rows, model_width = tokens.shape
    hot = host.shape[0]
    width = w_gate.shape[2]
    capacity = max(2, (3 * tok_rows + 2 * hot - 1) // (2 * hot))
    slots = hot * capacity
    labels = lax.broadcasted_iota(jnp.int32, (tok_rows, hot), 1)
    target = jnp.sum(jnp.where(route == labels, host[None, :], 0), axis=1)
    marked = (target[:, None] == labels).astype(jnp.int32)
    arrival = jnp.sum(jnp.cumsum(marked, axis=0) * marked, axis=1) - 1
    position = target * capacity + arrival
    pick = (lax.broadcasted_iota(jnp.int32, (slots, tok_rows), 0) == position[None, :]).astype(BF16)

    def exchange(value):
        split = value.astype(BF16).reshape(hot, capacity, model_width)
        return lax.all_to_all(split, "rep", split_axis=0, concat_axis=0, tiled=True).reshape(slots, model_width)

    slot_x, slot_dy = exchange(dot(pick, tokens, 1, 0)), exchange(dot(pick, cotangent, 1, 0))
    gate, up, down = (lax.all_gather(w[0], "own", axis=0, tiled=True) for w in (w_gate, w_up, w_down_t))
    gate_act, up_act, back_grad = dot(slot_x, gate, 1, 0), dot(slot_x, up, 1, 0), dot(slot_dy, down, 1, 0)
    sigmoid_g = jax.nn.sigmoid(gate_act)
    silu_gate = gate_act * sigmoid_g
    hidden = (silu_gate * up_act).astype(BF16)
    grad_gate_h = (back_grad * up_act * sigmoid_g * (1.0 + gate_act * (1.0 - sigmoid_g))).astype(BF16)
    grad_up_h = (back_grad * silu_gate).astype(BF16)
    returned = exchange(dot(grad_gate_h, gate, 1, 1) + dot(grad_up_h, up, 1, 1))
    x_grad = dot(pick, returned, 0, 0).astype(BF16)
    terms = [dot(slot_x, grad_gate_h, 0, 0), dot(slot_x, grad_up_h, 0, 0), dot(slot_dy, hidden, 0, 0)]
    summed = lax.psum_scatter(
        jnp.concatenate(terms, axis=1).astype(BF16), "own", scatter_dimension=0, tiled=True
    ).astype(F32)
    return (x_grad, *(summed[None, :, i * width : (i + 1) * width] for i in range(3)))


def solution(mesh):
    n_own, n_rep = mesh.shape["own"], mesh.shape["rep"]

    def shards(tokens, *rest):
        capacity = (3 * tokens.shape[0] + 2 * n_rep - 1) // (2 * n_rep)
        if n_own == 4 and n_rep == 8 and capacity % 8 == 0:
            return shards_by_partner(n_rep, tokens, *rest)
        return shards_whole(tokens, *rest)

    return jax.shard_map(
        shards,
        mesh=mesh,
        in_specs=(
            P(("own", "rep"), None),
            P(("own", "rep"), None),
            P(("own", "rep"), None),
            P(),
            P("rep", "own", None),
            P("rep", "own", None),
            P("rep", "own", None),
        ),
        out_specs=(
            P(("own", "rep"), None),
            P("rep", "own", None),
            P("rep", "own", None),
            P("rep", "own", None),
        ),
        check_vma=False,
    )
```

time: 81.7 us -> 85.2 us (1.043)
  waiting for transfers between devices: 29.8 us -> 45.4 us
  starting transfers between devices: 33.3 us -> 22.7 us
  Pallas kernels: 14.7 us -> 12.5 us
    ppermute x13 -> x12, waiting for transfers between devices: 12.9 us -> 39.8 us  [over_rep(): return lax.ppermute(value, 'rep', [(i, i ^ k) for i in range(n_rep)])]
    ppermute x10 -> x8, waiting for transfers between devices: 17 us -> 5.54 us  [over_own(): return lax.ppermute(value, 'own', [(i, i ^ k) for i in range(4)])]
    ppermute x13 -> x12, starting transfers between devices: 19.9 us -> 11.1 us  [over_rep(): return lax.ppermute(value, 'rep', [(i, i ^ k) for i in range(n_rep)])]
    pallas_call x7 -> x8, Pallas kernels: 14.7 us -> 12.5 us  [run(): pl.pallas_call(body, out_shape=outs, in_specs=[SMEM] * scalars + [VMEM] *...]
    ppermute x10 -> x8, starting transfers between devices: 13.4 us -> 11.6 us  [over_own(): return lax.ppermute(value, 'own', [(i, i ^ k) for i in range(4)])]
    unnamed x24 -> x12, local copies, waits for them, and re-layouts: 1.8 us -> 2.67 us
  transfers between devices with their start and end apart: 23 -> 20, of which waited for: 13 -> 9; matrix products, arithmetic and copies ran while one was open for 0% -> 0% of each run, Pallas kernels for 9% -> 11%
where the time goes in v6:
time: 85.2 us; the launch traced here: 84.9 us
  waiting for transfers between devices  45.4 us (53%)
  starting transfers between devices  22.7 us (27%)
  Pallas kernels  12.5 us (15%)
  local copies, waits for them, and re-layouts  2.67 us (3%)
  other arithmetic  0.92 us (1%)
    ppermute x12, waiting for transfers between devices, over_rep(): return lax.ppermute(value, 'rep', [(i, i ^ k) for i in range(n_rep)])  39.8 us
    pallas_call x8, Pallas kernels, run(): pl.pallas_call(body, out_shape=outs, in_specs=[SMEM] * scalars + [VMEM] *...  12.5 us
    ppermute x8, starting transfers between devices, over_own(): return lax.ppermute(value, 'own', [(i, i ^ k) for i in range(4)])  11.6 us
    ppermute x12, starting transfers between devices, over_rep(): return lax.ppermute(value, 'rep', [(i, i ^ k) for i in range(n_rep)])  11.1 us
    ppermute x8, waiting for transfers between devices, over_own(): return lax.ppermute(value, 'own', [(i, i ^ k) for i in range(4)])  5.54 us
    unnamed x12, local copies, waits for them, and re-layouts  2.67 us
  transfers between devices with their start and end apart: 20, of which 9 were waited for; matrix products, arithmetic and copies ran while one was open for 0% of the time, Pallas kernels for 11%

profile of v6, /device:TPU:0, one launch (start us, length us, event | category | flops | bytes accessed | tf_op | source)
XLA Modules:
  0.0 84.9 jit_solution(15332178004980946438)
XLA Ops:
  0.6 0.5 collective-permute-start.1
  1.1 0.1 collective-permute-start.2
  1.2 4.3 %shard_map.102 = (bf16[192,128]{1,0:T(8,128)(2,1)}, bf16[240,2048]{1,0:T(8,128)(2,1)}, bf16[512,768]{1,0:T(8,128)(2,1)}) custom-call(s32[1]{0:T(128)} %bitcast.refs_0_, s32[8]{0:T(128)} %refs_1_.4, s32[1,128]{1,0:T(1,128)} %bitcast.12, bf16[128,2048]{1,0:T(8,128)(2,1)} %refs_3_.1, bf16[128,2048]{1,0:T(8,128)(2,1)} %refs_1_.5, bf16[512,256]{1,0:T(8,128)(2,1)} %bitcast.9, ...), custom_call_target="tpu_custom_call" | custom-call | bytes 3654180 | tf_op jit(solution)/shard_map/pallas_call | solution.py:39
  5.5 0.0 copy-start.5
  5.6 3.0 %collective-permute-start.7 = (bf16[512,768]{1,0:T(8,128)(2,1)}, bf16[512,768]{1,0:T(8,128)(2,1)S(1)}, u32[]{:S(2)}, u32[]{:S(2)}) collective-permute-start(bf16[512,768]{1,0:T(8,128)(2,1)} %get-tuple-element.43.refs_2_.refs_7_), channel_id=1, source_target_pairs={{0,16},{8,24},{16,0},{24,8},{1,17},{9,25},{17,1},{25,9},{2,18},{10... | collective-permute-start | bytes 2359304 | tf_op jit(solution)/shard_map/ppermute | solution.py:258
  8.6 1.5 %collective-permute-start.6 = (bf16[512,768]{1,0:T(8,128)(2,1)}, bf16[512,768]{1,0:T(8,128)(2,1)S(1)}, u32[]{:S(2)}, u32[]{:S(2)}) collective-permute-start(bf16[512,768]{1,0:T(8,128)(2,1)} %get-tuple-element.43.refs_2_.refs_7_), channel_id=1, source_target_pairs={{0,8},{8,0},{16,24},{24,16},{1,9},{9,1},{17,25},{25,17},{2,10},{10... | collective-permute-start | bytes 2359304 | tf_op jit(solution)/shard_map/ppermute | solution.py:258
  10.1 0.0 copy-done.5
  10.1 0.0 collective-permute-start
  10.1 1.1 %collective-permute-done.refs_2_ = s32[1,128]{1,0:T(1,128)S(1)} collective-permute-done((s32[1,128]{1,0:T(1,128)S(1)}, s32[1,128]{1,0:T(1,128)S(1)}, u32[]{:S(2)}, u32[]{:S(2)}) %collective-permute-start) | collective-permute-done | bytes 544 | tf_op jit(solution)/shard_map/ppermute | solution.py:261
  11.2 0.0 collective-permute-done.1.refs_5_
  11.2 0.0 collective-permute-done.2.refs_6_.refs_2_
  11.2 0.0 copy-start.4
  11.2 0.7 copy-done.4
  11.8 0.0 copy-start.2
  11.8 1.2 %copy-done.2 = bf16[240,2048]{1,0:T(8,128)(2,1)S(1)} copy-done((bf16[240,2048]{1,0:T(8,128)(2,1)S(1)}, bf16[240,2048]{1,0:T(8,128)(2,1)}, u32[]{:S(2)}) %copy-start.2) | copy-done | bytes 983064
  13.0 0.0 copy-start.3
  13.0 0.8 copy-done.3
  13.8 0.0 copy-start.1
  13.8 1.9 %shard_map.103 = (bf16[192,256]{1,0:T(8,128)(2,1)S(1)}, bf16[48,2048]{1,0:T(8,128)(2,1)S(1)}, bf16[96,2048]{1,0:T(8,128)(2,1)}, bf16[48,2048]{1,0:T(8,128)(2,1)}, bf16[48,2048]{1,0:T(8,128)(2,1)}) custom-call(s32[1]{0:T(128)} %bitcast.refs_0_, s32[8]{0:T(128)S(1)} %copy-done.4, s32[1,128]{1,0:T(1,128)S(1)} %collective-permute-done.refs_2_, ...), custom_call_target="tpu_custom_call" | custom-call | bytes 3162660 | tf_op jit(solution)/shard_map/pallas_call | solution.py:39
  15.7 1.6 %collective-permute-start.3 = (bf16[96,2048]{1,0:T(8,128)(2,1)}, bf16[96,2048]{1,0:T(8,128)(2,1)S(1)}, u32[]{:S(2)}, u32[]{:S(2)}) collective-permute-start(bf16[96,2048]{1,0:T(8,128)(2,1)} %get-tuple-element.40), channel_id=1, source_target_pairs={{0,2},{1,3},{2,0},{3,1},{4,6},{5,7},{6,4},{7,5},{8,10},{9,11},{10,... | collective-permute-start | bytes 1179656 | tf_op jit(solution)/shard_map/ppermute | solution.py:261
  17.3 2.6 %collective-permute-start.4 = (bf16[48,2048]{1,0:T(8,128)(2,1)}, bf16[48,2048]{1,0:T(8,128)(2,1)}, u32[]{:S(2)}, u32[]{:S(2)}) collective-permute-start(bf16[48,2048]{1,0:T(8,128)(2,1)} %get-tuple-element.41), channel_id=1, source_target_pairs={{0,4},{1,5},{2,6},{3,7},{4,0},{5,1},{6,2},{7,3},{8,12},{9,13},{10,... | collective-permute-start | bytes 589832 | tf_op jit(solution)/shard_map/ppermute | solution.py:261
  19.9 0.2 collective-permute-start.5
  20.1 0.0 copy-done.1
  20.1 0.5 shard_map.104
  20.7 10.7 %collective-permute-done.4.refs_3_ = bf16[48,2048]{1,0:T(8,128)(2,1)} collective-permute-done((bf16[48,2048]{1,0:T(8,128)(2,1)}, bf16[48,2048]{1,0:T(8,128)(2,1)}, u32[]{:S(2)}, u32[]{:S(2)}) %collective-permute-start.4) | collective-permute-done | bytes 196640 | tf_op jit(solution)/shard_map/ppermute | solution.py:261
  31.4 6.5 %collective-permute-done.5.refs_4_ = bf16[48,2048]{1,0:T(8,128)(2,1)} collective-permute-done((bf16[48,2048]{1,0:T(8,128)(2,1)}, bf16[48,2048]{1,0:T(8,128)(2,1)}, u32[]{:S(2)}, u32[]{:S(2)}) %collective-permute-start.5) | collective-permute-done | bytes 196640 | tf_op jit(solution)/shard_map/ppermute | solution.py:261
  37.8 0.0 collective-permute-done.7.refs_6_.refs_4_.refs_9_
  37.9 0.0 collective-permute-done.6.refs_5_.refs_3_.refs_8_
  37.9 0.0 collective-permute-done.3.refs_2_.refs_4_
  37.9 0.0 copy-start
  37.9 1.2 %shard_map.105 = (bf16[192,2048]{1,0:T(8,128)(2,1)S(1)}, bf16[192,512]{1,0:T(8,128)(2,1)S(1)}, bf16[192,512]{1,0:T(8,128)(2,1)S(1)}, bf16[576,512]{1,0:T(8,128)(2,1)S(1)}, bf16[576,512]{1,0:T(8,128)(2,1)S(1)}) custom-call(s32[1]{0:T(128)} %bitcast.5.refs_0_, bf16[48,2048]{1,0:T(8,128)(2,1)S(1)} %get-tuple-element.39.refs_1_, ...), custom_call_target="tpu_custom_call" | custom-call | bytes 4915204 | tf_op jit(solution)/shard_map/pallas_call | solution.py:39
  39.1 0.6 collective-permute-start.10
  39.7 0.5 collective-permute-start.11
  40.2 1.7 %collective-permute-start.8 = (bf16[48,2048]{1,0:T(8,128)(2,1)S(1)}, bf16[48,2048]{1,0:T(8,128)(2,1)S(1)}, u32[]{:S(2)}, u32[]{:S(2)}) collective-permute-start(bf16[48,2048]{1,0:T(8,128)(2,1)S(1)} %get-tuple-element.49), channel_id=1, source_target_pairs={{0,4},{1,5},{2,6},{3,7},{4,0},{5,1},{6,2},{7,3},{8,12},{9,13},{10,... | collective-permute-start | bytes 589832 | tf_op jit(solution)/shard_map/ppermute | solution.py:261
  41.9 1.3 %collective-permute-start.9 = (bf16[48,2048]{1,0:T(8,128)(2,1)S(1)}, bf16[48,2048]{1,0:T(8,128)(2,1)S(1)}, u32[]{:S(2)}, u32[]{:S(2)}) collective-permute-start(bf16[48,2048]{1,0:T(8,128)(2,1)S(1)} %get-tuple-element.50), channel_id=1, source_target_pairs={{0,6},{1,7},{2,4},{3,5},{4,2},{5,3},{6,0},{7,1},{8,14},{9,15},{10,... | collective-permute-start | bytes 589832 | tf_op jit(solution)/shard_map/ppermute | solution.py:261
  43.3 2.4 %collective-permute-start.12 = (bf16[192,512]{1,0:T(8,128)(2,1)S(1)}, bf16[192,512]{1,0:T(8,128)(2,1)S(1)}, u32[]{:S(2)}, u32[]{:S(2)}) collective-permute-start(bf16[192,512]{1,0:T(8,128)(2,1)S(1)} %get-tuple-element.53), channel_id=1, source_target_pairs={{0,24},{8,16},{16,8},{24,0},{1,25},{9,17},{17,9},{25,1},{2,26},{10... | collective-permute-start | bytes 589832 | tf_op jit(solution)/shard_map/ppermute | solution.py:258
  45.7 0.0 copy-done
  45.7 0.5 shard_map.106.refs_1_
  46.2 9.1 %collective-permute-done.8.refs_5_ = bf16[48,2048]{1,0:T(8,128)(2,1)S(1)} collective-permute-done((bf16[48,2048]{1,0:T(8,128)(2,1)S(1)}, bf16[48,2048]{1,0:T(8,128)(2,1)S(1)}, u32[]{:S(2)}, u32[]{:S(2)}) %collective-permute-start.8) | collective-permute-done | bytes 196640 | tf_op jit(solution)/shard_map/ppermute | solution.py:261
  55.3 0.0 collective-permute-done.9.refs_6_
  55.3 3.9 %collective-permute-done.12.refs_12_.refs_3_ = bf16[192,512]{1,0:T(8,128)(2,1)S(1)} collective-permute-done((bf16[192,512]{1,0:T(8,128)(2,1)S(1)}, bf16[192,512]{1,0:T(8,128)(2,1)S(1)}, u32[]{:S(2)}, u32[]{:S(2)}) %collective-permute-start.12) | collective-permute-done | bytes 196640 | tf_op jit(solution)/shard_map/ppermute | solution.py:258
  59.1 0.0 collective-permute-done.10.refs_10_.refs_2_
  59.1 0.0 collective-permute-done.11.refs_11_.refs_1_
  59.1 1.6 %shard_map.108 = (bf16[48,2048]{1,0:T(8,128)(2,1)S(1)}, bf16[48,2048]{1,0:T(8,128)(2,1)S(1)}, bf16[48,2048]{1,0:T(8,128)(2,1)S(1)}, bf16[48,2048]{1,0:T(8,128)(2...) custom-call(s32[1]{0:T(128)} %bitcast.5.refs_0_, ...), custom_call_target="tpu_custom_call" | custom-call | bytes 8585220 | tf_op jit(solution)/shard_map/pallas_call | solution.py:39
  60.8 0.6 collective-permute-start.16
  61.4 0.5 collective-permute-start.17
  61.9 2.4 %collective-permute-start.18 = (bf16[448,512]{1,0:T(8,128)(2,1)S(1)}, bf16[448,512]{1,0:T(8,128)(2,1)S(1)}, u32[]{:S(2)}, u32[]{:S(2)}) collective-permute-start(bf16[448,512]{1,0:T(8,128)(2,1)S(1)} %get-tuple-element.60), channel_id=1, source_target_pairs={{0,24},{8,16},{16,8},{24,0},{1,25},{9,17},{17,9},{25,1},{2,26},{10... | collective-permute-start | bytes 1376264 | tf_op jit(solution)/shard_map/ppermute | solution.py:258
  64.3 0.0 collective-permute-start.13
  64.3 2.0 %collective-permute-start.14 = (bf16[48,2048]{1,0:T(8,128)(2,1)S(1)}, bf16[48,2048]{1,0:T(8,128)(2,1)S(1)}, u32[]{:S(2)}, u32[]{:S(2)}) collective-permute-start(bf16[48,2048]{1,0:T(8,128)(2,1)S(1)} %get-tuple-element.56), channel_id=1, source_target_pairs={{0,4},{1,5},{2,6},{3,7},{4,0},{5,1},{6,2},{7,3},{8,12},{9,13},{10,... | collective-permute-start | bytes 589832 | tf_op jit(solution)/shard_map/ppermute | solution.py:261
  66.3 5.9 %collective-permute-done.13.refs_2_ = bf16[48,2048]{1,0:T(8,128)(2,1)S(1)} collective-permute-done((bf16[48,2048]{1,0:T(8,128)(2,1)S(1)}, bf16[48,2048]{1,0:T(8,128)(2,1)S(1)}, u32[]{:S(2)}, u32[]{:S(2)}) %collective-permute-start.13) | collective-permute-done | bytes 196640 | tf_op jit(solution)/shard_map/ppermute | solution.py:261
  72.2 1.1 %collective-permute-start.15 = (bf16[48,2048]{1,0:T(8,128)(2,1)S(1)}, bf16[48,2048]{1,0:T(8,128)(2,1)S(1)}, u32[]{:S(2)}, u32[]{:S(2)}) collective-permute-start(bf16[48,2048]{1,0:T(8,128)(2,1)S(1)} %get-tuple-element.57), channel_id=1, source_target_pairs={{0,6},{1,7},{2,4},{3,5},{4,2},{5,3},{6,0},{7,1},{8,14},{9,15},{10,... | collective-permute-start | bytes 589832 | tf_op jit(solution)/shard_map/ppermute | solution.py:261
  73.3 3.3 %collective-permute-done.14.refs_3_ = bf16[48,2048]{1,0:T(8,128)(2,1)S(1)} collective-permute-done((bf16[48,2048]{1,0:T(8,128)(2,1)S(1)}, bf16[48,2048]{1,0:T(8,128)(2,1)S(1)}, u32[]{:S(2)}, u32[]{:S(2)}) %collective-permute-start.14) | collective-permute-done | bytes 196640 | tf_op jit(solution)/shard_map/ppermute | solution.py:261
  76.6 3.2 %collective-permute-done.15.refs_4_ = bf16[48,2048]{1,0:T(8,128)(2,1)S(1)} collective-permute-done((bf16[48,2048]{1,0:T(8,128)(2,1)S(1)}, bf16[48,2048]{1,0:T(8,128)(2,1)S(1)}, u32[]{:S(2)}, u32[]{:S(2)}) %collective-permute-start.15) | collective-permute-done | bytes 196640 | tf_op jit(solution)/shard_map/ppermute | solution.py:261
  79.8 0.0 collective-permute-done.16.refs_5_
  79.8 1.7 %collective-permute-done.17.refs_6_ = bf16[448,512]{1,0:T(8,128)(2,1)S(1)} collective-permute-done((bf16[448,512]{1,0:T(8,128)(2,1)S(1)}, bf16[448,512]{1,0:T(8,128)(2,1)S(1)}, u32[]{:S(2)}, u32[]{:S(2)}) %collective-permute-start.17) | collective-permute-done | bytes 458784 | tf_op jit(solution)/shard_map/ppermute | solution.py:258
  81.5 0.0 collective-permute-done.18.refs_7_
  81.5 0.5 shard_map.109
  81.9 0.1 collective-permute-start.19
  82.0 1.9 %shard_map.110 = (f32[512,256]{1,0:T(8,128)}, f32[512,256]{1,0:T(8,128)}, f32[512,256]{1,0:T(8,128)}) custom-call(bf16[192,512]{1,0:T(8,128)(2,1)S(1)} %get-tuple-element.48.refs_2_.refs_0_, bf16[576,512]{1,0:T(8,128)(2,1)S(1)} %collective-permute-done.11.refs_11_.refs_1_, bf16[576,512]{1,0:T(8,128)(2,1)S(1)} %collective-permute-done.10.refs_10_.refs_2_, ...), custom_call_target="tpu_custom_call" | custom-call | bytes 5242880 | tf_op jit(solution)/shard_map/pallas_call | solution.py:39
  84.0 0.0 collective-permute-done.19
  84.0 0.9 %add.3 = bf16[128,2048]{1,0:T(8,128)(2,1)} add(bf16[128,2048]{1,0:T(8,128)(2,1)S(1)} %get-tuple-element.61, bf16[128,2048]{1,0:T(8,128)(2,1)S(1)} %collective-permute-done.19) | non-fusion elementwise | flops 262144 | bytes 1572864 | tf_op jit(solution)/shard_map/add | solution.py:317
  (1 shorter events, 0.0 us)
Async XLA Ops:
  0.6 10.6 %collective-permute-start.1 = (bf16[128,2048]{1,0:T(8,128)(2,1)}, bf16[128,2048]{1,0:T(8,128)(2,1)S(1)}, u32[]{:S(2)}, u32[]{:S(2)}) collective-permute-start(bf16[128,2048]{1,0:T(8,128)(2,1)} %refs_3_.1), channel_id=1, source_target_pairs={{0,1},{1,0},{2,3},{3,2},{4,5},{5,4},{6,7},{7,6},{8,9},{9,8},{10,11... | collective-permute-start | bytes 1572872 | tf_op jit(solution)/shard_map/ppermute | solution.py:261
  1.1 10.0 %collective-permute-start.2 = (bf16[128,2048]{1,0:T(8,128)(2,1)}, bf16[128,2048]{1,0:T(8,128)(2,1)S(1)}, u32[]{:S(2)}, u32[]{:S(2)}) collective-permute-start(bf16[128,2048]{1,0:T(8,128)(2,1)} %refs_1_.5), channel_id=1, source_target_pairs={{0,1},{1,0},{2,3},{3,2},{4,5},{5,4},{6,7},{7,6},{8,9},{9,8},{10,11... | collective-permute-start | bytes 1572872 | tf_op jit(solution)/shard_map/ppermute | solution.py:261
  5.5 4.5 %copy-start.5 = (s32[128,1]{0,1:T(1,128)S(1)}, s32[128,1]{0,1:T(1,128)}, u32[]{:S(2)}) copy-start(s32[128,1]{0,1:T(1,128)} %param.9) | copy-start | bytes 1540
  5.6 32.3 %collective-permute-start.7 = (bf16[512,768]{1,0:T(8,128)(2,1)}, bf16[512,768]{1,0:T(8,128)(2,1)S(1)}, u32[]{:S(2)}, u32[]{:S(2)}) collective-permute-start(bf16[512,768]{1,0:T(8,128)(2,1)} %get-tuple-element.43.refs_2_.refs_7_), channel_id=1, source_target_pairs={{0,16},{8,24},{16,0},{24,8},{1,17},{9,25},{17,1},{25,9},{2,18},{10... | collective-permute-start | bytes 2359304 | tf_op jit(solution)/shard_map/ppermute | solution.py:258
  8.6 29.3 %collective-permute-start.6 = (bf16[512,768]{1,0:T(8,128)(2,1)}, bf16[512,768]{1,0:T(8,128)(2,1)S(1)}, u32[]{:S(2)}, u32[]{:S(2)}) collective-permute-start(bf16[512,768]{1,0:T(8,128)(2,1)} %get-tuple-element.43.refs_2_.refs_7_), channel_id=1, source_target_pairs={{0,8},{8,0},{16,24},{24,16},{1,9},{9,1},{17,25},{25,17},{2,10},{10... | collective-permute-start | bytes 2359304 | tf_op jit(solution)/shard_map/ppermute | solution.py:258
  10.1 1.1 %collective-permute-start = (s32[1,128]{1,0:T(1,128)S(1)}, s32[1,128]{1,0:T(1,128)S(1)}, u32[]{:S(2)}, u32[]{:S(2)}) collective-permute-start(s32[1,128]{1,0:T(1,128)S(1)} %bitcast.13), channel_id=1, source_target_pairs={{0,1},{1,0},{2,3},{3,2},{4,5},{5,4},{6,7},{7,6},{8,9},{9,8},{10,11... | collective-permute-start | bytes 1544 | tf_op jit(solution)/shard_map/ppermute | solution.py:261
  11.2 0.7 copy-start.4
  11.8 1.2 %copy-start.2 = (bf16[240,2048]{1,0:T(8,128)(2,1)S(1)}, bf16[240,2048]{1,0:T(8,128)(2,1)}, u32[]{:S(2)}) copy-start(bf16[240,2048]{1,0:T(8,128)(2,1)} %get-tuple-element.37.refs_4_) | copy-start | bytes 2949124
  13.0 0.8 copy-start.3
  13.8 6.3 %copy-start.1 = (bf16[128,2048]{1,0:T(8,128)(2,1)S(1)}, bf16[128,2048]{1,0:T(8,128)(2,1)}, u32[]{:S(2)}) copy-start(bf16[128,2048]{1,0:T(8,128)(2,1)} %refs_1_.5) | copy-start | bytes 1572868
  15.7 22.1 %collective-permute-start.3 = (bf16[96,2048]{1,0:T(8,128)(2,1)}, bf16[96,2048]{1,0:T(8,128)(2,1)S(1)}, u32[]{:S(2)}, u32[]{:S(2)}) collective-permute-start(bf16[96,2048]{1,0:T(8,128)(2,1)} %get-tuple-element.40), channel_id=1, source_target_pairs={{0,2},{1,3},{2,0},{3,1},{4,6},{5,7},{6,4},{7,5},{8,10},{9,11},{10,... | collective-permute-start | bytes 1179656 | tf_op jit(solution)/shard_map/ppermute | solution.py:261
  17.3 14.0 %collective-permute-start.4 = (bf16[48,2048]{1,0:T(8,128)(2,1)}, bf16[48,2048]{1,0:T(8,128)(2,1)}, u32[]{:S(2)}, u32[]{:S(2)}) collective-permute-start(bf16[48,2048]{1,0:T(8,128)(2,1)} %get-tuple-element.41), channel_id=1, source_target_pairs={{0,4},{1,5},{2,6},{3,7},{4,0},{5,1},{6,2},{7,3},{8,12},{9,13},{10,... | collective-permute-start | bytes 589832 | tf_op jit(solution)/shard_map/ppermute | solution.py:261
  19.9 17.9 %collective-permute-start.5 = (bf16[48,2048]{1,0:T(8,128)(2,1)}, bf16[48,2048]{1,0:T(8,128)(2,1)}, u32[]{:S(2)}, u32[]{:S(2)}) collective-permute-start(bf16[48,2048]{1,0:T(8,128)(2,1)} %get-tuple-element.42), channel_id=1, source_target_pairs={{0,6},{1,7},{2,4},{3,5},{4,2},{5,3},{6,0},{7,1},{8,14},{9,15},{10,... | collective-permute-start | bytes 589832 | tf_op jit(solution)/shard_map/ppermute | solution.py:261
  37.9 7.9 %copy-start = (bf16[512,768]{1,0:T(8,128)(2,1)S(1)}, bf16[512,768]{1,0:T(8,128)(2,1)}, u32[]{:S(2)}) copy-start(bf16[512,768]{1,0:T(8,128)(2,1)} %get-tuple-element.43.refs_2_.refs_7_) | copy-start | bytes 2359300
  39.1 20.0 %collective-permute-start.10 = (bf16[576,512]{1,0:T(8,128)(2,1)S(1)}, bf16[576,512]{1,0:T(8,128)(2,1)S(1)}, u32[]{:S(2)}, u32[]{:S(2)}) collective-permute-start(bf16[576,512]{1,0:T(8,128)(2,1)S(1)} %get-tuple-element.51), channel_id=1, source_target_pairs={{0,16},{8,24},{16,0},{24,8},{1,17},{9,25},{17,1},{25,9},{2,18},{10... | collective-permute-start | bytes 1769480 | tf_op jit(solution)/shard_map/ppermute | solution.py:258
  39.7 19.4 %collective-permute-start.11 = (bf16[576,512]{1,0:T(8,128)(2,1)S(1)}, bf16[576,512]{1,0:T(8,128)(2,1)S(1)}, u32[]{:S(2)}, u32[]{:S(2)}) collective-permute-start(bf16[576,512]{1,0:T(8,128)(2,1)S(1)} %get-tuple-element.52), channel_id=1, source_target_pairs={{0,8},{8,0},{16,24},{24,16},{1,9},{9,1},{17,25},{25,17},{2,10},{10... | collective-permute-start | bytes 1769480 | tf_op jit(solution)/shard_map/ppermute | solution.py:258
  40.2 15.0 %collective-permute-start.8 = (bf16[48,2048]{1,0:T(8,128)(2,1)S(1)}, bf16[48,2048]{1,0:T(8,128)(2,1)S(1)}, u32[]{:S(2)}, u32[]{:S(2)}) collective-permute-start(bf16[48,2048]{1,0:T(8,128)(2,1)S(1)} %get-tuple-element.49), channel_id=1, source_target_pairs={{0,4},{1,5},{2,6},{3,7},{4,0},{5,1},{6,2},{7,3},{8,12},{9,13},{10,... | collective-permute-start | bytes 589832 | tf_op jit(solution)/shard_map/ppermute | solution.py:261
  41.9 13.4 %collective-permute-start.9 = (bf16[48,2048]{1,0:T(8,128)(2,1)S(1)}, bf16[48,2048]{1,0:T(8,128)(2,1)S(1)}, u32[]{:S(2)}, u32[]{:S(2)}) collective-permute-start(bf16[48,2048]{1,0:T(8,128)(2,1)S(1)} %get-tuple-element.50), channel_id=1, source_target_pairs={{0,6},{1,7},{2,4},{3,5},{4,2},{5,3},{6,0},{7,1},{8,14},{9,15},{10,... | collective-permute-start | bytes 589832 | tf_op jit(solution)/shard_map/ppermute | solution.py:261
  43.3 15.9 %collective-permute-start.12 = (bf16[192,512]{1,0:T(8,128)(2,1)S(1)}, bf16[192,512]{1,0:T(8,128)(2,1)S(1)}, u32[]{:S(2)}, u32[]{:S(2)}) collective-permute-start(bf16[192,512]{1,0:T(8,128)(2,1)S(1)} %get-tuple-element.53), channel_id=1, source_target_pairs={{0,24},{8,16},{16,8},{24,0},{1,25},{9,17},{17,9},{25,1},{2,26},{10... | collective-permute-start | bytes 589832 | tf_op jit(solution)/shard_map/ppermute | solution.py:258
  60.8 19.0 %collective-permute-start.16 = (bf16[448,512]{1,0:T(8,128)(2,1)S(1)}, bf16[448,512]{1,0:T(8,128)(2,1)S(1)}, u32[]{:S(2)}, u32[]{:S(2)}) collective-permute-start(bf16[448,512]{1,0:T(8,128)(2,1)S(1)} %get-tuple-element.58), channel_id=1, source_target_pairs={{0,8},{8,0},{16,24},{24,16},{1,9},{9,1},{17,25},{25,17},{2,10},{10... | collective-permute-start | bytes 1376264 | tf_op jit(solution)/shard_map/ppermute | solution.py:258
  61.4 20.1 %collective-permute-start.17 = (bf16[448,512]{1,0:T(8,128)(2,1)S(1)}, bf16[448,512]{1,0:T(8,128)(2,1)S(1)}, u32[]{:S(2)}, u32[]{:S(2)}) collective-permute-start(bf16[448,512]{1,0:T(8,128)(2,1)S(1)} %get-tuple-element.59), channel_id=1, source_target_pairs={{0,16},{8,24},{16,0},{24,8},{1,17},{9,25},{17,1},{25,9},{2,18},{10... | collective-permute-start | bytes 1376264 | tf_op jit(solution)/shard_map/ppermute | solution.py:258
  61.9 19.6 %collective-permute-start.18 = (bf16[448,512]{1,0:T(8,128)(2,1)S(1)}, bf16[448,512]{1,0:T(8,128)(2,1)S(1)}, u32[]{:S(2)}, u32[]{:S(2)}) collective-permute-start(bf16[448,512]{1,0:T(8,128)(2,1)S(1)} %get-tuple-element.60), channel_id=1, source_target_pairs={{0,24},{8,16},{16,8},{24,0},{1,25},{9,17},{17,9},{25,1},{2,26},{10... | collective-permute-start | bytes 1376264 | tf_op jit(solution)/shard_map/ppermute | solution.py:258
  64.3 7.9 %collective-permute-start.13 = (bf16[48,2048]{1,0:T(8,128)(2,1)S(1)}, bf16[48,2048]{1,0:T(8,128)(2,1)S(1)}, u32[]{:S(2)}, u32[]{:S(2)}) collective-permute-start(bf16[48,2048]{1,0:T(8,128)(2,1)S(1)} %get-tuple-element.55), channel_id=1, source_target_pairs={{0,2},{1,3},{2,0},{3,1},{4,6},{5,7},{6,4},{7,5},{8,10},{9,11},{10,... | collective-permute-start | bytes 589832 | tf_op jit(solution)/shard_map/ppermute | solution.py:261
  64.3 12.3 %collective-permute-start.14 = (bf16[48,2048]{1,0:T(8,128)(2,1)S(1)}, bf16[48,2048]{1,0:T(8,128)(2,1)S(1)}, u32[]{:S(2)}, u32[]{:S(2)}) collective-permute-start(bf16[48,2048]{1,0:T(8,128)(2,1)S(1)} %get-tuple-element.56), channel_id=1, source_target_pairs={{0,4},{1,5},{2,6},{3,7},{4,0},{5,1},{6,2},{7,3},{8,12},{9,13},{10,... | collective-permute-start | bytes 589832 | tf_op jit(solution)/shard_map/ppermute | solution.py:261
  72.2 7.6 %collective-permute-start.15 = (bf16[48,2048]{1,0:T(8,128)(2,1)S(1)}, bf16[48,2048]{1,0:T(8,128)(2,1)S(1)}, u32[]{:S(2)}, u32[]{:S(2)}) collective-permute-start(bf16[48,2048]{1,0:T(8,128)(2,1)S(1)} %get-tuple-element.57), channel_id=1, source_target_pairs={{0,6},{1,7},{2,4},{3,5},{4,2},{5,3},{6,0},{7,1},{8,14},{9,15},{10,... | collective-permute-start | bytes 589832 | tf_op jit(solution)/shard_map/ppermute | solution.py:261
  81.9 2.0 %collective-permute-start.19 = (bf16[128,2048]{1,0:T(8,128)(2,1)S(1)}, bf16[128,2048]{1,0:T(8,128)(2,1)S(1)}, u32[]{:S(2)}, u32[]{:S(2)}) collective-permute-start(bf16[128,2048]{1,0:T(8,128)(2,1)S(1)} %get-tuple-element.62), channel_id=1, source_target_pairs={{0,1},{1,0},{2,3},{3,2},{4,5},{5,4},{6,7},{7,6},{8,9},{9,8},{10,11... | collective-permute-start | bytes 1572872 | tf_op jit(solution)/shard_map/ppermute | solution.py:261

commit v7 on v6

--- a/solution.py
+++ b/solution.py
@@ -9,7 +9,6 @@
 
 VMEM = pl.BlockSpec(memory_space=pltpu.VMEM)
 SMEM = pl.BlockSpec(memory_space=pltpu.SMEM)
-HBM = pl.BlockSpec(memory_space=pltpu.HBM)
 ANY = pl.BlockSpec(memory_space=pl.ANY)
 MIB = 1024 * 1024
 BF16 = jnp.bfloat16
@@ -26,7 +25,7 @@
     return jax.ShapeDtypeStruct((rows, cols), dtype)
 
 
-def call(kernel, outs, scalars=0, scratch=(), fetched=0, room=32, earlier=(), stored=()):
+def call(kernel, outs, scalars=0, scratch=(), earlier=()):
     earlier = list(earlier)
 
     def body(*refs):
@@ -34,16 +33,15 @@
         kernel(*refs[: inputs - len(earlier)], *refs[inputs:])
 
     def run(*operands):
-        placed = len(operands) - scalars - fetched
         moved = sum(value.size * value.dtype.itemsize for value in (*operands, *outs))
         return pl.pallas_call(
             body,
             out_shape=outs,
-            in_specs=[SMEM] * scalars + [VMEM] * placed + [HBM] * fetched + [ANY] * len(earlier),
-            out_specs=[HBM if i in stored else VMEM for i in range(len(outs))],
+            in_specs=[SMEM] * scalars + [VMEM] * (len(operands) - scalars) + [ANY] * len(earlier),
+            out_specs=[VMEM] * len(outs),
             scratch_shapes=list(scratch),
             cost_estimate=pl.CostEstimate(flops=0, bytes_accessed=moved, transcendentals=0),
-            compiler_params=pltpu.CompilerParams(vmem_limit_bytes=room * MIB),
+            compiler_params=pltpu.CompilerParams(vmem_limit_bytes=32 * MIB),
         )(*operands, *earlier)
 
     return run
@@ -58,13 +56,6 @@
         input_output_aliases={i: i for i in range(len(values))},
         compiler_params=pltpu.CompilerParams(vmem_limit_bytes=MIB),
     )(*values, *earlier)
-
-
-def start_copies(pairs, sems):
-    copies = [pltpu.make_async_copy(source, into, sems.at[i]) for i, (source, into) in enumerate(pairs)]
-    for copy in copies:
-        copy.start()
-    return copies
 
 
 def picks(capacity, offset, rank_ref, host_ref, route_ref, slots):
@@ -86,40 +77,21 @@
     return jnp.where(slot == position, 1.0, 0.0).astype(BF16)
 
 
-def pack_own_kernel(capacity, rank_ref, host_ref, route_ref, *refs):
-    sources, (pick_ref, filled_ref, joined_ref), (x, dy, filled, weights, sems, out_sems) = refs[:5], refs[5:8], refs[8:]
-    width = weights.shape[1] // 3
+def pack_kernel(capacity, rank_ref, host_ref, route_a, route_b, x_a, x_b, dy_a, dy_b, pick_ref, *refs):
+    *send_refs, rows_ref = refs
     slots = pick_ref.shape[0]
-    near = slice(2 * capacity, 4 * capacity)
-    loads = start_copies(
-        zip(sources, (x, dy) + tuple(weights.at[:, pl.ds(i * width, width)] for i in range(3))), sems
-    )
-    pick_ref[...] = picks(capacity, 0, rank_ref, host_ref, route_ref, slots)
-    for load in loads[2:]:
-        load.wait()
-    stores = start_copies([(weights, joined_ref)], out_sems.at[0])
-    loads[0].wait()
-    filled[:slots] = dot(pick_ref[...], x[...], 1, 0).astype(BF16)
-    loads[1].wait()
-    filled[slots:] = dot(pick_ref[near], dy[...], 1, 0).astype(BF16)
-    stores += start_copies([(filled, filled_ref)], out_sems.at[1])
-    for store in stores:
-        store.wait()
-
-
-def pack_kernel(capacity, rank_ref, host_ref, route_ref, pick_own, filled_ref, x_ref, dy_ref, *refs):
-    pick_ref, *send_refs = refs
-    slots, tokens = pick_own.shape
+    tokens = route_a.shape[1]
     block = 2 * capacity
-    near = slice(block, 2 * block)
-    pick = picks(capacity, capacity, rank_ref, host_ref, route_ref, slots)
-    pick_ref[:, :tokens] = pick_own[...]
-    pick_ref[:, tokens:] = pick
-    filled = (dot(pick, x_ref[...], 1, 0) + filled_ref[:slots].astype(F32)).astype(BF16)
+    pick_ref[:, :tokens] = picks(capacity, 0, rank_ref, host_ref, route_a, slots)
+    pick_ref[:, tokens:] = picks(capacity, capacity, rank_ref, host_ref, route_b, slots)
+    rows_ref[:tokens] = x_a[...]
+    rows_ref[tokens:] = x_b[...]
+    filled = dot(pick_ref[...], rows_ref[...], 1, 0).astype(BF16)
     for k, ref in enumerate(send_refs):
         ref[:block] = filled[k * block : (k + 1) * block]
+    near = slice(block, 2 * block)
     send_refs[1][block:] = (
-        dot(pick_ref[near, tokens:], dy_ref[...], 1, 0) + filled_ref[slots:].astype(F32)
+        dot(pick_ref[near, :tokens], dy_a[...], 1, 0) + dot(pick_ref[near, tokens:], dy_b[...], 1, 0)
     ).astype(BF16)
 
 
@@ -221,11 +193,15 @@
 
 
 def sum_kernel(*refs):
-    pieces, messages, own_term, (gate_ref, up_ref, down_ref) = refs[:4], refs[4:8], refs[8], refs[9:]
+    pieces, messages, own_term = refs[:4], refs[4:8], refs[8]
+    (gate_ref, up_ref, down_ref), (x_ref, grads_ref) = refs[9:12], refs[12:]
     slots = pieces[0].shape[0]
     depth, width = gate_ref.shape
     half = depth // 2
-    total = sum(dot(piece[-slots:], got[:slots], 0, 0) for piece, got in zip(pieces, messages))
+    for k, (piece, got) in enumerate(zip(pieces, messages)):
+        x_ref[k * slots : (k + 1) * slots] = piece[-slots:]
+        grads_ref[k * slots : (k + 1) * slots] = got[:slots]
+    total = dot(x_ref[...], grads_ref[...], 0, 0)
     gate_ref[...] = total[:, :width]
     up_ref[...] = total[:, width:]
     for rows, cols in ((slice(0, half), slice(0, width)), (slice(half, depth), slice(width, 2 * width))):
@@ -262,27 +238,16 @@
 
     route = route.reshape(1, tok_rows)
     route_b, tokens_b, cotangent_b = over_rep(route, 1), over_rep(tokens, 1), over_rep(cotangent, 1)
-    token_rows = pltpu.VMEM((tok_rows, model_width), BF16)
+    joined = jnp.concatenate([w_gate[0], w_up[0], w_down_t[0]], axis=1)
+    joined_1, joined_2 = over_own(joined, 1), over_own(joined, 2)
     slot_rows = pltpu.VMEM((slots, model_width), BF16)
-    dma = pltpu.SemaphoreType.DMA
-    pick, filled, joined = call(
-        functools.partial(pack_own_kernel, capacity),
-        [shape(slots, tok_rows), shape(slots + block, model_width), shape(depth, 3 * width)],
-        2,
-        [token_rows, token_rows, pltpu.VMEM((slots + block, model_width), BF16), pltpu.VMEM((depth, 3 * width), BF16)]
-        + [dma((5,)), dma((2, 1))],
-        5,
-        62,
-        (),
-        (1, 2),
-    )(rank, host, route, tokens, cotangent, w_gate[0], w_up[0], w_down_t[0])
-    joined_1, joined_2 = over_own(joined, 1), over_own(joined, 2)
     pick, own_x, near, far_xa, far_xb = call(
         functools.partial(pack_kernel, capacity),
         [shape(slots, 2 * tok_rows), shape(block, model_width), shape(2 * block, model_width)]
         + [shape(block, model_width)] * 2,
         2,
-    )(rank, host, route_b, pick, filled, tokens_b, cotangent_b)
+        [pltpu.VMEM((2 * tok_rows, model_width), BF16)],
+    )(rank, host, route, route_b, tokens, tokens_b, cotangent, cotangent_b)
     near, far_xa, far_xb = over_rep(near, 2), over_rep(far_xa, 4), over_rep(far_xb, 6)
     own_dy, far_a, far_b = call(pack_more_kernel, [shape(block, model_width)] * 3)(pick, cotangent, cotangent_b)
 
@@ -315,7 +280,7 @@
         pick, *returned
     )
     x_grad = mine + over_rep(other, 1)
-    out = call(sum_kernel, [shape(depth, width, F32)] * 3)(
+    out = call(sum_kernel, [shape(depth, width, F32)] * 3, 0, [pltpu.VMEM((4 * slots, depth), BF16)] * 2)(
         piece_0, onward_1, onward_2, piece_3, grads, *messages, own_term
     )
     return (x_grad, *(grad[None] for grad in out))

time: 85.2 us -> 82.7 us (0.971)
  Pallas kernels: 12.5 us -> 9.64 us
  other arithmetic: 0.92 us -> 2.14 us
  local copies, waits for them, and re-layouts: 2.67 us -> 1.73 us
    pallas_call x8 -> x7, Pallas kernels: 12.5 us -> 9.64 us  [run(): pl.pallas_call(body, out_shape=outs, in_specs=[SMEM] * scalars + [VMEM] *...]
    concatenate x0 -> x1, other arithmetic: none -> 1.22 us  [shards_by_partner(): joined = jnp.concatenate([w_gate[0], w_up[0], w_down_t[0]], axis=1)]
    unnamed x12, local copies, waits for them, and re-layouts: 2.67 us -> 1.73 us
  transfers between devices with their start and end apart: 20 -> 20, of which waited for: 9 -> 10; matrix products, arithmetic and copies ran while one was open for 0% -> 1% of each run, Pallas kernels for 11% -> 6%
where the time goes in v7:
time: 82.7 us; the launch traced here: 82.4 us
  waiting for transfers between devices  45.5 us (55%)
  starting transfers between devices  22.7 us (27%)
  Pallas kernels  9.64 us (12%)
  other arithmetic  2.14 us (3%)
  local copies, waits for them, and re-layouts  1.73 us (2%)
    ppermute x12, waiting for transfers between devices, over_rep(): return lax.ppermute(value, 'rep', [(i, i ^ k) for i in range(n_rep)])  40 us
    ppermute x8, starting transfers between devices, over_own(): return lax.ppermute(value, 'own', [(i, i ^ k) for i in range(4)])  11.6 us
    ppermute x12, starting transfers between devices, over_rep(): return lax.ppermute(value, 'rep', [(i, i ^ k) for i in range(n_rep)])  11 us
    pallas_call x7, Pallas kernels, run(): pl.pallas_call(body, out_shape=outs, in_specs=[SMEM] * scalars + [VMEM] *...  9.64 us
    ppermute x8, waiting for transfers between devices, over_own(): return lax.ppermute(value, 'own', [(i, i ^ k) for i in range(4)])  5.5 us
    unnamed x12, local copies, waits for them, and re-layouts  1.73 us
  transfers between devices with their start and end apart: 20, of which 10 were waited for; matrix products, arithmetic and copies ran while one was open for 1% of the time, Pallas kernels for 6%

profile of v7, /device:TPU:0, one launch (start us, length us, event | category | flops | bytes accessed | tf_op | source)
XLA Modules:
  0.0 82.4 jit_solution(15099293008002666347)
XLA Ops:
  0.6 0.5 collective-permute-start.1
  1.2 0.1 collective-permute-start.2
  1.2 0.0 copy-start.5
  1.2 0.0 copy-start
  1.2 0.0 copy-start.4
  1.2 1.2 %pad_maximum_fusion.refs_2_.refs_7_ = bf16[512,768]{1,0:T(8,128)(2,1)S(1)} fusion(bf16[512,256]{1,0:T(8,128)(2,1)} %bitcast.11, bf16[512,256]{1,0:T(8,128)(2,1)} %bitcast.12, bf16[512,256]{1,0:T(8,128)(2,1)} %bitcast.13), kind=kLoop, calls=%fused_computation | loop fusion | flops 2359296 | bytes 1572864 | tf_op jit(solution)/shard_map/concatenate | solution.py:241
  2.5 3.0 %collective-permute-start.7 = (bf16[512,768]{1,0:T(8,128)(2,1)S(1)}, bf16[512,768]{1,0:T(8,128)(2,1)S(1)}, u32[]{:S(2)}, u32[]{:S(2)}) collective-permute-start(bf16[512,768]{1,0:T(8,128)(2,1)S(1)} %pad_maximum_fusion.refs_2_.refs_7_), channel_id=1, source_target_pairs={{0,16},{8,24},{16,0},{24,8},{1,17},{9,25},{17,1},{25,9},{2,18},{10... | collective-permute-start | bytes 2359304 | tf_op jit(solution)/shard_map/ppermute | solution.py:234
  5.5 1.5 %collective-permute-start.6 = (bf16[512,768]{1,0:T(8,128)(2,1)S(1)}, bf16[512,768]{1,0:T(8,128)(2,1)S(1)}, u32[]{:S(2)}, u32[]{:S(2)}) collective-permute-start(bf16[512,768]{1,0:T(8,128)(2,1)S(1)} %pad_maximum_fusion.refs_2_.refs_7_), channel_id=1, source_target_pairs={{0,8},{8,0},{16,24},{24,16},{1,9},{9,1},{17,25},{25,17},{2,10},{10... | collective-permute-start | bytes 2359304 | tf_op jit(solution)/shard_map/ppermute | solution.py:234
  7.0 0.0 copy-done.5
  7.0 0.0 collective-permute-start
  7.0 1.1 %collective-permute-done.refs_3_ = s32[1,128]{1,0:T(1,128)S(1)} collective-permute-done((s32[1,128]{1,0:T(1,128)S(1)}, s32[1,128]{1,0:T(1,128)S(1)}, u32[]{:S(2)}, u32[]{:S(2)}) %collective-permute-start) | collective-permute-done | bytes 544 | tf_op jit(solution)/shard_map/ppermute | solution.py:237
  8.1 0.0 collective-permute-done.1.refs_5_
  8.1 0.0 collective-permute-done.2.refs_7_.refs_2_
  8.1 0.0 copy-done
  8.1 0.0 copy-done.4
  8.1 0.0 copy-start.1
  8.1 1.0 %copy-done.1 = bf16[128,2048]{1,0:T(8,128)(2,1)S(1)} copy-done((bf16[128,2048]{1,0:T(8,128)(2,1)S(1)}, bf16[128,2048]{1,0:T(8,128)(2,1)}, u32[]{:S(2)}) %copy-start.1) | copy-done | bytes 524312
  9.2 2.4 %shard_map.102 = (bf16[192,256]{1,0:T(8,128)(2,1)S(1)}, bf16[48,2048]{1,0:T(8,128)(2,1)S(1)}, bf16[96,2048]{1,0:T(8,128)(2,1)}, bf16[48,2048]{1,0:T(8,128)(2,1)}, bf16[48,2048]{1,0:T(8,128)(2,1)}) custom-call(s32[1]{0:T(128)} %bitcast.refs_0_, s32[8]{0:T(128)S(1)} %copy-done.4, s32[1,128]{1,0:T(1,128)S(1)} %bitcast.10, ...), custom_call_target="tpu_custom_call" | custom-call | bytes 3179556 | tf_op jit(solution)/shard_map/pallas_call | solution.py:37
  11.6 0.0 copy-start.2
  11.6 0.7 copy-done.2
  12.3 1.6 %collective-permute-start.3 = (bf16[96,2048]{1,0:T(8,128)(2,1)}, bf16[96,2048]{1,0:T(8,128)(2,1)}, u32[]{:S(2)}, u32[]{:S(2)}) collective-permute-start(bf16[96,2048]{1,0:T(8,128)(2,1)} %get-tuple-element.35), channel_id=1, source_target_pairs={{0,2},{1,3},{2,0},{3,1},{4,6},{5,7},{6,4},{7,5},{8,10},{9,11},{10,... | collective-permute-start | bytes 1179656 | tf_op jit(solution)/shard_map/ppermute | solution.py:237
  13.9 2.6 %collective-permute-start.4 = (bf16[48,2048]{1,0:T(8,128)(2,1)}, bf16[48,2048]{1,0:T(8,128)(2,1)}, u32[]{:S(2)}, u32[]{:S(2)}) collective-permute-start(bf16[48,2048]{1,0:T(8,128)(2,1)} %get-tuple-element.36), channel_id=1, source_target_pairs={{0,4},{1,5},{2,6},{3,7},{4,0},{5,1},{6,2},{7,3},{8,12},{9,13},{10,... | collective-permute-start | bytes 589832 | tf_op jit(solution)/shard_map/ppermute | solution.py:237
  16.4 0.2 collective-permute-start.5
  16.7 0.0 copy-start.3
  16.7 0.6 shard_map.103
  17.2 10.7 %collective-permute-done.4.refs_3_ = bf16[48,2048]{1,0:T(8,128)(2,1)} collective-permute-done((bf16[48,2048]{1,0:T(8,128)(2,1)}, bf16[48,2048]{1,0:T(8,128)(2,1)}, u32[]{:S(2)}, u32[]{:S(2)}) %collective-permute-start.4) | collective-permute-done | bytes 196640 | tf_op jit(solution)/shard_map/ppermute | solution.py:237
  27.9 6.5 %collective-permute-done.5.refs_4_ = bf16[48,2048]{1,0:T(8,128)(2,1)} collective-permute-done((bf16[48,2048]{1,0:T(8,128)(2,1)}, bf16[48,2048]{1,0:T(8,128)(2,1)}, u32[]{:S(2)}, u32[]{:S(2)}) %collective-permute-start.5) | collective-permute-done | bytes 196640 | tf_op jit(solution)/shard_map/ppermute | solution.py:237
  34.4 0.0 collective-permute-done.7.refs_6_.refs_4_.refs_9_
  34.4 0.0 collective-permute-done.6.refs_5_.refs_3_.refs_8_
  34.4 0.0 collective-permute-done.3.refs_2_.refs_4_
  34.4 0.0 copy-done.3
  34.4 1.3 %shard_map.104 = (bf16[192,2048]{1,0:T(8,128)(2,1)S(1)}, bf16[192,512]{1,0:T(8,128)(2,1)S(1)}, bf16[192,512]{1,0:T(8,128)(2,1)S(1)}, bf16[576,512]{1,0:T(8,128)(2,1)S(1)}, bf16[576,512]{1,0:T(8,128)(2,1)S(1)}) custom-call(s32[1]{0:T(128)} %bitcast.2.refs_0_, bf16[48,2048]{1,0:T(8,128)(2,1)S(1)} %copy-done.3, ...), custom_call_target="tpu_custom_call" | custom-call | bytes 4915204 | tf_op jit(solution)/shard_map/pallas_call | solution.py:37
  35.7 0.6 collective-permute-start.10
  36.3 0.5 collective-permute-start.11
  36.8 1.7 %collective-permute-start.8 = (bf16[48,2048]{1,0:T(8,128)(2,1)S(1)}, bf16[48,2048]{1,0:T(8,128)(2,1)S(1)}, u32[]{:S(2)}, u32[]{:S(2)}) collective-permute-start(bf16[48,2048]{1,0:T(8,128)(2,1)S(1)} %get-tuple-element.43), channel_id=1, source_target_pairs={{0,4},{1,5},{2,6},{3,7},{4,0},{5,1},{6,2},{7,3},{8,12},{9,13},{10,... | collective-permute-start | bytes 589832 | tf_op jit(solution)/shard_map/ppermute | solution.py:237
  38.5 1.3 %collective-permute-start.9 = (bf16[48,2048]{1,0:T(8,128)(2,1)S(1)}, bf16[48,2048]{1,0:T(8,128)(2,1)S(1)}, u32[]{:S(2)}, u32[]{:S(2)}) collective-permute-start(bf16[48,2048]{1,0:T(8,128)(2,1)S(1)} %get-tuple-element.44), channel_id=1, source_target_pairs={{0,6},{1,7},{2,4},{3,5},{4,2},{5,3},{6,0},{7,1},{8,14},{9,15},{10,... | collective-permute-start | bytes 589832 | tf_op jit(solution)/shard_map/ppermute | solution.py:237
  39.8 2.5 %collective-permute-start.12 = (bf16[192,512]{1,0:T(8,128)(2,1)S(1)}, bf16[192,512]{1,0:T(8,128)(2,1)S(1)}, u32[]{:S(2)}, u32[]{:S(2)}) collective-permute-start(bf16[192,512]{1,0:T(8,128)(2,1)S(1)} %get-tuple-element.47), channel_id=1, source_target_pairs={{0,24},{8,16},{16,8},{24,0},{1,25},{9,17},{17,9},{25,1},{2,26},{10... | collective-permute-start | bytes 589832 | tf_op jit(solution)/shard_map/ppermute | solution.py:234
  42.3 0.5 shard_map.105.refs_1_
  42.8 9.1 %collective-permute-done.8.refs_5_ = bf16[48,2048]{1,0:T(8,128)(2,1)S(1)} collective-permute-done((bf16[48,2048]{1,0:T(8,128)(2,1)S(1)}, bf16[48,2048]{1,0:T(8,128)(2,1)S(1)}, u32[]{:S(2)}, u32[]{:S(2)}) %collective-permute-start.8) | collective-permute-done | bytes 196640 | tf_op jit(solution)/shard_map/ppermute | solution.py:237
  51.9 0.0 collective-permute-done.9.refs_6_
  51.9 3.9 %collective-permute-done.12.refs_12_.refs_3_ = bf16[192,512]{1,0:T(8,128)(2,1)S(1)} collective-permute-done((bf16[192,512]{1,0:T(8,128)(2,1)S(1)}, bf16[192,512]{1,0:T(8,128)(2,1)S(1)}, u32[]{:S(2)}, u32[]{:S(2)}) %collective-permute-start.12) | collective-permute-done | bytes 196640 | tf_op jit(solution)/shard_map/ppermute | solution.py:234
  55.7 0.0 collective-permute-done.10.refs_10_.refs_2_
  55.7 0.0 collective-permute-done.11.refs_11_.refs_1_
  55.7 2.6 %shard_map.107 = (bf16[48,2048]{1,0:T(8,128)(2,1)S(1)}, bf16[48,2048]{1,0:T(8,128)(2,1)S(1)}, bf16[48,2048]{1,0:T(8,128)(2,1)S(1)}, bf16[48,2048]{1,0:T(8,128)(2...) custom-call(s32[1]{0:T(128)} %bitcast.2.refs_0_, ...), custom_call_target="tpu_custom_call" | custom-call | bytes 8585220 | tf_op jit(solution)/shard_map/pallas_call | solution.py:37
  58.4 0.6 collective-permute-start.16
  58.9 0.5 collective-permute-start.17
  59.5 2.5 %collective-permute-start.18 = (bf16[448,512]{1,0:T(8,128)(2,1)S(1)}, bf16[448,512]{1,0:T(8,128)(2,1)S(1)}, u32[]{:S(2)}, u32[]{:S(2)}) collective-permute-start(bf16[448,512]{1,0:T(8,128)(2,1)S(1)} %get-tuple-element.54), channel_id=1, source_target_pairs={{0,24},{8,16},{16,8},{24,0},{1,25},{9,17},{17,9},{25,1},{2,26},{10... | collective-permute-start | bytes 1376264 | tf_op jit(solution)/shard_map/ppermute | solution.py:234
  61.9 0.0 collective-permute-start.13
  61.9 1.9 %collective-permute-start.14 = (bf16[48,2048]{1,0:T(8,128)(2,1)S(1)}, bf16[48,2048]{1,0:T(8,128)(2,1)S(1)}, u32[]{:S(2)}, u32[]{:S(2)}) collective-permute-start(bf16[48,2048]{1,0:T(8,128)(2,1)S(1)} %get-tuple-element.50), channel_id=1, source_target_pairs={{0,4},{1,5},{2,6},{3,7},{4,0},{5,1},{6,2},{7,3},{8,12},{9,13},{10,... | collective-permute-start | bytes 589832 | tf_op jit(solution)/shard_map/ppermute | solution.py:237
  63.9 6.0 %collective-permute-done.13.refs_2_ = bf16[48,2048]{1,0:T(8,128)(2,1)S(1)} collective-permute-done((bf16[48,2048]{1,0:T(8,128)(2,1)S(1)}, bf16[48,2048]{1,0:T(8,128)(2,1)S(1)}, u32[]{:S(2)}, u32[]{:S(2)}) %collective-permute-start.13) | collective-permute-done | bytes 196640 | tf_op jit(solution)/shard_map/ppermute | solution.py:237
  69.9 1.0 %collective-permute-start.15 = (bf16[48,2048]{1,0:T(8,128)(2,1)S(1)}, bf16[48,2048]{1,0:T(8,128)(2,1)S(1)}, u32[]{:S(2)}, u32[]{:S(2)}) collective-permute-start(bf16[48,2048]{1,0:T(8,128)(2,1)S(1)} %get-tuple-element.51), channel_id=1, source_target_pairs={{0,6},{1,7},{2,4},{3,5},{4,2},{5,3},{6,0},{7,1},{8,14},{9,15},{10,... | collective-permute-start | bytes 589832 | tf_op jit(solution)/shard_map/ppermute | solution.py:237
  70.9 3.3 %collective-permute-done.14.refs_3_ = bf16[48,2048]{1,0:T(8,128)(2,1)S(1)} collective-permute-done((bf16[48,2048]{1,0:T(8,128)(2,1)S(1)}, bf16[48,2048]{1,0:T(8,128)(2,1)S(1)}, u32[]{:S(2)}, u32[]{:S(2)}) %collective-permute-start.14) | collective-permute-done | bytes 196640 | tf_op jit(solution)/shard_map/ppermute | solution.py:237
  74.1 3.3 %collective-permute-done.15.refs_4_ = bf16[48,2048]{1,0:T(8,128)(2,1)S(1)} collective-permute-done((bf16[48,2048]{1,0:T(8,128)(2,1)S(1)}, bf16[48,2048]{1,0:T(8,128)(2,1)S(1)}, u32[]{:S(2)}, u32[]{:S(2)}) %collective-permute-start.15) | collective-permute-done | bytes 196640 | tf_op jit(solution)/shard_map/ppermute | solution.py:237
  77.4 0.0 collective-permute-done.16.refs_5_
  77.4 1.6 %collective-permute-done.17.refs_6_ = bf16[448,512]{1,0:T(8,128)(2,1)S(1)} collective-permute-done((bf16[448,512]{1,0:T(8,128)(2,1)S(1)}, bf16[448,512]{1,0:T(8,128)(2,1)S(1)}, u32[]{:S(2)}, u32[]{:S(2)}) %collective-permute-start.17) | collective-permute-done | bytes 458784 | tf_op jit(solution)/shard_map/ppermute | solution.py:234
  79.0 0.0 collective-permute-done.18.refs_7_
  79.0 0.5 shard_map.108
  79.5 0.1 collective-permute-start.19
  79.6 1.8 %shard_map.109 = (f32[512,256]{1,0:T(8,128)}, f32[512,256]{1,0:T(8,128)}, f32[512,256]{1,0:T(8,128)}) custom-call(bf16[192,512]{1,0:T(8,128)(2,1)S(1)} %get-tuple-element.42.refs_2_.refs_0_, bf16[576,512]{1,0:T(8,128)(2,1)S(1)} %collective-permute-done.11.refs_11_.refs_1_, bf16[576,512]{1,0:T(8,128)(2,1)S(1)} %collective-permute-done.10.refs_10_.refs_2_, ...), custom_call_target="tpu_custom_call" | custom-call | bytes 5242880 | tf_op jit(solution)/shard_map/pallas_call | solution.py:37
  81.4 0.1 collective-permute-done.19
  81.5 0.9 %add.3 = bf16[128,2048]{1,0:T(8,128)(2,1)} add(bf16[128,2048]{1,0:T(8,128)(2,1)S(1)} %get-tuple-element.55, bf16[128,2048]{1,0:T(8,128)(2,1)S(1)} %collective-permute-done.19) | non-fusion elementwise | flops 262144 | bytes 1572864 | tf_op jit(solution)/shard_map/add | solution.py:282
  (1 shorter events, 0.0 us)
Async XLA Ops:
  0.6 7.5 %collective-permute-start.1 = (bf16[128,2048]{1,0:T(8,128)(2,1)}, bf16[128,2048]{1,0:T(8,128)(2,1)}, u32[]{:S(2)}, u32[]{:S(2)}) collective-permute-start(bf16[128,2048]{1,0:T(8,128)(2,1)} %refs_4_.1), channel_id=1, source_target_pairs={{0,1},{1,0},{2,3},{3,2},{4,5},{5,4},{6,7},{7,6},{8,9},{9,8},{10,11... | collective-permute-start | bytes 1572872 | tf_op jit(solution)/shard_map/ppermute | solution.py:237
  1.2 6.9 %collective-permute-start.2 = (bf16[128,2048]{1,0:T(8,128)(2,1)}, bf16[128,2048]{1,0:T(8,128)(2,1)S(1)}, u32[]{:S(2)}, u32[]{:S(2)}) collective-permute-start(bf16[128,2048]{1,0:T(8,128)(2,1)} %refs_1_.3), channel_id=1, source_target_pairs={{0,1},{1,0},{2,3},{3,2},{4,5},{5,4},{6,7},{7,6},{8,9},{9,8},{10,11... | collective-permute-start | bytes 1572872 | tf_op jit(solution)/shard_map/ppermute | solution.py:237
  1.2 5.7 %copy-start.5 = (s32[128,1]{0,1:T(1,128)S(1)}, s32[128,1]{0,1:T(1,128)}, u32[]{:S(2)}) copy-start(s32[128,1]{0,1:T(1,128)} %param.9) | copy-start | bytes 1540
  1.2 6.9 %copy-start = (bf16[128,2048]{1,0:T(8,128)(2,1)S(1)}, bf16[128,2048]{1,0:T(8,128)(2,1)}, u32[]{:S(2)}) copy-start(bf16[128,2048]{1,0:T(8,128)(2,1)} %refs_1_.3) | copy-start | bytes 1572868
  1.2 6.9 %copy-start.4 = (s32[8]{0:T(128)S(1)}, s32[8]{0:T(128)}, u32[]{:S(2)}) copy-start(s32[8]{0:T(128)} %refs_1_.2) | copy-start | bytes 100
  2.5 31.9 %collective-permute-start.7 = (bf16[512,768]{1,0:T(8,128)(2,1)S(1)}, bf16[512,768]{1,0:T(8,128)(2,1)S(1)}, u32[]{:S(2)}, u32[]{:S(2)}) collective-permute-start(bf16[512,768]{1,0:T(8,128)(2,1)S(1)} %pad_maximum_fusion.refs_2_.refs_7_), channel_id=1, source_target_pairs={{0,16},{8,24},{16,0},{24,8},{1,17},{9,25},{17,1},{25,9},{2,18},{10... | collective-permute-start | bytes 2359304 | tf_op jit(solution)/shard_map/ppermute | solution.py:234
  5.5 28.9 %collective-permute-start.6 = (bf16[512,768]{1,0:T(8,128)(2,1)S(1)}, bf16[512,768]{1,0:T(8,128)(2,1)S(1)}, u32[]{:S(2)}, u32[]{:S(2)}) collective-permute-start(bf16[512,768]{1,0:T(8,128)(2,1)S(1)} %pad_maximum_fusion.refs_2_.refs_7_), channel_id=1, source_target_pairs={{0,8},{8,0},{16,24},{24,16},{1,9},{9,1},{17,25},{25,17},{2,10},{10... | collective-permute-start | bytes 2359304 | tf_op jit(solution)/shard_map/ppermute | solution.py:234
  7.0 1.1 %collective-permute-start = (s32[1,128]{1,0:T(1,128)S(1)}, s32[1,128]{1,0:T(1,128)S(1)}, u32[]{:S(2)}, u32[]{:S(2)}) collective-permute-start(s32[1,128]{1,0:T(1,128)S(1)} %bitcast.9), channel_id=1, source_target_pairs={{0,1},{1,0},{2,3},{3,2},{4,5},{5,4},{6,7},{7,6},{8,9},{9,8},{10,11... | collective-permute-start | bytes 1544 | tf_op jit(solution)/shard_map/ppermute | solution.py:237
  8.1 1.0 %copy-start.1 = (bf16[128,2048]{1,0:T(8,128)(2,1)S(1)}, bf16[128,2048]{1,0:T(8,128)(2,1)}, u32[]{:S(2)}) copy-start(bf16[128,2048]{1,0:T(8,128)(2,1)} %refs_4_.1) | copy-start | bytes 1572868
  11.6 0.7 copy-start.2
  12.3 22.1 %collective-permute-start.3 = (bf16[96,2048]{1,0:T(8,128)(2,1)}, bf16[96,2048]{1,0:T(8,128)(2,1)}, u32[]{:S(2)}, u32[]{:S(2)}) collective-permute-start(bf16[96,2048]{1,0:T(8,128)(2,1)} %get-tuple-element.35), channel_id=1, source_target_pairs={{0,2},{1,3},{2,0},{3,1},{4,6},{5,7},{6,4},{7,5},{8,10},{9,11},{10,... | collective-permute-start | bytes 1179656 | tf_op jit(solution)/shard_map/ppermute | solution.py:237
  13.9 14.0 %collective-permute-start.4 = (bf16[48,2048]{1,0:T(8,128)(2,1)}, bf16[48,2048]{1,0:T(8,128)(2,1)}, u32[]{:S(2)}, u32[]{:S(2)}) collective-permute-start(bf16[48,2048]{1,0:T(8,128)(2,1)} %get-tuple-element.36), channel_id=1, source_target_pairs={{0,4},{1,5},{2,6},{3,7},{4,0},{5,1},{6,2},{7,3},{8,12},{9,13},{10,... | collective-permute-start | bytes 589832 | tf_op jit(solution)/shard_map/ppermute | solution.py:237
  16.4 17.9 %collective-permute-start.5 = (bf16[48,2048]{1,0:T(8,128)(2,1)}, bf16[48,2048]{1,0:T(8,128)(2,1)}, u32[]{:S(2)}, u32[]{:S(2)}) collective-permute-start(bf16[48,2048]{1,0:T(8,128)(2,1)} %get-tuple-element.37), channel_id=1, source_target_pairs={{0,6},{1,7},{2,4},{3,5},{4,2},{5,3},{6,0},{7,1},{8,14},{9,15},{10,... | collective-permute-start | bytes 589832 | tf_op jit(solution)/shard_map/ppermute | solution.py:237
  16.7 17.7 %copy-start.3 = (bf16[48,2048]{1,0:T(8,128)(2,1)S(1)}, bf16[48,2048]{1,0:T(8,128)(2,1)}, u32[]{:S(2)}) copy-start(bf16[48,2048]{1,0:T(8,128)(2,1)} %copy-done.2) | copy-start | bytes 589828
  35.7 20.0 %collective-permute-start.10 = (bf16[576,512]{1,0:T(8,128)(2,1)S(1)}, bf16[576,512]{1,0:T(8,128)(2,1)S(1)}, u32[]{:S(2)}, u32[]{:S(2)}) collective-permute-start(bf16[576,512]{1,0:T(8,128)(2,1)S(1)} %get-tuple-element.45), channel_id=1, source_target_pairs={{0,16},{8,24},{16,0},{24,8},{1,17},{9,25},{17,1},{25,9},{2,18},{10... | collective-permute-start | bytes 1769480 | tf_op jit(solution)/shard_map/ppermute | solution.py:234
  36.3 19.5 %collective-permute-start.11 = (bf16[576,512]{1,0:T(8,128)(2,1)S(1)}, bf16[576,512]{1,0:T(8,128)(2,1)S(1)}, u32[]{:S(2)}, u32[]{:S(2)}) collective-permute-start(bf16[576,512]{1,0:T(8,128)(2,1)S(1)} %get-tuple-element.46), channel_id=1, source_target_pairs={{0,8},{8,0},{16,24},{24,16},{1,9},{9,1},{17,25},{25,17},{2,10},{10... | collective-permute-start | bytes 1769480 | tf_op jit(solution)/shard_map/ppermute | solution.py:234
  36.8 15.0 %collective-permute-start.8 = (bf16[48,2048]{1,0:T(8,128)(2,1)S(1)}, bf16[48,2048]{1,0:T(8,128)(2,1)S(1)}, u32[]{:S(2)}, u32[]{:S(2)}) collective-permute-start(bf16[48,2048]{1,0:T(8,128)(2,1)S(1)} %get-tuple-element.43), channel_id=1, source_target_pairs={{0,4},{1,5},{2,6},{3,7},{4,0},{5,1},{6,2},{7,3},{8,12},{9,13},{10,... | collective-permute-start | bytes 589832 | tf_op jit(solution)/shard_map/ppermute | solution.py:237
  38.5 13.4 %collective-permute-start.9 = (bf16[48,2048]{1,0:T(8,128)(2,1)S(1)}, bf16[48,2048]{1,0:T(8,128)(2,1)S(1)}, u32[]{:S(2)}, u32[]{:S(2)}) collective-permute-start(bf16[48,2048]{1,0:T(8,128)(2,1)S(1)} %get-tuple-element.44), channel_id=1, source_target_pairs={{0,6},{1,7},{2,4},{3,5},{4,2},{5,3},{6,0},{7,1},{8,14},{9,15},{10,... | collective-permute-start | bytes 589832 | tf_op jit(solution)/shard_map/ppermute | solution.py:237
  39.8 15.9 %collective-permute-start.12 = (bf16[192,512]{1,0:T(8,128)(2,1)S(1)}, bf16[192,512]{1,0:T(8,128)(2,1)S(1)}, u32[]{:S(2)}, u32[]{:S(2)}) collective-permute-start(bf16[192,512]{1,0:T(8,128)(2,1)S(1)} %get-tuple-element.47), channel_id=1, source_target_pairs={{0,24},{8,16},{16,8},{24,0},{1,25},{9,17},{17,9},{25,1},{2,26},{10... | collective-permute-start | bytes 589832 | tf_op jit(solution)/shard_map/ppermute | solution.py:234
  58.4 19.1 %collective-permute-start.16 = (bf16[448,512]{1,0:T(8,128)(2,1)S(1)}, bf16[448,512]{1,0:T(8,128)(2,1)S(1)}, u32[]{:S(2)}, u32[]{:S(2)}) collective-permute-start(bf16[448,512]{1,0:T(8,128)(2,1)S(1)} %get-tuple-element.52), channel_id=1, source_target_pairs={{0,8},{8,0},{16,24},{24,16},{1,9},{9,1},{17,25},{25,17},{2,10},{10... | collective-permute-start | bytes 1376264 | tf_op jit(solution)/shard_map/ppermute | solution.py:234
  58.9 20.1 %collective-permute-start.17 = (bf16[448,512]{1,0:T(8,128)(2,1)S(1)}, bf16[448,512]{1,0:T(8,128)(2,1)S(1)}, u32[]{:S(2)}, u32[]{:S(2)}) collective-permute-start(bf16[448,512]{1,0:T(8,128)(2,1)S(1)} %get-tuple-element.53), channel_id=1, source_target_pairs={{0,16},{8,24},{16,0},{24,8},{1,17},{9,25},{17,1},{25,9},{2,18},{10... | collective-permute-start | bytes 1376264 | tf_op jit(solution)/shard_map/ppermute | solution.py:234
  59.5 19.6 %collective-permute-start.18 = (bf16[448,512]{1,0:T(8,128)(2,1)S(1)}, bf16[448,512]{1,0:T(8,128)(2,1)S(1)}, u32[]{:S(2)}, u32[]{:S(2)}) collective-permute-start(bf16[448,512]{1,0:T(8,128)(2,1)S(1)} %get-tuple-element.54), channel_id=1, source_target_pairs={{0,24},{8,16},{16,8},{24,0},{1,25},{9,17},{17,9},{25,1},{2,26},{10... | collective-permute-start | bytes 1376264 | tf_op jit(solution)/shard_map/ppermute | solution.py:234
  61.9 7.9 %collective-permute-start.13 = (bf16[48,2048]{1,0:T(8,128)(2,1)S(1)}, bf16[48,2048]{1,0:T(8,128)(2,1)S(1)}, u32[]{:S(2)}, u32[]{:S(2)}) collective-permute-start(bf16[48,2048]{1,0:T(8,128)(2,1)S(1)} %get-tuple-element.49), channel_id=1, source_target_pairs={{0,2},{1,3},{2,0},{3,1},{4,6},{5,7},{6,4},{7,5},{8,10},{9,11},{10,... | collective-permute-start | bytes 589832 | tf_op jit(solution)/shard_map/ppermute | solution.py:237
  61.9 12.2 %collective-permute-start.14 = (bf16[48,2048]{1,0:T(8,128)(2,1)S(1)}, bf16[48,2048]{1,0:T(8,128)(2,1)S(1)}, u32[]{:S(2)}, u32[]{:S(2)}) collective-permute-start(bf16[48,2048]{1,0:T(8,128)(2,1)S(1)} %get-tuple-element.50), channel_id=1, source_target_pairs={{0,4},{1,5},{2,6},{3,7},{4,0},{5,1},{6,2},{7,3},{8,12},{9,13},{10,... | collective-permute-start | bytes 589832 | tf_op jit(solution)/shard_map/ppermute | solution.py:237
  69.9 7.6 %collective-permute-start.15 = (bf16[48,2048]{1,0:T(8,128)(2,1)S(1)}, bf16[48,2048]{1,0:T(8,128)(2,1)S(1)}, u32[]{:S(2)}, u32[]{:S(2)}) collective-permute-start(bf16[48,2048]{1,0:T(8,128)(2,1)S(1)} %get-tuple-element.51), channel_id=1, source_target_pairs={{0,6},{1,7},{2,4},{3,5},{4,2},{5,3},{6,0},{7,1},{8,14},{9,15},{10,... | collective-permute-start | bytes 589832 | tf_op jit(solution)/shard_map/ppermute | solution.py:237
  79.5 2.0 %collective-permute-start.19 = (bf16[128,2048]{1,0:T(8,128)(2,1)S(1)}, bf16[128,2048]{1,0:T(8,128)(2,1)S(1)}, u32[]{:S(2)}, u32[]{:S(2)}) collective-permute-start(bf16[128,2048]{1,0:T(8,128)(2,1)S(1)} %get-tuple-element.56), channel_id=1, source_target_pairs={{0,1},{1,0},{2,3},{3,2},{4,5},{5,4},{6,7},{7,6},{8,9},{9,8},{10,11... | collective-permute-start | bytes 1572872 | tf_op jit(solution)/shard_map/ppermute | solution.py:237

commit v8 on v7

--- a/solution.py
+++ b/solution.py
@@ -11,6 +11,7 @@
 SMEM = pl.BlockSpec(memory_space=pltpu.SMEM)
 ANY = pl.BlockSpec(memory_space=pl.ANY)
 MIB = 1024 * 1024
+AHEAD = 1 << 33
 BF16 = jnp.bfloat16
 F32 = jnp.float32
 
@@ -47,13 +48,14 @@
     return run
 
 
-def after(values, *earlier):
+def after(values, *earlier, ahead=0):
     return pl.pallas_call(
         lambda *refs: None,
         out_shape=[shape(*value.shape, value.dtype) for value in values],
         in_specs=[ANY] * (len(values) + len(earlier)),
         out_specs=[ANY] * len(values),
         input_output_aliases={i: i for i in range(len(values))},
+        cost_estimate=pl.CostEstimate(flops=ahead, bytes_accessed=0, transcendentals=0),
         compiler_params=pltpu.CompilerParams(vmem_limit_bytes=MIB),
     )(*values, *earlier)
 
@@ -238,6 +240,7 @@
 
     route = route.reshape(1, tok_rows)
     route_b, tokens_b, cotangent_b = over_rep(route, 1), over_rep(tokens, 1), over_rep(cotangent, 1)
+    route_b = after([route_b], ahead=1<<33)[0]
     joined = jnp.concatenate([w_gate[0], w_up[0], w_down_t[0]], axis=1)
     joined_1, joined_2 = over_own(joined, 1), over_own(joined, 2)
     slot_rows = pltpu.VMEM((slots, model_width), BF16)
@@ -248,7 +251,8 @@
         2,
         [pltpu.VMEM((2 * tok_rows, model_width), BF16)],
     )(rank, host, route, route_b, tokens, tokens_b, cotangent, cotangent_b)
-    near, far_xa, far_xb = over_rep(near, 2), over_rep(far_xa, 4), over_rep(far_xb, 6)
+    far_xa, far_xb = after([over_rep(far_xa, 4), over_rep(far_xb, 6)], ahead=1<<29)
+    near = over_rep(near, 2)
     own_dy, far_a, far_b = call(pack_more_kernel, [shape(block, model_width)] * 3)(pick, cotangent, cotangent_b)
 
     onward = shape(depth // 2 + depth // 4 + slots, depth)
@@ -258,8 +262,8 @@
         1,
         earlier=[own_dy],
     )(own, own_x, near, far_xa, far_xb, joined_1, joined_2)
-    far_a, far_b = after([far_a, far_b], piece_0)
-    far_a, far_b = over_rep(far_a, 4), over_rep(far_b, 6)
+    far_a, far_b = after([far_a, far_b], far_xa, far_xb)
+    far_a, far_b = after([over_rep(far_a, 4), over_rep(far_b, 6)], ahead=AHEAD)
     onward_1, onward_2, piece_3 = over_own(onward_1, 1), over_own(onward_2, 2), over_own(piece_3, 3)
     weights = [joined, joined_1, joined_2]
     acts = call(act_kernel, [shape(slots, 2 * width, F32)], 1)(own, x, *weights)[0]
@@ -273,10 +277,11 @@
         [slot_rows],
         earlier=[piece_3],
     )(own, acts, x, own_dy, near, far_a, far_b, *weights, onward_2, onward_1)
-    returned = [back[0]] + [over_rep(back[k], 2 * k) for k in range(1, parts)]
-    messages = [over_own(message_1, 1), over_own(message_2, 2), over_own(message_3, 3)]
-
-    mine, other = call(unpack_kernel, [shape(tok_rows, model_width)] * 2, 0, [slot_rows], earlier=messages)(
+    far_a, far_b = after([over_rep(back[2], 4), over_rep(back[3], 6)], ahead=1<<33)
+    returned = [back[0], over_rep(after(back[1:2], far_a, far_b)[0], 2), far_a, far_b]
+    messages = after([over_own(message_1, 1), over_own(message_2, 2), over_own(message_3, 3)], ahead=AHEAD)
+
+    mine, other = call(unpack_kernel, [shape(tok_rows, model_width)] * 2, 0, [slot_rows])(
         pick, *returned
     )
     x_grad = mine + over_rep(other, 1)

time: 82.7 us -> 91.9 us (1.11)
  starting transfers between devices: 22.7 us -> 30.2 us
  local copies, waits for them, and re-layouts: 1.73 us -> 3.87 us
  waiting for transfers between devices: 45.5 us -> 44.2 us
    ppermute x12, starting transfers between devices: 11 us -> 19.1 us  [over_rep(): return lax.ppermute(value, 'rep', [(i, i ^ k) for i in range(n_rep)])]
    ppermute x12, waiting for transfers between devices: 40 us -> 34.6 us  [over_rep(): return lax.ppermute(value, 'rep', [(i, i ^ k) for i in range(n_rep)])]
    ppermute x8, waiting for transfers between devices: 5.5 us -> 9.61 us  [over_own(): return lax.ppermute(value, 'own', [(i, i ^ k) for i in range(4)])]
    unnamed x12 -> x22, local copies, waits for them, and re-layouts: 1.73 us -> 3.87 us
  transfers between devices with their start and end apart: 20 -> 20, of which waited for: 10 -> 7; matrix products, arithmetic and copies ran while one was open for 1% -> 1% of each run, Pallas kernels for 6% -> 8%
where the time goes in v8:
time: 91.9 us; the launch traced here: 91.7 us
  waiting for transfers between devices  44.2 us (48%)
  starting transfers between devices  30.2 us (33%)
  Pallas kernels  10.4 us (11%)
  local copies, waits for them, and re-layouts  3.87 us (4%)
  other arithmetic  2.14 us (2%)
    ppermute x12, waiting for transfers between devices, over_rep(): return lax.ppermute(value, 'rep', [(i, i ^ k) for i in range(n_rep)])  34.6 us
    ppermute x12, starting transfers between devices, over_rep(): return lax.ppermute(value, 'rep', [(i, i ^ k) for i in range(n_rep)])  19.1 us
    ppermute x8, starting transfers between devices, over_own(): return lax.ppermute(value, 'own', [(i, i ^ k) for i in range(4)])  11.1 us
    pallas_call x7, Pallas kernels, run(): pl.pallas_call(body, out_shape=outs, in_specs=[SMEM] * scalars + [VMEM] *...  10.4 us
    ppermute x8, waiting for transfers between devices, over_own(): return lax.ppermute(value, 'own', [(i, i ^ k) for i in range(4)])  9.61 us
    unnamed x22, local copies, waits for them, and re-layouts  3.87 us
  transfers between devices with their start and end apart: 20, of which 7 were waited for; matrix products, arithmetic and copies ran while one was open for 1% of the time, Pallas kernels for 8%

profile of v8, /device:TPU:0, one launch (start us, length us, event | category | flops | bytes accessed | tf_op | source)
XLA Modules:
  0.0 91.7 jit_solution(4338304914365169927)
XLA Ops:
  0.6 0.5 collective-permute-start
  1.1 0.0 copy-start
  1.2 1.2 %pad_maximum_fusion.refs_2_.refs_7_ = bf16[512,768]{1,0:T(8,128)(2,1)S(1)} fusion(bf16[512,256]{1,0:T(8,128)(2,1)} %bitcast.11, bf16[512,256]{1,0:T(8,128)(2,1)} %bitcast.12, bf16[512,256]{1,0:T(8,128)(2,1)} %bitcast.13), kind=kLoop, calls=%fused_computation | loop fusion | flops 2359296 | bytes 1572864 | tf_op jit(solution)/shard_map/concatenate | solution.py:244
  2.4 2.6 %collective-permute-start.7 = (bf16[512,768]{1,0:T(8,128)(2,1)S(1)}, bf16[512,768]{1,0:T(8,128)(2,1)S(1)}, u32[]{:S(2)}, u32[]{:S(2)}) collective-permute-start(bf16[512,768]{1,0:T(8,128)(2,1)S(1)} %pad_maximum_fusion.refs_2_.refs_7_), channel_id=1, source_target_pairs={{0,16},{8,24},{16,0},{24,8},{1,17},{9,25},{17,1},{25,9},{2,18},{10... | collective-permute-start | bytes 2359304 | tf_op jit(solution)/shard_map/ppermute | solution.py:236
  5.0 1.5 %collective-permute-start.6 = (bf16[512,768]{1,0:T(8,128)(2,1)S(1)}, bf16[512,768]{1,0:T(8,128)(2,1)S(1)}, u32[]{:S(2)}, u32[]{:S(2)}) collective-permute-start(bf16[512,768]{1,0:T(8,128)(2,1)S(1)} %pad_maximum_fusion.refs_2_.refs_7_), channel_id=1, source_target_pairs={{0,8},{8,0},{16,24},{24,16},{1,9},{9,1},{17,25},{25,17},{2,10},{10... | collective-permute-start | bytes 2359304 | tf_op jit(solution)/shard_map/ppermute | solution.py:236
  6.5 0.0 collective-permute-start.1
  6.5 0.0 copy-done
  6.5 0.5 collective-permute-start.2
  7.0 0.0 collective-permute-done.refs_0_
  7.0 2.4 %collective-permute-done.1.refs_5_ = bf16[128,2048]{1,0:T(8,128)(2,1)} collective-permute-done((bf16[128,2048]{1,0:T(8,128)(2,1)}, bf16[128,2048]{1,0:T(8,128)(2,1)}, u32[]{:S(2)}, u32[]{:S(2)}) %collective-permute-start.1) | collective-permute-done | bytes 524320 | tf_op jit(solution)/shard_map/ppermute | solution.py:239
  9.4 0.0 collective-permute-done.2.refs_7_.refs_2_
  9.4 0.0 copy-done.9
  9.4 0.0 copy-done.10
  9.4 2.6 %shard_map.103 = (bf16[192,256]{1,0:T(8,128)(2,1)S(1)}, bf16[48,2048]{1,0:T(8,128)(2,1)S(1)}, bf16[96,2048]{1,0:T(8,128)(2,1)}, bf16[48,2048]{1,0:T(8,128)(2,1)S(1)}, bf16[48,2048]{1,0:T(8,128)(2,1)S(1)}) custom-call(s32[1]{0:T(128)} %bitcast.refs_0_, s32[8]{0:T(128)S(1)} %copy-done.9, s32[1,128]{1,0:T(1,128)S(1)} %bitcast.10, ...), custom_call_target="tpu_custom_call" | custom-call | bytes 3179556 | tf_op jit(solution)/shard_map/pallas_call | solution.py:38
  12.0 0.7 copy-done.7
  12.7 2.6 %collective-permute-start.4 = (bf16[48,2048]{1,0:T(8,128)(2,1)S(1)}, bf16[48,2048]{1,0:T(8,128)(2,1)S(1)}, u32[]{:S(2)}, u32[]{:S(2)}) collective-permute-start(bf16[48,2048]{1,0:T(8,128)(2,1)S(1)} %get-tuple-element.45), channel_id=1, source_target_pairs={{0,4},{1,5},{2,6},{3,7},{4,0},{5,1},{6,2},{7,3},{8,12},{9,13},{10,... | collective-permute-start | bytes 589832 | tf_op jit(solution)/shard_map/ppermute | solution.py:239
  15.3 1.3 %collective-permute-start.5 = (bf16[48,2048]{1,0:T(8,128)(2,1)S(1)}, bf16[48,2048]{1,0:T(8,128)(2,1)S(1)}, u32[]{:S(2)}, u32[]{:S(2)}) collective-permute-start(bf16[48,2048]{1,0:T(8,128)(2,1)S(1)} %get-tuple-element.46), channel_id=1, source_target_pairs={{0,6},{1,7},{2,4},{3,5},{4,2},{5,3},{6,0},{7,1},{8,14},{9,15},{10,... | collective-permute-start | bytes 589832 | tf_op jit(solution)/shard_map/ppermute | solution.py:239
  16.6 0.2 collective-permute-start.3
  16.9 1.3 %shard_map.105 = (bf16[48,2048]{1,0:T(8,128)(2,1)S(1)}, bf16[48,2048]{1,0:T(8,128)(2,1)}, bf16[48,2048]{1,0:T(8,128)(2,1)}) custom-call(bf16[192,256]{1,0:T(8,128)(2,1)S(1)} %get-tuple-element.42.refs_0_, bf16[128,2048]{1,0:T(8,128)(2,1)S(1)} %copy-done, bf16[128,2048]{1,0:T(8,128)(2,1)S(1)} %collective-permute-done.2.refs_7_.refs_2_), custom_call_target="tpu_custom_call" | custom-call | bytes 1736704 | tf_op jit(solution)/shard_map/pallas_call | solution.py:38
  18.2 11.6 %collective-permute-done.4.refs_0_ = bf16[48,2048]{1,0:T(8,128)(2,1)S(1)} collective-permute-done((bf16[48,2048]{1,0:T(8,128)(2,1)S(1)}, bf16[48,2048]{1,0:T(8,128)(2,1)S(1)}, u32[]{:S(2)}, u32[]{:S(2)}) %collective-permute-start.4) | collective-permute-done | bytes 196640 | tf_op jit(solution)/shard_map/ppermute | solution.py:239
  29.8 0.0 collective-permute-done.5.refs_1_
  29.8 0.0 copy-done.1
  29.8 0.0 copy-start.8
  29.8 0.0 copy-start.2
  29.9 0.6 copy-done.5
  30.5 0.7 copy-done.3
  31.2 6.0 %collective-permute-start.8 = (bf16[48,2048]{1,0:T(8,128)(2,1)}, bf16[48,2048]{1,0:T(8,128)(2,1)S(1)}, u32[]{:S(2)}, u32[]{:S(2)}) collective-permute-start(bf16[48,2048]{1,0:T(8,128)(2,1)} %get-tuple-element.53), channel_id=1, source_target_pairs={{0,4},{1,5},{2,6},{3,7},{4,0},{5,1},{6,2},{7,3},{8,12},{9,13},{10,... | collective-permute-start | bytes 589832 | tf_op jit(solution)/shard_map/ppermute | solution.py:239
  37.2 0.4 collective-permute-start.9
  37.6 0.0 collective-permute-done.7.refs_6_.refs_4_.refs_9_
  37.6 0.0 collective-permute-done.6.refs_5_.refs_3_.refs_8_
  37.6 0.0 collective-permute-done.3.refs_2_.refs_4_
  37.6 0.0 copy-done.8
  37.6 0.0 copy-done.2
  37.6 0.0 copy-start.4
  37.7 0.9 %copy-done.4 = bf16[48,2048]{1,0:T(8,128)(2,1)S(1)} copy-done((bf16[48,2048]{1,0:T(8,128)(2,1)S(1)}, bf16[48,2048]{1,0:T(8,128)(2,1)}, u32[]{:S(2)}) %copy-start.4) | copy-done | bytes 196632
  38.6 0.9 %copy-done.6 = bf16[48,2048]{1,0:T(8,128)(2,1)S(1)} copy-done((bf16[48,2048]{1,0:T(8,128)(2,1)S(1)}, bf16[48,2048]{1,0:T(8,128)(2,1)}, u32[]{:S(2)}) %copy-start.6) | copy-done | bytes 196632
  39.5 1.1 %shard_map.106 = (bf16[192,2048]{1,0:T(8,128)(2,1)S(1)}, bf16[192,512]{1,0:T(8,128)(2,1)S(1)}, bf16[192,512]{1,0:T(8,128)(2,1)S(1)}, bf16[576,512]{1,0:T(8,128)(2,1)S(1)}, bf16[576,512]{1,0:T(8,128)(2,1)S(1)}) custom-call(s32[1]{0:T(128)} %bitcast.2.refs_0_, bf16[48,2048]{1,0:T(8,128)(2,1)S(1)} %copy-done.8, ...), custom_call_target="tpu_custom_call" | custom-call | bytes 4915204 | tf_op jit(solution)/shard_map/pallas_call | solution.py:38
  40.7 0.5 collective-permute-start.12
  41.2 1.5 %collective-permute-start.10 = (bf16[576,512]{1,0:T(8,128)(2,1)S(1)}, bf16[576,512]{1,0:T(8,128)(2,1)S(1)}, u32[]{:S(2)}, u32[]{:S(2)}) collective-permute-start(bf16[576,512]{1,0:T(8,128)(2,1)S(1)} %get-tuple-element.57), channel_id=1, source_target_pairs={{0,16},{8,24},{16,0},{24,8},{1,17},{9,25},{17,1},{25,9},{2,18},{10... | collective-permute-start | bytes 1769480 | tf_op jit(solution)/shard_map/ppermute | solution.py:236
  42.7 1.5 %collective-permute-start.11 = (bf16[576,512]{1,0:T(8,128)(2,1)S(1)}, bf16[576,512]{1,0:T(8,128)(2,1)S(1)}, u32[]{:S(2)}, u32[]{:S(2)}) collective-permute-start(bf16[576,512]{1,0:T(8,128)(2,1)S(1)} %get-tuple-element.58), channel_id=1, source_target_pairs={{0,8},{8,0},{16,24},{24,16},{1,9},{9,1},{17,25},{25,17},{2,10},{10... | collective-permute-start | bytes 1769480 | tf_op jit(solution)/shard_map/ppermute | solution.py:236
  44.2 7.0 %collective-permute-done.8.refs_0_ = bf16[48,2048]{1,0:T(8,128)(2,1)S(1)} collective-permute-done((bf16[48,2048]{1,0:T(8,128)(2,1)}, bf16[48,2048]{1,0:T(8,128)(2,1)S(1)}, u32[]{:S(2)}, u32[]{:S(2)}) %collective-permute-start.8) | collective-permute-done | bytes 196640 | tf_op jit(solution)/shard_map/ppermute | solution.py:239
  51.2 0.0 collective-permute-done.9.refs_1_
  51.2 0.5 shard_map.107.refs_1_
  51.7 0.0 collective-permute-done.12.refs_12_.refs_3_
  51.7 8.2 %collective-permute-done.10.refs_10_.refs_2_ = bf16[576,512]{1,0:T(8,128)(2,1)S(1)} collective-permute-done((bf16[576,512]{1,0:T(8,128)(2,1)S(1)}, bf16[576,512]{1,0:T(8,128)(2,1)S(1)}, u32[]{:S(2)}, u32[]{:S(2)}) %collective-permute-start.10) | collective-permute-done | bytes 589856 | tf_op jit(solution)/shard_map/ppermute | solution.py:236
  59.8 0.0 collective-permute-done.11.refs_11_.refs_1_
  59.8 2.6 %shard_map.110 = (bf16[48,2048]{1,0:T(8,128)(2,1)S(1)}, bf16[48,2048]{1,0:T(8,128)(2,1)S(1)}, bf16[48,2048]{1,0:T(8,128)(2,1)S(1)}, bf16[48,2048]{1,0:T(8,128)(2...) custom-call(s32[1]{0:T(128)} %bitcast.2.refs_0_, ...), custom_call_target="tpu_custom_call" | custom-call | bytes 8585220 | tf_op jit(solution)/shard_map/pallas_call | solution.py:38
  62.5 0.2 collective-permute-start.13
  62.7 3.3 %collective-permute-start.14 = (bf16[48,2048]{1,0:T(8,128)(2,1)S(1)}, bf16[48,2048]{1,0:T(8,128)(2,1)S(1)}, u32[]{:S(2)}, u32[]{:S(2)}) collective-permute-start(bf16[48,2048]{1,0:T(8,128)(2,1)S(1)} %get-tuple-element.63), channel_id=1, source_target_pairs={{0,6},{1,7},{2,4},{3,5},{4,2},{5,3},{6,0},{7,1},{8,14},{9,15},{10,... | collective-permute-start | bytes 589832 | tf_op jit(solution)/shard_map/ppermute | solution.py:239
  66.0 1.2 %collective-permute-start.17 = (bf16[448,512]{1,0:T(8,128)(2,1)S(1)}, bf16[448,512]{1,0:T(8,128)(2,1)S(1)}, u32[]{:S(2)}, u32[]{:S(2)}) collective-permute-start(bf16[448,512]{1,0:T(8,128)(2,1)S(1)} %get-tuple-element.70), channel_id=1, source_target_pairs={{0,8},{8,0},{16,24},{24,16},{1,9},{9,1},{17,25},{25,17},{2,10},{10... | collective-permute-start | bytes 1376264 | tf_op jit(solution)/shard_map/ppermute | solution.py:236
  67.2 0.6 collective-permute-start.18
  67.8 1.7 %collective-permute-start.19 = (bf16[448,512]{1,0:T(8,128)(2,1)S(1)}, bf16[448,512]{1,0:T(8,128)(2,1)S(1)}, u32[]{:S(2)}, u32[]{:S(2)}) collective-permute-start(bf16[448,512]{1,0:T(8,128)(2,1)S(1)} %get-tuple-element.72), channel_id=1, source_target_pairs={{0,24},{8,16},{16,8},{24,0},{1,25},{9,17},{17,9},{25,1},{2,26},{10... | collective-permute-start | bytes 1376264 | tf_op jit(solution)/shard_map/ppermute | solution.py:236
  69.5 9.3 %collective-permute-done.13.refs_0_ = bf16[48,2048]{1,0:T(8,128)(2,1)S(1)} collective-permute-done((bf16[48,2048]{1,0:T(8,128)(2,1)S(1)}, bf16[48,2048]{1,0:T(8,128)(2,1)S(1)}, u32[]{:S(2)}, u32[]{:S(2)}) %collective-permute-start.13) | collective-permute-done | bytes 196640 | tf_op jit(solution)/shard_map/ppermute | solution.py:239
  78.8 0.0 collective-permute-done.14.refs_1_
  78.8 3.9 %collective-permute-start.15 = (bf16[48,2048]{1,0:T(8,128)(2,1)S(1)}, bf16[48,2048]{1,0:T(8,128)(2,1)S(1)}, u32[]{:S(2)}, u32[]{:S(2)}) collective-permute-start(bf16[48,2048]{1,0:T(8,128)(2,1)S(1)} %shard_map.112), channel_id=1, source_target_pairs={{0,2},{1,3},{2,0},{3,1},{4,6},{5,7},{6,4},{7,5},{8,10},{9,11},{10,... | collective-permute-start | bytes 589832 | tf_op jit(solution)/shard_map/ppermute | solution.py:239
  82.7 4.3 %collective-permute-done.15.refs_2_ = bf16[48,2048]{1,0:T(8,128)(2,1)S(1)} collective-permute-done((bf16[48,2048]{1,0:T(8,128)(2,1)S(1)}, bf16[48,2048]{1,0:T(8,128)(2,1)S(1)}, u32[]{:S(2)}, u32[]{:S(2)}) %collective-permute-start.15) | collective-permute-done | bytes 196640 | tf_op jit(solution)/shard_map/ppermute | solution.py:239
  87.0 0.5 shard_map.113
  87.4 0.1 collective-permute-start.16
  87.5 0.0 collective-permute-done.17.refs_0_
  87.5 1.4 %collective-permute-done.18.refs_1_ = bf16[448,512]{1,0:T(8,128)(2,1)S(1)} collective-permute-done((bf16[448,512]{1,0:T(8,128)(2,1)S(1)}, bf16[448,512]{1,0:T(8,128)(2,1)S(1)}, u32[]{:S(2)}, u32[]{:S(2)}) %collective-permute-start.18) | collective-permute-done | bytes 458784 | tf_op jit(solution)/shard_map/ppermute | solution.py:236
  88.9 0.0 collective-permute-done.19.refs_2_
  88.9 1.8 %shard_map.115 = (f32[512,256]{1,0:T(8,128)}, f32[512,256]{1,0:T(8,128)}, f32[512,256]{1,0:T(8,128)}) custom-call(bf16[192,512]{1,0:T(8,128)(2,1)S(1)} %get-tuple-element.68.refs_0_, bf16[576,512]{1,0:T(8,128)(2,1)S(1)} %collective-permute-done.11.refs_11_.refs_1_, bf16[576,512]{1,0:T(8,128)(2,1)S(1)} %collective-permute-done.10.refs_10_.refs_2_, ...), custom_call_target="tpu_custom_call" | custom-call | bytes 5242880 | tf_op jit(solution)/shard_map/pallas_call | solution.py:38
  90.7 0.0 collective-permute-done.16
  90.7 0.9 %add.3 = bf16[128,2048]{1,0:T(8,128)(2,1)} add(bf16[128,2048]{1,0:T(8,128)(2,1)S(1)} %get-tuple-element.66, bf16[128,2048]{1,0:T(8,128)(2,1)S(1)} %collective-permute-done.16) | non-fusion elementwise | flops 262144 | bytes 1572864 | tf_op jit(solution)/shard_map/add | solution.py:287
  (14 shorter events, 0.0 us)
Async XLA Ops:
  0.6 6.4 %collective-permute-start = (s32[1,128]{1,0:T(1,128)}, s32[1,128]{1,0:T(1,128)S(1)}, u32[]{:S(2)}, u32[]{:S(2)}) collective-permute-start(s32[1,128]{1,0:T(1,128)} %bitcast.9), channel_id=1, source_target_pairs={{0,1},{1,0},{2,3},{3,2},{4,5},{5,4},{6,7},{7,6},{8,9},{9,8},{10,11... | collective-permute-start | bytes 1544 | tf_op jit(solution)/shard_map/ppermute | solution.py:239
  1.1 5.3 %copy-start = (bf16[128,2048]{1,0:T(8,128)(2,1)S(1)}, bf16[128,2048]{1,0:T(8,128)(2,1)}, u32[]{:S(2)}) copy-start(bf16[128,2048]{1,0:T(8,128)(2,1)} %refs_1_.3) | copy-start | bytes 1572868
  2.4 35.2 %collective-permute-start.7 = (bf16[512,768]{1,0:T(8,128)(2,1)S(1)}, bf16[512,768]{1,0:T(8,128)(2,1)S(1)}, u32[]{:S(2)}, u32[]{:S(2)}) collective-permute-start(bf16[512,768]{1,0:T(8,128)(2,1)S(1)} %pad_maximum_fusion.refs_2_.refs_7_), channel_id=1, source_target_pairs={{0,16},{8,24},{16,0},{24,8},{1,17},{9,25},{17,1},{25,9},{2,18},{10... | collective-permute-start | bytes 2359304 | tf_op jit(solution)/shard_map/ppermute | solution.py:236
  5.0 32.6 %collective-permute-start.6 = (bf16[512,768]{1,0:T(8,128)(2,1)S(1)}, bf16[512,768]{1,0:T(8,128)(2,1)S(1)}, u32[]{:S(2)}, u32[]{:S(2)}) collective-permute-start(bf16[512,768]{1,0:T(8,128)(2,1)S(1)} %pad_maximum_fusion.refs_2_.refs_7_), channel_id=1, source_target_pairs={{0,8},{8,0},{16,24},{24,16},{1,9},{9,1},{17,25},{25,17},{2,10},{10... | collective-permute-start | bytes 2359304 | tf_op jit(solution)/shard_map/ppermute | solution.py:236
  6.5 2.9 %collective-permute-start.1 = (bf16[128,2048]{1,0:T(8,128)(2,1)}, bf16[128,2048]{1,0:T(8,128)(2,1)}, u32[]{:S(2)}, u32[]{:S(2)}) collective-permute-start(bf16[128,2048]{1,0:T(8,128)(2,1)} %refs_4_.1), channel_id=1, source_target_pairs={{0,1},{1,0},{2,3},{3,2},{4,5},{5,4},{6,7},{7,6},{8,9},{9,8},{10,11... | collective-permute-start | bytes 1572872 | tf_op jit(solution)/shard_map/ppermute | solution.py:239
  6.5 2.9 %collective-permute-start.2 = (bf16[128,2048]{1,0:T(8,128)(2,1)S(1)}, bf16[128,2048]{1,0:T(8,128)(2,1)S(1)}, u32[]{:S(2)}, u32[]{:S(2)}) collective-permute-start(bf16[128,2048]{1,0:T(8,128)(2,1)S(1)} %copy-done), channel_id=1, source_target_pairs={{0,1},{1,0},{2,3},{3,2},{4,5},{5,4},{6,7},{7,6},{8,9},{9,8},{10,11... | collective-permute-start | bytes 1572872 | tf_op jit(solution)/shard_map/ppermute | solution.py:239
  7.0 2.4 %copy-start.9 = (s32[8]{0:T(128)S(1)}, s32[8]{0:T(128)}, u32[]{:S(2)}) copy-start(s32[8]{0:T(128)} %refs_1_.2) | copy-start | bytes 100
  7.0 2.4 %copy-start.10 = (s32[128,1]{0,1:T(1,128)S(1)}, s32[128,1]{0,1:T(1,128)}, u32[]{:S(2)}) copy-start(s32[128,1]{0,1:T(1,128)} %param.9) | copy-start | bytes 1540
  12.0 0.7 copy-start.7
  12.7 17.1 %collective-permute-start.4 = (bf16[48,2048]{1,0:T(8,128)(2,1)S(1)}, bf16[48,2048]{1,0:T(8,128)(2,1)S(1)}, u32[]{:S(2)}, u32[]{:S(2)}) collective-permute-start(bf16[48,2048]{1,0:T(8,128)(2,1)S(1)} %get-tuple-element.45), channel_id=1, source_target_pairs={{0,4},{1,5},{2,6},{3,7},{4,0},{5,1},{6,2},{7,3},{8,12},{9,13},{10,... | collective-permute-start | bytes 589832 | tf_op jit(solution)/shard_map/ppermute | solution.py:239
  15.3 14.5 %collective-permute-start.5 = (bf16[48,2048]{1,0:T(8,128)(2,1)S(1)}, bf16[48,2048]{1,0:T(8,128)(2,1)S(1)}, u32[]{:S(2)}, u32[]{:S(2)}) collective-permute-start(bf16[48,2048]{1,0:T(8,128)(2,1)S(1)} %get-tuple-element.46), channel_id=1, source_target_pairs={{0,6},{1,7},{2,4},{3,5},{4,2},{5,3},{6,0},{7,1},{8,14},{9,15},{10,... | collective-permute-start | bytes 589832 | tf_op jit(solution)/shard_map/ppermute | solution.py:239
  16.6 21.0 %collective-permute-start.3 = (bf16[96,2048]{1,0:T(8,128)(2,1)}, bf16[96,2048]{1,0:T(8,128)(2,1)}, u32[]{:S(2)}, u32[]{:S(2)}) collective-permute-start(bf16[96,2048]{1,0:T(8,128)(2,1)} %get-tuple-element.44), channel_id=1, source_target_pairs={{0,2},{1,3},{2,0},{3,1},{4,6},{5,7},{6,4},{7,5},{8,10},{9,11},{10,... | collective-permute-start | bytes 1179656 | tf_op jit(solution)/shard_map/ppermute | solution.py:239
  18.2 11.6 %copy-start.1 = (bf16[48,2048]{1,0:T(8,128)(2,1)}, bf16[48,2048]{1,0:T(8,128)(2,1)S(1)}, u32[]{:S(2)}) copy-start(bf16[48,2048]{1,0:T(8,128)(2,1)S(1)} %get-tuple-element.49.refs_7_.refs_3_) | copy-start | bytes 589828
  29.8 0.7 copy-start.5
  29.8 7.8 %copy-start.8 = (bf16[48,2048]{1,0:T(8,128)(2,1)S(1)}, bf16[48,2048]{1,0:T(8,128)(2,1)}, u32[]{:S(2)}) copy-start(bf16[48,2048]{1,0:T(8,128)(2,1)} %copy-done.7) | copy-start | bytes 589828
  29.8 7.8 %copy-start.2 = (bf16[48,2048]{1,0:T(8,128)(2,1)S(1)}, bf16[48,2048]{1,0:T(8,128)(2,1)}, u32[]{:S(2)}) copy-start(bf16[48,2048]{1,0:T(8,128)(2,1)} %copy-done.1) | copy-start | bytes 589828
  30.5 0.7 copy-start.3
  31.2 20.0 %collective-permute-start.8 = (bf16[48,2048]{1,0:T(8,128)(2,1)}, bf16[48,2048]{1,0:T(8,128)(2,1)S(1)}, u32[]{:S(2)}, u32[]{:S(2)}) collective-permute-start(bf16[48,2048]{1,0:T(8,128)(2,1)} %get-tuple-element.53), channel_id=1, source_target_pairs={{0,4},{1,5},{2,6},{3,7},{4,0},{5,1},{6,2},{7,3},{8,12},{9,13},{10,... | collective-permute-start | bytes 589832 | tf_op jit(solution)/shard_map/ppermute | solution.py:239
  37.2 14.0 %collective-permute-start.9 = (bf16[48,2048]{1,0:T(8,128)(2,1)}, bf16[48,2048]{1,0:T(8,128)(2,1)S(1)}, u32[]{:S(2)}, u32[]{:S(2)}) collective-permute-start(bf16[48,2048]{1,0:T(8,128)(2,1)} %get-tuple-element.54), channel_id=1, source_target_pairs={{0,6},{1,7},{2,4},{3,5},{4,2},{5,3},{6,0},{7,1},{8,14},{9,15},{10,... | collective-permute-start | bytes 589832 | tf_op jit(solution)/shard_map/ppermute | solution.py:239
  37.6 0.9 %copy-start.4 = (bf16[48,2048]{1,0:T(8,128)(2,1)S(1)}, bf16[48,2048]{1,0:T(8,128)(2,1)}, u32[]{:S(2)}) copy-start(bf16[48,2048]{1,0:T(8,128)(2,1)} %copy-done.3) | copy-start | bytes 589828
  38.6 0.9 %copy-start.6 = (bf16[48,2048]{1,0:T(8,128)(2,1)S(1)}, bf16[48,2048]{1,0:T(8,128)(2,1)}, u32[]{:S(2)}) copy-start(bf16[48,2048]{1,0:T(8,128)(2,1)} %copy-done.5) | copy-start | bytes 589828
  40.7 11.0 %collective-permute-start.12 = (bf16[192,512]{1,0:T(8,128)(2,1)S(1)}, bf16[192,512]{1,0:T(8,128)(2,1)S(1)}, u32[]{:S(2)}, u32[]{:S(2)}) collective-permute-start(bf16[192,512]{1,0:T(8,128)(2,1)S(1)} %get-tuple-element.59), channel_id=1, source_target_pairs={{0,24},{8,16},{16,8},{24,0},{1,25},{9,17},{17,9},{25,1},{2,26},{10... | collective-permute-start | bytes 589832 | tf_op jit(solution)/shard_map/ppermute | solution.py:236
  41.2 18.6 %collective-permute-start.10 = (bf16[576,512]{1,0:T(8,128)(2,1)S(1)}, bf16[576,512]{1,0:T(8,128)(2,1)S(1)}, u32[]{:S(2)}, u32[]{:S(2)}) collective-permute-start(bf16[576,512]{1,0:T(8,128)(2,1)S(1)} %get-tuple-element.57), channel_id=1, source_target_pairs={{0,16},{8,24},{16,0},{24,8},{1,17},{9,25},{17,1},{25,9},{2,18},{10... | collective-permute-start | bytes 1769480 | tf_op jit(solution)/shard_map/ppermute | solution.py:236
  42.7 17.1 %collective-permute-start.11 = (bf16[576,512]{1,0:T(8,128)(2,1)S(1)}, bf16[576,512]{1,0:T(8,128)(2,1)S(1)}, u32[]{:S(2)}, u32[]{:S(2)}) collective-permute-start(bf16[576,512]{1,0:T(8,128)(2,1)S(1)} %get-tuple-element.58), channel_id=1, source_target_pairs={{0,8},{8,0},{16,24},{24,16},{1,9},{9,1},{17,25},{25,17},{2,10},{10... | collective-permute-start | bytes 1769480 | tf_op jit(solution)/shard_map/ppermute | solution.py:236
  62.5 16.3 %collective-permute-start.13 = (bf16[48,2048]{1,0:T(8,128)(2,1)S(1)}, bf16[48,2048]{1,0:T(8,128)(2,1)S(1)}, u32[]{:S(2)}, u32[]{:S(2)}) collective-permute-start(bf16[48,2048]{1,0:T(8,128)(2,1)S(1)} %get-tuple-element.62), channel_id=1, source_target_pairs={{0,4},{1,5},{2,6},{3,7},{4,0},{5,1},{6,2},{7,3},{8,12},{9,13},{10,... | collective-permute-start | bytes 589832 | tf_op jit(solution)/shard_map/ppermute | solution.py:239
  62.7 16.2 %collective-permute-start.14 = (bf16[48,2048]{1,0:T(8,128)(2,1)S(1)}, bf16[48,2048]{1,0:T(8,128)(2,1)S(1)}, u32[]{:S(2)}, u32[]{:S(2)}) collective-permute-start(bf16[48,2048]{1,0:T(8,128)(2,1)S(1)} %get-tuple-element.63), channel_id=1, source_target_pairs={{0,6},{1,7},{2,4},{3,5},{4,2},{5,3},{6,0},{7,1},{8,14},{9,15},{10,... | collective-permute-start | bytes 589832 | tf_op jit(solution)/shard_map/ppermute | solution.py:239
  66.0 21.5 %collective-permute-start.17 = (bf16[448,512]{1,0:T(8,128)(2,1)S(1)}, bf16[448,512]{1,0:T(8,128)(2,1)S(1)}, u32[]{:S(2)}, u32[]{:S(2)}) collective-permute-start(bf16[448,512]{1,0:T(8,128)(2,1)S(1)} %get-tuple-element.70), channel_id=1, source_target_pairs={{0,8},{8,0},{16,24},{24,16},{1,9},{9,1},{17,25},{25,17},{2,10},{10... | collective-permute-start | bytes 1376264 | tf_op jit(solution)/shard_map/ppermute | solution.py:236
  67.2 21.7 %collective-permute-start.18 = (bf16[448,512]{1,0:T(8,128)(2,1)S(1)}, bf16[448,512]{1,0:T(8,128)(2,1)S(1)}, u32[]{:S(2)}, u32[]{:S(2)}) collective-permute-start(bf16[448,512]{1,0:T(8,128)(2,1)S(1)} %get-tuple-element.71), channel_id=1, source_target_pairs={{0,16},{8,24},{16,0},{24,8},{1,17},{9,25},{17,1},{25,9},{2,18},{10... | collective-permute-start | bytes 1376264 | tf_op jit(solution)/shard_map/ppermute | solution.py:236
  67.8 21.1 %collective-permute-start.19 = (bf16[448,512]{1,0:T(8,128)(2,1)S(1)}, bf16[448,512]{1,0:T(8,128)(2,1)S(1)}, u32[]{:S(2)}, u32[]{:S(2)}) collective-permute-start(bf16[448,512]{1,0:T(8,128)(2,1)S(1)} %get-tuple-element.72), channel_id=1, source_target_pairs={{0,24},{8,16},{16,8},{24,0},{1,25},{9,17},{17,9},{25,1},{2,26},{10... | collective-permute-start | bytes 1376264 | tf_op jit(solution)/shard_map/ppermute | solution.py:236
  78.8 8.1 %collective-permute-start.15 = (bf16[48,2048]{1,0:T(8,128)(2,1)S(1)}, bf16[48,2048]{1,0:T(8,128)(2,1)S(1)}, u32[]{:S(2)}, u32[]{:S(2)}) collective-permute-start(bf16[48,2048]{1,0:T(8,128)(2,1)S(1)} %shard_map.112), channel_id=1, source_target_pairs={{0,2},{1,3},{2,0},{3,1},{4,6},{5,7},{6,4},{7,5},{8,10},{9,11},{10,... | collective-permute-start | bytes 589832 | tf_op jit(solution)/shard_map/ppermute | solution.py:239
  87.4 3.3 %collective-permute-start.16 = (bf16[128,2048]{1,0:T(8,128)(2,1)S(1)}, bf16[128,2048]{1,0:T(8,128)(2,1)S(1)}, u32[]{:S(2)}, u32[]{:S(2)}) collective-permute-start(bf16[128,2048]{1,0:T(8,128)(2,1)S(1)} %get-tuple-element.67), channel_id=1, source_target_pairs={{0,1},{1,0},{2,3},{3,2},{4,5},{5,4},{6,7},{7,6},{8,9},{9,8},{10,11... | collective-permute-start | bytes 1572872 | tf_op jit(solution)/shard_map/ppermute | solution.py:239

commit v9 on v8

--- a/solution.py
+++ b/solution.py
@@ -240,7 +240,6 @@
 
     route = route.reshape(1, tok_rows)
     route_b, tokens_b, cotangent_b = over_rep(route, 1), over_rep(tokens, 1), over_rep(cotangent, 1)
-    route_b = after([route_b], ahead=1<<33)[0]
     joined = jnp.concatenate([w_gate[0], w_up[0], w_down_t[0]], axis=1)
     joined_1, joined_2 = over_own(joined, 1), over_own(joined, 2)
     slot_rows = pltpu.VMEM((slots, model_width), BF16)
@@ -251,7 +250,7 @@
         2,
         [pltpu.VMEM((2 * tok_rows, model_width), BF16)],
     )(rank, host, route, route_b, tokens, tokens_b, cotangent, cotangent_b)
-    far_xa, far_xb = after([over_rep(far_xa, 4), over_rep(far_xb, 6)], ahead=1<<29)
+    far_xa, far_xb = after([over_rep(far_xa, 4), over_rep(far_xb, 6)], ahead=1 << 31)
     near = over_rep(near, 2)
     own_dy, far_a, far_b = call(pack_more_kernel, [shape(block, model_width)] * 3)(pick, cotangent, cotangent_b)
 
@@ -262,7 +261,7 @@
         1,
         earlier=[own_dy],
     )(own, own_x, near, far_xa, far_xb, joined_1, joined_2)
-    far_a, far_b = after([far_a, far_b], far_xa, far_xb)
+    far_a, far_b = after([far_a, far_b], piece_0)
     far_a, far_b = after([over_rep(far_a, 4), over_rep(far_b, 6)], ahead=AHEAD)
     onward_1, onward_2, piece_3 = over_own(onward_1, 1), over_own(onward_2, 2), over_own(piece_3, 3)
     weights = [joined, joined_1, joined_2]
@@ -277,8 +276,9 @@
         [slot_rows],
         earlier=[piece_3],
     )(own, acts, x, own_dy, near, far_a, far_b, *weights, onward_2, onward_1)
-    far_a, far_b = after([over_rep(back[2], 4), over_rep(back[3], 6)], ahead=1<<33)
-    returned = [back[0], over_rep(after(back[1:2], far_a, far_b)[0], 2), far_a, far_b]
+    returned = [over_rep(back[1], 2), over_rep(back[2], 4)]
+    last = over_rep(after(back[3:], returned[0])[0], 6)
+    returned = [back[0], *after(returned, ahead=AHEAD), last]
     messages = after([over_own(message_1, 1), over_own(message_2, 2), over_own(message_3, 3)], ahead=AHEAD)
 
     mine, other = call(unpack_kernel, [shape(tok_rows, model_width)] * 2, 0, [slot_rows])(

time: 91.9 us -> 89.1 us (0.970)
  waiting for transfers between devices: 44.2 us -> 50 us
  starting transfers between devices: 30.2 us -> 24.5 us
  local copies, waits for them, and re-layouts: 3.87 us -> 1.73 us
    ppermute x12, starting transfers between devices: 19.1 us -> 13.1 us  [over_rep(): return lax.ppermute(value, 'rep', [(i, i ^ k) for i in range(n_rep)])]
    ppermute x8, waiting for transfers between devices: 9.61 us -> 13.3 us  [over_own(): return lax.ppermute(value, 'own', [(i, i ^ k) for i in range(4)])]
    unnamed x22 -> x12, local copies, waits for them, and re-layouts: 3.87 us -> 1.73 us
    ppermute x12, waiting for transfers between devices: 34.6 us -> 36.6 us  [over_rep(): return lax.ppermute(value, 'rep', [(i, i ^ k) for i in range(n_rep)])]
  transfers between devices with their start and end apart: 20 -> 20, of which waited for: 7 -> 8; matrix products, arithmetic and copies ran while one was open for 1% -> 1% of each run, Pallas kernels for 8% -> 6%
where the time goes in v9:
time: 89.1 us; the launch traced here: 88.8 us
  waiting for transfers between devices  50 us (56%)
  starting transfers between devices  24.5 us (27%)
  Pallas kernels  9.63 us (11%)
  other arithmetic  2.14 us (2%)
  local copies, waits for them, and re-layouts  1.73 us (2%)
    ppermute x12, waiting for transfers between devices, over_rep(): return lax.ppermute(value, 'rep', [(i, i ^ k) for i in range(n_rep)])  36.6 us
    ppermute x8, waiting for transfers between devices, over_own(): return lax.ppermute(value, 'own', [(i, i ^ k) for i in range(4)])  13.3 us
    ppermute x12, starting transfers between devices, over_rep(): return lax.ppermute(value, 'rep', [(i, i ^ k) for i in range(n_rep)])  13.1 us
    ppermute x8, starting transfers between devices, over_own(): return lax.ppermute(value, 'own', [(i, i ^ k) for i in range(4)])  11.5 us
    pallas_call x7, Pallas kernels, run(): pl.pallas_call(body, out_shape=outs, in_specs=[SMEM] * scalars + [VMEM] *...  9.63 us
  transfers between devices with their start and end apart: 20, of which 8 were waited for; matrix products, arithmetic and copies ran while one was open for 1% of the time, Pallas kernels for 6%

profile of v9, /device:TPU:0, one launch (start us, length us, event | category | flops | bytes accessed | tf_op | source)
XLA Modules:
  0.0 88.8 jit_solution(3226148750222613798)
XLA Ops:
  0.6 0.5 collective-permute-start.1
  1.2 0.1 collective-permute-start.2
  1.2 0.0 copy-start.5
  1.2 0.0 copy-start
  1.2 0.0 copy-start.4
  1.2 1.2 %pad_maximum_fusion.refs_2_.refs_7_ = bf16[512,768]{1,0:T(8,128)(2,1)S(1)} fusion(bf16[512,256]{1,0:T(8,128)(2,1)} %bitcast.11, bf16[512,256]{1,0:T(8,128)(2,1)} %bitcast.12, bf16[512,256]{1,0:T(8,128)(2,1)} %bitcast.13), kind=kLoop, calls=%fused_computation | loop fusion | flops 2359296 | bytes 1572864 | tf_op jit(solution)/shard_map/concatenate | solution.py:243
  2.5 3.0 %collective-permute-start.7 = (bf16[512,768]{1,0:T(8,128)(2,1)S(1)}, bf16[512,768]{1,0:T(8,128)(2,1)S(1)}, u32[]{:S(2)}, u32[]{:S(2)}) collective-permute-start(bf16[512,768]{1,0:T(8,128)(2,1)S(1)} %pad_maximum_fusion.refs_2_.refs_7_), channel_id=1, source_target_pairs={{0,16},{8,24},{16,0},{24,8},{1,17},{9,25},{17,1},{25,9},{2,18},{10... | collective-permute-start | bytes 2359304 | tf_op jit(solution)/shard_map/ppermute | solution.py:236
  5.5 1.5 %collective-permute-start.6 = (bf16[512,768]{1,0:T(8,128)(2,1)S(1)}, bf16[512,768]{1,0:T(8,128)(2,1)S(1)}, u32[]{:S(2)}, u32[]{:S(2)}) collective-permute-start(bf16[512,768]{1,0:T(8,128)(2,1)S(1)} %pad_maximum_fusion.refs_2_.refs_7_), channel_id=1, source_target_pairs={{0,8},{8,0},{16,24},{24,16},{1,9},{9,1},{17,25},{25,17},{2,10},{10... | collective-permute-start | bytes 2359304 | tf_op jit(solution)/shard_map/ppermute | solution.py:236
  7.0 0.0 copy-done.5
  7.0 0.0 collective-permute-start
  7.0 1.1 %collective-permute-done.refs_3_ = s32[1,128]{1,0:T(1,128)S(1)} collective-permute-done((s32[1,128]{1,0:T(1,128)S(1)}, s32[1,128]{1,0:T(1,128)S(1)}, u32[]{:S(2)}, u32[]{:S(2)}) %collective-permute-start) | collective-permute-done | bytes 544 | tf_op jit(solution)/shard_map/ppermute | solution.py:239
  8.1 0.0 collective-permute-done.1.refs_5_
  8.1 0.0 collective-permute-done.2.refs_7_.refs_2_
  8.1 0.0 copy-done
  8.1 0.0 copy-done.4
  8.1 0.0 copy-start.1
  8.1 1.0 %copy-done.1 = bf16[128,2048]{1,0:T(8,128)(2,1)S(1)} copy-done((bf16[128,2048]{1,0:T(8,128)(2,1)S(1)}, bf16[128,2048]{1,0:T(8,128)(2,1)}, u32[]{:S(2)}) %copy-start.1) | copy-done | bytes 524312
  9.2 2.4 %shard_map.102 = (bf16[192,256]{1,0:T(8,128)(2,1)S(1)}, bf16[48,2048]{1,0:T(8,128)(2,1)S(1)}, bf16[96,2048]{1,0:T(8,128)(2,1)}, bf16[48,2048]{1,0:T(8,128)(2,1)}, bf16[48,2048]{1,0:T(8,128)(2,1)}) custom-call(s32[1]{0:T(128)} %bitcast.refs_0_, s32[8]{0:T(128)S(1)} %copy-done.4, s32[1,128]{1,0:T(1,128)S(1)} %bitcast.10, ...), custom_call_target="tpu_custom_call" | custom-call | bytes 3179556 | tf_op jit(solution)/shard_map/pallas_call | solution.py:38
  11.6 0.0 copy-start.2
  11.6 0.7 copy-done.2
  12.3 2.6 %collective-permute-start.4 = (bf16[48,2048]{1,0:T(8,128)(2,1)}, bf16[48,2048]{1,0:T(8,128)(2,1)}, u32[]{:S(2)}, u32[]{:S(2)}) collective-permute-start(bf16[48,2048]{1,0:T(8,128)(2,1)} %get-tuple-element.45), channel_id=1, source_target_pairs={{0,4},{1,5},{2,6},{3,7},{4,0},{5,1},{6,2},{7,3},{8,12},{9,13},{10,... | collective-permute-start | bytes 589832 | tf_op jit(solution)/shard_map/ppermute | solution.py:239
  14.9 1.4 %collective-permute-start.5 = (bf16[48,2048]{1,0:T(8,128)(2,1)}, bf16[48,2048]{1,0:T(8,128)(2,1)}, u32[]{:S(2)}, u32[]{:S(2)}) collective-permute-start(bf16[48,2048]{1,0:T(8,128)(2,1)} %get-tuple-element.46), channel_id=1, source_target_pairs={{0,6},{1,7},{2,4},{3,5},{4,2},{5,3},{6,0},{7,1},{8,14},{9,15},{10,... | collective-permute-start | bytes 589832 | tf_op jit(solution)/shard_map/ppermute | solution.py:239
  16.2 0.2 collective-permute-start.3
  16.4 0.5 shard_map.104
  17.0 0.0 copy-start.3
  17.0 12.7 %collective-permute-done.4.refs_0_ = bf16[48,2048]{1,0:T(8,128)(2,1)} collective-permute-done((bf16[48,2048]{1,0:T(8,128)(2,1)}, bf16[48,2048]{1,0:T(8,128)(2,1)}, u32[]{:S(2)}, u32[]{:S(2)}) %collective-permute-start.4) | collective-permute-done | bytes 196640 | tf_op jit(solution)/shard_map/ppermute | solution.py:239
  29.7 0.0 collective-permute-done.5.refs_1_
  29.7 0.0 collective-permute-done.7.refs_6_.refs_4_.refs_9_
  29.7 0.0 collective-permute-done.6.refs_5_.refs_3_.refs_8_
  29.7 4.8 %collective-permute-done.3.refs_2_.refs_4_ = bf16[96,2048]{1,0:T(8,128)(2,1)} collective-permute-done((bf16[96,2048]{1,0:T(8,128)(2,1)}, bf16[96,2048]{1,0:T(8,128)(2,1)}, u32[]{:S(2)}, u32[]{:S(2)}) %collective-permute-start.3) | collective-permute-done | bytes 393248 | tf_op jit(solution)/shard_map/ppermute | solution.py:239
  34.5 0.0 copy-done.3
  34.5 1.3 %shard_map.105 = (bf16[192,2048]{1,0:T(8,128)(2,1)S(1)}, bf16[192,512]{1,0:T(8,128)(2,1)S(1)}, bf16[192,512]{1,0:T(8,128)(2,1)S(1)}, bf16[576,512]{1,0:T(8,128)(2,1)S(1)}, bf16[576,512]{1,0:T(8,128)(2,1)S(1)}) custom-call(s32[1]{0:T(128)} %bitcast.2.refs_0_, bf16[48,2048]{1,0:T(8,128)(2,1)S(1)} %copy-done.3, ...), custom_call_target="tpu_custom_call" | custom-call | bytes 4915204 | tf_op jit(solution)/shard_map/pallas_call | solution.py:38
  35.8 1.6 %collective-permute-start.8 = (bf16[48,2048]{1,0:T(8,128)(2,1)S(1)}, bf16[48,2048]{1,0:T(8,128)(2,1)S(1)}, u32[]{:S(2)}, u32[]{:S(2)}) collective-permute-start(bf16[48,2048]{1,0:T(8,128)(2,1)S(1)} %get-tuple-element.54), channel_id=1, source_target_pairs={{0,4},{1,5},{2,6},{3,7},{4,0},{5,1},{6,2},{7,3},{8,12},{9,13},{10,... | collective-permute-start | bytes 589832 | tf_op jit(solution)/shard_map/ppermute | solution.py:239
  37.5 2.0 %collective-permute-start.9 = (bf16[48,2048]{1,0:T(8,128)(2,1)S(1)}, bf16[48,2048]{1,0:T(8,128)(2,1)S(1)}, u32[]{:S(2)}, u32[]{:S(2)}) collective-permute-start(bf16[48,2048]{1,0:T(8,128)(2,1)S(1)} %get-tuple-element.55), channel_id=1, source_target_pairs={{0,6},{1,7},{2,4},{3,5},{4,2},{5,3},{6,0},{7,1},{8,14},{9,15},{10,... | collective-permute-start | bytes 589832 | tf_op jit(solution)/shard_map/ppermute | solution.py:239
  39.5 0.5 collective-permute-start.12
  39.9 1.5 %collective-permute-start.10 = (bf16[576,512]{1,0:T(8,128)(2,1)S(1)}, bf16[576,512]{1,0:T(8,128)(2,1)S(1)}, u32[]{:S(2)}, u32[]{:S(2)}) collective-permute-start(bf16[576,512]{1,0:T(8,128)(2,1)S(1)} %get-tuple-element.58), channel_id=1, source_target_pairs={{0,16},{8,24},{16,0},{24,8},{1,17},{9,25},{17,1},{25,9},{2,18},{10... | collective-permute-start | bytes 1769480 | tf_op jit(solution)/shard_map/ppermute | solution.py:236
  41.5 1.5 %collective-permute-start.11 = (bf16[576,512]{1,0:T(8,128)(2,1)S(1)}, bf16[576,512]{1,0:T(8,128)(2,1)S(1)}, u32[]{:S(2)}, u32[]{:S(2)}) collective-permute-start(bf16[576,512]{1,0:T(8,128)(2,1)S(1)} %get-tuple-element.59), channel_id=1, source_target_pairs={{0,8},{8,0},{16,24},{24,16},{1,9},{9,1},{17,25},{25,17},{2,10},{10... | collective-permute-start | bytes 1769480 | tf_op jit(solution)/shard_map/ppermute | solution.py:236
  43.0 0.5 shard_map.106.refs_1_
  43.4 8.3 %collective-permute-done.8.refs_0_ = bf16[48,2048]{1,0:T(8,128)(2,1)S(1)} collective-permute-done((bf16[48,2048]{1,0:T(8,128)(2,1)S(1)}, bf16[48,2048]{1,0:T(8,128)(2,1)S(1)}, u32[]{:S(2)}, u32[]{:S(2)}) %collective-permute-start.8) | collective-permute-done | bytes 196640 | tf_op jit(solution)/shard_map/ppermute | solution.py:239
  51.8 0.0 collective-permute-done.9.refs_1_
  51.8 0.0 collective-permute-done.12.refs_12_.refs_3_
  51.8 5.8 %collective-permute-done.10.refs_10_.refs_2_ = bf16[576,512]{1,0:T(8,128)(2,1)S(1)} collective-permute-done((bf16[576,512]{1,0:T(8,128)(2,1)S(1)}, bf16[576,512]{1,0:T(8,128)(2,1)S(1)}, u32[]{:S(2)}, u32[]{:S(2)}) %collective-permute-start.10) | collective-permute-done | bytes 589856 | tf_op jit(solution)/shard_map/ppermute | solution.py:236
  57.6 0.0 collective-permute-done.11.refs_11_.refs_1_
  57.6 2.6 %shard_map.109 = (bf16[48,2048]{1,0:T(8,128)(2,1)S(1)}, bf16[48,2048]{1,0:T(8,128)(2,1)S(1)}, bf16[48,2048]{1,0:T(8,128)(2,1)S(1)}, bf16[48,2048]{1,0:T(8,128)(2...) custom-call(s32[1]{0:T(128)} %bitcast.2.refs_0_, ...), custom_call_target="tpu_custom_call" | custom-call | bytes 8585220 | tf_op jit(solution)/shard_map/pallas_call | solution.py:38
  60.2 0.6 collective-permute-start.13
  60.7 2.6 %collective-permute-start.14 = (bf16[48,2048]{1,0:T(8,128)(2,1)S(1)}, bf16[48,2048]{1,0:T(8,128)(2,1)S(1)}, u32[]{:S(2)}, u32[]{:S(2)}) collective-permute-start(bf16[48,2048]{1,0:T(8,128)(2,1)S(1)} %get-tuple-element.63), channel_id=1, source_target_pairs={{0,4},{1,5},{2,6},{3,7},{4,0},{5,1},{6,2},{7,3},{8,12},{9,13},{10,... | collective-permute-start | bytes 589832 | tf_op jit(solution)/shard_map/ppermute | solution.py:239
  63.4 1.2 %collective-permute-start.17 = (bf16[448,512]{1,0:T(8,128)(2,1)S(1)}, bf16[448,512]{1,0:T(8,128)(2,1)S(1)}, u32[]{:S(2)}, u32[]{:S(2)}) collective-permute-start(bf16[448,512]{1,0:T(8,128)(2,1)S(1)} %get-tuple-element.70), channel_id=1, source_target_pairs={{0,8},{8,0},{16,24},{24,16},{1,9},{9,1},{17,25},{25,17},{2,10},{10... | collective-permute-start | bytes 1376264 | tf_op jit(solution)/shard_map/ppermute | solution.py:236
  64.6 0.6 collective-permute-start.18
  65.2 1.6 %collective-permute-start.19 = (bf16[448,512]{1,0:T(8,128)(2,1)S(1)}, bf16[448,512]{1,0:T(8,128)(2,1)S(1)}, u32[]{:S(2)}, u32[]{:S(2)}) collective-permute-start(bf16[448,512]{1,0:T(8,128)(2,1)S(1)} %get-tuple-element.72), channel_id=1, source_target_pairs={{0,24},{8,16},{16,8},{24,0},{1,25},{9,17},{17,9},{25,1},{2,26},{10... | collective-permute-start | bytes 1376264 | tf_op jit(solution)/shard_map/ppermute | solution.py:236
  66.9 3.5 %collective-permute-done.13.refs_0_.refs_1_ = bf16[48,2048]{1,0:T(8,128)(2,1)S(1)} collective-permute-done((bf16[48,2048]{1,0:T(8,128)(2,1)S(1)}, bf16[48,2048]{1,0:T(8,128)(2,1)S(1)}, u32[]{:S(2)}, u32[]{:S(2)}) %collective-permute-start.13) | collective-permute-done | bytes 196640 | tf_op jit(solution)/shard_map/ppermute | solution.py:239
  70.4 1.4 %collective-permute-start.15 = (bf16[48,2048]{1,0:T(8,128)(2,1)S(1)}, bf16[48,2048]{1,0:T(8,128)(2,1)S(1)}, u32[]{:S(2)}, u32[]{:S(2)}) collective-permute-start(bf16[48,2048]{1,0:T(8,128)(2,1)S(1)} %shard_map.111), channel_id=1, source_target_pairs={{0,6},{1,7},{2,4},{3,5},{4,2},{5,3},{6,0},{7,1},{8,14},{9,15},{10,... | collective-permute-start | bytes 589832 | tf_op jit(solution)/shard_map/ppermute | solution.py:239
  71.8 0.0 collective-permute-done.14.refs_1_
  71.8 6.1 %collective-permute-done.15.refs_4_ = bf16[48,2048]{1,0:T(8,128)(2,1)S(1)} collective-permute-done((bf16[48,2048]{1,0:T(8,128)(2,1)S(1)}, bf16[48,2048]{1,0:T(8,128)(2,1)S(1)}, u32[]{:S(2)}, u32[]{:S(2)}) %collective-permute-start.15) | collective-permute-done | bytes 196640 | tf_op jit(solution)/shard_map/ppermute | solution.py:239
  77.9 0.5 shard_map.112
  78.4 0.1 collective-permute-start.16
  78.5 0.0 collective-permute-done.17.refs_0_
  78.5 7.6 %collective-permute-done.18.refs_1_ = bf16[448,512]{1,0:T(8,128)(2,1)S(1)} collective-permute-done((bf16[448,512]{1,0:T(8,128)(2,1)S(1)}, bf16[448,512]{1,0:T(8,128)(2,1)S(1)}, u32[]{:S(2)}, u32[]{:S(2)}) %collective-permute-start.18) | collective-permute-done | bytes 458784 | tf_op jit(solution)/shard_map/ppermute | solution.py:236
  86.1 0.0 collective-permute-done.19.refs_2_
  86.1 1.8 %shard_map.114 = (f32[512,256]{1,0:T(8,128)}, f32[512,256]{1,0:T(8,128)}, f32[512,256]{1,0:T(8,128)}) custom-call(bf16[192,512]{1,0:T(8,128)(2,1)S(1)} %get-tuple-element.53.refs_2_.refs_0_, bf16[576,512]{1,0:T(8,128)(2,1)S(1)} %collective-permute-done.11.refs_11_.refs_1_, bf16[576,512]{1,0:T(8,128)(2,1)S(1)} %collective-permute-done.10.refs_10_.refs_2_, ...), custom_call_target="tpu_custom_call" | custom-call | bytes 5242880 | tf_op jit(solution)/shard_map/pallas_call | solution.py:38
  87.8 0.0 collective-permute-done.16
  87.9 0.9 %add.3 = bf16[128,2048]{1,0:T(8,128)(2,1)} add(bf16[128,2048]{1,0:T(8,128)(2,1)S(1)} %get-tuple-element.67, bf16[128,2048]{1,0:T(8,128)(2,1)S(1)} %collective-permute-done.16) | non-fusion elementwise | flops 262144 | bytes 1572864 | tf_op jit(solution)/shard_map/add | solution.py:287
  (6 shorter events, 0.0 us)
Async XLA Ops:
  0.6 7.5 %collective-permute-start.1 = (bf16[128,2048]{1,0:T(8,128)(2,1)}, bf16[128,2048]{1,0:T(8,128)(2,1)}, u32[]{:S(2)}, u32[]{:S(2)}) collective-permute-start(bf16[128,2048]{1,0:T(8,128)(2,1)} %refs_4_.1), channel_id=1, source_target_pairs={{0,1},{1,0},{2,3},{3,2},{4,5},{5,4},{6,7},{7,6},{8,9},{9,8},{10,11... | collective-permute-start | bytes 1572872 | tf_op jit(solution)/shard_map/ppermute | solution.py:239
  1.2 6.9 %collective-permute-start.2 = (bf16[128,2048]{1,0:T(8,128)(2,1)}, bf16[128,2048]{1,0:T(8,128)(2,1)S(1)}, u32[]{:S(2)}, u32[]{:S(2)}) collective-permute-start(bf16[128,2048]{1,0:T(8,128)(2,1)} %refs_1_.3), channel_id=1, source_target_pairs={{0,1},{1,0},{2,3},{3,2},{4,5},{5,4},{6,7},{7,6},{8,9},{9,8},{10,11... | collective-permute-start | bytes 1572872 | tf_op jit(solution)/shard_map/ppermute | solution.py:239
  1.2 5.7 %copy-start.5 = (s32[128,1]{0,1:T(1,128)S(1)}, s32[128,1]{0,1:T(1,128)}, u32[]{:S(2)}) copy-start(s32[128,1]{0,1:T(1,128)} %param.9) | copy-start | bytes 1540
  1.2 6.9 %copy-start = (bf16[128,2048]{1,0:T(8,128)(2,1)S(1)}, bf16[128,2048]{1,0:T(8,128)(2,1)}, u32[]{:S(2)}) copy-start(bf16[128,2048]{1,0:T(8,128)(2,1)} %refs_1_.3) | copy-start | bytes 1572868
  1.2 6.9 %copy-start.4 = (s32[8]{0:T(128)S(1)}, s32[8]{0:T(128)}, u32[]{:S(2)}) copy-start(s32[8]{0:T(128)} %refs_1_.2) | copy-start | bytes 100
  2.5 27.2 %collective-permute-start.7 = (bf16[512,768]{1,0:T(8,128)(2,1)S(1)}, bf16[512,768]{1,0:T(8,128)(2,1)S(1)}, u32[]{:S(2)}, u32[]{:S(2)}) collective-permute-start(bf16[512,768]{1,0:T(8,128)(2,1)S(1)} %pad_maximum_fusion.refs_2_.refs_7_), channel_id=1, source_target_pairs={{0,16},{8,24},{16,0},{24,8},{1,17},{9,25},{17,1},{25,9},{2,18},{10... | collective-permute-start | bytes 2359304 | tf_op jit(solution)/shard_map/ppermute | solution.py:236
  5.5 24.2 %collective-permute-start.6 = (bf16[512,768]{1,0:T(8,128)(2,1)S(1)}, bf16[512,768]{1,0:T(8,128)(2,1)S(1)}, u32[]{:S(2)}, u32[]{:S(2)}) collective-permute-start(bf16[512,768]{1,0:T(8,128)(2,1)S(1)} %pad_maximum_fusion.refs_2_.refs_7_), channel_id=1, source_target_pairs={{0,8},{8,0},{16,24},{24,16},{1,9},{9,1},{17,25},{25,17},{2,10},{10... | collective-permute-start | bytes 2359304 | tf_op jit(solution)/shard_map/ppermute | solution.py:236
  7.0 1.1 %collective-permute-start = (s32[1,128]{1,0:T(1,128)S(1)}, s32[1,128]{1,0:T(1,128)S(1)}, u32[]{:S(2)}, u32[]{:S(2)}) collective-permute-start(s32[1,128]{1,0:T(1,128)S(1)} %bitcast.9), channel_id=1, source_target_pairs={{0,1},{1,0},{2,3},{3,2},{4,5},{5,4},{6,7},{7,6},{8,9},{9,8},{10,11... | collective-permute-start | bytes 1544 | tf_op jit(solution)/shard_map/ppermute | solution.py:239
  8.1 1.0 %copy-start.1 = (bf16[128,2048]{1,0:T(8,128)(2,1)S(1)}, bf16[128,2048]{1,0:T(8,128)(2,1)}, u32[]{:S(2)}) copy-start(bf16[128,2048]{1,0:T(8,128)(2,1)} %refs_4_.1) | copy-start | bytes 1572868
  11.6 0.7 copy-start.2
  12.3 17.4 %collective-permute-start.4 = (bf16[48,2048]{1,0:T(8,128)(2,1)}, bf16[48,2048]{1,0:T(8,128)(2,1)}, u32[]{:S(2)}, u32[]{:S(2)}) collective-permute-start(bf16[48,2048]{1,0:T(8,128)(2,1)} %get-tuple-element.45), channel_id=1, source_target_pairs={{0,4},{1,5},{2,6},{3,7},{4,0},{5,1},{6,2},{7,3},{8,12},{9,13},{10,... | collective-permute-start | bytes 589832 | tf_op jit(solution)/shard_map/ppermute | solution.py:239
  14.9 14.8 %collective-permute-start.5 = (bf16[48,2048]{1,0:T(8,128)(2,1)}, bf16[48,2048]{1,0:T(8,128)(2,1)}, u32[]{:S(2)}, u32[]{:S(2)}) collective-permute-start(bf16[48,2048]{1,0:T(8,128)(2,1)} %get-tuple-element.46), channel_id=1, source_target_pairs={{0,6},{1,7},{2,4},{3,5},{4,2},{5,3},{6,0},{7,1},{8,14},{9,15},{10,... | collective-permute-start | bytes 589832 | tf_op jit(solution)/shard_map/ppermute | solution.py:239
  16.2 18.3 %collective-permute-start.3 = (bf16[96,2048]{1,0:T(8,128)(2,1)}, bf16[96,2048]{1,0:T(8,128)(2,1)}, u32[]{:S(2)}, u32[]{:S(2)}) collective-permute-start(bf16[96,2048]{1,0:T(8,128)(2,1)} %get-tuple-element.44), channel_id=1, source_target_pairs={{0,2},{1,3},{2,0},{3,1},{4,6},{5,7},{6,4},{7,5},{8,10},{9,11},{10,... | collective-permute-start | bytes 1179656 | tf_op jit(solution)/shard_map/ppermute | solution.py:239
  17.0 17.5 %copy-start.3 = (bf16[48,2048]{1,0:T(8,128)(2,1)S(1)}, bf16[48,2048]{1,0:T(8,128)(2,1)}, u32[]{:S(2)}) copy-start(bf16[48,2048]{1,0:T(8,128)(2,1)} %copy-done.2) | copy-start | bytes 589828
  35.8 16.0 %collective-permute-start.8 = (bf16[48,2048]{1,0:T(8,128)(2,1)S(1)}, bf16[48,2048]{1,0:T(8,128)(2,1)S(1)}, u32[]{:S(2)}, u32[]{:S(2)}) collective-permute-start(bf16[48,2048]{1,0:T(8,128)(2,1)S(1)} %get-tuple-element.54), channel_id=1, source_target_pairs={{0,4},{1,5},{2,6},{3,7},{4,0},{5,1},{6,2},{7,3},{8,12},{9,13},{10,... | collective-permute-start | bytes 589832 | tf_op jit(solution)/shard_map/ppermute | solution.py:239
  37.5 14.3 %collective-permute-start.9 = (bf16[48,2048]{1,0:T(8,128)(2,1)S(1)}, bf16[48,2048]{1,0:T(8,128)(2,1)S(1)}, u32[]{:S(2)}, u32[]{:S(2)}) collective-permute-start(bf16[48,2048]{1,0:T(8,128)(2,1)S(1)} %get-tuple-element.55), channel_id=1, source_target_pairs={{0,6},{1,7},{2,4},{3,5},{4,2},{5,3},{6,0},{7,1},{8,14},{9,15},{10,... | collective-permute-start | bytes 589832 | tf_op jit(solution)/shard_map/ppermute | solution.py:239
  39.5 12.3 %collective-permute-start.12 = (bf16[192,512]{1,0:T(8,128)(2,1)S(1)}, bf16[192,512]{1,0:T(8,128)(2,1)S(1)}, u32[]{:S(2)}, u32[]{:S(2)}) collective-permute-start(bf16[192,512]{1,0:T(8,128)(2,1)S(1)} %get-tuple-element.60), channel_id=1, source_target_pairs={{0,24},{8,16},{16,8},{24,0},{1,25},{9,17},{17,9},{25,1},{2,26},{10... | collective-permute-start | bytes 589832 | tf_op jit(solution)/shard_map/ppermute | solution.py:236
  39.9 17.6 %collective-permute-start.10 = (bf16[576,512]{1,0:T(8,128)(2,1)S(1)}, bf16[576,512]{1,0:T(8,128)(2,1)S(1)}, u32[]{:S(2)}, u32[]{:S(2)}) collective-permute-start(bf16[576,512]{1,0:T(8,128)(2,1)S(1)} %get-tuple-element.58), channel_id=1, source_target_pairs={{0,16},{8,24},{16,0},{24,8},{1,17},{9,25},{17,1},{25,9},{2,18},{10... | collective-permute-start | bytes 1769480 | tf_op jit(solution)/shard_map/ppermute | solution.py:236
  41.5 16.1 %collective-permute-start.11 = (bf16[576,512]{1,0:T(8,128)(2,1)S(1)}, bf16[576,512]{1,0:T(8,128)(2,1)S(1)}, u32[]{:S(2)}, u32[]{:S(2)}) collective-permute-start(bf16[576,512]{1,0:T(8,128)(2,1)S(1)} %get-tuple-element.59), channel_id=1, source_target_pairs={{0,8},{8,0},{16,24},{24,16},{1,9},{9,1},{17,25},{25,17},{2,10},{10... | collective-permute-start | bytes 1769480 | tf_op jit(solution)/shard_map/ppermute | solution.py:236
  60.2 10.2 %collective-permute-start.13 = (bf16[48,2048]{1,0:T(8,128)(2,1)S(1)}, bf16[48,2048]{1,0:T(8,128)(2,1)S(1)}, u32[]{:S(2)}, u32[]{:S(2)}) collective-permute-start(bf16[48,2048]{1,0:T(8,128)(2,1)S(1)} %get-tuple-element.62), channel_id=1, source_target_pairs={{0,2},{1,3},{2,0},{3,1},{4,6},{5,7},{6,4},{7,5},{8,10},{9,11},{10,... | collective-permute-start | bytes 589832 | tf_op jit(solution)/shard_map/ppermute | solution.py:239
  60.7 11.1 %collective-permute-start.14 = (bf16[48,2048]{1,0:T(8,128)(2,1)S(1)}, bf16[48,2048]{1,0:T(8,128)(2,1)S(1)}, u32[]{:S(2)}, u32[]{:S(2)}) collective-permute-start(bf16[48,2048]{1,0:T(8,128)(2,1)S(1)} %get-tuple-element.63), channel_id=1, source_target_pairs={{0,4},{1,5},{2,6},{3,7},{4,0},{5,1},{6,2},{7,3},{8,12},{9,13},{10,... | collective-permute-start | bytes 589832 | tf_op jit(solution)/shard_map/ppermute | solution.py:239
  63.4 15.1 %collective-permute-start.17 = (bf16[448,512]{1,0:T(8,128)(2,1)S(1)}, bf16[448,512]{1,0:T(8,128)(2,1)S(1)}, u32[]{:S(2)}, u32[]{:S(2)}) collective-permute-start(bf16[448,512]{1,0:T(8,128)(2,1)S(1)} %get-tuple-element.70), channel_id=1, source_target_pairs={{0,8},{8,0},{16,24},{24,16},{1,9},{9,1},{17,25},{25,17},{2,10},{10... | collective-permute-start | bytes 1376264 | tf_op jit(solution)/shard_map/ppermute | solution.py:236
  64.6 21.4 %collective-permute-start.18 = (bf16[448,512]{1,0:T(8,128)(2,1)S(1)}, bf16[448,512]{1,0:T(8,128)(2,1)S(1)}, u32[]{:S(2)}, u32[]{:S(2)}) collective-permute-start(bf16[448,512]{1,0:T(8,128)(2,1)S(1)} %get-tuple-element.71), channel_id=1, source_target_pairs={{0,16},{8,24},{16,0},{24,8},{1,17},{9,25},{17,1},{25,9},{2,18},{10... | collective-permute-start | bytes 1376264 | tf_op jit(solution)/shard_map/ppermute | solution.py:236
  65.2 20.8 %collective-permute-start.19 = (bf16[448,512]{1,0:T(8,128)(2,1)S(1)}, bf16[448,512]{1,0:T(8,128)(2,1)S(1)}, u32[]{:S(2)}, u32[]{:S(2)}) collective-permute-start(bf16[448,512]{1,0:T(8,128)(2,1)S(1)} %get-tuple-element.72), channel_id=1, source_target_pairs={{0,24},{8,16},{16,8},{24,0},{1,25},{9,17},{17,9},{25,1},{2,26},{10... | collective-permute-start | bytes 1376264 | tf_op jit(solution)/shard_map/ppermute | solution.py:236
  70.4 7.5 %collective-permute-start.15 = (bf16[48,2048]{1,0:T(8,128)(2,1)S(1)}, bf16[48,2048]{1,0:T(8,128)(2,1)S(1)}, u32[]{:S(2)}, u32[]{:S(2)}) collective-permute-start(bf16[48,2048]{1,0:T(8,128)(2,1)S(1)} %shard_map.111), channel_id=1, source_target_pairs={{0,6},{1,7},{2,4},{3,5},{4,2},{5,3},{6,0},{7,1},{8,14},{9,15},{10,... | collective-permute-start | bytes 589832 | tf_op jit(solution)/shard_map/ppermute | solution.py:239
  78.4 9.4 %collective-permute-start.16 = (bf16[128,2048]{1,0:T(8,128)(2,1)S(1)}, bf16[128,2048]{1,0:T(8,128)(2,1)S(1)}, u32[]{:S(2)}, u32[]{:S(2)}) collective-permute-start(bf16[128,2048]{1,0:T(8,128)(2,1)S(1)} %get-tuple-element.68), channel_id=1, source_target_pairs={{0,1},{1,0},{2,3},{3,2},{4,5},{5,4},{6,7},{7,6},{8,9},{9,8},{10,11... | collective-permute-start | bytes 1572872 | tf_op jit(solution)/shard_map/ppermute | solution.py:239

commit v10 on v7

--- a/solution.py
+++ b/solution.py
@@ -47,13 +47,14 @@
     return run
 
 
-def after(values, *earlier):
+def after(values, *earlier, ahead=0):
     return pl.pallas_call(
         lambda *refs: None,
         out_shape=[shape(*value.shape, value.dtype) for value in values],
         in_specs=[ANY] * (len(values) + len(earlier)),
         out_specs=[ANY] * len(values),
         input_output_aliases={i: i for i in range(len(values))},
+        cost_estimate=pl.CostEstimate(flops=ahead, bytes_accessed=0, transcendentals=0),
         compiler_params=pltpu.CompilerParams(vmem_limit_bytes=MIB),
     )(*values, *earlier)
 
@@ -105,107 +106,87 @@
         ref[...] = filled[k * block : (k + 1) * block]
 
 
+def weight_parts(own_ref, weights):
+    depth = weights[0].shape[0]
+    half = depth // 2
+    for k, ref in enumerate(weights):
+        partner, start = (k, 0) if k < 3 else (3, (k - 3) * half)
+        yield pl.ds(pl.multiple_of((own_ref[0] ^ partner) * depth + start, half), ref.shape[0]), ref
+
+
 def columns_of(own_ref, depth):
     return [pl.ds(pl.multiple_of((own_ref[0] ^ k) * depth, depth), depth) for k in range(4)]
 
 
-def onward_parts(own_ref, onward):
-    for at, ref in enumerate(onward):
-        half = ref.shape[1] // 2
-        quarter = half // 2
-        start = ((own_ref[0] ^ 3) * 2 + at) * half
-        both = pl.ds(pl.multiple_of(start, half), half), ref[:half]
-        downs = [
-            (
-                pl.ds(pl.multiple_of(start + i * quarter, quarter), quarter),
-                ref[half : half + quarter, i * half : (i + 1) * half],
-            )
-            for i in range(2)
-        ]
-        yield both, downs
-
-
 def spread_kernel(own_ref, *refs):
-    got, (joined_1, joined_2), (x_ref, piece_0, piece_3, onward_1, onward_2) = refs[:4], refs[4:6], refs[6:]
-    slots, depth = piece_0.shape
+    got, own_dy, (x_ref, *piece_refs) = refs[:4], refs[4], refs[5:]
+    slots = x_ref.shape[0]
     block = slots // 4
-    half, quarter = depth // 2, depth // 4
-    columns = columns_of(own_ref, depth)
+    columns = columns_of(own_ref, piece_refs[0].shape[1])
     for j, ref in enumerate(got):
-        rows = pl.ds(j * block, block)
+        rows = slice(j * block, (j + 1) * block)
         x_ref[rows] = ref[:block]
-        for into, cols in zip(
-            (piece_0, onward_1.at[pl.ds(half + quarter, slots)], onward_2.at[pl.ds(half + quarter, slots)], piece_3),
-            columns,
-        ):
-            into[rows] = ref[:block, cols]
-    for joined, start, into in ((joined_2, half, onward_1), (joined_1, 0, onward_2)):
-        into[:half] = joined[start : start + half, :depth]
-        into[half : half + quarter, :half] = joined[start : start + quarter, depth:]
-        into[half : half + quarter, half:] = joined[start + quarter : start + half, depth:]
+        for cols, piece_ref in zip(columns, piece_refs):
+            piece_ref[rows] = ref[:block, cols]
+    for cols, piece_ref in zip(columns, piece_refs):
+        piece_ref[slots : slots + block] = own_dy[:, cols]
+        piece_ref[slots + block :] = got[1][block:, cols]
 
 
 def act_kernel(own_ref, x_ref, *refs):
     weights, acts_ref = refs[:-1], refs[-1]
     both = acts_ref.shape[1]
-    columns = columns_of(own_ref, weights[0].shape[0])
-    acts_ref[...] = sum(dot(x_ref[:, cols], ref[:, :both], 1, 0) for cols, ref in zip(columns, weights))
-
-
-def grad_kernel(own_ref, acts_ref, x_ref, *refs):
-    got, weights, onward, outs, dy_ref = refs[:4], refs[4:7], refs[7:9], refs[9:-1], refs[-1]
-    back_refs, own_term, (own_grads, *messages) = outs[:4], outs[4], outs[5:]
+    acts_ref[...] = sum(dot(x_ref[:, cols], ref[:, :both], 1, 0) for cols, ref in weight_parts(own_ref, weights))
+
+
+def grad_kernel(parts, own_ref, acts_ref, *refs):
+    got, weights, outs, dy_ref = refs[:parts], refs[parts : parts + 5], refs[parts + 5 : -1], refs[-1]
+    back_refs, messages = outs[:parts], outs[parts:]
     slots, both = acts_ref.shape
     width = both // 2
-    block = slots // 4
+    half = slots // 2
+    block = slots // parts
     depth = weights[0].shape[0]
-    half = depth // 2
-    columns = columns_of(own_ref, depth)
     for j, ref in enumerate(got):
         dy_ref[j * block : (j + 1) * block] = ref[ref.shape[0] - block :]
-    acts = acts_ref[...]
-    back_grad = sum(dot(dy_ref[:, cols], ref[:, both:], 1, 0) for cols, ref in zip(columns, weights))
-    for (cols, rows), downs in onward_parts(own_ref, onward):
-        acts += dot(x_ref[:, cols], rows, 1, 0)
-        for cols, rows in downs:
-            back_grad += dot(dy_ref[:, cols], rows, 1, 0)
-    gate_act, up_act = acts[:, :width], acts[:, width:]
+    back_grad = sum(dot(dy_ref[:, cols], ref[:, both:], 1, 0) for cols, ref in weight_parts(own_ref, weights))
+    gate_act, up_act = acts_ref[:, :width], acts_ref[:, width:]
     sigmoid_g = jax.nn.sigmoid(gate_act)
     silu_gate = gate_act * sigmoid_g
     hidden = (silu_gate * up_act).astype(BF16)
-    gate_h = back_grad * up_act * sigmoid_g * (1.0 + gate_act * (1.0 - sigmoid_g))
-    own_grads[:, :width] = gate_h.astype(BF16)
-    own_grads[:, width:] = (back_grad * silu_gate).astype(BF16)
-    grads = own_grads[...]
-    for k, cols in enumerate(columns):
-        term = dot(dy_ref[:, cols], hidden, 0, 0)
-        if k == 0:
-            own_term[...] = term
-        else:
-            messages[k - 1][:slots] = grads
-            messages[k - 1][slots:, :width] = term[:half].astype(BF16)
-            messages[k - 1][slots:, width:] = term[half:].astype(BF16)
-    pairs = [(cols, ref[:, :both]) for cols, ref in zip(columns, weights)]
-    for cols, rows in pairs + [part for part, _ in onward_parts(own_ref, onward)]:
-        slot_grad = dot(grads, rows, 1, 1).astype(BF16)
+    gate_h = (back_grad * up_act * sigmoid_g * (1.0 + gate_act * (1.0 - sigmoid_g))).astype(BF16)
+    up_h = (back_grad * silu_gate).astype(BF16)
+    for message, cols in zip(messages, columns_of(own_ref, depth)):
+        message[:slots, :width] = gate_h
+        message[:slots, width:] = up_h
+        message[slots : slots + half, :width] = hidden[:half]
+        message[slots : slots + half, width:] = hidden[half:]
+        message[slots + half :] = dy_ref[half:, cols]
+    grads = messages[0][:slots]
+    for cols, ref in weight_parts(own_ref, weights):
+        slot_grad = dot(grads, ref[:, :both], 1, 1).astype(BF16)
         for j, back_ref in enumerate(back_refs):
             back_ref[:, cols] = slot_grad[j * block : (j + 1) * block]
 
 
 def sum_kernel(*refs):
-    pieces, messages, own_term = refs[:4], refs[4:8], refs[8]
-    (gate_ref, up_ref, down_ref), (x_ref, grads_ref) = refs[9:12], refs[12:]
-    slots = pieces[0].shape[0]
-    depth, width = gate_ref.shape
-    half = depth // 2
+    pieces, messages = refs[:4], refs[4:8]
+    (gate_ref, up_ref, down_ref), (x_ref, dy_ref, grads_ref, hidden_ref) = refs[8:11], refs[11:]
+    width = gate_ref.shape[1]
+    slots = x_ref.shape[0] // 4
+    half = slots // 2
     for k, (piece, got) in enumerate(zip(pieces, messages)):
-        x_ref[k * slots : (k + 1) * slots] = piece[-slots:]
-        grads_ref[k * slots : (k + 1) * slots] = got[:slots]
+        start, middle, stop = k * slots, k * slots + half, (k + 1) * slots
+        x_ref[start:stop] = piece[:slots]
+        dy_ref[start:middle] = piece[slots:]
+        dy_ref[middle:stop] = got[slots + half :]
+        grads_ref[start:stop] = got[:slots]
+        hidden_ref[start:middle] = got[slots : slots + half, :width]
+        hidden_ref[middle:stop] = got[slots : slots + half, width:]
     total = dot(x_ref[...], grads_ref[...], 0, 0)
     gate_ref[...] = total[:, :width]
     up_ref[...] = total[:, width:]
-    for rows, cols in ((slice(0, half), slice(0, width)), (slice(half, depth), slice(width, 2 * width))):
-        down_ref[rows] = own_term[rows] + sum(got[slots:, cols].astype(F32) for got in messages[1:])
+    down_ref[...] = dot(dy_ref[...], hidden_ref[...], 0, 0)
 
 
 def unpack_kernel(pick_ref, *refs):
@@ -248,41 +229,42 @@
         2,
         [pltpu.VMEM((2 * tok_rows, model_width), BF16)],
     )(rank, host, route, route_b, tokens, tokens_b, cotangent, cotangent_b)
-    near, far_xa, far_xb = over_rep(near, 2), over_rep(far_xa, 4), over_rep(far_xb, 6)
+    far_x = [over_rep(far_xa, 4), over_rep(far_xb, 6)]
+    far_x = after(far_x, ahead=1<<31)
+    near = over_rep(near, 2)
     own_dy, far_a, far_b = call(pack_more_kernel, [shape(block, model_width)] * 3)(pick, cotangent, cotangent_b)
-
-    onward = shape(depth // 2 + depth // 4 + slots, depth)
-    x, piece_0, piece_3, onward_1, onward_2 = call(
-        spread_kernel,
-        [shape(slots, model_width), shape(slots, depth), shape(slots, depth), onward, onward],
-        1,
-        earlier=[own_dy],
-    )(own, own_x, near, far_xa, far_xb, joined_1, joined_2)
-    far_a, far_b = after([far_a, far_b], piece_0)
-    far_a, far_b = over_rep(far_a, 4), over_rep(far_b, 6)
-    onward_1, onward_2, piece_3 = over_own(onward_1, 1), over_own(onward_2, 2), over_own(piece_3, 3)
-    weights = [joined, joined_1, joined_2]
+    joined_3 = [over_own(joined_1[: depth // 2], 2), over_own(joined_2[depth // 2 :], 1)]
+    joined_3 = after(joined_3, ahead=1<<33)
+    weights = [joined, joined_1, joined_2, *joined_3]
+
+    x, *pieces = call(spread_kernel, [shape(slots, model_width)] + [shape(slots + slots // 2, depth)] * 4, 1)(
+        own, own_x, near, *far_x, own_dy
+    )
+    far_dy = after([far_a, far_b], pieces[0])
+    far_dy = [over_rep(far_dy[0], 4), over_rep(far_dy[1], 6)]
+    pieces = [pieces[0]] + [over_own(pieces[k], k) for k in range(1, 4)]
     acts = call(act_kernel, [shape(slots, 2 * width, F32)], 1)(own, x, *weights)[0]
 
-    message = shape(slots + depth // 2, 2 * width)
-    *back, own_term, grads, message_1, message_2, message_3 = call(
-        grad_kernel,
-        [shape(block, model_width)] * parts
-        + [shape(depth, width, F32), shape(slots, 2 * width), message, message, message],
+    *back, own_message, message_1, message_2, message_3 = call(
+        functools.partial(grad_kernel, parts),
+        [shape(block, model_width)] * parts + [shape(2 * slots, 2 * width)] * 4,
         1,
         [slot_rows],
-        earlier=[piece_3],
-    )(own, acts, x, own_dy, near, far_a, far_b, *weights, onward_2, onward_1)
+        earlier=pieces[1:],
+    )(own, acts, own_dy, near, *far_dy, *weights)
     returned = [back[0]] + [over_rep(back[k], 2 * k) for k in range(1, parts)]
-    messages = [over_own(message_1, 1), over_own(message_2, 2), over_own(message_3, 3)]
-
-    mine, other = call(unpack_kernel, [shape(tok_rows, model_width)] * 2, 0, [slot_rows], earlier=messages)(
+    messages = [own_message, over_own(message_1, 1), over_own(message_2, 2), over_own(message_3, 3)]
+
+    mine, other = call(unpack_kernel, [shape(tok_rows, model_width)] * 2, 0, [slot_rows], earlier=messages[1:])(
         pick, *returned
     )
     x_grad = mine + over_rep(other, 1)
-    out = call(sum_kernel, [shape(depth, width, F32)] * 3, 0, [pltpu.VMEM((4 * slots, depth), BF16)] * 2)(
-        piece_0, onward_1, onward_2, piece_3, grads, *messages, own_term
-    )
+    out = call(
+        sum_kernel,
+        [shape(depth, width, F32)] * 3,
+        0,
+        [pltpu.VMEM((4 * slots, cols), BF16) for cols in (depth, depth, 2 * width, width)],
+    )(*pieces, *messages)
     return (x_grad, *(grad[None] for grad in out))
 
 

time: 82.7 us -> 83 us (level); the launches traced: 82.4 us -> 81.6 us
  waiting for transfers between devices: 45.5 us -> 35.4 us
  starting transfers between devices: 22.7 us -> 30.7 us
  Pallas kernels: 9.64 us -> 11.1 us
    ppermute x12, waiting for transfers between devices: 40 us -> 27.4 us  [over_rep(): return lax.ppermute(value, 'rep', [(i, i ^ k) for i in range(n_rep)])]
    ppermute x12, starting transfers between devices: 11 us -> 15.9 us  [over_rep(): return lax.ppermute(value, 'rep', [(i, i ^ k) for i in range(n_rep)])]
    ppermute x8 -> x10, starting transfers between devices: 11.6 us -> 14.7 us  [over_own(): return lax.ppermute(value, 'own', [(i, i ^ k) for i in range(4)])]
    ppermute x8 -> x10, waiting for transfers between devices: 5.5 us -> 7.98 us  [over_own(): return lax.ppermute(value, 'own', [(i, i ^ k) for i in range(4)])]
    unnamed x12 -> x10, local copies, waits for them, and re-layouts: 1.73 us -> 0.02 us
    slice x0 -> x2, local copies, waits for them, and re-layouts: none -> 1.54 us  [the longest x1 0.77 us: shards_by_partner(): joined_1[:depth // 2]]
    pallas_call x7, Pallas kernels: 9.64 us -> 11.1 us  [run(): pl.pallas_call(body, out_shape=outs, in_specs=[SMEM] * scalars + [VMEM] *...]
  transfers between devices with their start and end apart: 20 -> 22, of which waited for: 10 -> 9; matrix products, arithmetic and copies ran while one was open for 1% -> 2% of each run, Pallas kernels for 6% -> 10%
where the time goes in v10:
time: 83 us; the launch traced here: 81.6 us
  waiting for transfers between devices  35.4 us (43%)
  starting transfers between devices  30.7 us (37%)
  Pallas kernels  11.1 us (13%)
  other arithmetic  2.14 us (3%)
  local copies, waits for them, and re-layouts  1.56 us (2%)
    ppermute x12, waiting for transfers between devices, over_rep(): return lax.ppermute(value, 'rep', [(i, i ^ k) for i in range(n_rep)])  27.4 us
    ppermute x12, starting transfers between devices, over_rep(): return lax.ppermute(value, 'rep', [(i, i ^ k) for i in range(n_rep)])  15.9 us
    ppermute x10, starting transfers between devices, over_own(): return lax.ppermute(value, 'own', [(i, i ^ k) for i in range(4)])  14.7 us
    pallas_call x7, Pallas kernels, run(): pl.pallas_call(body, out_shape=outs, in_specs=[SMEM] * scalars + [VMEM] *...  11.1 us
    ppermute x10, waiting for transfers between devices, over_own(): return lax.ppermute(value, 'own', [(i, i ^ k) for i in range(4)])  7.98 us
  transfers between devices with their start and end apart: 22, of which 9 were waited for; matrix products, arithmetic and copies ran while one was open for 2% of the time, Pallas kernels for 10%

profile of v10, /device:TPU:0, one launch (start us, length us, event | category | flops | bytes accessed | tf_op | source)
XLA Modules:
  0.0 81.6 jit_solution(16808568279336536024)
XLA Ops:
  0.6 0.0 copy-start
  0.6 0.0 copy-start.4
  0.7 0.0 copy-start.3
  0.7 1.2 %pad_maximum_fusion.refs_2_.refs_6_ = bf16[512,768]{1,0:T(8,128)(2,1)S(1)} fusion(bf16[512,256]{1,0:T(8,128)(2,1)} %bitcast.11, bf16[512,256]{1,0:T(8,128)(2,1)} %bitcast.12, bf16[512,256]{1,0:T(8,128)(2,1)} %bitcast.13), kind=kLoop, calls=%fused_computation | loop fusion | flops 2359296 | bytes 1572864 | tf_op jit(solution)/shard_map/concatenate | solution.py:222
  1.9 3.0 %collective-permute-start.7 = (bf16[512,768]{1,0:T(8,128)(2,1)S(1)}, bf16[512,768]{1,0:T(8,128)(2,1)S(1)}, u32[]{:S(2)}, u32[]{:S(2)}) collective-permute-start(bf16[512,768]{1,0:T(8,128)(2,1)S(1)} %pad_maximum_fusion.refs_2_.refs_6_), channel_id=1, source_target_pairs={{0,16},{8,24},{16,0},{24,8},{1,17},{9,25},{17,1},{25,9},{2,18},{10... | collective-permute-start | bytes 2359304 | tf_op jit(solution)/shard_map/ppermute | solution.py:215
  4.9 1.5 %collective-permute-start.6 = (bf16[512,768]{1,0:T(8,128)(2,1)S(1)}, bf16[512,768]{1,0:T(8,128)(2,1)S(1)}, u32[]{:S(2)}, u32[]{:S(2)}) collective-permute-start(bf16[512,768]{1,0:T(8,128)(2,1)S(1)} %pad_maximum_fusion.refs_2_.refs_6_), channel_id=1, source_target_pairs={{0,8},{8,0},{16,24},{24,16},{1,9},{9,1},{17,25},{25,17},{2,10},{10... | collective-permute-start | bytes 2359304 | tf_op jit(solution)/shard_map/ppermute | solution.py:215
  6.4 0.0 collective-permute-start.1
  6.4 0.0 copy-done
  6.4 0.5 collective-permute-start.2
  6.9 0.0 copy-done.4
  6.9 0.1 collective-permute-start
  7.0 2.1 %collective-permute-done.refs_3_ = s32[1,128]{1,0:T(1,128)S(1)} collective-permute-done((s32[1,128]{1,0:T(1,128)S(1)}, s32[1,128]{1,0:T(1,128)S(1)}, u32[]{:S(2)}, u32[]{:S(2)}) %collective-permute-start) | collective-permute-done | bytes 544 | tf_op jit(solution)/shard_map/ppermute | solution.py:218
  9.1 0.3 collective-permute-done.1.refs_5_
  9.3 0.0 collective-permute-done.2.refs_7_.refs_2_
  9.3 0.0 copy-done.3
  9.3 2.6 %shard_map.102 = (bf16[192,256]{1,0:T(8,128)(2,1)S(1)}, bf16[48,2048]{1,0:T(8,128)(2,1)S(1)}, bf16[96,2048]{1,0:T(8,128)(2,1)}, bf16[48,2048]{1,0:T(8,128)(2,1)}, bf16[48,2048]{1,0:T(8,128)(2,1)}) custom-call(s32[1]{0:T(128)} %bitcast.refs_0_, s32[8]{0:T(128)S(1)} %copy-done.3, s32[1,128]{1,0:T(1,128)S(1)} %bitcast.10, ...), custom_call_target="tpu_custom_call" | custom-call | bytes 3179556 | tf_op jit(solution)/shard_map/pallas_call | solution.py:37
  11.9 2.6 %collective-permute-start.4 = (bf16[48,2048]{1,0:T(8,128)(2,1)}, bf16[48,2048]{1,0:T(8,128)(2,1)}, u32[]{:S(2)}, u32[]{:S(2)}) collective-permute-start(bf16[48,2048]{1,0:T(8,128)(2,1)} %get-tuple-element.39), channel_id=1, source_target_pairs={{0,4},{1,5},{2,6},{3,7},{4,0},{5,1},{6,2},{7,3},{8,12},{9,13},{10,... | collective-permute-start | bytes 589832 | tf_op jit(solution)/shard_map/ppermute | solution.py:218
  14.5 1.3 %collective-permute-start.5 = (bf16[48,2048]{1,0:T(8,128)(2,1)}, bf16[48,2048]{1,0:T(8,128)(2,1)}, u32[]{:S(2)}, u32[]{:S(2)}) collective-permute-start(bf16[48,2048]{1,0:T(8,128)(2,1)} %get-tuple-element.40), channel_id=1, source_target_pairs={{0,6},{1,7},{2,4},{3,5},{4,2},{5,3},{6,0},{7,1},{8,14},{9,15},{10,... | collective-permute-start | bytes 589832 | tf_op jit(solution)/shard_map/ppermute | solution.py:218
  15.9 0.2 collective-permute-start.3
  16.1 6.3 %collective-permute-done.7.refs_4_.refs_8_ = bf16[512,768]{1,0:T(8,128)(2,1)S(1)} collective-permute-done((bf16[512,768]{1,0:T(8,128)(2,1)S(1)}, bf16[512,768]{1,0:T(8,128)(2,1)S(1)}, u32[]{:S(2)}, u32[]{:S(2)}) %collective-permute-start.7) | collective-permute-done | bytes 786464 | tf_op jit(solution)/shard_map/ppermute | solution.py:215
  22.5 0.8 slice.9
  23.2 1.7 %collective-permute-start.9 = (bf16[256,768]{1,0:T(8,128)(2,1)}, bf16[256,768]{1,0:T(8,128)(2,1)}, u32[]{:S(2)}, u32[]{:S(2)}) collective-permute-start(bf16[256,768]{1,0:T(8,128)(2,1)} %slice.9), channel_id=1, source_target_pairs={{0,8},{8,0},{16,24},{24,16},{1,9},{9,1},{17,25},{25,17},{2,10},{10... | collective-permute-start | bytes 1179656 | tf_op jit(solution)/shard_map/ppermute | solution.py:215
  24.9 0.0 collective-permute-done.6.refs_3_.refs_7_
  24.9 0.8 slice.8
  25.7 0.0 copy-done.1
  25.7 1.5 %collective-permute-start.8 = (bf16[256,768]{1,0:T(8,128)(2,1)}, bf16[256,768]{1,0:T(8,128)(2,1)}, u32[]{:S(2)}, u32[]{:S(2)}) collective-permute-start(bf16[256,768]{1,0:T(8,128)(2,1)} %slice.8), channel_id=1, source_target_pairs={{0,16},{8,24},{16,0},{24,8},{1,17},{9,25},{17,1},{25,9},{2,18},{10... | collective-permute-start | bytes 1179656 | tf_op jit(solution)/shard_map/ppermute | solution.py:215
  27.2 0.5 shard_map.104
  27.8 0.0 copy-start.2
  27.8 1.6 %collective-permute-done.4.refs_0_ = bf16[48,2048]{1,0:T(8,128)(2,1)} collective-permute-done((bf16[48,2048]{1,0:T(8,128)(2,1)}, bf16[48,2048]{1,0:T(8,128)(2,1)}, u32[]{:S(2)}, u32[]{:S(2)}) %collective-permute-start.4) | collective-permute-done | bytes 196640 | tf_op jit(solution)/shard_map/ppermute | solution.py:218
  29.4 0.0 collective-permute-done.5.refs_1_
  29.4 4.7 %collective-permute-done.3.refs_2_.refs_3_ = bf16[96,2048]{1,0:T(8,128)(2,1)} collective-permute-done((bf16[96,2048]{1,0:T(8,128)(2,1)}, bf16[96,2048]{1,0:T(8,128)(2,1)}, u32[]{:S(2)}, u32[]{:S(2)}) %collective-permute-start.3) | collective-permute-done | bytes 393248 | tf_op jit(solution)/shard_map/ppermute | solution.py:218
  34.1 0.0 copy-done.2
  34.1 1.3 %shard_map.105 = (bf16[192,2048]{1,0:T(8,128)(2,1)S(1)}, bf16[288,512]{1,0:T(8,128)(2,1)S(1)}, bf16[288,512]{1,0:T(8,128)(2,1)S(1)}, bf16[288,512]{1,0:T(8,128)(2,1)S(1)}, bf16[288,512]{1,0:T(8,128)(2,1)S(1)}) custom-call(s32[1]{0:T(128)} %bitcast.2.refs_0_, bf16[48,2048]{1,0:T(8,128)(2,1)S(1)} %copy-done.2, ...), custom_call_target="tpu_custom_call" | custom-call | bytes 3145732 | tf_op jit(solution)/shard_map/pallas_call | solution.py:37
  35.4 1.6 %collective-permute-start.10 = (bf16[48,2048]{1,0:T(8,128)(2,1)S(1)}, bf16[48,2048]{1,0:T(8,128)(2,1)S(1)}, u32[]{:S(2)}, u32[]{:S(2)}) collective-permute-start(bf16[48,2048]{1,0:T(8,128)(2,1)S(1)} %get-tuple-element.50), channel_id=1, source_target_pairs={{0,4},{1,5},{2,6},{3,7},{4,0},{5,1},{6,2},{7,3},{8,12},{9,13},{10,... | collective-permute-start | bytes 589832 | tf_op jit(solution)/shard_map/ppermute | solution.py:218
  37.0 2.0 %collective-permute-start.11 = (bf16[48,2048]{1,0:T(8,128)(2,1)S(1)}, bf16[48,2048]{1,0:T(8,128)(2,1)S(1)}, u32[]{:S(2)}, u32[]{:S(2)}) collective-permute-start(bf16[48,2048]{1,0:T(8,128)(2,1)S(1)} %get-tuple-element.51), channel_id=1, source_target_pairs={{0,6},{1,7},{2,4},{3,5},{4,2},{5,3},{6,0},{7,1},{8,14},{9,15},{10,... | collective-permute-start | bytes 589832 | tf_op jit(solution)/shard_map/ppermute | solution.py:218
  39.0 0.5 collective-permute-start.12
  39.6 0.0 collective-permute-done.9.refs_1_
  39.6 0.5 collective-permute-start.13
  40.1 0.0 collective-permute-done.8.refs_0_
  40.1 2.4 %collective-permute-start.14 = (bf16[288,512]{1,0:T(8,128)(2,1)S(1)}, bf16[288,512]{1,0:T(8,128)(2,1)S(1)}, u32[]{:S(2)}, u32[]{:S(2)}) collective-permute-start(bf16[288,512]{1,0:T(8,128)(2,1)S(1)} %get-tuple-element.54), channel_id=1, source_target_pairs={{0,24},{8,16},{16,8},{24,0},{1,25},{9,17},{17,9},{25,1},{2,26},{10... | collective-permute-start | bytes 884744 | tf_op jit(solution)/shard_map/ppermute | solution.py:215
  42.5 1.7 %shard_map.107.refs_1_ = f32[192,512]{1,0:T(8,128)S(1)} custom-call(s32[1]{0:T(128)} %bitcast.2.refs_0_, bf16[192,2048]{1,0:T(8,128)(2,1)S(1)} %get-tuple-element.44.refs_1_, bf16[512,768]{1,0:T(8,128)(2,1)S(1)} %pad_maximum_fusion.refs_2_.refs_6_, bf16[512,768]{1,0:T(8,128)(2,1)S(1)} %collective-permute-done.6.refs_3_.refs_7_, ...), custom_call_target="tpu_custom_call" | custom-call | bytes 4325380 | tf_op jit(solution)/shard_map/pallas_call | solution.py:37
  44.3 7.0 %collective-permute-done.10.refs_4_ = bf16[48,2048]{1,0:T(8,128)(2,1)S(1)} collective-permute-done((bf16[48,2048]{1,0:T(8,128)(2,1)S(1)}, bf16[48,2048]{1,0:T(8,128)(2,1)S(1)}, u32[]{:S(2)}, u32[]{:S(2)}) %collective-permute-start.10) | collective-permute-done | bytes 196640 | tf_op jit(solution)/shard_map/ppermute | solution.py:218
  51.3 0.0 collective-permute-done.11.refs_5_
  51.3 0.0 collective-permute-done.12.refs_11_.refs_1_
  51.3 1.6 %collective-permute-done.13.refs_12_.refs_2_ = bf16[288,512]{1,0:T(8,128)(2,1)S(1)} collective-permute-done((bf16[288,512]{1,0:T(8,128)(2,1)S(1)}, bf16[288,512]{1,0:T(8,128)(2,1)S(1)}, u32[]{:S(2)}, u32[]{:S(2)}) %collective-permute-start.13) | collective-permute-done | bytes 294944 | tf_op jit(solution)/shard_map/ppermute | solution.py:215
  52.9 0.0 collective-permute-done.14.refs_13_.refs_3_
  52.9 2.7 %shard_map.109 = (bf16[48,2048]{1,0:T(8,128)(2,1)S(1)}, bf16[48,2048]{1,0:T(8,128)(2,1)S(1)}, bf16[48,2048]{1,0:T(8,128)(2,1)S(1)}, bf16[48,2048]{1,0:T(8,128)(2...) custom-call(s32[1]{0:T(128)} %bitcast.2.refs_0_, ...), custom_call_target="tpu_custom_call" | custom-call | bytes 6881284 | tf_op jit(solution)/shard_map/pallas_call | solution.py:37
  55.6 2.3 %collective-permute-start.15 = (bf16[48,2048]{1,0:T(8,128)(2,1)S(1)}, bf16[48,2048]{1,0:T(8,128)(2,1)S(1)}, u32[]{:S(2)}, u32[]{:S(2)}) collective-permute-start(bf16[48,2048]{1,0:T(8,128)(2,1)S(1)} %get-tuple-element.56), channel_id=1, source_target_pairs={{0,2},{1,3},{2,0},{3,1},{4,6},{5,7},{6,4},{7,5},{8,10},{9,11},{10,... | collective-permute-start | bytes 589832 | tf_op jit(solution)/shard_map/ppermute | solution.py:218
  57.9 0.5 collective-permute-start.18
  58.5 0.5 collective-permute-start.19
  59.0 2.4 %collective-permute-start.20 = (bf16[384,512]{1,0:T(8,128)(2,1)S(1)}, bf16[384,512]{1,0:T(8,128)(2,1)S(1)}, u32[]{:S(2)}, u32[]{:S(2)}) collective-permute-start(bf16[384,512]{1,0:T(8,128)(2,1)S(1)} %get-tuple-element.61), channel_id=1, source_target_pairs={{0,24},{8,16},{16,8},{24,0},{1,25},{9,17},{17,9},{25,1},{2,26},{10... | collective-permute-start | bytes 1179656 | tf_op jit(solution)/shard_map/ppermute | solution.py:215
  61.4 2.0 %collective-permute-start.16 = (bf16[48,2048]{1,0:T(8,128)(2,1)S(1)}, bf16[48,2048]{1,0:T(8,128)(2,1)S(1)}, u32[]{:S(2)}, u32[]{:S(2)}) collective-permute-start(bf16[48,2048]{1,0:T(8,128)(2,1)S(1)} %get-tuple-element.57), channel_id=1, source_target_pairs={{0,4},{1,5},{2,6},{3,7},{4,0},{5,1},{6,2},{7,3},{8,12},{9,13},{10,... | collective-permute-start | bytes 589832 | tf_op jit(solution)/shard_map/ppermute | solution.py:218
  63.4 0.0 collective-permute-done.15.refs_2_
  63.4 3.2 %collective-permute-start.17 = (bf16[48,2048]{1,0:T(8,128)(2,1)S(1)}, bf16[48,2048]{1,0:T(8,128)(2,1)S(1)}, u32[]{:S(2)}, u32[]{:S(2)}) collective-permute-start(bf16[48,2048]{1,0:T(8,128)(2,1)S(1)} %get-tuple-element.58), channel_id=1, source_target_pairs={{0,6},{1,7},{2,4},{3,5},{4,2},{5,3},{6,0},{7,1},{8,14},{9,15},{10,... | collective-permute-start | bytes 589832 | tf_op jit(solution)/shard_map/ppermute | solution.py:218
  66.6 11.6 %collective-permute-done.16.refs_3_ = bf16[48,2048]{1,0:T(8,128)(2,1)S(1)} collective-permute-done((bf16[48,2048]{1,0:T(8,128)(2,1)S(1)}, bf16[48,2048]{1,0:T(8,128)(2,1)S(1)}, u32[]{:S(2)}, u32[]{:S(2)}) %collective-permute-start.16) | collective-permute-done | bytes 196640 | tf_op jit(solution)/shard_map/ppermute | solution.py:218
  78.2 0.0 collective-permute-done.17.refs_4_
  78.2 0.0 collective-permute-done.18.refs_5_
  78.2 0.0 collective-permute-done.19.refs_6_
  78.2 0.0 collective-permute-done.20.refs_7_
  78.2 0.5 shard_map.110
  78.7 0.1 collective-permute-start.21
  78.7 1.8 %shard_map.111 = (f32[512,256]{1,0:T(8,128)}, f32[512,256]{1,0:T(8,128)}, f32[512,256]{1,0:T(8,128)}) custom-call(bf16[288,512]{1,0:T(8,128)(2,1)S(1)} %get-tuple-element.49.refs_2_.refs_0_, bf16[288,512]{1,0:T(8,128)(2,1)S(1)} %collective-permute-done.12.refs_11_.refs_1_, bf16[288,512]{1,0:T(8,128)(2,1)S(1)} %collective-permute-done.13.refs_12_.refs_2_, ...), custom_call_target="tpu_custom_call" | custom-call | bytes 4325376 | tf_op jit(solution)/shard_map/pallas_call | solution.py:37
  80.5 0.1 collective-permute-done.21
  80.6 0.9 %add.3 = bf16[128,2048]{1,0:T(8,128)(2,1)} add(bf16[128,2048]{1,0:T(8,128)(2,1)S(1)} %get-tuple-element.62, bf16[128,2048]{1,0:T(8,128)(2,1)S(1)} %collective-permute-done.21) | non-fusion elementwise | flops 262144 | bytes 1572864 | tf_op jit(solution)/shard_map/add | solution.py:261
  (4 shorter events, 0.0 us)
Async XLA Ops:
  0.6 5.8 %copy-start = (bf16[128,2048]{1,0:T(8,128)(2,1)S(1)}, bf16[128,2048]{1,0:T(8,128)(2,1)}, u32[]{:S(2)}) copy-start(bf16[128,2048]{1,0:T(8,128)(2,1)} %refs_1_.3) | copy-start | bytes 1572868
  0.6 6.3 %copy-start.4 = (s32[128,1]{0,1:T(1,128)S(1)}, s32[128,1]{0,1:T(1,128)}, u32[]{:S(2)}) copy-start(s32[128,1]{0,1:T(1,128)} %param.9) | copy-start | bytes 1540
  0.7 8.7 %copy-start.3 = (s32[8]{0:T(128)S(1)}, s32[8]{0:T(128)}, u32[]{:S(2)}) copy-start(s32[8]{0:T(128)} %refs_1_.2) | copy-start | bytes 100
  1.9 20.6 %collective-permute-start.7 = (bf16[512,768]{1,0:T(8,128)(2,1)S(1)}, bf16[512,768]{1,0:T(8,128)(2,1)S(1)}, u32[]{:S(2)}, u32[]{:S(2)}) collective-permute-start(bf16[512,768]{1,0:T(8,128)(2,1)S(1)} %pad_maximum_fusion.refs_2_.refs_6_), channel_id=1, source_target_pairs={{0,16},{8,24},{16,0},{24,8},{1,17},{9,25},{17,1},{25,9},{2,18},{10... | collective-permute-start | bytes 2359304 | tf_op jit(solution)/shard_map/ppermute | solution.py:215
  4.9 20.0 %collective-permute-start.6 = (bf16[512,768]{1,0:T(8,128)(2,1)S(1)}, bf16[512,768]{1,0:T(8,128)(2,1)S(1)}, u32[]{:S(2)}, u32[]{:S(2)}) collective-permute-start(bf16[512,768]{1,0:T(8,128)(2,1)S(1)} %pad_maximum_fusion.refs_2_.refs_6_), channel_id=1, source_target_pairs={{0,8},{8,0},{16,24},{24,16},{1,9},{9,1},{17,25},{25,17},{2,10},{10... | collective-permute-start | bytes 2359304 | tf_op jit(solution)/shard_map/ppermute | solution.py:215
  6.4 2.9 %collective-permute-start.1 = (bf16[128,2048]{1,0:T(8,128)(2,1)}, bf16[128,2048]{1,0:T(8,128)(2,1)}, u32[]{:S(2)}, u32[]{:S(2)}) collective-permute-start(bf16[128,2048]{1,0:T(8,128)(2,1)} %refs_4_.1), channel_id=1, source_target_pairs={{0,1},{1,0},{2,3},{3,2},{4,5},{5,4},{6,7},{7,6},{8,9},{9,8},{10,11... | collective-permute-start | bytes 1572872 | tf_op jit(solution)/shard_map/ppermute | solution.py:218
  6.4 2.9 %collective-permute-start.2 = (bf16[128,2048]{1,0:T(8,128)(2,1)S(1)}, bf16[128,2048]{1,0:T(8,128)(2,1)S(1)}, u32[]{:S(2)}, u32[]{:S(2)}) collective-permute-start(bf16[128,2048]{1,0:T(8,128)(2,1)S(1)} %copy-done), channel_id=1, source_target_pairs={{0,1},{1,0},{2,3},{3,2},{4,5},{5,4},{6,7},{7,6},{8,9},{9,8},{10,11... | collective-permute-start | bytes 1572872 | tf_op jit(solution)/shard_map/ppermute | solution.py:218
  6.9 2.1 %collective-permute-start = (s32[1,128]{1,0:T(1,128)S(1)}, s32[1,128]{1,0:T(1,128)S(1)}, u32[]{:S(2)}, u32[]{:S(2)}) collective-permute-start(s32[1,128]{1,0:T(1,128)S(1)} %bitcast.9), channel_id=1, source_target_pairs={{0,1},{1,0},{2,3},{3,2},{4,5},{5,4},{6,7},{7,6},{8,9},{9,8},{10,11... | collective-permute-start | bytes 1544 | tf_op jit(solution)/shard_map/ppermute | solution.py:218
  11.9 13.8 %copy-start.1 = (bf16[48,2048]{1,0:T(8,128)(2,1)}, bf16[48,2048]{1,0:T(8,128)(2,1)S(1)}, u32[]{:S(2)}) copy-start(bf16[48,2048]{1,0:T(8,128)(2,1)S(1)} %get-tuple-element.37.refs_1_) | copy-start | bytes 589828
  11.9 17.4 %collective-permute-start.4 = (bf16[48,2048]{1,0:T(8,128)(2,1)}, bf16[48,2048]{1,0:T(8,128)(2,1)}, u32[]{:S(2)}, u32[]{:S(2)}) collective-permute-start(bf16[48,2048]{1,0:T(8,128)(2,1)} %get-tuple-element.39), channel_id=1, source_target_pairs={{0,4},{1,5},{2,6},{3,7},{4,0},{5,1},{6,2},{7,3},{8,12},{9,13},{10,... | collective-permute-start | bytes 589832 | tf_op jit(solution)/shard_map/ppermute | solution.py:218
  14.5 14.8 %collective-permute-start.5 = (bf16[48,2048]{1,0:T(8,128)(2,1)}, bf16[48,2048]{1,0:T(8,128)(2,1)}, u32[]{:S(2)}, u32[]{:S(2)}) collective-permute-start(bf16[48,2048]{1,0:T(8,128)(2,1)} %get-tuple-element.40), channel_id=1, source_target_pairs={{0,6},{1,7},{2,4},{3,5},{4,2},{5,3},{6,0},{7,1},{8,14},{9,15},{10,... | collective-permute-start | bytes 589832 | tf_op jit(solution)/shard_map/ppermute | solution.py:218
  15.9 18.2 %collective-permute-start.3 = (bf16[96,2048]{1,0:T(8,128)(2,1)}, bf16[96,2048]{1,0:T(8,128)(2,1)}, u32[]{:S(2)}, u32[]{:S(2)}) collective-permute-start(bf16[96,2048]{1,0:T(8,128)(2,1)} %get-tuple-element.38), channel_id=1, source_target_pairs={{0,2},{1,3},{2,0},{3,1},{4,6},{5,7},{6,4},{7,5},{8,10},{9,11},{10,... | collective-permute-start | bytes 1179656 | tf_op jit(solution)/shard_map/ppermute | solution.py:218
  23.2 16.4 %collective-permute-start.9 = (bf16[256,768]{1,0:T(8,128)(2,1)}, bf16[256,768]{1,0:T(8,128)(2,1)}, u32[]{:S(2)}, u32[]{:S(2)}) collective-permute-start(bf16[256,768]{1,0:T(8,128)(2,1)} %slice.9), channel_id=1, source_target_pairs={{0,8},{8,0},{16,24},{24,16},{1,9},{9,1},{17,25},{25,17},{2,10},{10... | collective-permute-start | bytes 1179656 | tf_op jit(solution)/shard_map/ppermute | solution.py:215
  25.7 14.4 %collective-permute-start.8 = (bf16[256,768]{1,0:T(8,128)(2,1)}, bf16[256,768]{1,0:T(8,128)(2,1)}, u32[]{:S(2)}, u32[]{:S(2)}) collective-permute-start(bf16[256,768]{1,0:T(8,128)(2,1)} %slice.8), channel_id=1, source_target_pairs={{0,16},{8,24},{16,0},{24,8},{1,17},{9,25},{17,1},{25,9},{2,18},{10... | collective-permute-start | bytes 1179656 | tf_op jit(solution)/shard_map/ppermute | solution.py:215
  27.8 6.3 %copy-start.2 = (bf16[48,2048]{1,0:T(8,128)(2,1)S(1)}, bf16[48,2048]{1,0:T(8,128)(2,1)}, u32[]{:S(2)}) copy-start(bf16[48,2048]{1,0:T(8,128)(2,1)} %copy-done.1) | copy-start | bytes 589828
  35.4 15.9 %collective-permute-start.10 = (bf16[48,2048]{1,0:T(8,128)(2,1)S(1)}, bf16[48,2048]{1,0:T(8,128)(2,1)S(1)}, u32[]{:S(2)}, u32[]{:S(2)}) collective-permute-start(bf16[48,2048]{1,0:T(8,128)(2,1)S(1)} %get-tuple-element.50), channel_id=1, source_target_pairs={{0,4},{1,5},{2,6},{3,7},{4,0},{5,1},{6,2},{7,3},{8,12},{9,13},{10,... | collective-permute-start | bytes 589832 | tf_op jit(solution)/shard_map/ppermute | solution.py:218
  37.0 14.2 %collective-permute-start.11 = (bf16[48,2048]{1,0:T(8,128)(2,1)S(1)}, bf16[48,2048]{1,0:T(8,128)(2,1)S(1)}, u32[]{:S(2)}, u32[]{:S(2)}) collective-permute-start(bf16[48,2048]{1,0:T(8,128)(2,1)S(1)} %get-tuple-element.51), channel_id=1, source_target_pairs={{0,6},{1,7},{2,4},{3,5},{4,2},{5,3},{6,0},{7,1},{8,14},{9,15},{10,... | collective-permute-start | bytes 589832 | tf_op jit(solution)/shard_map/ppermute | solution.py:218
  39.0 12.2 %collective-permute-start.12 = (bf16[288,512]{1,0:T(8,128)(2,1)S(1)}, bf16[288,512]{1,0:T(8,128)(2,1)S(1)}, u32[]{:S(2)}, u32[]{:S(2)}) collective-permute-start(bf16[288,512]{1,0:T(8,128)(2,1)S(1)} %get-tuple-element.52), channel_id=1, source_target_pairs={{0,8},{8,0},{16,24},{24,16},{1,9},{9,1},{17,25},{25,17},{2,10},{10... | collective-permute-start | bytes 884744 | tf_op jit(solution)/shard_map/ppermute | solution.py:215
  39.6 13.3 %collective-permute-start.13 = (bf16[288,512]{1,0:T(8,128)(2,1)S(1)}, bf16[288,512]{1,0:T(8,128)(2,1)S(1)}, u32[]{:S(2)}, u32[]{:S(2)}) collective-permute-start(bf16[288,512]{1,0:T(8,128)(2,1)S(1)} %get-tuple-element.53), channel_id=1, source_target_pairs={{0,16},{8,24},{16,0},{24,8},{1,17},{9,25},{17,1},{25,9},{2,18},{10... | collective-permute-start | bytes 884744 | tf_op jit(solution)/shard_map/ppermute | solution.py:215
  40.1 12.8 %collective-permute-start.14 = (bf16[288,512]{1,0:T(8,128)(2,1)S(1)}, bf16[288,512]{1,0:T(8,128)(2,1)S(1)}, u32[]{:S(2)}, u32[]{:S(2)}) collective-permute-start(bf16[288,512]{1,0:T(8,128)(2,1)S(1)} %get-tuple-element.54), channel_id=1, source_target_pairs={{0,24},{8,16},{16,8},{24,0},{1,25},{9,17},{17,9},{25,1},{2,26},{10... | collective-permute-start | bytes 884744 | tf_op jit(solution)/shard_map/ppermute | solution.py:215
  55.6 7.8 %collective-permute-start.15 = (bf16[48,2048]{1,0:T(8,128)(2,1)S(1)}, bf16[48,2048]{1,0:T(8,128)(2,1)S(1)}, u32[]{:S(2)}, u32[]{:S(2)}) collective-permute-start(bf16[48,2048]{1,0:T(8,128)(2,1)S(1)} %get-tuple-element.56), channel_id=1, source_target_pairs={{0,2},{1,3},{2,0},{3,1},{4,6},{5,7},{6,4},{7,5},{8,10},{9,11},{10,... | collective-permute-start | bytes 589832 | tf_op jit(solution)/shard_map/ppermute | solution.py:218
  57.9 20.2 %collective-permute-start.18 = (bf16[384,512]{1,0:T(8,128)(2,1)S(1)}, bf16[384,512]{1,0:T(8,128)(2,1)S(1)}, u32[]{:S(2)}, u32[]{:S(2)}) collective-permute-start(bf16[384,512]{1,0:T(8,128)(2,1)S(1)} %get-tuple-element.59), channel_id=1, source_target_pairs={{0,8},{8,0},{16,24},{24,16},{1,9},{9,1},{17,25},{25,17},{2,10},{10... | collective-permute-start | bytes 1179656 | tf_op jit(solution)/shard_map/ppermute | solution.py:215
  58.5 19.7 %collective-permute-start.19 = (bf16[384,512]{1,0:T(8,128)(2,1)S(1)}, bf16[384,512]{1,0:T(8,128)(2,1)S(1)}, u32[]{:S(2)}, u32[]{:S(2)}) collective-permute-start(bf16[384,512]{1,0:T(8,128)(2,1)S(1)} %get-tuple-element.60), channel_id=1, source_target_pairs={{0,16},{8,24},{16,0},{24,8},{1,17},{9,25},{17,1},{25,9},{2,18},{10... | collective-permute-start | bytes 1179656 | tf_op jit(solution)/shard_map/ppermute | solution.py:215
  59.0 19.2 %collective-permute-start.20 = (bf16[384,512]{1,0:T(8,128)(2,1)S(1)}, bf16[384,512]{1,0:T(8,128)(2,1)S(1)}, u32[]{:S(2)}, u32[]{:S(2)}) collective-permute-start(bf16[384,512]{1,0:T(8,128)(2,1)S(1)} %get-tuple-element.61), channel_id=1, source_target_pairs={{0,24},{8,16},{16,8},{24,0},{1,25},{9,17},{17,9},{25,1},{2,26},{10... | collective-permute-start | bytes 1179656 | tf_op jit(solution)/shard_map/ppermute | solution.py:215
  61.4 16.7 %collective-permute-start.16 = (bf16[48,2048]{1,0:T(8,128)(2,1)S(1)}, bf16[48,2048]{1,0:T(8,128)(2,1)S(1)}, u32[]{:S(2)}, u32[]{:S(2)}) collective-permute-start(bf16[48,2048]{1,0:T(8,128)(2,1)S(1)} %get-tuple-element.57), channel_id=1, source_target_pairs={{0,4},{1,5},{2,6},{3,7},{4,0},{5,1},{6,2},{7,3},{8,12},{9,13},{10,... | collective-permute-start | bytes 589832 | tf_op jit(solution)/shard_map/ppermute | solution.py:218
  63.4 14.8 %collective-permute-start.17 = (bf16[48,2048]{1,0:T(8,128)(2,1)S(1)}, bf16[48,2048]{1,0:T(8,128)(2,1)S(1)}, u32[]{:S(2)}, u32[]{:S(2)}) collective-permute-start(bf16[48,2048]{1,0:T(8,128)(2,1)S(1)} %get-tuple-element.58), channel_id=1, source_target_pairs={{0,6},{1,7},{2,4},{3,5},{4,2},{5,3},{6,0},{7,1},{8,14},{9,15},{10,... | collective-permute-start | bytes 589832 | tf_op jit(solution)/shard_map/ppermute | solution.py:218
  78.7 2.0 %collective-permute-start.21 = (bf16[128,2048]{1,0:T(8,128)(2,1)S(1)}, bf16[128,2048]{1,0:T(8,128)(2,1)S(1)}, u32[]{:S(2)}, u32[]{:S(2)}) collective-permute-start(bf16[128,2048]{1,0:T(8,128)(2,1)S(1)} %get-tuple-element.63), channel_id=1, source_target_pairs={{0,1},{1,0},{2,3},{3,2},{4,5},{5,4},{6,7},{7,6},{8,9},{9,8},{10,11... | collective-permute-start | bytes 1572872 | tf_op jit(solution)/shard_map/ppermute | solution.py:218

commit v11 on v10

--- a/solution.py
+++ b/solution.py
@@ -11,6 +11,7 @@
 SMEM = pl.BlockSpec(memory_space=pltpu.SMEM)
 ANY = pl.BlockSpec(memory_space=pl.ANY)
 MIB = 1024 * 1024
+AHEAD = 1 << 33
 BF16 = jnp.bfloat16
 F32 = jnp.float32
 
@@ -230,8 +231,7 @@
         [pltpu.VMEM((2 * tok_rows, model_width), BF16)],
     )(rank, host, route, route_b, tokens, tokens_b, cotangent, cotangent_b)
     far_x = [over_rep(far_xa, 4), over_rep(far_xb, 6)]
-    far_x = after(far_x, ahead=1<<31)
-    near = over_rep(near, 2)
+    near, *far_x = after([over_rep(near, 2), *far_x], ahead=1<<31)
     own_dy, far_a, far_b = call(pack_more_kernel, [shape(block, model_width)] * 3)(pick, cotangent, cotangent_b)
     joined_3 = [over_own(joined_1[: depth // 2], 2), over_own(joined_2[depth // 2 :], 1)]
     joined_3 = after(joined_3, ahead=1<<33)
@@ -252,10 +252,13 @@
         [slot_rows],
         earlier=pieces[1:],
     )(own, acts, own_dy, near, *far_dy, *weights)
-    returned = [back[0]] + [over_rep(back[k], 2 * k) for k in range(1, parts)]
-    messages = [own_message, over_own(message_1, 1), over_own(message_2, 2), over_own(message_3, 3)]
-
-    mine, other = call(unpack_kernel, [shape(tok_rows, model_width)] * 2, 0, [slot_rows], earlier=messages[1:])(
+    far_back = after([over_rep(back[2], 4), over_rep(back[3], 6)], ahead=AHEAD)
+    returned = [back[0], over_rep(back[1], 2), *far_back]
+    message_3 = after([message_3], returned[1])[0]
+    messages = after([over_own(message_1, 1), over_own(message_2, 2), over_own(message_3, 3)], ahead=AHEAD)
+    messages = [own_message, *messages]
+
+    mine, other = call(unpack_kernel, [shape(tok_rows, model_width)] * 2, 0, [slot_rows])(
         pick, *returned
     )
     x_grad = mine + over_rep(other, 1)

time: 83 us -> 80.7 us (0.972); the launches traced: 81.6 us -> 80.5 us
  starting transfers between devices: 30.7 us -> 26.5 us
  waiting for transfers between devices: 35.4 us -> 38.4 us
    ppermute x12, starting transfers between devices: 15.9 us -> 13.8 us  [over_rep(): return lax.ppermute(value, 'rep', [(i, i ^ k) for i in range(n_rep)])]
    ppermute x10, waiting for transfers between devices: 7.98 us -> 10.1 us  [over_own(): return lax.ppermute(value, 'own', [(i, i ^ k) for i in range(4)])]
    ppermute x10, starting transfers between devices: 14.7 us -> 12.7 us  [over_own(): return lax.ppermute(value, 'own', [(i, i ^ k) for i in range(4)])]
    ppermute x12, waiting for transfers between devices: 27.4 us -> 28.3 us  [over_rep(): return lax.ppermute(value, 'rep', [(i, i ^ k) for i in range(n_rep)])]
where the time goes in v11:
time: 80.7 us; the launch traced here: 80.5 us
  waiting for transfers between devices  38.4 us (48%)
  starting transfers between devices  26.5 us (33%)
  Pallas kernels  11.1 us (14%)
  other arithmetic  2.14 us (3%)
  local copies, waits for them, and re-layouts  1.56 us (2%)
    ppermute x12, waiting for transfers between devices, over_rep(): return lax.ppermute(value, 'rep', [(i, i ^ k) for i in range(n_rep)])  28.3 us
    ppermute x12, starting transfers between devices, over_rep(): return lax.ppermute(value, 'rep', [(i, i ^ k) for i in range(n_rep)])  13.8 us
    ppermute x10, starting transfers between devices, over_own(): return lax.ppermute(value, 'own', [(i, i ^ k) for i in range(4)])  12.7 us
    pallas_call x7, Pallas kernels, run(): pl.pallas_call(body, out_shape=outs, in_specs=[SMEM] * scalars + [VMEM] *...  11.1 us
    ppermute x10, waiting for transfers between devices, over_own(): return lax.ppermute(value, 'own', [(i, i ^ k) for i in range(4)])  10.1 us
  transfers between devices with their start and end apart: 22, of which 9 were waited for; matrix products, arithmetic and copies ran while one was open for 2% of the time, Pallas kernels for 10%

profile of v11, /device:TPU:0, one launch (start us, length us, event | category | flops | bytes accessed | tf_op | source)
XLA Modules:
  0.0 80.5 jit_solution(9141953440941786340)
XLA Ops:
  0.6 0.0 copy-start
  0.6 0.0 copy-start.4
  0.7 0.0 copy-start.3
  0.7 1.2 %pad_maximum_fusion.refs_2_.refs_6_ = bf16[512,768]{1,0:T(8,128)(2,1)S(1)} fusion(bf16[512,256]{1,0:T(8,128)(2,1)} %bitcast.11, bf16[512,256]{1,0:T(8,128)(2,1)} %bitcast.12, bf16[512,256]{1,0:T(8,128)(2,1)} %bitcast.13), kind=kLoop, calls=%fused_computation | loop fusion | flops 2359296 | bytes 1572864 | tf_op jit(solution)/shard_map/concatenate | solution.py:223
  1.9 3.0 %collective-permute-start.7 = (bf16[512,768]{1,0:T(8,128)(2,1)S(1)}, bf16[512,768]{1,0:T(8,128)(2,1)S(1)}, u32[]{:S(2)}, u32[]{:S(2)}) collective-permute-start(bf16[512,768]{1,0:T(8,128)(2,1)S(1)} %pad_maximum_fusion.refs_2_.refs_6_), channel_id=1, source_target_pairs={{0,16},{8,24},{16,0},{24,8},{1,17},{9,25},{17,1},{25,9},{2,18},{10... | collective-permute-start | bytes 2359304 | tf_op jit(solution)/shard_map/ppermute | solution.py:216
  4.9 1.5 %collective-permute-start.6 = (bf16[512,768]{1,0:T(8,128)(2,1)S(1)}, bf16[512,768]{1,0:T(8,128)(2,1)S(1)}, u32[]{:S(2)}, u32[]{:S(2)}) collective-permute-start(bf16[512,768]{1,0:T(8,128)(2,1)S(1)} %pad_maximum_fusion.refs_2_.refs_6_), channel_id=1, source_target_pairs={{0,8},{8,0},{16,24},{24,16},{1,9},{9,1},{17,25},{25,17},{2,10},{10... | collective-permute-start | bytes 2359304 | tf_op jit(solution)/shard_map/ppermute | solution.py:216
  6.4 0.0 collective-permute-start.1
  6.4 0.0 copy-done
  6.4 0.5 collective-permute-start.2
  6.9 0.0 copy-done.4
  6.9 0.1 collective-permute-start
  7.0 2.1 %collective-permute-done.refs_3_ = s32[1,128]{1,0:T(1,128)S(1)} collective-permute-done((s32[1,128]{1,0:T(1,128)S(1)}, s32[1,128]{1,0:T(1,128)S(1)}, u32[]{:S(2)}, u32[]{:S(2)}) %collective-permute-start) | collective-permute-done | bytes 544 | tf_op jit(solution)/shard_map/ppermute | solution.py:219
  9.1 0.3 collective-permute-done.1.refs_5_
  9.3 0.0 collective-permute-done.2.refs_7_.refs_2_
  9.3 0.0 copy-done.3
  9.3 2.6 %shard_map.102 = (bf16[192,256]{1,0:T(8,128)(2,1)S(1)}, bf16[48,2048]{1,0:T(8,128)(2,1)S(1)}, bf16[96,2048]{1,0:T(8,128)(2,1)}, bf16[48,2048]{1,0:T(8,128)(2,1)}, bf16[48,2048]{1,0:T(8,128)(2,1)}) custom-call(s32[1]{0:T(128)} %bitcast.refs_0_, s32[8]{0:T(128)S(1)} %copy-done.3, s32[1,128]{1,0:T(1,128)S(1)} %bitcast.10, ...), custom_call_target="tpu_custom_call" | custom-call | bytes 3179556 | tf_op jit(solution)/shard_map/pallas_call | solution.py:38
  11.9 1.6 %collective-permute-start.3 = (bf16[96,2048]{1,0:T(8,128)(2,1)}, bf16[96,2048]{1,0:T(8,128)(2,1)}, u32[]{:S(2)}, u32[]{:S(2)}) collective-permute-start(bf16[96,2048]{1,0:T(8,128)(2,1)} %get-tuple-element.44), channel_id=1, source_target_pairs={{0,2},{1,3},{2,0},{3,1},{4,6},{5,7},{6,4},{7,5},{8,10},{9,11},{10,... | collective-permute-start | bytes 1179656 | tf_op jit(solution)/shard_map/ppermute | solution.py:219
  13.5 2.6 %collective-permute-start.4 = (bf16[48,2048]{1,0:T(8,128)(2,1)}, bf16[48,2048]{1,0:T(8,128)(2,1)}, u32[]{:S(2)}, u32[]{:S(2)}) collective-permute-start(bf16[48,2048]{1,0:T(8,128)(2,1)} %get-tuple-element.45), channel_id=1, source_target_pairs={{0,4},{1,5},{2,6},{3,7},{4,0},{5,1},{6,2},{7,3},{8,12},{9,13},{10,... | collective-permute-start | bytes 589832 | tf_op jit(solution)/shard_map/ppermute | solution.py:219
  16.1 0.2 collective-permute-start.5
  16.3 6.1 %collective-permute-done.7.refs_4_.refs_8_ = bf16[512,768]{1,0:T(8,128)(2,1)S(1)} collective-permute-done((bf16[512,768]{1,0:T(8,128)(2,1)S(1)}, bf16[512,768]{1,0:T(8,128)(2,1)S(1)}, u32[]{:S(2)}, u32[]{:S(2)}) %collective-permute-start.7) | collective-permute-done | bytes 786464 | tf_op jit(solution)/shard_map/ppermute | solution.py:216
  22.5 0.8 slice.9
  23.2 1.7 %collective-permute-start.9 = (bf16[256,768]{1,0:T(8,128)(2,1)}, bf16[256,768]{1,0:T(8,128)(2,1)}, u32[]{:S(2)}, u32[]{:S(2)}) collective-permute-start(bf16[256,768]{1,0:T(8,128)(2,1)} %slice.9), channel_id=1, source_target_pairs={{0,8},{8,0},{16,24},{24,16},{1,9},{9,1},{17,25},{25,17},{2,10},{10... | collective-permute-start | bytes 1179656 | tf_op jit(solution)/shard_map/ppermute | solution.py:216
  24.9 0.0 collective-permute-done.6.refs_3_.refs_7_
  24.9 0.8 slice.8
  25.7 0.0 copy-done.1
  25.7 1.5 %collective-permute-start.8 = (bf16[256,768]{1,0:T(8,128)(2,1)}, bf16[256,768]{1,0:T(8,128)(2,1)}, u32[]{:S(2)}, u32[]{:S(2)}) collective-permute-start(bf16[256,768]{1,0:T(8,128)(2,1)} %slice.8), channel_id=1, source_target_pairs={{0,16},{8,24},{16,0},{24,8},{1,17},{9,25},{17,1},{25,9},{2,18},{10... | collective-permute-start | bytes 1179656 | tf_op jit(solution)/shard_map/ppermute | solution.py:216
  27.2 0.5 shard_map.104
  27.8 0.0 copy-start.2
  27.8 0.0 collective-permute-done.4.refs_1_
  27.8 6.2 %collective-permute-done.5.refs_2_ = bf16[48,2048]{1,0:T(8,128)(2,1)} collective-permute-done((bf16[48,2048]{1,0:T(8,128)(2,1)}, bf16[48,2048]{1,0:T(8,128)(2,1)}, u32[]{:S(2)}, u32[]{:S(2)}) %collective-permute-start.5) | collective-permute-done | bytes 196640 | tf_op jit(solution)/shard_map/ppermute | solution.py:219
  34.0 0.0 collective-permute-done.3.refs_0_
  34.0 0.0 copy-done.2
  34.0 1.3 %shard_map.105 = (bf16[192,2048]{1,0:T(8,128)(2,1)S(1)}, bf16[288,512]{1,0:T(8,128)(2,1)S(1)}, bf16[288,512]{1,0:T(8,128)(2,1)S(1)}, bf16[288,512]{1,0:T(8,128)(2,1)S(1)}, bf16[288,512]{1,0:T(8,128)(2,1)S(1)}) custom-call(s32[1]{0:T(128)} %bitcast.2.refs_0_, bf16[48,2048]{1,0:T(8,128)(2,1)S(1)} %copy-done.2, ...), custom_call_target="tpu_custom_call" | custom-call | bytes 3145732 | tf_op jit(solution)/shard_map/pallas_call | solution.py:38
  35.3 1.7 %collective-permute-start.10 = (bf16[48,2048]{1,0:T(8,128)(2,1)S(1)}, bf16[48,2048]{1,0:T(8,128)(2,1)S(1)}, u32[]{:S(2)}, u32[]{:S(2)}) collective-permute-start(bf16[48,2048]{1,0:T(8,128)(2,1)S(1)} %get-tuple-element.57), channel_id=1, source_target_pairs={{0,4},{1,5},{2,6},{3,7},{4,0},{5,1},{6,2},{7,3},{8,12},{9,13},{10,... | collective-permute-start | bytes 589832 | tf_op jit(solution)/shard_map/ppermute | solution.py:219
  37.0 1.4 %collective-permute-start.11 = (bf16[48,2048]{1,0:T(8,128)(2,1)S(1)}, bf16[48,2048]{1,0:T(8,128)(2,1)S(1)}, u32[]{:S(2)}, u32[]{:S(2)}) collective-permute-start(bf16[48,2048]{1,0:T(8,128)(2,1)S(1)} %get-tuple-element.58), channel_id=1, source_target_pairs={{0,6},{1,7},{2,4},{3,5},{4,2},{5,3},{6,0},{7,1},{8,14},{9,15},{10,... | collective-permute-start | bytes 589832 | tf_op jit(solution)/shard_map/ppermute | solution.py:219
  38.4 0.5 collective-permute-start.12
  38.9 0.0 collective-permute-done.9.refs_1_
  38.9 0.5 collective-permute-start.13
  39.4 0.0 collective-permute-done.8.refs_0_
  39.4 2.5 %collective-permute-start.14 = (bf16[288,512]{1,0:T(8,128)(2,1)S(1)}, bf16[288,512]{1,0:T(8,128)(2,1)S(1)}, u32[]{:S(2)}, u32[]{:S(2)}) collective-permute-start(bf16[288,512]{1,0:T(8,128)(2,1)S(1)} %get-tuple-element.61), channel_id=1, source_target_pairs={{0,24},{8,16},{16,8},{24,0},{1,25},{9,17},{17,9},{25,1},{2,26},{10... | collective-permute-start | bytes 884744 | tf_op jit(solution)/shard_map/ppermute | solution.py:216
  41.9 1.7 %shard_map.107.refs_1_ = f32[192,512]{1,0:T(8,128)S(1)} custom-call(s32[1]{0:T(128)} %bitcast.2.refs_0_, bf16[192,2048]{1,0:T(8,128)(2,1)S(1)} %get-tuple-element.51.refs_1_, bf16[512,768]{1,0:T(8,128)(2,1)S(1)} %pad_maximum_fusion.refs_2_.refs_6_, bf16[512,768]{1,0:T(8,128)(2,1)S(1)} %collective-permute-done.6.refs_3_.refs_7_, ...), custom_call_target="tpu_custom_call" | custom-call | bytes 4325380 | tf_op jit(solution)/shard_map/pallas_call | solution.py:38
  43.6 6.8 %collective-permute-done.10.refs_4_ = bf16[48,2048]{1,0:T(8,128)(2,1)S(1)} collective-permute-done((bf16[48,2048]{1,0:T(8,128)(2,1)S(1)}, bf16[48,2048]{1,0:T(8,128)(2,1)S(1)}, u32[]{:S(2)}, u32[]{:S(2)}) %collective-permute-start.10) | collective-permute-done | bytes 196640 | tf_op jit(solution)/shard_map/ppermute | solution.py:219
  50.4 0.0 collective-permute-done.11.refs_5_
  50.4 0.0 collective-permute-done.12.refs_11_.refs_1_
  50.4 0.9 %collective-permute-done.13.refs_12_.refs_2_ = bf16[288,512]{1,0:T(8,128)(2,1)S(1)} collective-permute-done((bf16[288,512]{1,0:T(8,128)(2,1)S(1)}, bf16[288,512]{1,0:T(8,128)(2,1)S(1)}, u32[]{:S(2)}, u32[]{:S(2)}) %collective-permute-start.13) | collective-permute-done | bytes 294944 | tf_op jit(solution)/shard_map/ppermute | solution.py:216
  51.3 0.0 collective-permute-done.14.refs_13_.refs_3_
  51.3 2.7 %shard_map.109 = (bf16[48,2048]{1,0:T(8,128)(2,1)S(1)}, bf16[48,2048]{1,0:T(8,128)(2,1)S(1)}, bf16[48,2048]{1,0:T(8,128)(2,1)S(1)}, bf16[48,2048]{1,0:T(8,128)(2...) custom-call(s32[1]{0:T(128)} %bitcast.2.refs_0_, ...), custom_call_target="tpu_custom_call" | custom-call | bytes 6881284 | tf_op jit(solution)/shard_map/pallas_call | solution.py:38
  54.0 3.1 %collective-permute-start.15 = (bf16[48,2048]{1,0:T(8,128)(2,1)S(1)}, bf16[48,2048]{1,0:T(8,128)(2,1)S(1)}, u32[]{:S(2)}, u32[]{:S(2)}) collective-permute-start(bf16[48,2048]{1,0:T(8,128)(2,1)S(1)} %get-tuple-element.63), channel_id=1, source_target_pairs={{0,2},{1,3},{2,0},{3,1},{4,6},{5,7},{6,4},{7,5},{8,10},{9,11},{10,... | collective-permute-start | bytes 589832 | tf_op jit(solution)/shard_map/ppermute | solution.py:219
  57.1 1.3 %collective-permute-start.16 = (bf16[48,2048]{1,0:T(8,128)(2,1)S(1)}, bf16[48,2048]{1,0:T(8,128)(2,1)S(1)}, u32[]{:S(2)}, u32[]{:S(2)}) collective-permute-start(bf16[48,2048]{1,0:T(8,128)(2,1)S(1)} %get-tuple-element.64), channel_id=1, source_target_pairs={{0,4},{1,5},{2,6},{3,7},{4,0},{5,1},{6,2},{7,3},{8,12},{9,13},{10,... | collective-permute-start | bytes 589832 | tf_op jit(solution)/shard_map/ppermute | solution.py:219
  58.3 1.4 %collective-permute-start.17 = (bf16[48,2048]{1,0:T(8,128)(2,1)S(1)}, bf16[48,2048]{1,0:T(8,128)(2,1)S(1)}, u32[]{:S(2)}, u32[]{:S(2)}) collective-permute-start(bf16[48,2048]{1,0:T(8,128)(2,1)S(1)} %get-tuple-element.65), channel_id=1, source_target_pairs={{0,6},{1,7},{2,4},{3,5},{4,2},{5,3},{6,0},{7,1},{8,14},{9,15},{10,... | collective-permute-start | bytes 589832 | tf_op jit(solution)/shard_map/ppermute | solution.py:219
  59.7 0.5 collective-permute-start.19
  60.2 0.5 collective-permute-start.20
  60.7 3.3 %collective-permute-done.15.refs_2_.refs_1_ = bf16[48,2048]{1,0:T(8,128)(2,1)S(1)} collective-permute-done((bf16[48,2048]{1,0:T(8,128)(2,1)S(1)}, bf16[48,2048]{1,0:T(8,128)(2,1)S(1)}, u32[]{:S(2)}, u32[]{:S(2)}) %collective-permute-start.15) | collective-permute-done | bytes 196640 | tf_op jit(solution)/shard_map/ppermute | solution.py:219
  64.0 0.4 collective-permute-start.21
  64.5 9.7 %collective-permute-done.16.refs_0_ = bf16[48,2048]{1,0:T(8,128)(2,1)S(1)} collective-permute-done((bf16[48,2048]{1,0:T(8,128)(2,1)S(1)}, bf16[48,2048]{1,0:T(8,128)(2,1)S(1)}, u32[]{:S(2)}, u32[]{:S(2)}) %collective-permute-start.16) | collective-permute-done | bytes 196640 | tf_op jit(solution)/shard_map/ppermute | solution.py:219
  74.2 0.0 collective-permute-done.17.refs_1_
  74.2 0.5 shard_map.111
  74.6 0.1 collective-permute-start.18
  74.7 0.0 collective-permute-done.19.refs_0_
  74.7 3.1 %collective-permute-done.20.refs_1_ = bf16[384,512]{1,0:T(8,128)(2,1)S(1)} collective-permute-done((bf16[384,512]{1,0:T(8,128)(2,1)S(1)}, bf16[384,512]{1,0:T(8,128)(2,1)S(1)}, u32[]{:S(2)}, u32[]{:S(2)}) %collective-permute-start.20) | collective-permute-done | bytes 393248 | tf_op jit(solution)/shard_map/ppermute | solution.py:216
  77.8 0.0 collective-permute-done.21.refs_2_
  77.8 1.8 %shard_map.114 = (f32[512,256]{1,0:T(8,128)}, f32[512,256]{1,0:T(8,128)}, f32[512,256]{1,0:T(8,128)}) custom-call(bf16[288,512]{1,0:T(8,128)(2,1)S(1)} %get-tuple-element.56.refs_2_.refs_0_, bf16[288,512]{1,0:T(8,128)(2,1)S(1)} %collective-permute-done.12.refs_11_.refs_1_, bf16[288,512]{1,0:T(8,128)(2,1)S(1)} %collective-permute-done.13.refs_12_.refs_2_, ...), custom_call_target="tpu_custom_call" | custom-call | bytes 4325376 | tf_op jit(solution)/shard_map/pallas_call | solution.py:38
  79.5 0.0 collective-permute-done.18
  79.6 0.9 %add.3 = bf16[128,2048]{1,0:T(8,128)(2,1)} add(bf16[128,2048]{1,0:T(8,128)(2,1)S(1)} %get-tuple-element.68, bf16[128,2048]{1,0:T(8,128)(2,1)S(1)} %collective-permute-done.18) | non-fusion elementwise | flops 262144 | bytes 1572864 | tf_op jit(solution)/shard_map/add | solution.py:264
  (7 shorter events, 0.0 us)
Async XLA Ops:
  0.6 5.8 %copy-start = (bf16[128,2048]{1,0:T(8,128)(2,1)S(1)}, bf16[128,2048]{1,0:T(8,128)(2,1)}, u32[]{:S(2)}) copy-start(bf16[128,2048]{1,0:T(8,128)(2,1)} %refs_1_.3) | copy-start | bytes 1572868
  0.6 6.3 %copy-start.4 = (s32[128,1]{0,1:T(1,128)S(1)}, s32[128,1]{0,1:T(1,128)}, u32[]{:S(2)}) copy-start(s32[128,1]{0,1:T(1,128)} %param.9) | copy-start | bytes 1540
  0.7 8.7 %copy-start.3 = (s32[8]{0:T(128)S(1)}, s32[8]{0:T(128)}, u32[]{:S(2)}) copy-start(s32[8]{0:T(128)} %refs_1_.2) | copy-start | bytes 100
  1.9 20.6 %collective-permute-start.7 = (bf16[512,768]{1,0:T(8,128)(2,1)S(1)}, bf16[512,768]{1,0:T(8,128)(2,1)S(1)}, u32[]{:S(2)}, u32[]{:S(2)}) collective-permute-start(bf16[512,768]{1,0:T(8,128)(2,1)S(1)} %pad_maximum_fusion.refs_2_.refs_6_), channel_id=1, source_target_pairs={{0,16},{8,24},{16,0},{24,8},{1,17},{9,25},{17,1},{25,9},{2,18},{10... | collective-permute-start | bytes 2359304 | tf_op jit(solution)/shard_map/ppermute | solution.py:216
  4.9 20.0 %collective-permute-start.6 = (bf16[512,768]{1,0:T(8,128)(2,1)S(1)}, bf16[512,768]{1,0:T(8,128)(2,1)S(1)}, u32[]{:S(2)}, u32[]{:S(2)}) collective-permute-start(bf16[512,768]{1,0:T(8,128)(2,1)S(1)} %pad_maximum_fusion.refs_2_.refs_6_), channel_id=1, source_target_pairs={{0,8},{8,0},{16,24},{24,16},{1,9},{9,1},{17,25},{25,17},{2,10},{10... | collective-permute-start | bytes 2359304 | tf_op jit(solution)/shard_map/ppermute | solution.py:216
  6.4 2.9 %collective-permute-start.1 = (bf16[128,2048]{1,0:T(8,128)(2,1)}, bf16[128,2048]{1,0:T(8,128)(2,1)}, u32[]{:S(2)}, u32[]{:S(2)}) collective-permute-start(bf16[128,2048]{1,0:T(8,128)(2,1)} %refs_4_.1), channel_id=1, source_target_pairs={{0,1},{1,0},{2,3},{3,2},{4,5},{5,4},{6,7},{7,6},{8,9},{9,8},{10,11... | collective-permute-start | bytes 1572872 | tf_op jit(solution)/shard_map/ppermute | solution.py:219
  6.4 2.9 %collective-permute-start.2 = (bf16[128,2048]{1,0:T(8,128)(2,1)S(1)}, bf16[128,2048]{1,0:T(8,128)(2,1)S(1)}, u32[]{:S(2)}, u32[]{:S(2)}) collective-permute-start(bf16[128,2048]{1,0:T(8,128)(2,1)S(1)} %copy-done), channel_id=1, source_target_pairs={{0,1},{1,0},{2,3},{3,2},{4,5},{5,4},{6,7},{7,6},{8,9},{9,8},{10,11... | collective-permute-start | bytes 1572872 | tf_op jit(solution)/shard_map/ppermute | solution.py:219
  6.9 2.1 %collective-permute-start = (s32[1,128]{1,0:T(1,128)S(1)}, s32[1,128]{1,0:T(1,128)S(1)}, u32[]{:S(2)}, u32[]{:S(2)}) collective-permute-start(s32[1,128]{1,0:T(1,128)S(1)} %bitcast.9), channel_id=1, source_target_pairs={{0,1},{1,0},{2,3},{3,2},{4,5},{5,4},{6,7},{7,6},{8,9},{9,8},{10,11... | collective-permute-start | bytes 1544 | tf_op jit(solution)/shard_map/ppermute | solution.py:219
  11.9 13.8 %copy-start.1 = (bf16[48,2048]{1,0:T(8,128)(2,1)}, bf16[48,2048]{1,0:T(8,128)(2,1)S(1)}, u32[]{:S(2)}) copy-start(bf16[48,2048]{1,0:T(8,128)(2,1)S(1)} %get-tuple-element.43.refs_1_) | copy-start | bytes 589828
  11.9 22.0 %collective-permute-start.3 = (bf16[96,2048]{1,0:T(8,128)(2,1)}, bf16[96,2048]{1,0:T(8,128)(2,1)}, u32[]{:S(2)}, u32[]{:S(2)}) collective-permute-start(bf16[96,2048]{1,0:T(8,128)(2,1)} %get-tuple-element.44), channel_id=1, source_target_pairs={{0,2},{1,3},{2,0},{3,1},{4,6},{5,7},{6,4},{7,5},{8,10},{9,11},{10,... | collective-permute-start | bytes 1179656 | tf_op jit(solution)/shard_map/ppermute | solution.py:219
  13.5 14.3 %collective-permute-start.4 = (bf16[48,2048]{1,0:T(8,128)(2,1)}, bf16[48,2048]{1,0:T(8,128)(2,1)}, u32[]{:S(2)}, u32[]{:S(2)}) collective-permute-start(bf16[48,2048]{1,0:T(8,128)(2,1)} %get-tuple-element.45), channel_id=1, source_target_pairs={{0,4},{1,5},{2,6},{3,7},{4,0},{5,1},{6,2},{7,3},{8,12},{9,13},{10,... | collective-permute-start | bytes 589832 | tf_op jit(solution)/shard_map/ppermute | solution.py:219
  16.1 17.9 %collective-permute-start.5 = (bf16[48,2048]{1,0:T(8,128)(2,1)}, bf16[48,2048]{1,0:T(8,128)(2,1)}, u32[]{:S(2)}, u32[]{:S(2)}) collective-permute-start(bf16[48,2048]{1,0:T(8,128)(2,1)} %get-tuple-element.46), channel_id=1, source_target_pairs={{0,6},{1,7},{2,4},{3,5},{4,2},{5,3},{6,0},{7,1},{8,14},{9,15},{10,... | collective-permute-start | bytes 589832 | tf_op jit(solution)/shard_map/ppermute | solution.py:219
  23.2 15.7 %collective-permute-start.9 = (bf16[256,768]{1,0:T(8,128)(2,1)}, bf16[256,768]{1,0:T(8,128)(2,1)}, u32[]{:S(2)}, u32[]{:S(2)}) collective-permute-start(bf16[256,768]{1,0:T(8,128)(2,1)} %slice.9), channel_id=1, source_target_pairs={{0,8},{8,0},{16,24},{24,16},{1,9},{9,1},{17,25},{25,17},{2,10},{10... | collective-permute-start | bytes 1179656 | tf_op jit(solution)/shard_map/ppermute | solution.py:216
  25.7 13.7 %collective-permute-start.8 = (bf16[256,768]{1,0:T(8,128)(2,1)}, bf16[256,768]{1,0:T(8,128)(2,1)}, u32[]{:S(2)}, u32[]{:S(2)}) collective-permute-start(bf16[256,768]{1,0:T(8,128)(2,1)} %slice.8), channel_id=1, source_target_pairs={{0,16},{8,24},{16,0},{24,8},{1,17},{9,25},{17,1},{25,9},{2,18},{10... | collective-permute-start | bytes 1179656 | tf_op jit(solution)/shard_map/ppermute | solution.py:216
  27.8 6.2 %copy-start.2 = (bf16[48,2048]{1,0:T(8,128)(2,1)S(1)}, bf16[48,2048]{1,0:T(8,128)(2,1)}, u32[]{:S(2)}) copy-start(bf16[48,2048]{1,0:T(8,128)(2,1)} %copy-done.1) | copy-start | bytes 589828
  35.3 15.1 %collective-permute-start.10 = (bf16[48,2048]{1,0:T(8,128)(2,1)S(1)}, bf16[48,2048]{1,0:T(8,128)(2,1)S(1)}, u32[]{:S(2)}, u32[]{:S(2)}) collective-permute-start(bf16[48,2048]{1,0:T(8,128)(2,1)S(1)} %get-tuple-element.57), channel_id=1, source_target_pairs={{0,4},{1,5},{2,6},{3,7},{4,0},{5,1},{6,2},{7,3},{8,12},{9,13},{10,... | collective-permute-start | bytes 589832 | tf_op jit(solution)/shard_map/ppermute | solution.py:219
  37.0 13.4 %collective-permute-start.11 = (bf16[48,2048]{1,0:T(8,128)(2,1)S(1)}, bf16[48,2048]{1,0:T(8,128)(2,1)S(1)}, u32[]{:S(2)}, u32[]{:S(2)}) collective-permute-start(bf16[48,2048]{1,0:T(8,128)(2,1)S(1)} %get-tuple-element.58), channel_id=1, source_target_pairs={{0,6},{1,7},{2,4},{3,5},{4,2},{5,3},{6,0},{7,1},{8,14},{9,15},{10,... | collective-permute-start | bytes 589832 | tf_op jit(solution)/shard_map/ppermute | solution.py:219
  38.4 12.0 %collective-permute-start.12 = (bf16[288,512]{1,0:T(8,128)(2,1)S(1)}, bf16[288,512]{1,0:T(8,128)(2,1)S(1)}, u32[]{:S(2)}, u32[]{:S(2)}) collective-permute-start(bf16[288,512]{1,0:T(8,128)(2,1)S(1)} %get-tuple-element.59), channel_id=1, source_target_pairs={{0,8},{8,0},{16,24},{24,16},{1,9},{9,1},{17,25},{25,17},{2,10},{10... | collective-permute-start | bytes 884744 | tf_op jit(solution)/shard_map/ppermute | solution.py:216
  38.9 12.4 %collective-permute-start.13 = (bf16[288,512]{1,0:T(8,128)(2,1)S(1)}, bf16[288,512]{1,0:T(8,128)(2,1)S(1)}, u32[]{:S(2)}, u32[]{:S(2)}) collective-permute-start(bf16[288,512]{1,0:T(8,128)(2,1)S(1)} %get-tuple-element.60), channel_id=1, source_target_pairs={{0,16},{8,24},{16,0},{24,8},{1,17},{9,25},{17,1},{25,9},{2,18},{10... | collective-permute-start | bytes 884744 | tf_op jit(solution)/shard_map/ppermute | solution.py:216
  39.4 11.9 %collective-permute-start.14 = (bf16[288,512]{1,0:T(8,128)(2,1)S(1)}, bf16[288,512]{1,0:T(8,128)(2,1)S(1)}, u32[]{:S(2)}, u32[]{:S(2)}) collective-permute-start(bf16[288,512]{1,0:T(8,128)(2,1)S(1)} %get-tuple-element.61), channel_id=1, source_target_pairs={{0,24},{8,16},{16,8},{24,0},{1,25},{9,17},{17,9},{25,1},{2,26},{10... | collective-permute-start | bytes 884744 | tf_op jit(solution)/shard_map/ppermute | solution.py:216
  54.0 10.0 %collective-permute-start.15 = (bf16[48,2048]{1,0:T(8,128)(2,1)S(1)}, bf16[48,2048]{1,0:T(8,128)(2,1)S(1)}, u32[]{:S(2)}, u32[]{:S(2)}) collective-permute-start(bf16[48,2048]{1,0:T(8,128)(2,1)S(1)} %get-tuple-element.63), channel_id=1, source_target_pairs={{0,2},{1,3},{2,0},{3,1},{4,6},{5,7},{6,4},{7,5},{8,10},{9,11},{10,... | collective-permute-start | bytes 589832 | tf_op jit(solution)/shard_map/ppermute | solution.py:219
  57.1 17.1 %collective-permute-start.16 = (bf16[48,2048]{1,0:T(8,128)(2,1)S(1)}, bf16[48,2048]{1,0:T(8,128)(2,1)S(1)}, u32[]{:S(2)}, u32[]{:S(2)}) collective-permute-start(bf16[48,2048]{1,0:T(8,128)(2,1)S(1)} %get-tuple-element.64), channel_id=1, source_target_pairs={{0,4},{1,5},{2,6},{3,7},{4,0},{5,1},{6,2},{7,3},{8,12},{9,13},{10,... | collective-permute-start | bytes 589832 | tf_op jit(solution)/shard_map/ppermute | solution.py:219
  58.3 15.9 %collective-permute-start.17 = (bf16[48,2048]{1,0:T(8,128)(2,1)S(1)}, bf16[48,2048]{1,0:T(8,128)(2,1)S(1)}, u32[]{:S(2)}, u32[]{:S(2)}) collective-permute-start(bf16[48,2048]{1,0:T(8,128)(2,1)S(1)} %get-tuple-element.65), channel_id=1, source_target_pairs={{0,6},{1,7},{2,4},{3,5},{4,2},{5,3},{6,0},{7,1},{8,14},{9,15},{10,... | collective-permute-start | bytes 589832 | tf_op jit(solution)/shard_map/ppermute | solution.py:219
  59.7 15.0 %collective-permute-start.19 = (bf16[384,512]{1,0:T(8,128)(2,1)S(1)}, bf16[384,512]{1,0:T(8,128)(2,1)S(1)}, u32[]{:S(2)}, u32[]{:S(2)}) collective-permute-start(bf16[384,512]{1,0:T(8,128)(2,1)S(1)} %get-tuple-element.71), channel_id=1, source_target_pairs={{0,8},{8,0},{16,24},{24,16},{1,9},{9,1},{17,25},{25,17},{2,10},{10... | collective-permute-start | bytes 1179656 | tf_op jit(solution)/shard_map/ppermute | solution.py:216
  60.2 17.6 %collective-permute-start.20 = (bf16[384,512]{1,0:T(8,128)(2,1)S(1)}, bf16[384,512]{1,0:T(8,128)(2,1)S(1)}, u32[]{:S(2)}, u32[]{:S(2)}) collective-permute-start(bf16[384,512]{1,0:T(8,128)(2,1)S(1)} %get-tuple-element.72), channel_id=1, source_target_pairs={{0,16},{8,24},{16,0},{24,8},{1,17},{9,25},{17,1},{25,9},{2,18},{10... | collective-permute-start | bytes 1179656 | tf_op jit(solution)/shard_map/ppermute | solution.py:216
  64.0 13.8 %collective-permute-start.21 = (bf16[384,512]{1,0:T(8,128)(2,1)S(1)}, bf16[384,512]{1,0:T(8,128)(2,1)S(1)}, u32[]{:S(2)}, u32[]{:S(2)}) collective-permute-start(bf16[384,512]{1,0:T(8,128)(2,1)S(1)} %shard_map.112), channel_id=1, source_target_pairs={{0,24},{8,16},{16,8},{24,0},{1,25},{9,17},{17,9},{25,1},{2,26},{10... | collective-permute-start | bytes 1179656 | tf_op jit(solution)/shard_map/ppermute | solution.py:216
  74.6 4.9 %collective-permute-start.18 = (bf16[128,2048]{1,0:T(8,128)(2,1)S(1)}, bf16[128,2048]{1,0:T(8,128)(2,1)S(1)}, u32[]{:S(2)}, u32[]{:S(2)}) collective-permute-start(bf16[128,2048]{1,0:T(8,128)(2,1)S(1)} %get-tuple-element.69), channel_id=1, source_target_pairs={{0,1},{1,0},{2,3},{3,2},{4,5},{5,4},{6,7},{7,6},{8,9},{9,8},{10,11... | collective-permute-start | bytes 1572872 | tf_op jit(solution)/shard_map/ppermute | solution.py:219

commit v12 on v11

--- a/solution.py
+++ b/solution.py
@@ -250,10 +250,10 @@
         [shape(block, model_width)] * parts + [shape(2 * slots, 2 * width)] * 4,
         1,
         [slot_rows],
-        earlier=pieces[1:],
     )(own, acts, own_dy, near, *far_dy, *weights)
     far_back = after([over_rep(back[2], 4), over_rep(back[3], 6)], ahead=AHEAD)
     returned = [back[0], over_rep(back[1], 2), *far_back]
+    message_1, message_2 = after([message_1, message_2], *pieces[1:])
     message_3 = after([message_3], returned[1])[0]
     messages = after([over_own(message_1, 1), over_own(message_2, 2), over_own(message_3, 3)], ahead=AHEAD)
     messages = [own_message, *messages]

time: 80.7 us -> 80.7 us (level)
  starting transfers between devices: 26.5 us -> 27.4 us
  waiting for transfers between devices: 38.4 us -> 37.5 us
    ppermute x12, starting transfers between devices: 13.8 us -> 14.7 us  [over_rep(): return lax.ppermute(value, 'rep', [(i, i ^ k) for i in range(n_rep)])]
    ppermute x10, waiting for transfers between devices: 10.1 us -> 9.21 us  [over_own(): return lax.ppermute(value, 'own', [(i, i ^ k) for i in range(4)])]
  transfers between devices with their start and end apart: 22 -> 22, of which waited for: 9 -> 8; matrix products, arithmetic and copies ran while one was open for 2% -> 2% of each run, Pallas kernels for 10% -> 14%
where the time goes in v12:
time: 80.7 us; the launch traced here: 80.5 us
  waiting for transfers between devices  37.5 us (46%)
  starting transfers between devices  27.4 us (34%)
  Pallas kernels  11 us (14%)
  other arithmetic  2.14 us (3%)
  local copies, waits for them, and re-layouts  1.56 us (2%)
    ppermute x12, waiting for transfers between devices, over_rep(): return lax.ppermute(value, 'rep', [(i, i ^ k) for i in range(n_rep)])  28.3 us
    ppermute x12, starting transfers between devices, over_rep(): return lax.ppermute(value, 'rep', [(i, i ^ k) for i in range(n_rep)])  14.7 us
    ppermute x10, starting transfers between devices, over_own(): return lax.ppermute(value, 'own', [(i, i ^ k) for i in range(4)])  12.7 us
    pallas_call x7, Pallas kernels, run(): pl.pallas_call(body, out_shape=outs, in_specs=[SMEM] * scalars + [VMEM] *...  11 us
    ppermute x10, waiting for transfers between devices, over_own(): return lax.ppermute(value, 'own', [(i, i ^ k) for i in range(4)])  9.21 us
  transfers between devices with their start and end apart: 22, of which 8 were waited for; matrix products, arithmetic and copies ran while one was open for 2% of the time, Pallas kernels for 14%

profile of v12, /device:TPU:0, one launch (start us, length us, event | category | flops | bytes accessed | tf_op | source)
XLA Modules:
  0.0 80.5 jit_solution(7764385212922400337)
XLA Ops:
  0.6 0.0 copy-start
  0.6 0.0 copy-start.4
  0.7 0.0 copy-start.3
  0.7 1.2 %pad_maximum_fusion.refs_2_.refs_6_ = bf16[512,768]{1,0:T(8,128)(2,1)S(1)} fusion(bf16[512,256]{1,0:T(8,128)(2,1)} %bitcast.11, bf16[512,256]{1,0:T(8,128)(2,1)} %bitcast.12, bf16[512,256]{1,0:T(8,128)(2,1)} %bitcast.13), kind=kLoop, calls=%fused_computation | loop fusion | flops 2359296 | bytes 1572864 | tf_op jit(solution)/shard_map/concatenate | solution.py:223
  1.9 3.0 %collective-permute-start.7 = (bf16[512,768]{1,0:T(8,128)(2,1)S(1)}, bf16[512,768]{1,0:T(8,128)(2,1)S(1)}, u32[]{:S(2)}, u32[]{:S(2)}) collective-permute-start(bf16[512,768]{1,0:T(8,128)(2,1)S(1)} %pad_maximum_fusion.refs_2_.refs_6_), channel_id=1, source_target_pairs={{0,16},{8,24},{16,0},{24,8},{1,17},{9,25},{17,1},{25,9},{2,18},{10... | collective-permute-start | bytes 2359304 | tf_op jit(solution)/shard_map/ppermute | solution.py:216
  4.9 1.5 %collective-permute-start.6 = (bf16[512,768]{1,0:T(8,128)(2,1)S(1)}, bf16[512,768]{1,0:T(8,128)(2,1)S(1)}, u32[]{:S(2)}, u32[]{:S(2)}) collective-permute-start(bf16[512,768]{1,0:T(8,128)(2,1)S(1)} %pad_maximum_fusion.refs_2_.refs_6_), channel_id=1, source_target_pairs={{0,8},{8,0},{16,24},{24,16},{1,9},{9,1},{17,25},{25,17},{2,10},{10... | collective-permute-start | bytes 2359304 | tf_op jit(solution)/shard_map/ppermute | solution.py:216
  6.4 0.0 collective-permute-start.1
  6.4 0.0 copy-done
  6.4 0.5 collective-permute-start.2
  6.9 0.0 copy-done.4
  6.9 0.1 collective-permute-start
  7.0 2.1 %collective-permute-done.refs_3_ = s32[1,128]{1,0:T(1,128)S(1)} collective-permute-done((s32[1,128]{1,0:T(1,128)S(1)}, s32[1,128]{1,0:T(1,128)S(1)}, u32[]{:S(2)}, u32[]{:S(2)}) %collective-permute-start) | collective-permute-done | bytes 544 | tf_op jit(solution)/shard_map/ppermute | solution.py:219
  9.1 0.3 collective-permute-done.1.refs_5_
  9.3 0.0 collective-permute-done.2.refs_7_.refs_2_
  9.3 0.0 copy-done.3
  9.3 2.6 %shard_map.102 = (bf16[192,256]{1,0:T(8,128)(2,1)S(1)}, bf16[48,2048]{1,0:T(8,128)(2,1)S(1)}, bf16[96,2048]{1,0:T(8,128)(2,1)}, bf16[48,2048]{1,0:T(8,128)(2,1)}, bf16[48,2048]{1,0:T(8,128)(2,1)}) custom-call(s32[1]{0:T(128)} %bitcast.refs_0_, s32[8]{0:T(128)S(1)} %copy-done.3, s32[1,128]{1,0:T(1,128)S(1)} %bitcast.10, ...), custom_call_target="tpu_custom_call" | custom-call | bytes 3179556 | tf_op jit(solution)/shard_map/pallas_call | solution.py:38
  11.9 1.6 %collective-permute-start.3 = (bf16[96,2048]{1,0:T(8,128)(2,1)}, bf16[96,2048]{1,0:T(8,128)(2,1)}, u32[]{:S(2)}, u32[]{:S(2)}) collective-permute-start(bf16[96,2048]{1,0:T(8,128)(2,1)} %get-tuple-element.46), channel_id=1, source_target_pairs={{0,2},{1,3},{2,0},{3,1},{4,6},{5,7},{6,4},{7,5},{8,10},{9,11},{10,... | collective-permute-start | bytes 1179656 | tf_op jit(solution)/shard_map/ppermute | solution.py:219
  13.5 2.6 %collective-permute-start.4 = (bf16[48,2048]{1,0:T(8,128)(2,1)}, bf16[48,2048]{1,0:T(8,128)(2,1)}, u32[]{:S(2)}, u32[]{:S(2)}) collective-permute-start(bf16[48,2048]{1,0:T(8,128)(2,1)} %get-tuple-element.47), channel_id=1, source_target_pairs={{0,4},{1,5},{2,6},{3,7},{4,0},{5,1},{6,2},{7,3},{8,12},{9,13},{10,... | collective-permute-start | bytes 589832 | tf_op jit(solution)/shard_map/ppermute | solution.py:219
  16.1 0.2 collective-permute-start.5
  16.3 6.1 %collective-permute-done.7.refs_4_.refs_8_ = bf16[512,768]{1,0:T(8,128)(2,1)S(1)} collective-permute-done((bf16[512,768]{1,0:T(8,128)(2,1)S(1)}, bf16[512,768]{1,0:T(8,128)(2,1)S(1)}, u32[]{:S(2)}, u32[]{:S(2)}) %collective-permute-start.7) | collective-permute-done | bytes 786464 | tf_op jit(solution)/shard_map/ppermute | solution.py:216
  22.5 0.8 slice.9
  23.2 1.7 %collective-permute-start.9 = (bf16[256,768]{1,0:T(8,128)(2,1)}, bf16[256,768]{1,0:T(8,128)(2,1)}, u32[]{:S(2)}, u32[]{:S(2)}) collective-permute-start(bf16[256,768]{1,0:T(8,128)(2,1)} %slice.9), channel_id=1, source_target_pairs={{0,8},{8,0},{16,24},{24,16},{1,9},{9,1},{17,25},{25,17},{2,10},{10... | collective-permute-start | bytes 1179656 | tf_op jit(solution)/shard_map/ppermute | solution.py:216
  24.9 0.0 collective-permute-done.6.refs_3_.refs_7_
  24.9 0.8 slice.8
  25.7 0.0 copy-done.1
  25.7 1.5 %collective-permute-start.8 = (bf16[256,768]{1,0:T(8,128)(2,1)}, bf16[256,768]{1,0:T(8,128)(2,1)}, u32[]{:S(2)}, u32[]{:S(2)}) collective-permute-start(bf16[256,768]{1,0:T(8,128)(2,1)} %slice.8), channel_id=1, source_target_pairs={{0,16},{8,24},{16,0},{24,8},{1,17},{9,25},{17,1},{25,9},{2,18},{10... | collective-permute-start | bytes 1179656 | tf_op jit(solution)/shard_map/ppermute | solution.py:216
  27.2 0.5 shard_map.104
  27.8 0.0 copy-start.2
  27.8 0.0 collective-permute-done.4.refs_1_
  27.8 6.2 %collective-permute-done.5.refs_2_ = bf16[48,2048]{1,0:T(8,128)(2,1)} collective-permute-done((bf16[48,2048]{1,0:T(8,128)(2,1)}, bf16[48,2048]{1,0:T(8,128)(2,1)}, u32[]{:S(2)}, u32[]{:S(2)}) %collective-permute-start.5) | collective-permute-done | bytes 196640 | tf_op jit(solution)/shard_map/ppermute | solution.py:219
  34.0 0.0 collective-permute-done.3.refs_0_
  34.0 0.0 copy-done.2
  34.0 1.3 %shard_map.105 = (bf16[192,2048]{1,0:T(8,128)(2,1)S(1)}, bf16[288,512]{1,0:T(8,128)(2,1)S(1)}, bf16[288,512]{1,0:T(8,128)(2,1)S(1)}, bf16[288,512]{1,0:T(8,128)(2,1)S(1)}, bf16[288,512]{1,0:T(8,128)(2,1)S(1)}) custom-call(s32[1]{0:T(128)} %bitcast.2.refs_0_, bf16[48,2048]{1,0:T(8,128)(2,1)S(1)} %copy-done.2, ...), custom_call_target="tpu_custom_call" | custom-call | bytes 3145732 | tf_op jit(solution)/shard_map/pallas_call | solution.py:38
  35.3 1.7 %collective-permute-start.10 = (bf16[48,2048]{1,0:T(8,128)(2,1)S(1)}, bf16[48,2048]{1,0:T(8,128)(2,1)S(1)}, u32[]{:S(2)}, u32[]{:S(2)}) collective-permute-start(bf16[48,2048]{1,0:T(8,128)(2,1)S(1)} %get-tuple-element.59), channel_id=1, source_target_pairs={{0,4},{1,5},{2,6},{3,7},{4,0},{5,1},{6,2},{7,3},{8,12},{9,13},{10,... | collective-permute-start | bytes 589832 | tf_op jit(solution)/shard_map/ppermute | solution.py:219
  37.0 1.4 %collective-permute-start.11 = (bf16[48,2048]{1,0:T(8,128)(2,1)S(1)}, bf16[48,2048]{1,0:T(8,128)(2,1)S(1)}, u32[]{:S(2)}, u32[]{:S(2)}) collective-permute-start(bf16[48,2048]{1,0:T(8,128)(2,1)S(1)} %get-tuple-element.60), channel_id=1, source_target_pairs={{0,6},{1,7},{2,4},{3,5},{4,2},{5,3},{6,0},{7,1},{8,14},{9,15},{10,... | collective-permute-start | bytes 589832 | tf_op jit(solution)/shard_map/ppermute | solution.py:219
  38.4 0.5 collective-permute-start.16
  38.9 0.0 collective-permute-done.9.refs_1_
  38.9 0.5 collective-permute-start.17
  39.4 0.0 collective-permute-done.8.refs_0_
  39.4 2.5 %collective-permute-start.18 = (bf16[288,512]{1,0:T(8,128)(2,1)S(1)}, bf16[288,512]{1,0:T(8,128)(2,1)S(1)}, u32[]{:S(2)}, u32[]{:S(2)}) collective-permute-start(bf16[288,512]{1,0:T(8,128)(2,1)S(1)} %get-tuple-element.71), channel_id=1, source_target_pairs={{0,24},{8,16},{16,8},{24,0},{1,25},{9,17},{17,9},{25,1},{2,26},{10... | collective-permute-start | bytes 884744 | tf_op jit(solution)/shard_map/ppermute | solution.py:216
  41.9 1.7 %shard_map.107.refs_1_ = f32[192,512]{1,0:T(8,128)S(1)} custom-call(s32[1]{0:T(128)} %bitcast.2.refs_0_, bf16[192,2048]{1,0:T(8,128)(2,1)S(1)} %get-tuple-element.53.refs_1_, bf16[512,768]{1,0:T(8,128)(2,1)S(1)} %pad_maximum_fusion.refs_2_.refs_6_, bf16[512,768]{1,0:T(8,128)(2,1)S(1)} %collective-permute-done.6.refs_3_.refs_7_, ...), custom_call_target="tpu_custom_call" | custom-call | bytes 4325380 | tf_op jit(solution)/shard_map/pallas_call | solution.py:38
  43.6 6.8 %collective-permute-done.10.refs_4_ = bf16[48,2048]{1,0:T(8,128)(2,1)S(1)} collective-permute-done((bf16[48,2048]{1,0:T(8,128)(2,1)S(1)}, bf16[48,2048]{1,0:T(8,128)(2,1)S(1)}, u32[]{:S(2)}, u32[]{:S(2)}) %collective-permute-start.10) | collective-permute-done | bytes 196640 | tf_op jit(solution)/shard_map/ppermute | solution.py:219
  50.4 0.0 collective-permute-done.11.refs_5_
  50.4 2.7 %shard_map.109 = (bf16[48,2048]{1,0:T(8,128)(2,1)S(1)}, bf16[48,2048]{1,0:T(8,128)(2,1)S(1)}, bf16[48,2048]{1,0:T(8,128)(2,1)S(1)}, bf16[48,2048]{1,0:T(8,128)(2...) custom-call(s32[1]{0:T(128)} %bitcast.2.refs_0_, ...), custom_call_target="tpu_custom_call" | custom-call | bytes 6881284 | tf_op jit(solution)/shard_map/pallas_call | solution.py:38
  53.1 3.9 %collective-permute-start.12 = (bf16[48,2048]{1,0:T(8,128)(2,1)S(1)}, bf16[48,2048]{1,0:T(8,128)(2,1)S(1)}, u32[]{:S(2)}, u32[]{:S(2)}) collective-permute-start(bf16[48,2048]{1,0:T(8,128)(2,1)S(1)} %get-tuple-element.62), channel_id=1, source_target_pairs={{0,2},{1,3},{2,0},{3,1},{4,6},{5,7},{6,4},{7,5},{8,10},{9,11},{10,... | collective-permute-start | bytes 589832 | tf_op jit(solution)/shard_map/ppermute | solution.py:219
  57.0 1.3 %collective-permute-start.13 = (bf16[48,2048]{1,0:T(8,128)(2,1)S(1)}, bf16[48,2048]{1,0:T(8,128)(2,1)S(1)}, u32[]{:S(2)}, u32[]{:S(2)}) collective-permute-start(bf16[48,2048]{1,0:T(8,128)(2,1)S(1)} %get-tuple-element.63), channel_id=1, source_target_pairs={{0,4},{1,5},{2,6},{3,7},{4,0},{5,1},{6,2},{7,3},{8,12},{9,13},{10,... | collective-permute-start | bytes 589832 | tf_op jit(solution)/shard_map/ppermute | solution.py:219
  58.3 0.0 collective-permute-done.16.refs_2_.refs_1_
  58.3 1.4 %collective-permute-start.14 = (bf16[48,2048]{1,0:T(8,128)(2,1)S(1)}, bf16[48,2048]{1,0:T(8,128)(2,1)S(1)}, u32[]{:S(2)}, u32[]{:S(2)}) collective-permute-start(bf16[48,2048]{1,0:T(8,128)(2,1)S(1)} %get-tuple-element.64), channel_id=1, source_target_pairs={{0,6},{1,7},{2,4},{3,5},{4,2},{5,3},{6,0},{7,1},{8,14},{9,15},{10,... | collective-permute-start | bytes 589832 | tf_op jit(solution)/shard_map/ppermute | solution.py:219
  59.7 0.0 collective-permute-done.17.refs_3_.refs_2_
  59.7 0.0 collective-permute-done.18.refs_4_.refs_3_
  59.7 0.5 collective-permute-start.19
  60.2 0.5 collective-permute-start.20
  60.7 3.3 %collective-permute-done.12.refs_2_.refs_1_ = bf16[48,2048]{1,0:T(8,128)(2,1)S(1)} collective-permute-done((bf16[48,2048]{1,0:T(8,128)(2,1)S(1)}, bf16[48,2048]{1,0:T(8,128)(2,1)S(1)}, u32[]{:S(2)}, u32[]{:S(2)}) %collective-permute-start.12) | collective-permute-done | bytes 196640 | tf_op jit(solution)/shard_map/ppermute | solution.py:219
  64.0 0.4 collective-permute-start.21
  64.4 9.7 %collective-permute-done.13.refs_0_ = bf16[48,2048]{1,0:T(8,128)(2,1)S(1)} collective-permute-done((bf16[48,2048]{1,0:T(8,128)(2,1)S(1)}, bf16[48,2048]{1,0:T(8,128)(2,1)S(1)}, u32[]{:S(2)}, u32[]{:S(2)}) %collective-permute-start.13) | collective-permute-done | bytes 196640 | tf_op jit(solution)/shard_map/ppermute | solution.py:219
  74.1 0.0 collective-permute-done.14.refs_1_
  74.1 0.5 shard_map.111
  74.6 0.1 collective-permute-start.15
  74.7 0.0 collective-permute-done.19.refs_0_
  74.7 3.1 %collective-permute-done.20.refs_1_ = bf16[384,512]{1,0:T(8,128)(2,1)S(1)} collective-permute-done((bf16[384,512]{1,0:T(8,128)(2,1)S(1)}, bf16[384,512]{1,0:T(8,128)(2,1)S(1)}, u32[]{:S(2)}, u32[]{:S(2)}) %collective-permute-start.20) | collective-permute-done | bytes 393248 | tf_op jit(solution)/shard_map/ppermute | solution.py:216
  77.8 0.0 collective-permute-done.21.refs_2_
  77.8 1.8 %shard_map.115 = (f32[512,256]{1,0:T(8,128)}, f32[512,256]{1,0:T(8,128)}, f32[512,256]{1,0:T(8,128)}) custom-call(bf16[288,512]{1,0:T(8,128)(2,1)S(1)} %get-tuple-element.58.refs_2_.refs_0_, bf16[288,512]{1,0:T(8,128)(2,1)S(1)} %collective-permute-done.16.refs_2_.refs_1_, bf16[288,512]{1,0:T(8,128)(2,1)S(1)} %collective-permute-done.17.refs_3_.refs_2_, ...), custom_call_target="tpu_custom_call" | custom-call | bytes 4325376 | tf_op jit(solution)/shard_map/pallas_call | solution.py:38
  79.5 0.0 collective-permute-done.15
  79.5 0.9 %add.3 = bf16[128,2048]{1,0:T(8,128)(2,1)} add(bf16[128,2048]{1,0:T(8,128)(2,1)S(1)} %get-tuple-element.67, bf16[128,2048]{1,0:T(8,128)(2,1)S(1)} %collective-permute-done.15) | non-fusion elementwise | flops 262144 | bytes 1572864 | tf_op jit(solution)/shard_map/add | solution.py:264
  (8 shorter events, 0.0 us)
Async XLA Ops:
  0.6 5.8 %copy-start = (bf16[128,2048]{1,0:T(8,128)(2,1)S(1)}, bf16[128,2048]{1,0:T(8,128)(2,1)}, u32[]{:S(2)}) copy-start(bf16[128,2048]{1,0:T(8,128)(2,1)} %refs_1_.3) | copy-start | bytes 1572868
  0.6 6.3 %copy-start.4 = (s32[128,1]{0,1:T(1,128)S(1)}, s32[128,1]{0,1:T(1,128)}, u32[]{:S(2)}) copy-start(s32[128,1]{0,1:T(1,128)} %param.9) | copy-start | bytes 1540
  0.7 8.7 %copy-start.3 = (s32[8]{0:T(128)S(1)}, s32[8]{0:T(128)}, u32[]{:S(2)}) copy-start(s32[8]{0:T(128)} %refs_1_.2) | copy-start | bytes 100
  1.9 20.6 %collective-permute-start.7 = (bf16[512,768]{1,0:T(8,128)(2,1)S(1)}, bf16[512,768]{1,0:T(8,128)(2,1)S(1)}, u32[]{:S(2)}, u32[]{:S(2)}) collective-permute-start(bf16[512,768]{1,0:T(8,128)(2,1)S(1)} %pad_maximum_fusion.refs_2_.refs_6_), channel_id=1, source_target_pairs={{0,16},{8,24},{16,0},{24,8},{1,17},{9,25},{17,1},{25,9},{2,18},{10... | collective-permute-start | bytes 2359304 | tf_op jit(solution)/shard_map/ppermute | solution.py:216
  4.9 20.0 %collective-permute-start.6 = (bf16[512,768]{1,0:T(8,128)(2,1)S(1)}, bf16[512,768]{1,0:T(8,128)(2,1)S(1)}, u32[]{:S(2)}, u32[]{:S(2)}) collective-permute-start(bf16[512,768]{1,0:T(8,128)(2,1)S(1)} %pad_maximum_fusion.refs_2_.refs_6_), channel_id=1, source_target_pairs={{0,8},{8,0},{16,24},{24,16},{1,9},{9,1},{17,25},{25,17},{2,10},{10... | collective-permute-start | bytes 2359304 | tf_op jit(solution)/shard_map/ppermute | solution.py:216
  6.4 2.9 %collective-permute-start.1 = (bf16[128,2048]{1,0:T(8,128)(2,1)}, bf16[128,2048]{1,0:T(8,128)(2,1)}, u32[]{:S(2)}, u32[]{:S(2)}) collective-permute-start(bf16[128,2048]{1,0:T(8,128)(2,1)} %refs_4_.1), channel_id=1, source_target_pairs={{0,1},{1,0},{2,3},{3,2},{4,5},{5,4},{6,7},{7,6},{8,9},{9,8},{10,11... | collective-permute-start | bytes 1572872 | tf_op jit(solution)/shard_map/ppermute | solution.py:219
  6.4 2.9 %collective-permute-start.2 = (bf16[128,2048]{1,0:T(8,128)(2,1)S(1)}, bf16[128,2048]{1,0:T(8,128)(2,1)S(1)}, u32[]{:S(2)}, u32[]{:S(2)}) collective-permute-start(bf16[128,2048]{1,0:T(8,128)(2,1)S(1)} %copy-done), channel_id=1, source_target_pairs={{0,1},{1,0},{2,3},{3,2},{4,5},{5,4},{6,7},{7,6},{8,9},{9,8},{10,11... | collective-permute-start | bytes 1572872 | tf_op jit(solution)/shard_map/ppermute | solution.py:219
  6.9 2.1 %collective-permute-start = (s32[1,128]{1,0:T(1,128)S(1)}, s32[1,128]{1,0:T(1,128)S(1)}, u32[]{:S(2)}, u32[]{:S(2)}) collective-permute-start(s32[1,128]{1,0:T(1,128)S(1)} %bitcast.9), channel_id=1, source_target_pairs={{0,1},{1,0},{2,3},{3,2},{4,5},{5,4},{6,7},{7,6},{8,9},{9,8},{10,11... | collective-permute-start | bytes 1544 | tf_op jit(solution)/shard_map/ppermute | solution.py:219
  11.9 13.8 %copy-start.1 = (bf16[48,2048]{1,0:T(8,128)(2,1)}, bf16[48,2048]{1,0:T(8,128)(2,1)S(1)}, u32[]{:S(2)}) copy-start(bf16[48,2048]{1,0:T(8,128)(2,1)S(1)} %get-tuple-element.45.refs_1_) | copy-start | bytes 589828
  11.9 22.0 %collective-permute-start.3 = (bf16[96,2048]{1,0:T(8,128)(2,1)}, bf16[96,2048]{1,0:T(8,128)(2,1)}, u32[]{:S(2)}, u32[]{:S(2)}) collective-permute-start(bf16[96,2048]{1,0:T(8,128)(2,1)} %get-tuple-element.46), channel_id=1, source_target_pairs={{0,2},{1,3},{2,0},{3,1},{4,6},{5,7},{6,4},{7,5},{8,10},{9,11},{10,... | collective-permute-start | bytes 1179656 | tf_op jit(solution)/shard_map/ppermute | solution.py:219
  13.5 14.3 %collective-permute-start.4 = (bf16[48,2048]{1,0:T(8,128)(2,1)}, bf16[48,2048]{1,0:T(8,128)(2,1)}, u32[]{:S(2)}, u32[]{:S(2)}) collective-permute-start(bf16[48,2048]{1,0:T(8,128)(2,1)} %get-tuple-element.47), channel_id=1, source_target_pairs={{0,4},{1,5},{2,6},{3,7},{4,0},{5,1},{6,2},{7,3},{8,12},{9,13},{10,... | collective-permute-start | bytes 589832 | tf_op jit(solution)/shard_map/ppermute | solution.py:219
  16.1 17.9 %collective-permute-start.5 = (bf16[48,2048]{1,0:T(8,128)(2,1)}, bf16[48,2048]{1,0:T(8,128)(2,1)}, u32[]{:S(2)}, u32[]{:S(2)}) collective-permute-start(bf16[48,2048]{1,0:T(8,128)(2,1)} %get-tuple-element.48), channel_id=1, source_target_pairs={{0,6},{1,7},{2,4},{3,5},{4,2},{5,3},{6,0},{7,1},{8,14},{9,15},{10,... | collective-permute-start | bytes 589832 | tf_op jit(solution)/shard_map/ppermute | solution.py:219
  23.2 15.7 %collective-permute-start.9 = (bf16[256,768]{1,0:T(8,128)(2,1)}, bf16[256,768]{1,0:T(8,128)(2,1)}, u32[]{:S(2)}, u32[]{:S(2)}) collective-permute-start(bf16[256,768]{1,0:T(8,128)(2,1)} %slice.9), channel_id=1, source_target_pairs={{0,8},{8,0},{16,24},{24,16},{1,9},{9,1},{17,25},{25,17},{2,10},{10... | collective-permute-start | bytes 1179656 | tf_op jit(solution)/shard_map/ppermute | solution.py:216
  25.7 13.7 %collective-permute-start.8 = (bf16[256,768]{1,0:T(8,128)(2,1)}, bf16[256,768]{1,0:T(8,128)(2,1)}, u32[]{:S(2)}, u32[]{:S(2)}) collective-permute-start(bf16[256,768]{1,0:T(8,128)(2,1)} %slice.8), channel_id=1, source_target_pairs={{0,16},{8,24},{16,0},{24,8},{1,17},{9,25},{17,1},{25,9},{2,18},{10... | collective-permute-start | bytes 1179656 | tf_op jit(solution)/shard_map/ppermute | solution.py:216
  27.8 6.2 %copy-start.2 = (bf16[48,2048]{1,0:T(8,128)(2,1)S(1)}, bf16[48,2048]{1,0:T(8,128)(2,1)}, u32[]{:S(2)}) copy-start(bf16[48,2048]{1,0:T(8,128)(2,1)} %copy-done.1) | copy-start | bytes 589828
  35.3 15.1 %collective-permute-start.10 = (bf16[48,2048]{1,0:T(8,128)(2,1)S(1)}, bf16[48,2048]{1,0:T(8,128)(2,1)S(1)}, u32[]{:S(2)}, u32[]{:S(2)}) collective-permute-start(bf16[48,2048]{1,0:T(8,128)(2,1)S(1)} %get-tuple-element.59), channel_id=1, source_target_pairs={{0,4},{1,5},{2,6},{3,7},{4,0},{5,1},{6,2},{7,3},{8,12},{9,13},{10,... | collective-permute-start | bytes 589832 | tf_op jit(solution)/shard_map/ppermute | solution.py:219
  37.0 13.4 %collective-permute-start.11 = (bf16[48,2048]{1,0:T(8,128)(2,1)S(1)}, bf16[48,2048]{1,0:T(8,128)(2,1)S(1)}, u32[]{:S(2)}, u32[]{:S(2)}) collective-permute-start(bf16[48,2048]{1,0:T(8,128)(2,1)S(1)} %get-tuple-element.60), channel_id=1, source_target_pairs={{0,6},{1,7},{2,4},{3,5},{4,2},{5,3},{6,0},{7,1},{8,14},{9,15},{10,... | collective-permute-start | bytes 589832 | tf_op jit(solution)/shard_map/ppermute | solution.py:219
  38.4 19.9 %collective-permute-start.16 = (bf16[288,512]{1,0:T(8,128)(2,1)S(1)}, bf16[288,512]{1,0:T(8,128)(2,1)S(1)}, u32[]{:S(2)}, u32[]{:S(2)}) collective-permute-start(bf16[288,512]{1,0:T(8,128)(2,1)S(1)} %get-tuple-element.69), channel_id=1, source_target_pairs={{0,8},{8,0},{16,24},{24,16},{1,9},{9,1},{17,25},{25,17},{2,10},{10... | collective-permute-start | bytes 884744 | tf_op jit(solution)/shard_map/ppermute | solution.py:216
  38.9 20.8 %collective-permute-start.17 = (bf16[288,512]{1,0:T(8,128)(2,1)S(1)}, bf16[288,512]{1,0:T(8,128)(2,1)S(1)}, u32[]{:S(2)}, u32[]{:S(2)}) collective-permute-start(bf16[288,512]{1,0:T(8,128)(2,1)S(1)} %get-tuple-element.70), channel_id=1, source_target_pairs={{0,16},{8,24},{16,0},{24,8},{1,17},{9,25},{17,1},{25,9},{2,18},{10... | collective-permute-start | bytes 884744 | tf_op jit(solution)/shard_map/ppermute | solution.py:216
  39.4 20.3 %collective-permute-start.18 = (bf16[288,512]{1,0:T(8,128)(2,1)S(1)}, bf16[288,512]{1,0:T(8,128)(2,1)S(1)}, u32[]{:S(2)}, u32[]{:S(2)}) collective-permute-start(bf16[288,512]{1,0:T(8,128)(2,1)S(1)} %get-tuple-element.71), channel_id=1, source_target_pairs={{0,24},{8,16},{16,8},{24,0},{1,25},{9,17},{17,9},{25,1},{2,26},{10... | collective-permute-start | bytes 884744 | tf_op jit(solution)/shard_map/ppermute | solution.py:216
  53.1 10.9 %collective-permute-start.12 = (bf16[48,2048]{1,0:T(8,128)(2,1)S(1)}, bf16[48,2048]{1,0:T(8,128)(2,1)S(1)}, u32[]{:S(2)}, u32[]{:S(2)}) collective-permute-start(bf16[48,2048]{1,0:T(8,128)(2,1)S(1)} %get-tuple-element.62), channel_id=1, source_target_pairs={{0,2},{1,3},{2,0},{3,1},{4,6},{5,7},{6,4},{7,5},{8,10},{9,11},{10,... | collective-permute-start | bytes 589832 | tf_op jit(solution)/shard_map/ppermute | solution.py:219
  57.0 17.1 %collective-permute-start.13 = (bf16[48,2048]{1,0:T(8,128)(2,1)S(1)}, bf16[48,2048]{1,0:T(8,128)(2,1)S(1)}, u32[]{:S(2)}, u32[]{:S(2)}) collective-permute-start(bf16[48,2048]{1,0:T(8,128)(2,1)S(1)} %get-tuple-element.63), channel_id=1, source_target_pairs={{0,4},{1,5},{2,6},{3,7},{4,0},{5,1},{6,2},{7,3},{8,12},{9,13},{10,... | collective-permute-start | bytes 589832 | tf_op jit(solution)/shard_map/ppermute | solution.py:219
  58.3 15.9 %collective-permute-start.14 = (bf16[48,2048]{1,0:T(8,128)(2,1)S(1)}, bf16[48,2048]{1,0:T(8,128)(2,1)S(1)}, u32[]{:S(2)}, u32[]{:S(2)}) collective-permute-start(bf16[48,2048]{1,0:T(8,128)(2,1)S(1)} %get-tuple-element.64), channel_id=1, source_target_pairs={{0,6},{1,7},{2,4},{3,5},{4,2},{5,3},{6,0},{7,1},{8,14},{9,15},{10,... | collective-permute-start | bytes 589832 | tf_op jit(solution)/shard_map/ppermute | solution.py:219
  59.7 15.0 %collective-permute-start.19 = (bf16[384,512]{1,0:T(8,128)(2,1)S(1)}, bf16[384,512]{1,0:T(8,128)(2,1)S(1)}, u32[]{:S(2)}, u32[]{:S(2)}) collective-permute-start(bf16[384,512]{1,0:T(8,128)(2,1)S(1)} %get-tuple-element.75), channel_id=1, source_target_pairs={{0,8},{8,0},{16,24},{24,16},{1,9},{9,1},{17,25},{25,17},{2,10},{10... | collective-permute-start | bytes 1179656 | tf_op jit(solution)/shard_map/ppermute | solution.py:216
  60.2 17.6 %collective-permute-start.20 = (bf16[384,512]{1,0:T(8,128)(2,1)S(1)}, bf16[384,512]{1,0:T(8,128)(2,1)S(1)}, u32[]{:S(2)}, u32[]{:S(2)}) collective-permute-start(bf16[384,512]{1,0:T(8,128)(2,1)S(1)} %get-tuple-element.76), channel_id=1, source_target_pairs={{0,16},{8,24},{16,0},{24,8},{1,17},{9,25},{17,1},{25,9},{2,18},{10... | collective-permute-start | bytes 1179656 | tf_op jit(solution)/shard_map/ppermute | solution.py:216
  64.0 13.8 %collective-permute-start.21 = (bf16[384,512]{1,0:T(8,128)(2,1)S(1)}, bf16[384,512]{1,0:T(8,128)(2,1)S(1)}, u32[]{:S(2)}, u32[]{:S(2)}) collective-permute-start(bf16[384,512]{1,0:T(8,128)(2,1)S(1)} %shard_map.113), channel_id=1, source_target_pairs={{0,24},{8,16},{16,8},{24,0},{1,25},{9,17},{17,9},{25,1},{2,26},{10... | collective-permute-start | bytes 1179656 | tf_op jit(solution)/shard_map/ppermute | solution.py:216
  74.6 4.9 %collective-permute-start.15 = (bf16[128,2048]{1,0:T(8,128)(2,1)S(1)}, bf16[128,2048]{1,0:T(8,128)(2,1)S(1)}, u32[]{:S(2)}, u32[]{:S(2)}) collective-permute-start(bf16[128,2048]{1,0:T(8,128)(2,1)S(1)} %get-tuple-element.68), channel_id=1, source_target_pairs={{0,1},{1,0},{2,3},{3,2},{4,5},{5,4},{6,7},{7,6},{8,9},{9,8},{10,11... | collective-permute-start | bytes 1572872 | tf_op jit(solution)/shard_map/ppermute | solution.py:219

commit v13 on v11

--- a/solution.py
+++ b/solution.py
@@ -267,6 +267,7 @@
         [shape(depth, width, F32)] * 3,
         0,
         [pltpu.VMEM((4 * slots, cols), BF16) for cols in (depth, depth, 2 * width, width)],
+        earlier=[x_grad],
     )(*pieces, *messages)
     return (x_grad, *(grad[None] for grad in out))
 

time: 80.7 us -> 79.9 us (0.990)
  transfers between devices with their start and end apart: 22 -> 22, of which waited for: 9 -> 9; matrix products, arithmetic and copies ran while one was open for 2% -> 2% of each run, Pallas kernels for 10% -> 8%
where the time goes in v13:
time: 79.9 us; the launch traced here: 79.7 us
  waiting for transfers between devices  38.4 us (48%)
  starting transfers between devices  26.5 us (33%)
  Pallas kernels  11.1 us (14%)
  local copies, waits for them, and re-layouts  1.57 us (2%)
  other arithmetic  1.34 us (2%)
    ppermute x12, waiting for transfers between devices, over_rep(): return lax.ppermute(value, 'rep', [(i, i ^ k) for i in range(n_rep)])  28.4 us
    ppermute x12, starting transfers between devices, over_rep(): return lax.ppermute(value, 'rep', [(i, i ^ k) for i in range(n_rep)])  13.8 us
    ppermute x10, starting transfers between devices, over_own(): return lax.ppermute(value, 'own', [(i, i ^ k) for i in range(4)])  12.7 us
    pallas_call x7, Pallas kernels, run(): pl.pallas_call(body, out_shape=outs, in_specs=[SMEM] * scalars + [VMEM] *...  11.1 us
    ppermute x10, waiting for transfers between devices, over_own(): return lax.ppermute(value, 'own', [(i, i ^ k) for i in range(4)])  10.1 us
  transfers between devices with their start and end apart: 22, of which 9 were waited for; matrix products, arithmetic and copies ran while one was open for 2% of the time, Pallas kernels for 8%

profile of v13, /device:TPU:0, one launch (start us, length us, event | category | flops | bytes accessed | tf_op | source)
XLA Modules:
  0.0 79.7 jit_solution(2735841626124275538)
XLA Ops:
  0.6 0.0 copy-start.1
  0.6 0.0 copy-start.5
  0.7 0.0 copy-start.4
  0.7 1.2 %pad_maximum_fusion.refs_2_.refs_6_ = bf16[512,768]{1,0:T(8,128)(2,1)S(1)} fusion(bf16[512,256]{1,0:T(8,128)(2,1)} %bitcast.11, bf16[512,256]{1,0:T(8,128)(2,1)} %bitcast.12, bf16[512,256]{1,0:T(8,128)(2,1)} %bitcast.13), kind=kLoop, calls=%fused_computation | loop fusion | flops 2359296 | bytes 1572864 | tf_op jit(solution)/shard_map/concatenate | solution.py:223
  1.9 3.0 %collective-permute-start.7 = (bf16[512,768]{1,0:T(8,128)(2,1)S(1)}, bf16[512,768]{1,0:T(8,128)(2,1)S(1)}, u32[]{:S(2)}, u32[]{:S(2)}) collective-permute-start(bf16[512,768]{1,0:T(8,128)(2,1)S(1)} %pad_maximum_fusion.refs_2_.refs_6_), channel_id=1, source_target_pairs={{0,16},{8,24},{16,0},{24,8},{1,17},{9,25},{17,1},{25,9},{2,18},{10... | collective-permute-start | bytes 2359304 | tf_op jit(solution)/shard_map/ppermute | solution.py:216
  4.9 1.5 %collective-permute-start.6 = (bf16[512,768]{1,0:T(8,128)(2,1)S(1)}, bf16[512,768]{1,0:T(8,128)(2,1)S(1)}, u32[]{:S(2)}, u32[]{:S(2)}) collective-permute-start(bf16[512,768]{1,0:T(8,128)(2,1)S(1)} %pad_maximum_fusion.refs_2_.refs_6_), channel_id=1, source_target_pairs={{0,8},{8,0},{16,24},{24,16},{1,9},{9,1},{17,25},{25,17},{2,10},{10... | collective-permute-start | bytes 2359304 | tf_op jit(solution)/shard_map/ppermute | solution.py:216
  6.4 0.0 collective-permute-start.1
  6.4 0.0 copy-done.1
  6.4 0.5 collective-permute-start.2
  6.9 0.0 copy-done.5
  6.9 0.1 collective-permute-start
  7.0 2.1 %collective-permute-done.refs_3_ = s32[1,128]{1,0:T(1,128)S(1)} collective-permute-done((s32[1,128]{1,0:T(1,128)S(1)}, s32[1,128]{1,0:T(1,128)S(1)}, u32[]{:S(2)}, u32[]{:S(2)}) %collective-permute-start) | collective-permute-done | bytes 544 | tf_op jit(solution)/shard_map/ppermute | solution.py:219
  9.1 0.3 collective-permute-done.1.refs_5_
  9.3 0.0 collective-permute-done.2.refs_7_.refs_2_
  9.3 0.0 copy-done.4
  9.3 2.6 %shard_map.102 = (bf16[192,256]{1,0:T(8,128)(2,1)S(1)}, bf16[48,2048]{1,0:T(8,128)(2,1)S(1)}, bf16[96,2048]{1,0:T(8,128)(2,1)}, bf16[48,2048]{1,0:T(8,128)(2,1)}, bf16[48,2048]{1,0:T(8,128)(2,1)}) custom-call(s32[1]{0:T(128)} %bitcast.refs_0_, s32[8]{0:T(128)S(1)} %copy-done.4, s32[1,128]{1,0:T(1,128)S(1)} %bitcast.10, ...), custom_call_target="tpu_custom_call" | custom-call | bytes 3179556 | tf_op jit(solution)/shard_map/pallas_call | solution.py:38
  11.9 1.6 %collective-permute-start.3 = (bf16[96,2048]{1,0:T(8,128)(2,1)}, bf16[96,2048]{1,0:T(8,128)(2,1)}, u32[]{:S(2)}, u32[]{:S(2)}) collective-permute-start(bf16[96,2048]{1,0:T(8,128)(2,1)} %get-tuple-element.44), channel_id=1, source_target_pairs={{0,2},{1,3},{2,0},{3,1},{4,6},{5,7},{6,4},{7,5},{8,10},{9,11},{10,... | collective-permute-start | bytes 1179656 | tf_op jit(solution)/shard_map/ppermute | solution.py:219
  13.5 2.6 %collective-permute-start.4 = (bf16[48,2048]{1,0:T(8,128)(2,1)}, bf16[48,2048]{1,0:T(8,128)(2,1)}, u32[]{:S(2)}, u32[]{:S(2)}) collective-permute-start(bf16[48,2048]{1,0:T(8,128)(2,1)} %get-tuple-element.45), channel_id=1, source_target_pairs={{0,4},{1,5},{2,6},{3,7},{4,0},{5,1},{6,2},{7,3},{8,12},{9,13},{10,... | collective-permute-start | bytes 589832 | tf_op jit(solution)/shard_map/ppermute | solution.py:219
  16.1 0.2 collective-permute-start.5
  16.3 6.1 %collective-permute-done.7.refs_4_.refs_8_ = bf16[512,768]{1,0:T(8,128)(2,1)S(1)} collective-permute-done((bf16[512,768]{1,0:T(8,128)(2,1)S(1)}, bf16[512,768]{1,0:T(8,128)(2,1)S(1)}, u32[]{:S(2)}, u32[]{:S(2)}) %collective-permute-start.7) | collective-permute-done | bytes 786464 | tf_op jit(solution)/shard_map/ppermute | solution.py:216
  22.5 0.8 slice.9
  23.2 1.7 %collective-permute-start.9 = (bf16[256,768]{1,0:T(8,128)(2,1)}, bf16[256,768]{1,0:T(8,128)(2,1)}, u32[]{:S(2)}, u32[]{:S(2)}) collective-permute-start(bf16[256,768]{1,0:T(8,128)(2,1)} %slice.9), channel_id=1, source_target_pairs={{0,8},{8,0},{16,24},{24,16},{1,9},{9,1},{17,25},{25,17},{2,10},{10... | collective-permute-start | bytes 1179656 | tf_op jit(solution)/shard_map/ppermute | solution.py:216
  24.9 0.0 collective-permute-done.6.refs_3_.refs_7_
  24.9 0.8 slice.8
  25.7 0.0 copy-done.2
  25.7 1.5 %collective-permute-start.8 = (bf16[256,768]{1,0:T(8,128)(2,1)}, bf16[256,768]{1,0:T(8,128)(2,1)}, u32[]{:S(2)}, u32[]{:S(2)}) collective-permute-start(bf16[256,768]{1,0:T(8,128)(2,1)} %slice.8), channel_id=1, source_target_pairs={{0,16},{8,24},{16,0},{24,8},{1,17},{9,25},{17,1},{25,9},{2,18},{10... | collective-permute-start | bytes 1179656 | tf_op jit(solution)/shard_map/ppermute | solution.py:216
  27.2 0.5 shard_map.104
  27.8 0.0 copy-start.3
  27.8 0.0 collective-permute-done.4.refs_1_
  27.8 6.2 %collective-permute-done.5.refs_2_ = bf16[48,2048]{1,0:T(8,128)(2,1)} collective-permute-done((bf16[48,2048]{1,0:T(8,128)(2,1)}, bf16[48,2048]{1,0:T(8,128)(2,1)}, u32[]{:S(2)}, u32[]{:S(2)}) %collective-permute-start.5) | collective-permute-done | bytes 196640 | tf_op jit(solution)/shard_map/ppermute | solution.py:219
  34.0 0.0 collective-permute-done.3.refs_0_
  34.0 1.3 %shard_map.105 = (bf16[192,2048]{1,0:T(8,128)(2,1)S(1)}, bf16[288,512]{1,0:T(8,128)(2,1)S(1)}, bf16[288,512]{1,0:T(8,128)(2,1)S(1)}, bf16[288,512]{1,0:T(8,128)(2,1)S(1)}, bf16[288,512]{1,0:T(8,128)(2,1)S(1)}) custom-call(s32[1]{0:T(128)} %bitcast.2.refs_0_, bf16[48,2048]{1,0:T(8,128)(2,1)S(1)} %copy-done.3, ...), custom_call_target="tpu_custom_call" | custom-call | bytes 3145732 | tf_op jit(solution)/shard_map/pallas_call | solution.py:38
  35.3 1.7 %collective-permute-start.10 = (bf16[48,2048]{1,0:T(8,128)(2,1)S(1)}, bf16[48,2048]{1,0:T(8,128)(2,1)S(1)}, u32[]{:S(2)}, u32[]{:S(2)}) collective-permute-start(bf16[48,2048]{1,0:T(8,128)(2,1)S(1)} %get-tuple-element.57), channel_id=1, source_target_pairs={{0,4},{1,5},{2,6},{3,7},{4,0},{5,1},{6,2},{7,3},{8,12},{9,13},{10,... | collective-permute-start | bytes 589832 | tf_op jit(solution)/shard_map/ppermute | solution.py:219
  37.0 1.4 %collective-permute-start.11 = (bf16[48,2048]{1,0:T(8,128)(2,1)S(1)}, bf16[48,2048]{1,0:T(8,128)(2,1)S(1)}, u32[]{:S(2)}, u32[]{:S(2)}) collective-permute-start(bf16[48,2048]{1,0:T(8,128)(2,1)S(1)} %get-tuple-element.58), channel_id=1, source_target_pairs={{0,6},{1,7},{2,4},{3,5},{4,2},{5,3},{6,0},{7,1},{8,14},{9,15},{10,... | collective-permute-start | bytes 589832 | tf_op jit(solution)/shard_map/ppermute | solution.py:219
  38.4 0.5 collective-permute-start.12
  38.9 0.0 collective-permute-done.9.refs_1_
  38.9 0.5 collective-permute-start.13
  39.4 0.0 collective-permute-done.8.refs_0_
  39.4 2.5 %collective-permute-start.14 = (bf16[288,512]{1,0:T(8,128)(2,1)S(1)}, bf16[288,512]{1,0:T(8,128)(2,1)S(1)}, u32[]{:S(2)}, u32[]{:S(2)}) collective-permute-start(bf16[288,512]{1,0:T(8,128)(2,1)S(1)} %get-tuple-element.61), channel_id=1, source_target_pairs={{0,24},{8,16},{16,8},{24,0},{1,25},{9,17},{17,9},{25,1},{2,26},{10... | collective-permute-start | bytes 884744 | tf_op jit(solution)/shard_map/ppermute | solution.py:216
  41.9 1.7 %shard_map.107.refs_1_ = f32[192,512]{1,0:T(8,128)S(1)} custom-call(s32[1]{0:T(128)} %bitcast.2.refs_0_, bf16[192,2048]{1,0:T(8,128)(2,1)S(1)} %get-tuple-element.51.refs_1_, bf16[512,768]{1,0:T(8,128)(2,1)S(1)} %pad_maximum_fusion.refs_2_.refs_6_, bf16[512,768]{1,0:T(8,128)(2,1)S(1)} %collective-permute-done.6.refs_3_.refs_7_, ...), custom_call_target="tpu_custom_call" | custom-call | bytes 4325380 | tf_op jit(solution)/shard_map/pallas_call | solution.py:38
  43.6 6.8 %collective-permute-done.10.refs_4_ = bf16[48,2048]{1,0:T(8,128)(2,1)S(1)} collective-permute-done((bf16[48,2048]{1,0:T(8,128)(2,1)S(1)}, bf16[48,2048]{1,0:T(8,128)(2,1)S(1)}, u32[]{:S(2)}, u32[]{:S(2)}) %collective-permute-start.10) | collective-permute-done | bytes 196640 | tf_op jit(solution)/shard_map/ppermute | solution.py:219
  50.4 0.0 collective-permute-done.11.refs_5_
  50.4 0.0 collective-permute-done.12.refs_11_.refs_1_
  50.4 0.9 %collective-permute-done.13.refs_12_.refs_2_ = bf16[288,512]{1,0:T(8,128)(2,1)S(1)} collective-permute-done((bf16[288,512]{1,0:T(8,128)(2,1)S(1)}, bf16[288,512]{1,0:T(8,128)(2,1)S(1)}, u32[]{:S(2)}, u32[]{:S(2)}) %collective-permute-start.13) | collective-permute-done | bytes 294944 | tf_op jit(solution)/shard_map/ppermute | solution.py:216
  51.3 0.0 collective-permute-done.14.refs_13_.refs_3_
  51.3 2.7 %shard_map.109 = (bf16[48,2048]{1,0:T(8,128)(2,1)S(1)}, bf16[48,2048]{1,0:T(8,128)(2,1)S(1)}, bf16[48,2048]{1,0:T(8,128)(2,1)S(1)}, bf16[48,2048]{1,0:T(8,128)(2...) custom-call(s32[1]{0:T(128)} %bitcast.2.refs_0_, ...), custom_call_target="tpu_custom_call" | custom-call | bytes 6881284 | tf_op jit(solution)/shard_map/pallas_call | solution.py:38
  54.0 3.1 %collective-permute-start.15 = (bf16[48,2048]{1,0:T(8,128)(2,1)S(1)}, bf16[48,2048]{1,0:T(8,128)(2,1)S(1)}, u32[]{:S(2)}, u32[]{:S(2)}) collective-permute-start(bf16[48,2048]{1,0:T(8,128)(2,1)S(1)} %get-tuple-element.63), channel_id=1, source_target_pairs={{0,2},{1,3},{2,0},{3,1},{4,6},{5,7},{6,4},{7,5},{8,10},{9,11},{10,... | collective-permute-start | bytes 589832 | tf_op jit(solution)/shard_map/ppermute | solution.py:219
  57.1 1.3 %collective-permute-start.16 = (bf16[48,2048]{1,0:T(8,128)(2,1)S(1)}, bf16[48,2048]{1,0:T(8,128)(2,1)S(1)}, u32[]{:S(2)}, u32[]{:S(2)}) collective-permute-start(bf16[48,2048]{1,0:T(8,128)(2,1)S(1)} %get-tuple-element.64), channel_id=1, source_target_pairs={{0,4},{1,5},{2,6},{3,7},{4,0},{5,1},{6,2},{7,3},{8,12},{9,13},{10,... | collective-permute-start | bytes 589832 | tf_op jit(solution)/shard_map/ppermute | solution.py:219
  58.3 1.4 %collective-permute-start.17 = (bf16[48,2048]{1,0:T(8,128)(2,1)S(1)}, bf16[48,2048]{1,0:T(8,128)(2,1)S(1)}, u32[]{:S(2)}, u32[]{:S(2)}) collective-permute-start(bf16[48,2048]{1,0:T(8,128)(2,1)S(1)} %get-tuple-element.65), channel_id=1, source_target_pairs={{0,6},{1,7},{2,4},{3,5},{4,2},{5,3},{6,0},{7,1},{8,14},{9,15},{10,... | collective-permute-start | bytes 589832 | tf_op jit(solution)/shard_map/ppermute | solution.py:219
  59.7 0.5 collective-permute-start.19
  60.2 0.5 collective-permute-start.20
  60.7 3.3 %collective-permute-done.15.refs_2_.refs_1_ = bf16[48,2048]{1,0:T(8,128)(2,1)S(1)} collective-permute-done((bf16[48,2048]{1,0:T(8,128)(2,1)S(1)}, bf16[48,2048]{1,0:T(8,128)(2,1)S(1)}, u32[]{:S(2)}, u32[]{:S(2)}) %collective-permute-start.15) | collective-permute-done | bytes 196640 | tf_op jit(solution)/shard_map/ppermute | solution.py:219
  64.0 0.4 collective-permute-start.21
  64.5 9.7 %collective-permute-done.16.refs_0_ = bf16[48,2048]{1,0:T(8,128)(2,1)S(1)} collective-permute-done((bf16[48,2048]{1,0:T(8,128)(2,1)S(1)}, bf16[48,2048]{1,0:T(8,128)(2,1)S(1)}, u32[]{:S(2)}, u32[]{:S(2)}) %collective-permute-start.16) | collective-permute-done | bytes 196640 | tf_op jit(solution)/shard_map/ppermute | solution.py:219
  74.2 0.0 collective-permute-done.17.refs_1_
  74.2 0.5 shard_map.111
  74.6 0.1 collective-permute-start.18
  74.7 0.0 collective-permute-done.19.refs_0_
  74.7 3.1 %collective-permute-done.20.refs_1_ = bf16[384,512]{1,0:T(8,128)(2,1)S(1)} collective-permute-done((bf16[384,512]{1,0:T(8,128)(2,1)S(1)}, bf16[384,512]{1,0:T(8,128)(2,1)S(1)}, u32[]{:S(2)}, u32[]{:S(2)}) %collective-permute-start.20) | collective-permute-done | bytes 393248 | tf_op jit(solution)/shard_map/ppermute | solution.py:216
  77.8 0.0 collective-permute-done.21.refs_2_
  77.8 0.0 collective-permute-done.18
  77.8 0.1 add.3.refs_8_
  77.9 0.0 copy-start
  77.9 1.8 %shard_map.114 = (f32[512,256]{1,0:T(8,128)}, f32[512,256]{1,0:T(8,128)}, f32[512,256]{1,0:T(8,128)}) custom-call(bf16[288,512]{1,0:T(8,128)(2,1)S(1)} %get-tuple-element.56.refs_2_.refs_0_, bf16[288,512]{1,0:T(8,128)(2,1)S(1)} %collective-permute-done.12.refs_11_.refs_1_, bf16[288,512]{1,0:T(8,128)(2,1)S(1)} %collective-permute-done.13.refs_12_.refs_2_, ...), custom_call_target="tpu_custom_call" | custom-call | bytes 4325376 | tf_op jit(solution)/shard_map/pallas_call | solution.py:38
  (9 shorter events, 0.0 us)
Async XLA Ops:
  0.6 5.8 %copy-start.1 = (bf16[128,2048]{1,0:T(8,128)(2,1)S(1)}, bf16[128,2048]{1,0:T(8,128)(2,1)}, u32[]{:S(2)}) copy-start(bf16[128,2048]{1,0:T(8,128)(2,1)} %refs_1_.3) | copy-start | bytes 1572868
  0.6 6.3 %copy-start.5 = (s32[128,1]{0,1:T(1,128)S(1)}, s32[128,1]{0,1:T(1,128)}, u32[]{:S(2)}) copy-start(s32[128,1]{0,1:T(1,128)} %param.9) | copy-start | bytes 1540
  0.7 8.7 %copy-start.4 = (s32[8]{0:T(128)S(1)}, s32[8]{0:T(128)}, u32[]{:S(2)}) copy-start(s32[8]{0:T(128)} %refs_1_.2) | copy-start | bytes 100
  1.9 20.6 %collective-permute-start.7 = (bf16[512,768]{1,0:T(8,128)(2,1)S(1)}, bf16[512,768]{1,0:T(8,128)(2,1)S(1)}, u32[]{:S(2)}, u32[]{:S(2)}) collective-permute-start(bf16[512,768]{1,0:T(8,128)(2,1)S(1)} %pad_maximum_fusion.refs_2_.refs_6_), channel_id=1, source_target_pairs={{0,16},{8,24},{16,0},{24,8},{1,17},{9,25},{17,1},{25,9},{2,18},{10... | collective-permute-start | bytes 2359304 | tf_op jit(solution)/shard_map/ppermute | solution.py:216
  4.9 20.0 %collective-permute-start.6 = (bf16[512,768]{1,0:T(8,128)(2,1)S(1)}, bf16[512,768]{1,0:T(8,128)(2,1)S(1)}, u32[]{:S(2)}, u32[]{:S(2)}) collective-permute-start(bf16[512,768]{1,0:T(8,128)(2,1)S(1)} %pad_maximum_fusion.refs_2_.refs_6_), channel_id=1, source_target_pairs={{0,8},{8,0},{16,24},{24,16},{1,9},{9,1},{17,25},{25,17},{2,10},{10... | collective-permute-start | bytes 2359304 | tf_op jit(solution)/shard_map/ppermute | solution.py:216
  6.4 2.9 %collective-permute-start.1 = (bf16[128,2048]{1,0:T(8,128)(2,1)}, bf16[128,2048]{1,0:T(8,128)(2,1)}, u32[]{:S(2)}, u32[]{:S(2)}) collective-permute-start(bf16[128,2048]{1,0:T(8,128)(2,1)} %refs_4_.1), channel_id=1, source_target_pairs={{0,1},{1,0},{2,3},{3,2},{4,5},{5,4},{6,7},{7,6},{8,9},{9,8},{10,11... | collective-permute-start | bytes 1572872 | tf_op jit(solution)/shard_map/ppermute | solution.py:219
  6.4 2.9 %collective-permute-start.2 = (bf16[128,2048]{1,0:T(8,128)(2,1)S(1)}, bf16[128,2048]{1,0:T(8,128)(2,1)S(1)}, u32[]{:S(2)}, u32[]{:S(2)}) collective-permute-start(bf16[128,2048]{1,0:T(8,128)(2,1)S(1)} %copy-done.1), channel_id=1, source_target_pairs={{0,1},{1,0},{2,3},{3,2},{4,5},{5,4},{6,7},{7,6},{8,9},{9,8},{10,11... | collective-permute-start | bytes 1572872 | tf_op jit(solution)/shard_map/ppermute | solution.py:219
  6.9 2.1 %collective-permute-start = (s32[1,128]{1,0:T(1,128)S(1)}, s32[1,128]{1,0:T(1,128)S(1)}, u32[]{:S(2)}, u32[]{:S(2)}) collective-permute-start(s32[1,128]{1,0:T(1,128)S(1)} %bitcast.9), channel_id=1, source_target_pairs={{0,1},{1,0},{2,3},{3,2},{4,5},{5,4},{6,7},{7,6},{8,9},{9,8},{10,11... | collective-permute-start | bytes 1544 | tf_op jit(solution)/shard_map/ppermute | solution.py:219
  11.9 13.8 %copy-start.2 = (bf16[48,2048]{1,0:T(8,128)(2,1)}, bf16[48,2048]{1,0:T(8,128)(2,1)S(1)}, u32[]{:S(2)}) copy-start(bf16[48,2048]{1,0:T(8,128)(2,1)S(1)} %get-tuple-element.43.refs_1_) | copy-start | bytes 589828
  11.9 22.0 %collective-permute-start.3 = (bf16[96,2048]{1,0:T(8,128)(2,1)}, bf16[96,2048]{1,0:T(8,128)(2,1)}, u32[]{:S(2)}, u32[]{:S(2)}) collective-permute-start(bf16[96,2048]{1,0:T(8,128)(2,1)} %get-tuple-element.44), channel_id=1, source_target_pairs={{0,2},{1,3},{2,0},{3,1},{4,6},{5,7},{6,4},{7,5},{8,10},{9,11},{10,... | collective-permute-start | bytes 1179656 | tf_op jit(solution)/shard_map/ppermute | solution.py:219
  13.5 14.3 %collective-permute-start.4 = (bf16[48,2048]{1,0:T(8,128)(2,1)}, bf16[48,2048]{1,0:T(8,128)(2,1)}, u32[]{:S(2)}, u32[]{:S(2)}) collective-permute-start(bf16[48,2048]{1,0:T(8,128)(2,1)} %get-tuple-element.45), channel_id=1, source_target_pairs={{0,4},{1,5},{2,6},{3,7},{4,0},{5,1},{6,2},{7,3},{8,12},{9,13},{10,... | collective-permute-start | bytes 589832 | tf_op jit(solution)/shard_map/ppermute | solution.py:219
  16.1 17.9 %collective-permute-start.5 = (bf16[48,2048]{1,0:T(8,128)(2,1)}, bf16[48,2048]{1,0:T(8,128)(2,1)}, u32[]{:S(2)}, u32[]{:S(2)}) collective-permute-start(bf16[48,2048]{1,0:T(8,128)(2,1)} %get-tuple-element.46), channel_id=1, source_target_pairs={{0,6},{1,7},{2,4},{3,5},{4,2},{5,3},{6,0},{7,1},{8,14},{9,15},{10,... | collective-permute-start | bytes 589832 | tf_op jit(solution)/shard_map/ppermute | solution.py:219
  23.2 15.7 %collective-permute-start.9 = (bf16[256,768]{1,0:T(8,128)(2,1)}, bf16[256,768]{1,0:T(8,128)(2,1)}, u32[]{:S(2)}, u32[]{:S(2)}) collective-permute-start(bf16[256,768]{1,0:T(8,128)(2,1)} %slice.9), channel_id=1, source_target_pairs={{0,8},{8,0},{16,24},{24,16},{1,9},{9,1},{17,25},{25,17},{2,10},{10... | collective-permute-start | bytes 1179656 | tf_op jit(solution)/shard_map/ppermute | solution.py:216
  25.7 13.7 %collective-permute-start.8 = (bf16[256,768]{1,0:T(8,128)(2,1)}, bf16[256,768]{1,0:T(8,128)(2,1)}, u32[]{:S(2)}, u32[]{:S(2)}) collective-permute-start(bf16[256,768]{1,0:T(8,128)(2,1)} %slice.8), channel_id=1, source_target_pairs={{0,16},{8,24},{16,0},{24,8},{1,17},{9,25},{17,1},{25,9},{2,18},{10... | collective-permute-start | bytes 1179656 | tf_op jit(solution)/shard_map/ppermute | solution.py:216
  27.8 6.2 %copy-start.3 = (bf16[48,2048]{1,0:T(8,128)(2,1)S(1)}, bf16[48,2048]{1,0:T(8,128)(2,1)}, u32[]{:S(2)}) copy-start(bf16[48,2048]{1,0:T(8,128)(2,1)} %copy-done.2) | copy-start | bytes 589828
  35.3 15.1 %collective-permute-start.10 = (bf16[48,2048]{1,0:T(8,128)(2,1)S(1)}, bf16[48,2048]{1,0:T(8,128)(2,1)S(1)}, u32[]{:S(2)}, u32[]{:S(2)}) collective-permute-start(bf16[48,2048]{1,0:T(8,128)(2,1)S(1)} %get-tuple-element.57), channel_id=1, source_target_pairs={{0,4},{1,5},{2,6},{3,7},{4,0},{5,1},{6,2},{7,3},{8,12},{9,13},{10,... | collective-permute-start | bytes 589832 | tf_op jit(solution)/shard_map/ppermute | solution.py:219
  37.0 13.4 %collective-permute-start.11 = (bf16[48,2048]{1,0:T(8,128)(2,1)S(1)}, bf16[48,2048]{1,0:T(8,128)(2,1)S(1)}, u32[]{:S(2)}, u32[]{:S(2)}) collective-permute-start(bf16[48,2048]{1,0:T(8,128)(2,1)S(1)} %get-tuple-element.58), channel_id=1, source_target_pairs={{0,6},{1,7},{2,4},{3,5},{4,2},{5,3},{6,0},{7,1},{8,14},{9,15},{10,... | collective-permute-start | bytes 589832 | tf_op jit(solution)/shard_map/ppermute | solution.py:219
  38.4 12.0 %collective-permute-start.12 = (bf16[288,512]{1,0:T(8,128)(2,1)S(1)}, bf16[288,512]{1,0:T(8,128)(2,1)S(1)}, u32[]{:S(2)}, u32[]{:S(2)}) collective-permute-start(bf16[288,512]{1,0:T(8,128)(2,1)S(1)} %get-tuple-element.59), channel_id=1, source_target_pairs={{0,8},{8,0},{16,24},{24,16},{1,9},{9,1},{17,25},{25,17},{2,10},{10... | collective-permute-start | bytes 884744 | tf_op jit(solution)/shard_map/ppermute | solution.py:216
  38.9 12.4 %collective-permute-start.13 = (bf16[288,512]{1,0:T(8,128)(2,1)S(1)}, bf16[288,512]{1,0:T(8,128)(2,1)S(1)}, u32[]{:S(2)}, u32[]{:S(2)}) collective-permute-start(bf16[288,512]{1,0:T(8,128)(2,1)S(1)} %get-tuple-element.60), channel_id=1, source_target_pairs={{0,16},{8,24},{16,0},{24,8},{1,17},{9,25},{17,1},{25,9},{2,18},{10... | collective-permute-start | bytes 884744 | tf_op jit(solution)/shard_map/ppermute | solution.py:216
  39.4 11.9 %collective-permute-start.14 = (bf16[288,512]{1,0:T(8,128)(2,1)S(1)}, bf16[288,512]{1,0:T(8,128)(2,1)S(1)}, u32[]{:S(2)}, u32[]{:S(2)}) collective-permute-start(bf16[288,512]{1,0:T(8,128)(2,1)S(1)} %get-tuple-element.61), channel_id=1, source_target_pairs={{0,24},{8,16},{16,8},{24,0},{1,25},{9,17},{17,9},{25,1},{2,26},{10... | collective-permute-start | bytes 884744 | tf_op jit(solution)/shard_map/ppermute | solution.py:216
  54.0 10.0 %collective-permute-start.15 = (bf16[48,2048]{1,0:T(8,128)(2,1)S(1)}, bf16[48,2048]{1,0:T(8,128)(2,1)S(1)}, u32[]{:S(2)}, u32[]{:S(2)}) collective-permute-start(bf16[48,2048]{1,0:T(8,128)(2,1)S(1)} %get-tuple-element.63), channel_id=1, source_target_pairs={{0,2},{1,3},{2,0},{3,1},{4,6},{5,7},{6,4},{7,5},{8,10},{9,11},{10,... | collective-permute-start | bytes 589832 | tf_op jit(solution)/shard_map/ppermute | solution.py:219
  57.1 17.1 %collective-permute-start.16 = (bf16[48,2048]{1,0:T(8,128)(2,1)S(1)}, bf16[48,2048]{1,0:T(8,128)(2,1)S(1)}, u32[]{:S(2)}, u32[]{:S(2)}) collective-permute-start(bf16[48,2048]{1,0:T(8,128)(2,1)S(1)} %get-tuple-element.64), channel_id=1, source_target_pairs={{0,4},{1,5},{2,6},{3,7},{4,0},{5,1},{6,2},{7,3},{8,12},{9,13},{10,... | collective-permute-start | bytes 589832 | tf_op jit(solution)/shard_map/ppermute | solution.py:219
  58.3 15.9 %collective-permute-start.17 = (bf16[48,2048]{1,0:T(8,128)(2,1)S(1)}, bf16[48,2048]{1,0:T(8,128)(2,1)S(1)}, u32[]{:S(2)}, u32[]{:S(2)}) collective-permute-start(bf16[48,2048]{1,0:T(8,128)(2,1)S(1)} %get-tuple-element.65), channel_id=1, source_target_pairs={{0,6},{1,7},{2,4},{3,5},{4,2},{5,3},{6,0},{7,1},{8,14},{9,15},{10,... | collective-permute-start | bytes 589832 | tf_op jit(solution)/shard_map/ppermute | solution.py:219
  59.7 15.0 %collective-permute-start.19 = (bf16[384,512]{1,0:T(8,128)(2,1)S(1)}, bf16[384,512]{1,0:T(8,128)(2,1)S(1)}, u32[]{:S(2)}, u32[]{:S(2)}) collective-permute-start(bf16[384,512]{1,0:T(8,128)(2,1)S(1)} %get-tuple-element.71), channel_id=1, source_target_pairs={{0,8},{8,0},{16,24},{24,16},{1,9},{9,1},{17,25},{25,17},{2,10},{10... | collective-permute-start | bytes 1179656 | tf_op jit(solution)/shard_map/ppermute | solution.py:216
  60.2 17.6 %collective-permute-start.20 = (bf16[384,512]{1,0:T(8,128)(2,1)S(1)}, bf16[384,512]{1,0:T(8,128)(2,1)S(1)}, u32[]{:S(2)}, u32[]{:S(2)}) collective-permute-start(bf16[384,512]{1,0:T(8,128)(2,1)S(1)} %get-tuple-element.72), channel_id=1, source_target_pairs={{0,16},{8,24},{16,0},{24,8},{1,17},{9,25},{17,1},{25,9},{2,18},{10... | collective-permute-start | bytes 1179656 | tf_op jit(solution)/shard_map/ppermute | solution.py:216
  64.0 13.8 %collective-permute-start.21 = (bf16[384,512]{1,0:T(8,128)(2,1)S(1)}, bf16[384,512]{1,0:T(8,128)(2,1)S(1)}, u32[]{:S(2)}, u32[]{:S(2)}) collective-permute-start(bf16[384,512]{1,0:T(8,128)(2,1)S(1)} %shard_map.112), channel_id=1, source_target_pairs={{0,24},{8,16},{16,8},{24,0},{1,25},{9,17},{17,9},{25,1},{2,26},{10... | collective-permute-start | bytes 1179656 | tf_op jit(solution)/shard_map/ppermute | solution.py:216
  74.6 3.2 %collective-permute-start.18 = (bf16[128,2048]{1,0:T(8,128)(2,1)S(1)}, bf16[128,2048]{1,0:T(8,128)(2,1)S(1)}, u32[]{:S(2)}, u32[]{:S(2)}) collective-permute-start(bf16[128,2048]{1,0:T(8,128)(2,1)S(1)} %get-tuple-element.69), channel_id=1, source_target_pairs={{0,1},{1,0},{2,3},{3,2},{4,5},{5,4},{6,7},{7,6},{8,9},{9,8},{10,11... | collective-permute-start | bytes 1572872 | tf_op jit(solution)/shard_map/ppermute | solution.py:219
  77.9 1.8 %copy-start = (bf16[128,2048]{1,0:T(8,128)(2,1)}, bf16[128,2048]{1,0:T(8,128)(2,1)S(1)}, u32[]{:S(2)}) copy-start(bf16[128,2048]{1,0:T(8,128)(2,1)S(1)} %add.3.refs_8_) | copy-start | bytes 1572868
